TPU v7x, 128 devices: a whole 4x4x4 slice. The times are simulated.
128 devices in a mesh: dp: 8 (over z, core), dom: 16 (over x, y).
Axes of the slice: x: 4, y: 4, z: 4, core: 2. Of those that a mesh axis runs over, the one named last changes fastest.
Arguments:
- hidden: bfloat16 [2048, 16, 1024], P(('dp', 'dom')), may hold values from -6 to 6
- desc_len: int32 [2048], P(('dp', 'dom')), may hold values from 1 to 16
- w_in: bfloat16 [1024, 4096], P(None, 'dom'), may hold values from -0.1875 to 0.1875
- w_out: bfloat16 [4096, 1024], P('dom'), may hold values from -0.09375 to 0.09375
- send_order: int32 [128, 16], P(('dp', 'dom')), may hold values from 0 to 15, each once within a row
- place_order: int32 [128, 16], P(('dp', 'dom')), may hold values from 0 to 15, each once within a row
- cache: bfloat16 [30720, 1024], P(('dp', 'dom')), may hold values from -6 to 6
- halo_rows: int32 [128, 128], P(('dp', 'dom')), may hold values from 0 to 255
- edge_src: int32 [128, 2048], P(('dp', 'dom')), may hold values from 0 to 383
- edge_dst: int32 [128, 2048], P(('dp', 'dom')), may hold values from 0 to 255
- edge_rel: int32 [128, 16], P(('dp', 'dom')), may hold values from 0 to 831
- rel_table: bfloat16 [832, 1024], P('dom'), may hold values from -6 to 6
- w_msg: bfloat16 [1024, 1024], replicated, may hold values from -0.1875 to 0.1875
- w_self: bfloat16 [1024, 1024], replicated, may hold values from -0.1875 to 0.1875
- d_out: bfloat16 [32768, 1024], P(('dp', 'dom')), may hold values from -0.0625 to 0.0625
Outputs:
- graph_out: bfloat16 [32768, 1024], P(('dp', 'dom'))
- grad_w_in: float32 [1024, 4096], P(None, 'dom')
- grad_w_out: float32 [4096, 1024], P('dom')
- grad_rel: float32 [832, 1024], P('dom')
- grad_msg: float32 [1024, 1024], P(('dp', 'dom'))
- grad_self: float32 [1024, 1024], P(('dp', 'dom'))
All inputs are finite; a program needn't handle non-finite values.
Results may differ from a plain program's by a relative error of at most 0.022.
Values may be sent and summed in bfloat16 or wider, within the bound.
No kernel may reach another device: no remote copies, remote signals or barrier semaphores. Data moves between devices by JAX's collectives and lax.ppermute only.
A program may use at most 128 MiB of HBM per device.

v0:
```python
import jax
import jax.numpy as jnp
import numpy as np
from jax import lax
from jax.experimental import pallas as pl
from jax.experimental.pallas import tpu as pltpu
from jax.sharding import Mesh
from jax.sharding import PartitionSpec as P

BF = jnp.bfloat16
F32 = jnp.float32
I32 = jnp.int32
GROUP = ("x", "y")
SHIFTS = (1, 3, 2)
ORIGINS = (0, 3, 1, 2)
GELU_SCALE = float(np.sqrt(2.0 / np.pi))
GELU_CUBE = 0.044715


def shift_by(value, axis, shift):
    count = lax.axis_size(axis)
    return lax.ppermute(value, axis, [(i, (i + shift) % count) for i in range(count)])


def dot(a, b):
    return jnp.dot(a, b, preferred_element_type=F32)


def dot_t(a, b):
    return lax.dot_general(a, b, (((0,), (0,)), ((), ())), preferred_element_type=F32)


def dot_bt(a, b):
    return lax.dot_general(a, b, (((1,), (1,)), ((), ())), preferred_element_type=F32)


def one_hot(index, count):
    return (index[:, None] == jnp.arange(count, dtype=I32)[None, :]).astype(BF)


def one_hot_t(index, count):
    return (index[None, :] == jnp.arange(count, dtype=I32)[:, None]).astype(BF)


def lanes(shape):
    return lax.broadcasted_iota(I32, shape, 1)


def sublanes(shape):
    return lax.broadcasted_iota(I32, shape, 0)


def row_of(values, width):
    return jnp.pad(values.astype(BF), (0, width - values.shape[0]))[None, :]


def fresh_row(side, place):
    return (place % 4) * 16 + (side + 1) * 4 + place // 4


def local_call(body, outs, operands, scratch=(), flops=0, limit=48):
    return pl.pallas_call(
        body,
        out_shape=[jax.ShapeDtypeStruct(shape, kind) for shape, kind in outs],
        in_specs=[pl.BlockSpec(memory_space=pltpu.SMEM)]
        + [pl.BlockSpec(memory_space=pltpu.VMEM)] * (len(operands) - 1),
        out_specs=[pl.BlockSpec(memory_space=pltpu.VMEM)] * len(outs),
        scratch_shapes=list(scratch),
        compiler_params=pltpu.CompilerParams(vmem_limit_bytes=limit * 1024 * 1024),
        cost_estimate=pl.CostEstimate(flops=flops, bytes_accessed=1024 * 1024, transcendentals=0),
    )(*operands)


def length_column(meta):
    shape = meta.shape
    return jnp.sum(jnp.where(lanes(shape) == sublanes(shape), meta, 0.0), axis=1, keepdims=True)


def pool_rows(length, tokens):
    shape = (16, tokens)
    line = lanes(shape)
    inside = (line // 16 == sublanes(shape)) & ((line % 16).astype(F32) < length)
    return inside.astype(F32).astype(BF)


def norm_kernel(where_ref, hidden_ref, meta_ref, block_ref, sum_ref):
    values = hidden_ref[...].astype(F32)
    center = values - jnp.mean(values, axis=-1, keepdims=True)
    spread = jnp.mean(center * center, axis=-1, keepdims=True)
    tokens = values.shape[0]
    block_ref[0:tokens, :] = (center * lax.rsqrt(spread + 1e-05)).astype(BF)
    block_ref[tokens : tokens + 16, :] = meta_ref[...]
    pool = pool_rows(length_column(meta_ref[:, 0:128].astype(F32)), tokens)
    sum_ref[...] = dot(pool, hidden_ref[...])


def encode_kernel(
    where_ref,
    b0, b1, b2, b3,
    own_in, own_out,
    m1, m2, m3,
    o1, o2, o3,
    hidden_sum_ref,
    outgoing_ref, normed_ref, slope_ref, pooled_ref, all_out_ref, route_ref, length_ref, rel_hot_ref,
    in_ref, pool_ref,
):
    core, my_x = where_ref[1], where_ref[2]
    for s, block in enumerate((b0, b1, b2, b3)):
        normed_ref[s * 256 : (s + 1) * 256, :] = block[0:256, :]
    in_ref[:, 0:256] = own_in[...]
    all_out_ref[0:256, :] = own_out[...]
    for t, (mine, other) in enumerate(((m1, o1), (m2, o2), (m3, o3)), 1):
        for part, half in ((mine, core), (other, 1 - core)):
            for i in range(2):
                rows = pl.ds(pl.multiple_of(half * 512 + i * 256, 256), 256)
                in_ref[rows, t * 256 : (t + 1) * 256] = part[0:256, i * 256 : (i + 1) * 256]
                rows = pl.ds(pl.multiple_of(t * 256 + half * 128, 128), 128)
                all_out_ref[rows, i * 512 : (i + 1) * 512] = part[256 + i * 128 : 384 + i * 128, :]

    wide = (16, 256)
    slot = lanes(wide) % 16
    bound = lanes((128, 256))
    bound = (bound // 16 + (bound % 16) // 4 + 15) % 16
    bound_hot = (sublanes((128, 256)) == bound + 16).astype(F32).astype(BF)
    ids = jnp.zeros((16, 64), F32)
    for s, block in enumerate((b0, b1, b2, b3)):
        meta = block[256:272, 0:128]
        length = length_column(meta.astype(F32))
        length_ref[s * 16 : (s + 1) * 16, :] = jnp.broadcast_to(1.0 / length, (16, 128))
        pool_ref[s * 16 : (s + 1) * 16, :] = pool_rows(length, 256)
        sent = dot(meta, bound_hot)
        encoder = lax.rem(my_x + ORIGINS[s], 4)
        chosen = (sent == sublanes(wide).astype(F32)) & (slot % 4 == encoder) & (slot < 12)
        route_ref[s * 16 : (s + 1) * 16, :] = chosen.astype(F32).astype(BF)
        at, to = sublanes((128, 64)), lanes((128, 64)) - s * 16
        inside = (to >= 0) & (to < 16)
        select = jnp.where(inside & (at == 32 + to), 32.0, jnp.where(inside & (at == 48 + to), 1.0, 0.0))
        ids = ids + dot(meta, select.astype(BF))
    line = sublanes((512, 64))
    local = (line // 64) % 2 * 32 + (line // 16) % 4 * 8 + line % 16
    name = (my_x * 4 + line // 128) * 52 + local
    good = (line % 16 < 8) & (local < 52)
    rel_hot_ref[...] = ((name.astype(F32) == ids[0:1, :]) & good).astype(F32).astype(BF)

    @pl.loop(0, 16)
    def _(step):
        s, t = step // 4, step % 4
        rows = pl.ds(pl.multiple_of(s * 256, 256), 256)
        cols = pl.ds(pl.multiple_of(t * 256, 256), 256)
        few = pl.ds(pl.multiple_of(s * 16, 16), 16)
        pre = dot(normed_ref[rows, :], in_ref[:, cols])
        square = pre * pre
        tanh = jnp.tanh(GELU_SCALE * pre * (1.0 + GELU_CUBE * square))
        upper = 0.5 + 0.5 * tanh
        slope = upper + (0.5 * GELU_SCALE) * pre * (1.0 - tanh * tanh) * (1.0 + 3.0 * GELU_CUBE * square)
        slope_ref[rows, cols] = slope.astype(BF)
        pooled_ref[few, cols] = dot(pool_ref[few, :], (pre * upper).astype(BF)).astype(BF)

    partial = dot(pooled_ref[...], all_out_ref[...])
    partial = jnp.concatenate([partial[0:16] + hidden_sum_ref[...], partial[16:64]], axis=0)
    partial = (partial * length_ref[:, 0:1]).astype(BF)
    outgoing_ref[...] = dot_t(route_ref[...], partial).astype(BF)


def graph_kernel(
    where_ref,
    arrived_ref, base_ref, row_hot_ref, own_hot_t_ref, rel_ref,
    src_hot_ref, dst_hot_ref, dst_hot_t_ref, src_row_hot_ref,
    w_msg_ref, w_self_ref, d_out_ref,
    table_out_ref, blocks_ref, graph_out_ref, aggregate_ref, nodes_ref, pre_ref,
    ext_ref, sources_ref, edges_ref, agg_grad_ref, sums_ref,
):
    scale = (256 / 2048) ** 0.5
    total = arrived_ref[0:64, :].astype(F32)
    for i in range(1, 4):
        total = total + arrived_ref[i * 64 : (i + 1) * 64, :].astype(F32)
    table = total.astype(BF)
    ext_ref[...] = (base_ref[...].astype(F32) + dot(row_hot_ref[...], table)).astype(BF)
    nodes_ref[...] = ext_ref[0:256, :]

    @pl.loop(0, 16)
    def _(j):
        rows = pl.ds(pl.multiple_of(j * 128, 128), 128)
        taken = dot(src_hot_ref[rows, :], ext_ref[...])
        sources_ref[rows, :] = taken.astype(BF)
        edges_ref[rows, :] = (taken * rel_ref[j]).astype(BF)

    @pl.loop(0, 4)
    def _(n):
        cols = pl.ds(pl.multiple_of(n * 256, 256), 256)
        aggregate_ref[:, cols] = (scale * dot(dst_hot_t_ref[...], edges_ref[:, cols])).astype(BF)

    @pl.loop(0, 4)
    def _(n):
        cols = pl.ds(pl.multiple_of(n * 256, 256), 256)
        out_pre = dot(aggregate_ref[...], w_msg_ref[:, cols]) + dot(nodes_ref[...], w_self_ref[:, cols])
        squashed = jnp.tanh(out_pre)
        graph_out_ref[:, cols] = squashed.astype(BF)
        pre_ref[:, cols] = (d_out_ref[:, cols].astype(F32) * (1.0 - squashed * squashed)).astype(BF)

    @pl.loop(0, 4)
    def _(n):
        cols = pl.ds(pl.multiple_of(n * 256, 256), 256)
        agg_grad_ref[:, cols] = (scale * dot_bt(pre_ref[...], w_msg_ref[cols, :])).astype(BF)

    @pl.loop(0, 16)
    def _(j):
        rows = pl.ds(pl.multiple_of(j * 128, 128), 128)
        at_dest = dot(dst_hot_ref[rows, :], agg_grad_ref[...])
        edges_ref[rows, :] = (at_dest * rel_ref[j]).astype(BF)
        sums_ref[j] = jnp.sum(at_dest * sources_ref[rows, :].astype(F32), axis=0, keepdims=True)

    blocks_ref[...] = jnp.concatenate([sums_ref[j] for j in range(16)], axis=0).astype(BF)
    own_pre = dot(own_hot_t_ref[...], pre_ref[0:16, :]).astype(BF)

    @pl.loop(0, 4)
    def _(n):
        cols = pl.ds(pl.multiple_of(n * 256, 256), 256)
        grad = dot(src_row_hot_ref[...], edges_ref[:, cols]) + dot_bt(own_pre, w_self_ref[cols, :])
        table_out_ref[:, cols] = grad.astype(BF)


def back_kernel(
    where_ref,
    returned_ref, route_ref, length_ref, all_out_ref, slope_ref, pooled_ref, normed_t_ref,
    rel_hot_ref, r0, r1, r2, r3,
    kept_ref, given_ref,
    scaled_ref, grad_ref,
):
    core, my_y = where_ref[1], where_ref[3]
    scaled_ref[...] = (dot(route_ref[...], returned_ref[...]) * length_ref[:, 0:1]).astype(BF)
    blocks = jnp.concatenate([r0[...], r1[...], r2[...], r3[...]], axis=0)
    for half, chunk_ref in ((core, kept_ref), (1 - core, given_ref)):
        for y in range(4):
            rows = pl.ds(pl.multiple_of(y * 128 + half * 64, 64), 64)
            rel = dot(rel_hot_ref[rows, :], blocks).astype(BF)
            for z in range(4):
                chunk_ref[z, y, 64:80, :] = rel[z * 16 : (z + 1) * 16]

    @pl.loop(0, 4)
    def _(t):
        cols = pl.ds(pl.multiple_of(t * 256, 256), 256)
        origin = jnp.where(t == 0, 0, jnp.where(t == 1, 3, t - 1))
        owner = lax.rem(my_y + origin, 4)
        upstream = dot_bt(scaled_ref[...], all_out_ref[cols, :]).astype(BF)
        for s in range(4):
            rows = slice(s * 256, (s + 1) * 256)
            shape = (16, 256)
            line = lanes(shape)
            length = 1.0 / length_ref[s * 16 : (s + 1) * 16, 0:1]
            inside = (line // 16 == sublanes(shape)) & ((line % 16).astype(F32) + 0.5 < length)
            pool = inside.astype(F32).astype(BF)
            at_tokens = dot_t(pool, upstream[s * 16 : (s + 1) * 16])
            grad_ref[rows, :] = (slope_ref[rows, cols].astype(F32) * at_tokens).astype(BF)
        for half, chunk_ref in ((1 - core, given_ref), (core, kept_ref)):
            units = pl.ds(pl.multiple_of(t * 256 + half * 128, 128), 128)
            out = dot_t(pooled_ref[:, units], scaled_ref[...]).astype(BF)
            inner = dot(normed_t_ref[pl.ds(pl.multiple_of(half * 512, 512), 512), :], grad_ref[...]).astype(BF)
            for z in range(4):
                chunk_ref[z, owner, 32:64, :] = out[z * 32 : (z + 1) * 32]
                for i in range(4):
                    piece = inner[z * 128 + i * 32 : z * 128 + (i + 1) * 32]
                    chunk_ref[z, owner, 0:32, i * 256 : (i + 1) * 256] = piece


def place_kernel(where_ref, a0, a1, a2, a3, c0, c1, c2, c3, in_ref, out_ref, rel_ref):
    my_z, core = where_ref[0], where_ref[1]
    for pieces, half in (((a0, a1, a2, a3), core), ((c0, c1, c2, c3), 1 - core)):
        for piece, origin in zip(pieces, ORIGINS):
            z = lax.rem(my_z + origin, 4)
            values = piece[...].astype(F32)
            for i in range(4):
                rows = pl.ds(pl.multiple_of(half * 512 + z * 128 + i * 32, 32), 32)
                in_ref[rows, :] = values[0:32, i * 256 : (i + 1) * 256]
            out_ref[pl.ds(pl.multiple_of(half * 128 + z * 32, 32), 32), :] = values[32:64]
            rel_ref[pl.ds(pl.multiple_of(half * 32 + z * 8, 8), 8), :] = values[64:72]


def scatter_four(chunks, axis):
    me = lax.axis_index(axis)
    total = lax.dynamic_index_in_dim(chunks, me, 0, keepdims=False).astype(F32)
    for shift in SHIFTS:
        chunk = lax.dynamic_index_in_dim(chunks, (me + shift) % 4, 0, keepdims=False)
        total = total + shift_by(chunk, axis, shift).astype(F32)
    return total


def shards(
    hidden,
    desc_len,
    w_in,
    w_out,
    send_order,
    place_order,
    cache,
    halo_rows,
    edge_src,
    edge_dst,
    edge_rel,
    rel_table,
    w_msg,
    w_self,
    d_out,
):
    entities, length, width = hidden.shape
    tokens = entities * length
    units = w_in.shape[1]
    my_core = lax.axis_index("core")
    where = jnp.stack([lax.axis_index(name) for name in ("z", "core", "x", "y")]).astype(I32)
    src, dst, rel = edge_src[0], edge_dst[0], edge_rel[0]
    shard_rows = rel_table.shape[0]

    full_table = lax.all_gather(rel_table, GROUP, axis=0, tiled=True)

    meta = row_of(jnp.concatenate([desc_len, send_order[0], rel // 32, rel % 32]), width)
    block, hidden_sum = local_call(
        norm_kernel,
        [((tokens + 16, width), BF), ((entities, width), F32)],
        [where, hidden.reshape(tokens, width), jnp.broadcast_to(meta, (16, width))],
    )
    blocks = [block] + [shift_by(block, "x", s) for s in SHIFTS]

    half_k, half_u = width // 2, units // 2
    in_half = lax.dynamic_slice_in_dim(w_in, my_core * half_k, half_k, 0)
    out_half = lax.dynamic_slice_in_dim(w_out, my_core * half_u, half_u, 0)
    weights = jnp.concatenate(
        [
            jnp.concatenate([in_half[:units], in_half[units:]], axis=1),
            out_half[:, : 2 * units],
            out_half[:, 2 * units :],
        ],
        axis=0,
    )
    mine = [shift_by(weights, "y", s) for s in SHIFTS]
    other = [shift_by(part, "core", 1) for part in mine]

    halo = halo_rows[0]
    place = place_order[0]
    side = halo.shape[0] // 2
    cache_count = cache.shape[0]
    boundary = dot(one_hot(halo - entities, cache_count), cache).astype(BF)
    halo_hot = halo[:, None] == jnp.arange(entities, dtype=I32)[None, :]
    halo_place = jnp.where(halo < entities, jnp.sum(jnp.where(halo_hot, place[None, :], 0), axis=1), 16)

    def edge_of(rows, places):
        return jnp.concatenate([rows, jnp.pad(row_of(places, width), ((0, 15), (0, 0)))], axis=0)

    from_low = shift_by(edge_of(boundary[side:], halo_place[side:]), GROUP, 1)
    from_high = shift_by(edge_of(boundary[:side], halo_place[:side]), GROUP, 15)
    low_place = from_low[side, :side].astype(I32)
    high_place = from_high[side, :side].astype(I32)
    own_row = fresh_row(0, place)
    low_row = jnp.where(low_place < 16, fresh_row(-1, low_place), -1)
    high_row = jnp.where(high_place < 16, fresh_row(1, high_place), -1)
    table_row = jnp.concatenate([own_row, jnp.full((cache_count,), -1, I32), low_row, high_row])
    row_hot = one_hot(table_row, 64)
    base = jnp.concatenate([jnp.zeros((entities, width), BF), cache, from_low[:side], from_high[:side]], axis=0)
    node_count = entities + cache_count
    extended_count = node_count + 2 * side
    edge_count = src.shape[0]
    block_count = rel.shape[0]
    src_hot = one_hot(src, extended_count)
    src_row_hot = dot_bt(one_hot_t(table_row, 64), src_hot).astype(BF)
    rel_rows = dot(one_hot(rel, full_table.shape[0]), full_table).reshape(block_count, 1, width)

    outgoing, normed, slope, pooled, all_out, route, inverse, rel_hot = local_call(
        encode_kernel,
        [
            ((256, width), BF),
            ((4 * tokens, width), BF),
            ((4 * tokens, 4 * units), BF),
            ((4 * entities, 4 * units), BF),
            ((4 * units, width), BF),
            ((4 * entities, 256), BF),
            ((4 * entities, 128), F32),
            ((512, 64), BF),
        ],
        [where, *blocks, w_in, w_out, *mine, *other, hidden_sum],
        [pltpu.VMEM((width, 4 * units), BF), pltpu.VMEM((4 * entities, tokens), BF)],
        flops=2 * 4 * tokens * width * 4 * units,
    )
    arrived = lax.all_to_all(outgoing.reshape(16, 16, width), GROUP, 0, 0, tiled=True).reshape(256, width)
    normed_t = normed.T

    grad_table, grad_blocks, graph_out, aggregate, nodes, grad_pre = local_call(
        graph_kernel,
        [
            ((64, width), BF),
            ((block_count, width), BF),
            ((node_count, width), BF),
            ((node_count, width), BF),
            ((node_count, width), BF),
            ((node_count, width), BF),
        ],
        [
            where,
            arrived,
            base,
            row_hot,
            one_hot_t(own_row, 64),
            rel_rows,
            src_hot,
            one_hot(dst, node_count),
            one_hot_t(dst, node_count),
            src_row_hot,
            w_msg,
            w_self,
            d_out,
        ],
        [
            pltpu.VMEM((extended_count, width), BF),
            pltpu.VMEM((edge_count, width), BF),
            pltpu.VMEM((edge_count, width), BF),
            pltpu.VMEM((node_count, width), BF),
            pltpu.VMEM((block_count, 1, width), F32),
        ],
        flops=6 * 10**9,
    )

    back = jnp.broadcast_to(grad_table.reshape(1, 4, 16, width), (4, 4, 16, width))
    returned = lax.all_to_all(back.reshape(16, 16, width), GROUP, 0, 0, tiled=True).reshape(256, width)
    rel_blocks = [grad_blocks] + [shift_by(grad_blocks, "x", s) for s in SHIFTS]

    graph_grads = jnp.stack([dot_t(aggregate, grad_pre).astype(BF), dot_t(nodes, grad_pre).astype(BF)])
    graph_grads = graph_grads.reshape(2, 4, 2, 128, width)
    graph_kept = lax.dynamic_index_in_dim(graph_grads, my_core, 2, keepdims=False)
    graph_given = lax.dynamic_index_in_dim(graph_grads, 1 - my_core, 2, keepdims=False)
    chip = (graph_kept.astype(F32) + shift_by(graph_given, "core", 1).astype(F32)).astype(BF)
    line_sum = scatter_four(chip.transpose(1, 0, 2, 3), "z").astype(BF)
    plane = line_sum.reshape(2, 16, 8, width).transpose(1, 0, 2, 3).reshape(16, 16, width)
    plane = lax.all_to_all(plane, GROUP, 0, 0, tiled=True)
    weight_rows = jnp.sum(plane.astype(F32), axis=0)
    grad_msg, grad_self = weight_rows[:8], weight_rows[8:]

    kept, given = local_call(
        back_kernel,
        [((4, 4, 80, width), BF), ((4, 4, 80, width), BF)],
        [where, returned, route, inverse, all_out, slope, pooled, normed_t, rel_hot, *rel_blocks],
        [pltpu.VMEM((4 * entities, width), BF), pltpu.VMEM((4 * tokens, units), BF)],
        flops=2 * 4 * tokens * width * 4 * units,
    )
    chunks = (kept.astype(F32) + shift_by(given, "core", 1).astype(F32)).astype(BF)
    chunks = lax.all_to_all(chunks.reshape(16, 80, width), ("z", "y"), 0, 0, tiled=True)
    part = jnp.sum(chunks.astype(F32), axis=0).astype(BF)
    parts = [part] + [shift_by(part, "z", s) for s in SHIFTS]
    others = [shift_by(piece, "core", 1) for piece in parts]
    grad_w_in, grad_w_out, grad_rel = local_call(
        place_kernel,
        [((width, units), F32), ((units, width), F32), ((64, width), F32)],
        [where, *parts, *others],
    )
    return (graph_out, grad_w_in, grad_w_out, grad_rel[:shard_rows], grad_msg, grad_self)


def solution(mesh):
    fine = Mesh(mesh.devices.reshape(4, 2, 4, 4), ("z", "core", "x", "y"))
    every = ("z", "core", "x", "y")
    placed = (
        P(every, None, None),
        P(every),
        P(None, GROUP),
        P(GROUP, None),
        P(every, None),
        P(every, None),
        P(every, None),
        P(every, None),
        P(every, None),
        P(every, None),
        P(every, None),
        P(GROUP, None),
        P(),
        P(),
        P(every, None),
    )
    return jax.shard_map(
        shards,
        mesh=fine,
        in_specs=placed,
        out_specs=(
            P(every, None),
            P(None, GROUP),
            P(GROUP, None),
            P(GROUP, None),
            P(every, None),
            P(every, None),
        ),
        check_vma=False,
    )
```

profile of v0, /device:TPU:0, one launch (start us, length us, event | category | flops | bytes accessed | tf_op | source)
XLA Modules:
  0.0 270.6 jit_solution(6139833969235849563)
XLA Ops:
  7.3 1.1 constant_dynamic-slice_fusion
  8.4 1.0 constant_dynamic-slice_fusion.1
  9.4 1.7 collective-permute-start.3
  11.1 1.6 collective-permute-start.4
  12.7 2.1 collective-permute-start.5
  15.0 1.7 shard_map.190
  16.7 1.5 collective-permute-start
  18.8 2.3 collective-permute-start.10
  21.7 1.4 fusion.2.src_hot_ref
  23.2 17.3 %collective-permute-done.10 = bf16[80,1024]{1,0:T(8,128)(2,1)S(1)} collective-permute-done((bf16[80,1024]{1,0:T(8,128)(2,1)S(1)}, bf16[80,1024]{1,0:T(8,128)(2,1)S(1)}, u32[]{:S(2)}, u32[]{:S(2)}) %collective-permute-start.10) | collective-permute-done | bytes 163872 | tf_op jit(solution)/shard_map/ppermute | solution.py:22
  40.5 1.7 collective-permute-start.9
  42.2 7.0 %collective-permute-done.9 = bf16[80,1024]{1,0:T(8,128)(2,1)S(1)} collective-permute-done((bf16[80,1024]{1,0:T(8,128)(2,1)S(1)}, bf16[80,1024]{1,0:T(8,128)(2,1)S(1)}, u32[]{:S(2)}, u32[]{:S(2)}) %collective-permute-start.9) | collective-permute-done | bytes 163872 | tf_op jit(solution)/shard_map/ppermute | solution.py:22
  49.1 1.7 collective-permute-start.1
  50.9 0.7 collective-permute-start.2
  52.3 1.5 fusion.3.src_row_hot_ref
  54.0 18.3 %collective-permute-done.1.b2 = bf16[272,1024]{1,0:T(8,128)(2,1)S(1)} collective-permute-done((bf16[272,1024]{1,0:T(8,128)(2,1)}, bf16[272,1024]{1,0:T(8,128)(2,1)S(1)}, u32[]{:S(2)}, u32[]{:S(2)}) %collective-permute-start.1) | collective-permute-done | bytes 557088 | tf_op jit(solution)/shard_map/ppermute | solution.py:22
  72.3 0.8 copy-done.31
  73.3 13.8 %shard_map.191 = (bf16[256,1024]{1,0:T(8,128)(2,1)}, bf16[1024,1024]{1,0:T(8,128)(2,1)}, bf16[1024,1024]{1,0:T(8,128)(2,1)}, bf16[64,1024]{1,0:T(8,128)(2,1)S(1)...) custom-call(s32[4]{0:T(128)S(1)} %pad_add_fusion.1.where_ref, ...), custom_call_target="tpu_custom_call" | custom-call | flops 2147483648 | bytes 1048576 | tf_op jit(solution)/shard_map/pallas_call | solution.py:62
  87.1 0.7 copy-done.16
  87.8 0.6 copy-done.18
  89.6 12.4 %all-to-all-start = ((bf16[16,16,1024]{2,1,0:T(8,128)(2,1)}), bf16[16,16,1024]{2,1,0:T(8,128)(2,1)S(1)}, u32[]{:S(2)}, u32[]{:S(2)}) async-start(bf16[16,16,1024]{2,1,0:T(8,128)(2,1)} %bitcast.7), calls=%async_computation | async-start | bytes 1048576 | tf_op jit(solution)/shard_map/all_to_all | solution.py:382
  102.2 3.5 %reshape.88 = bf16[832,1024]{1,0:T(8,128)(2,1)} reshape(bf16[16,52,1024]{2,1,0:T(8,128)(2,1)} %all-gather.3.cloned.1.call-done) | data formatting | bytes 3407872
  105.7 1.8 fusion.19
  107.6 0.7 reshape.77.rel_ref
  108.2 3.9 %all-to-all-done = bf16[16,16,1024]{2,1,0:T(8,128)(2,1)S(1)} async-done(((bf16[16,16,1024]{2,1,0:T(8,128)(2,1)}), bf16[16,16,1024]{2,1,0:T(8,128)(2,1)S(1)}, u32[]{:S(2)}, u32[]{:S(2)}) %all-to-all-start) | async-done | bytes 524320 | tf_op jit(solution)/shard_map/all_to_all | solution.py:382
  112.2 0.8 copy-done.1
  113.0 1.0 copy-done.2
  114.0 0.8 copy-done.9
  114.9 1.0 copy-done.10
  115.9 0.9 copy-done.15
  116.9 19.9 %shard_map.192 = (bf16[64,1024]{1,0:T(8,128)(2,1)S(1)}, bf16[16,1024]{1,0:T(8,128)(2,1)S(1)}, bf16[256,1024]{1,0:T(8,128)(2,1)}, bf16[256,1024]{1,0:T(8,128)(2,1...) custom-call(s32[4]{0:T(128)S(1)} %pad_add_fusion.1.where_ref, bf16[256,1024]{1,0:T(8,128)(2,1)S(1)} %bitcast.80, ...), custom_call_target="tpu_custom_call" | custom-call | flops 6000000000 | bytes 1048576 | tf_op jit(solution)/shard_map/pallas_call | solution.py:62
  136.7 0.8 copy-done.3
  137.5 0.8 copy-done.5
  138.3 0.9 broadcast_in_dim.66
  139.2 3.6 %all-to-all-start.1 = ((bf16[16,16,1024]{2,1,0:T(8,128)(2,1)}), bf16[16,16,1024]{2,1,0:T(8,128)(2,1)S(1)}, u32[]{:S(2)}, u32[]{:S(2)}) async-start(bf16[16,16,1024]{2,1,0:T(8,128)(2,1)} %bitcast.20), calls=%async_computation.1 | async-start | bytes 1048576 | tf_op jit(solution)/shard_map/all_to_all | solution.py:421
  142.7 1.8 collective-permute-start.11
  144.6 1.5 collective-permute-start.12
  146.1 2.0 collective-permute-start.13
  148.2 4.0 %copy.31 = bf16[1024,1024]{0,1:T(8,128)(2,1)} copy(bf16[1024,1024]{1,0:T(8,128)(2,1)} %get-tuple-element.37) | data formatting | bytes 4194304 | tf_op jit(solution)/shard_map/pallas_call | solution.py:62
  152.8 1.6 copy-done.13
  154.4 1.6 copy-done.14
  156.0 10.3 %shard_map.193 = (bf16[4,4,80,1024]{3,2,1,0:T(8,128)(2,1)}, bf16[4,4,80,1024]{3,2,1,0:T(8,128)(2,1)}) custom-call(s32[4]{0:T(128)S(1)} %pad_add_fusion.1.where_ref, bf16[256,1024]{1,0:T(8,128)(2,1)S(1)} %bitcast.79, bf16[64,256]{1,0:T(8,128)(2,1)S(1)} %copy-done.21, f32[64,128]{1,0:T(8,128)S(1)} %copy-done.23, bf16[1024,1024]{1,0:T(8,128)(2,1)S(1)} %copy-done.14, ...), custom_call_target="tpu_custom_call" | custom-call | flops 2147483648 | bytes 1048576 | tf_op jit(solution)/shard_map/pallas_call | solution.py:62
  166.4 0.7 convolution_convert_fusion.1
  167.4 0.7 convolution_convert_fusion
  168.2 1.7 fusion.5
  169.9 1.5 copy.43
  171.6 0.7 copy-done.24
  172.3 4.5 %add_convert_fusion = bf16[4,4,80,1024]{3,2,1,0:T(8,128)(2,1)} fusion(bf16[4,4,80,1024]{3,2,1,0:T(8,128)(2,1)} %collective-permute-done.14, bf16[4,4,80,1024]{3,2,1,0:T(8,128)(2,1)S(1)} %copy-done.24), kind=kLoop, calls=%fused_computation | loop fusion | flops 5242880 | bytes 7864320 | tf_op jit(solution)/shard_map/convert_element_type | solution.py:442
  176.8 7.4 %all-to-all-start.2 = ((bf16[16,80,1024]{2,1,0:T(8,128)(2,1)}), bf16[16,80,1024]{2,1,0:T(8,128)(2,1)S(1)}, u32[]{:S(2)}, u32[]{:S(2)}) async-start(bf16[16,80,1024]{2,1,0:T(8,128)(2,1)} %bitcast.82), calls=%async_computation.2 | async-start | bytes 5242880 | tf_op jit(solution)/shard_map/all_to_all | solution.py:443
  184.3 4.6 %fusion = bf16[2,4,128,1024]{3,2,0,1:T(8,128)(2,1)} fusion(bf16[2,4,128,1024]{3,2,0,1:T(8,128)(2,1)} %collective-permute-done.22, bf16[2,4,1,128,1024]{4,3,2,1,0:T(8,128)(2,1)} %get-tuple-element.48), kind=kLoop, calls=%fused_computation.6 | loop fusion | flops 4194304 | bytes 6291456 | tf_op jit(solution)/shard_map/convert_element_type | solution.py:428
  188.9 2.5 dynamic-slice_bitcast_fusion.2
  191.4 3.4 %collective-permute-start.25 = (bf16[2,128,1024]{2,1,0:T(8,128)(2,1)}, bf16[2,128,1024]{2,1,0:T(8,128)(2,1)}, u32[]{:S(2)}, u32[]{:S(2)}) collective-permute-start(bf16[2,128,1024]{2,1,0:T(8,128)(2,1)} %get-tuple-element.51), channel_id=1, source_target_pairs={{0,64},{32,96},{64,0},{96,32},{1,65},{33,97},{65,1},{97,33},{2,66}... | collective-permute-start | bytes 1572872 | tf_op jit(solution)/shard_map/ppermute | solution.py:22
  194.8 1.2 collective-permute-start.24
  196.0 0.9 collective-permute-start.23
  196.9 32.2 %collective-permute-done.25 = bf16[2,128,1024]{2,1,0:T(8,128)(2,1)} collective-permute-done((bf16[2,128,1024]{2,1,0:T(8,128)(2,1)}, bf16[2,128,1024]{2,1,0:T(8,128)(2,1)}, u32[]{:S(2)}, u32[]{:S(2)}) %collective-permute-start.25) | collective-permute-done | bytes 524320 | tf_op jit(solution)/shard_map/ppermute | solution.py:22
  229.1 9.0 %collective-permute-done.24 = bf16[2,128,1024]{2,1,0:T(8,128)(2,1)} collective-permute-done((bf16[2,128,1024]{2,1,0:T(8,128)(2,1)}, bf16[2,128,1024]{2,1,0:T(8,128)(2,1)}, u32[]{:S(2)}, u32[]{:S(2)}) %collective-permute-start.24) | collective-permute-done | bytes 524320 | tf_op jit(solution)/shard_map/ppermute | solution.py:22
  238.1 1.0 collective-permute-done.23
  239.1 2.7 copy_bitcast_fusion.2
  241.8 5.3 %all-to-all-start.3 = ((bf16[16,16,1024]{2,1,0:T(8,128)(2,1)}), bf16[16,16,1024]{2,1,0:T(8,128)(2,1)S(1)}, u32[]{:S(2)}, u32[]{:S(2)}) async-start(bf16[16,16,1024]{2,1,0:T(8,128)(2,1)} %copy_bitcast_fusion.2), calls=%async_computation.3 | async-start | bytes 1048576 | tf_op jit(solution)/shard_map/all_to_all | solution.py:431
  247.8 3.0 %collective-permute-start.16 = (bf16[80,1024]{1,0:T(8,128)(2,1)S(1)}, bf16[80,1024]{1,0:T(8,128)(2,1)S(1)}, u32[]{:S(2)}, u32[]{:S(2)}) collective-permute-start(bf16[80,1024]{1,0:T(8,128)(2,1)S(1)} %reduce_sum.31.a0), channel_id=1, source_target_pairs={{0,96},{32,0},{64,32},{96,64},{1,97},{33,1},{65,33},{97,65},{2,98}... | collective-permute-start | bytes 491528 | tf_op jit(solution)/shard_map/ppermute | solution.py:22
  250.9 1.5 collective-permute-start.17
  252.4 6.3 %all-to-all-done.3 = bf16[16,16,1024]{2,1,0:T(8,128)(2,1)S(1)} async-done(((bf16[16,16,1024]{2,1,0:T(8,128)(2,1)}), bf16[16,16,1024]{2,1,0:T(8,128)(2,1)S(1)}, u32[]{:S(2)}, u32[]{:S(2)}) %all-to-all-start.3) | async-done | bytes 524320 | tf_op jit(solution)/shard_map/all_to_all | solution.py:431
  261.0 2.0 shard_map.194
  263.0 0.7 slice.59
  (130 shorter events, 8.2 us)
Async XLA Ops:
  7.2 7.6 %copy-start.30 = (s32[1,16]{1,0:T(1,128)S(1)}, s32[1,16]{1,0:T(1,128)}, u32[]{:S(2)}) copy-start(s32[1,16]{1,0:T(1,128)} %param.25) | copy-start | bytes 196
  7.2 7.6 %copy-start.33 = (s32[1,16]{1,0:T(1,128)S(1)}, s32[1,16]{1,0:T(1,128)}, u32[]{:S(2)}) copy-start(s32[1,16]{1,0:T(1,128)} %param.19) | copy-start | bytes 196
  7.2 7.6 %copy-start.34 = (s32[16]{0:T(128)S(1)}, s32[16]{0:T(128)}, u32[]{:S(2)}) copy-start(s32[16]{0:T(128)} %param.16) | copy-start | bytes 196
  7.2 7.8 %copy-start = (bf16[16,16,1024]{2,1,0:T(8,128)(2,1)S(1)}, bf16[16,16,1024]{2,1,0:T(8,128)(2,1)}, u32[]{:S(2)}) copy-start(bf16[16,16,1024]{2,1,0:T(8,128)(2,1)} %param.15) | copy-start | bytes 1572868
  7.2 11.0 %copy-start.35 = (s32[1,16]{1,0:T(1,128)S(1)}, s32[1,16]{1,0:T(1,128)}, u32[]{:S(2)}) copy-start(s32[1,16]{1,0:T(1,128)} %param.20) | copy-start | bytes 196
  7.2 11.0 %copy-start.29 = (s32[1,128]{1,0:T(1,128)S(1)}, s32[1,128]{1,0:T(1,128)}, u32[]{:S(2)}) copy-start(s32[1,128]{1,0:T(1,128)} %param.22) | copy-start | bytes 1540
  7.2 11.2 %copy-start.25 = (bf16[240,1024]{1,0:T(8,128)(2,1)S(1)}, bf16[240,1024]{1,0:T(8,128)(2,1)}, u32[]{:S(2)}) copy-start(bf16[240,1024]{1,0:T(8,128)(2,1)} %param.21) | copy-start | bytes 1474564
  7.2 95.0 %all-gather.3.cloned.1.call-start = ((), (), s32[]{:S(2)}) async-start(), calls=%async_computation.4 | async-start | bytes 1949696 | tf_op jit(solution)/shard_map/all_gather | solution.py:313
  8.4 12.8 %copy-start.27 = (s32[1,2048]{1,0:T(1,128)S(1)}, s32[1,2048]{1,0:T(1,128)}, u32[]{:S(2)}) copy-start(s32[1,2048]{1,0:T(1,128)} %param.24) | copy-start | bytes 24580
  9.4 41.5 %collective-permute-start.3 = (bf16[512,512]{1,0:T(8,128)(2,1)S(1)}, bf16[512,512]{1,0:T(8,128)(2,1)}, u32[]{:S(2)}, u32[]{:S(2)}) collective-permute-start(bf16[512,512]{1,0:T(8,128)(2,1)S(1)} %pad_maximum_fusion.1), channel_id=1, source_target_pairs={{0,1},{1,2},{2,3},{3,0},{4,5},{5,6},{6,7},{7,4},{8,9},{9,10},{10,1... | collective-permute-start | bytes 1572872 | tf_op jit(solution)/shard_map/ppermute | solution.py:22
  11.1 40.5 %collective-permute-start.4 = (bf16[512,512]{1,0:T(8,128)(2,1)S(1)}, bf16[512,512]{1,0:T(8,128)(2,1)}, u32[]{:S(2)}, u32[]{:S(2)}) collective-permute-start(bf16[512,512]{1,0:T(8,128)(2,1)S(1)} %pad_maximum_fusion.1), channel_id=1, source_target_pairs={{0,3},{1,0},{2,1},{3,2},{4,7},{5,4},{6,5},{7,6},{8,11},{9,8},{10,9... | collective-permute-start | bytes 1572872 | tf_op jit(solution)/shard_map/ppermute | solution.py:22
  12.7 38.9 %collective-permute-start.5 = (bf16[512,512]{1,0:T(8,128)(2,1)S(1)}, bf16[512,512]{1,0:T(8,128)(2,1)}, u32[]{:S(2)}, u32[]{:S(2)}) collective-permute-start(bf16[512,512]{1,0:T(8,128)(2,1)S(1)} %pad_maximum_fusion.1), channel_id=1, source_target_pairs={{0,2},{1,3},{2,0},{3,1},{4,6},{5,7},{6,4},{7,5},{8,10},{9,11},{10,... | collective-permute-start | bytes 1572872 | tf_op jit(solution)/shard_map/ppermute | solution.py:22
  15.0 6.7 %copy-start.28 = (s32[1,2048]{1,0:T(1,128)S(1)}, s32[1,2048]{1,0:T(1,128)}, u32[]{:S(2)}) copy-start(s32[1,2048]{1,0:T(1,128)} %param.23) | copy-start | bytes 24580
  16.7 35.4 %collective-permute-start = (bf16[272,1024]{1,0:T(8,128)(2,1)}, bf16[272,1024]{1,0:T(8,128)(2,1)}, u32[]{:S(2)}, u32[]{:S(2)}) collective-permute-start(bf16[272,1024]{1,0:T(8,128)(2,1)} %get-tuple-element.27.b0), channel_id=1, source_target_pairs={{0,4},{4,8},{8,12},{12,0},{1,5},{5,9},{9,13},{13,1},{2,6},{6,10},{... | collective-permute-start | bytes 1671176 | tf_op jit(solution)/shard_map/ppermute | solution.py:22
  18.8 21.7 %collective-permute-start.10 = (bf16[80,1024]{1,0:T(8,128)(2,1)S(1)}, bf16[80,1024]{1,0:T(8,128)(2,1)S(1)}, u32[]{:S(2)}, u32[]{:S(2)}) collective-permute-start(bf16[80,1024]{1,0:T(8,128)(2,1)S(1)} %fusion.17), channel_id=1, source_target_pairs={{0,15},{1,0},{2,1},{3,2},{4,3},{5,4},{6,5},{7,6},{8,7},{9,8},{10,9... | collective-permute-start | bytes 491528 | tf_op jit(solution)/shard_map/ppermute | solution.py:22
  21.5 32.3 %copy-start.26 = (bf16[240,1024]{1,0:T(8,128)(2,1)S(1)}, bf16[240,1024]{1,0:T(8,128)(2,1)}, u32[]{:S(2)}) copy-start(bf16[240,1024]{1,0:T(8,128)(2,1)} %param.21) | copy-start | bytes 1474564
  23.1 50.1 %copy-start.7 = (bf16[1024,256]{1,0:T(8,128)(2,1)S(1)}, bf16[1024,256]{1,0:T(8,128)(2,1)}, u32[]{:S(2)}) copy-start(bf16[1024,256]{1,0:T(8,128)(2,1)} %own_in.1) | copy-start | bytes 1572868
  23.1 50.1 %copy-start.8 = (bf16[256,1024]{1,0:T(8,128)(2,1)S(1)}, bf16[256,1024]{1,0:T(8,128)(2,1)}, u32[]{:S(2)}) copy-start(bf16[256,1024]{1,0:T(8,128)(2,1)} %own_out.1) | copy-start | bytes 1572868
  40.5 8.6 %collective-permute-start.9 = (bf16[80,1024]{1,0:T(8,128)(2,1)S(1)}, bf16[80,1024]{1,0:T(8,128)(2,1)S(1)}, u32[]{:S(2)}, u32[]{:S(2)}) collective-permute-start(bf16[80,1024]{1,0:T(8,128)(2,1)S(1)} %fusion.16), channel_id=1, source_target_pairs={{0,1},{1,2},{2,3},{3,4},{4,5},{5,6},{6,7},{7,8},{8,9},{9,10},{10,1... | collective-permute-start | bytes 491528 | tf_op jit(solution)/shard_map/ppermute | solution.py:22
  49.1 23.1 %collective-permute-start.1 = (bf16[272,1024]{1,0:T(8,128)(2,1)}, bf16[272,1024]{1,0:T(8,128)(2,1)S(1)}, u32[]{:S(2)}, u32[]{:S(2)}) collective-permute-start(bf16[272,1024]{1,0:T(8,128)(2,1)} %get-tuple-element.27.b0), channel_id=1, source_target_pairs={{0,12},{4,0},{8,4},{12,8},{1,13},{5,1},{9,5},{13,9},{2,14},{6,2},{... | collective-permute-start | bytes 1671176 | tf_op jit(solution)/shard_map/ppermute | solution.py:22
  50.9 21.4 %collective-permute-start.2 = (bf16[272,1024]{1,0:T(8,128)(2,1)}, bf16[272,1024]{1,0:T(8,128)(2,1)S(1)}, u32[]{:S(2)}, u32[]{:S(2)}) collective-permute-start(bf16[272,1024]{1,0:T(8,128)(2,1)} %get-tuple-element.27.b0), channel_id=1, source_target_pairs={{0,8},{4,12},{8,0},{12,4},{1,9},{5,13},{9,1},{13,5},{2,10},{6,14},... | collective-permute-start | bytes 1671176 | tf_op jit(solution)/shard_map/ppermute | solution.py:22
  51.6 20.7 %collective-permute-start.6 = (bf16[512,512]{1,0:T(8,128)(2,1)}, bf16[512,512]{1,0:T(8,128)(2,1)S(1)}, u32[]{:S(2)}, u32[]{:S(2)}) collective-permute-start(bf16[512,512]{1,0:T(8,128)(2,1)} %collective-permute-done.3.m1), channel_id=1, source_target_pairs={{0,16},{16,0},{1,17},{17,1},{2,18},{18,2},{3,19},{19,3},{4,20},{20... | collective-permute-start | bytes 1572872 | tf_op jit(solution)/shard_map/ppermute | solution.py:22
  51.6 20.7 %collective-permute-start.7 = (bf16[512,512]{1,0:T(8,128)(2,1)}, bf16[512,512]{1,0:T(8,128)(2,1)S(1)}, u32[]{:S(2)}, u32[]{:S(2)}) collective-permute-start(bf16[512,512]{1,0:T(8,128)(2,1)} %collective-permute-done.4.m2), channel_id=1, source_target_pairs={{0,16},{16,0},{1,17},{17,1},{2,18},{18,2},{3,19},{19,3},{4,20},{20... | collective-permute-start | bytes 1572872 | tf_op jit(solution)/shard_map/ppermute | solution.py:22
  52.1 20.2 %collective-permute-start.8 = (bf16[512,512]{1,0:T(8,128)(2,1)}, bf16[512,512]{1,0:T(8,128)(2,1)S(1)}, u32[]{:S(2)}, u32[]{:S(2)}) collective-permute-start(bf16[512,512]{1,0:T(8,128)(2,1)} %collective-permute-done.5.m3), channel_id=1, source_target_pairs={{0,16},{16,0},{1,17},{17,1},{2,18},{18,2},{3,19},{19,3},{4,20},{20... | collective-permute-start | bytes 1572872 | tf_op jit(solution)/shard_map/ppermute | solution.py:22
  72.3 0.8 copy-start.31
  72.3 1.0 copy-start.32
  87.1 0.7 copy-start.16
  89.6 22.5 %all-to-all-start = ((bf16[16,16,1024]{2,1,0:T(8,128)(2,1)}), bf16[16,16,1024]{2,1,0:T(8,128)(2,1)S(1)}, u32[]{:S(2)}, u32[]{:S(2)}) async-start(bf16[16,16,1024]{2,1,0:T(8,128)(2,1)} %bitcast.7), calls=%async_computation | async-start | bytes 1048576 | tf_op jit(solution)/shard_map/all_to_all | solution.py:382
  112.2 0.8 copy-start.1
  113.0 1.0 copy-start.2
  114.0 0.8 copy-start.9
  114.9 1.0 copy-start.10
  115.9 0.9 copy-start.15
  136.7 0.8 copy-start.3
  137.5 0.8 copy-start.5
  138.3 0.9 copy-start.11
  139.2 13.6 %all-to-all-start.1 = ((bf16[16,16,1024]{2,1,0:T(8,128)(2,1)}), bf16[16,16,1024]{2,1,0:T(8,128)(2,1)S(1)}, u32[]{:S(2)}, u32[]{:S(2)}) async-start(bf16[16,16,1024]{2,1,0:T(8,128)(2,1)} %bitcast.20), calls=%async_computation.1 | async-start | bytes 1048576 | tf_op jit(solution)/shard_map/all_to_all | solution.py:421
  142.7 9.4 %collective-permute-start.11 = (bf16[16,1024]{1,0:T(8,128)(2,1)}, bf16[16,1024]{1,0:T(8,128)(2,1)S(1)}, u32[]{:S(2)}, u32[]{:S(2)}) collective-permute-start(bf16[16,1024]{1,0:T(8,128)(2,1)} %copy-done.11), channel_id=1, source_target_pairs={{0,4},{4,8},{8,12},{12,0},{1,5},{5,9},{9,13},{13,1},{2,6},{6,10},{... | collective-permute-start | bytes 98312 | tf_op jit(solution)/shard_map/ppermute | solution.py:22
  144.6 7.6 %collective-permute-start.12 = (bf16[16,1024]{1,0:T(8,128)(2,1)}, bf16[16,1024]{1,0:T(8,128)(2,1)S(1)}, u32[]{:S(2)}, u32[]{:S(2)}) collective-permute-start(bf16[16,1024]{1,0:T(8,128)(2,1)} %copy-done.11), channel_id=1, source_target_pairs={{0,12},{4,0},{8,4},{12,8},{1,13},{5,1},{9,5},{13,9},{2,14},{6,2},{... | collective-permute-start | bytes 98312 | tf_op jit(solution)/shard_map/ppermute | solution.py:22
  146.1 6.1 %collective-permute-start.13 = (bf16[16,1024]{1,0:T(8,128)(2,1)}, bf16[16,1024]{1,0:T(8,128)(2,1)S(1)}, u32[]{:S(2)}, u32[]{:S(2)}) collective-permute-start(bf16[16,1024]{1,0:T(8,128)(2,1)} %copy-done.11), channel_id=1, source_target_pairs={{0,8},{4,12},{8,0},{12,4},{1,9},{5,13},{9,1},{13,5},{2,10},{6,14},... | collective-permute-start | bytes 98312 | tf_op jit(solution)/shard_map/ppermute | solution.py:22
  148.1 4.7 %copy-start.12 = (bf16[16,1024]{1,0:T(8,128)(2,1)S(1)}, bf16[16,1024]{1,0:T(8,128)(2,1)}, u32[]{:S(2)}) copy-start(bf16[16,1024]{1,0:T(8,128)(2,1)} %copy-done.11) | copy-start | bytes 98308
  148.1 4.7 %copy-start.17 = (bf16[64,1024]{1,0:T(8,128)(2,1)S(1)}, bf16[64,1024]{1,0:T(8,128)(2,1)}, u32[]{:S(2)}) copy-start(bf16[64,1024]{1,0:T(8,128)(2,1)} %copy-done.16) | copy-start | bytes 393220
  148.1 4.7 %copy-start.19 = (bf16[512,64]{1,0:T(8,128)(2,1)S(1)}, bf16[512,64]{1,0:T(8,128)(2,1)}, u32[]{:S(2)}) copy-start(bf16[512,64]{1,0:T(8,128)(2,1)} %copy-done.18) | copy-start | bytes 196612
  148.1 4.7 %copy-start.21 = (bf16[64,256]{1,0:T(8,128)(2,1)S(1)}, bf16[64,256]{1,0:T(8,128)(2,1)}, u32[]{:S(2)}) copy-start(bf16[64,256]{1,0:T(8,128)(2,1)} %copy-done.20) | copy-start | bytes 98308
  148.1 4.7 %copy-start.23 = (f32[64,128]{1,0:T(8,128)S(1)}, f32[64,128]{1,0:T(8,128)}, u32[]{:S(2)}) copy-start(f32[64,128]{1,0:T(8,128)} %copy-done.22) | copy-start | bytes 98308
  152.8 1.6 copy-start.13
  154.4 1.6 copy-start.14
  156.0 10.3 %copy-start.6 = (bf16[256,1024]{1,0:T(8,128)(2,1)S(1)}, bf16[256,1024]{1,0:T(8,128)(2,1)}, u32[]{:S(2)}) copy-start(bf16[256,1024]{1,0:T(8,128)(2,1)} %copy-done.5) | copy-start | bytes 1572868
  166.4 1.0 copy-start.4
  166.4 5.3 %collective-permute-start.14 = (bf16[4,4,80,1024]{3,2,1,0:T(8,128)(2,1)}, bf16[4,4,80,1024]{3,2,1,0:T(8,128)(2,1)}, u32[]{:S(2)}, u32[]{:S(2)}) collective-permute-start(bf16[4,4,80,1024]{3,2,1,0:T(8,128)(2,1)} %get-tuple-element.41), channel_id=1, source_target_pairs={{0,16},{16,0},{1,17},{17,1},{2,18},{18,2},{3,19},{19,3},{4,20},{20... | collective-permute-start | bytes 7864328 | tf_op jit(solution)/shard_map/ppermute | solution.py:22
  169.8 2.5 copy-start.24
  171.3 13.0 %collective-permute-start.22 = (bf16[2,4,128,1024]{3,2,0,1:T(8,128)(2,1)}, bf16[2,4,128,1024]{3,2,0,1:T(8,128)(2,1)}, u32[]{:S(2)}, u32[]{:S(2)}) collective-permute-start(bf16[2,4,128,1024]{3,2,0,1:T(8,128)(2,1)} %bitcast.77), channel_id=1, source_target_pairs={{0,16},{16,0},{1,17},{17,1},{2,18},{18,2},{3,19},{19,3},{4,20},{20... | collective-permute-start | bytes 6291464 | tf_op jit(solution)/shard_map/ppermute | solution.py:22
  176.8 64.9 %all-to-all-start.2 = ((bf16[16,80,1024]{2,1,0:T(8,128)(2,1)}), bf16[16,80,1024]{2,1,0:T(8,128)(2,1)S(1)}, u32[]{:S(2)}, u32[]{:S(2)}) async-start(bf16[16,80,1024]{2,1,0:T(8,128)(2,1)} %bitcast.82), calls=%async_computation.2 | async-start | bytes 5242880 | tf_op jit(solution)/shard_map/all_to_all | solution.py:443
  191.4 37.6 %collective-permute-start.25 = (bf16[2,128,1024]{2,1,0:T(8,128)(2,1)}, bf16[2,128,1024]{2,1,0:T(8,128)(2,1)}, u32[]{:S(2)}, u32[]{:S(2)}) collective-permute-start(bf16[2,128,1024]{2,1,0:T(8,128)(2,1)} %get-tuple-element.51), channel_id=1, source_target_pairs={{0,64},{32,96},{64,0},{96,32},{1,65},{33,97},{65,1},{97,33},{2,66}... | collective-permute-start | bytes 1572872 | tf_op jit(solution)/shard_map/ppermute | solution.py:22
  194.8 43.3 %collective-permute-start.24 = (bf16[2,128,1024]{2,1,0:T(8,128)(2,1)}, bf16[2,128,1024]{2,1,0:T(8,128)(2,1)}, u32[]{:S(2)}, u32[]{:S(2)}) collective-permute-start(bf16[2,128,1024]{2,1,0:T(8,128)(2,1)} %get-tuple-element.52), channel_id=1, source_target_pairs={{0,96},{32,0},{64,32},{96,64},{1,97},{33,1},{65,33},{97,65},{2,98}... | collective-permute-start | bytes 1572872 | tf_op jit(solution)/shard_map/ppermute | solution.py:22
  196.0 43.1 %collective-permute-start.23 = (bf16[2,128,1024]{2,1,0:T(8,128)(2,1)S(1)}, bf16[2,128,1024]{2,1,0:T(8,128)(2,1)}, u32[]{:S(2)}, u32[]{:S(2)}) collective-permute-start(bf16[2,128,1024]{2,1,0:T(8,128)(2,1)S(1)} %get-tuple-element.50), channel_id=1, source_target_pairs={{0,32},{32,64},{64,96},{96,0},{1,33},{33,65},{65,97},{97,1},{2,34}... | collective-permute-start | bytes 1572872 | tf_op jit(solution)/shard_map/ppermute | solution.py:22
  241.8 17.0 %all-to-all-start.3 = ((bf16[16,16,1024]{2,1,0:T(8,128)(2,1)}), bf16[16,16,1024]{2,1,0:T(8,128)(2,1)S(1)}, u32[]{:S(2)}, u32[]{:S(2)}) async-start(bf16[16,16,1024]{2,1,0:T(8,128)(2,1)} %copy_bitcast_fusion.2), calls=%async_computation.3 | async-start | bytes 1048576 | tf_op jit(solution)/shard_map/all_to_all | solution.py:431
  247.6 11.3 %collective-permute-start.15 = (bf16[80,1024]{1,0:T(8,128)(2,1)S(1)}, bf16[80,1024]{1,0:T(8,128)(2,1)S(1)}, u32[]{:S(2)}, u32[]{:S(2)}) collective-permute-start(bf16[80,1024]{1,0:T(8,128)(2,1)S(1)} %reduce_sum.31.a0), channel_id=1, source_target_pairs={{0,32},{32,64},{64,96},{96,0},{1,33},{33,65},{65,97},{97,1},{2,34}... | collective-permute-start | bytes 491528 | tf_op jit(solution)/shard_map/ppermute | solution.py:22
  247.8 11.6 %collective-permute-start.16 = (bf16[80,1024]{1,0:T(8,128)(2,1)S(1)}, bf16[80,1024]{1,0:T(8,128)(2,1)S(1)}, u32[]{:S(2)}, u32[]{:S(2)}) collective-permute-start(bf16[80,1024]{1,0:T(8,128)(2,1)S(1)} %reduce_sum.31.a0), channel_id=1, source_target_pairs={{0,96},{32,0},{64,32},{96,64},{1,97},{33,1},{65,33},{97,65},{2,98}... | collective-permute-start | bytes 491528 | tf_op jit(solution)/shard_map/ppermute | solution.py:22
  250.9 8.6 %collective-permute-start.17 = (bf16[80,1024]{1,0:T(8,128)(2,1)S(1)}, bf16[80,1024]{1,0:T(8,128)(2,1)S(1)}, u32[]{:S(2)}, u32[]{:S(2)}) collective-permute-start(bf16[80,1024]{1,0:T(8,128)(2,1)S(1)} %reduce_sum.31.a0), channel_id=1, source_target_pairs={{0,64},{32,96},{64,0},{96,32},{1,65},{33,97},{65,1},{97,33},{2,66}... | collective-permute-start | bytes 491528 | tf_op jit(solution)/shard_map/ppermute | solution.py:22
  258.8 1.7 collective-permute-start.18
  258.9 1.6 collective-permute-start.19
  259.4 1.4 collective-permute-start.20
  259.5 1.5 collective-permute-start.21
  (3 other events, 1.9 us)
Sparse Core Ops, SparseCore 0:
  21.2 50.1 all-gather.2
where the time goes:
time: 273 us; the launch traced here: 271 us
  waiting for transfers between devices  96.3 us (35%)
  starting transfers between devices  59.6 us (22%)
  Pallas kernels  47.8 us (18%)
  local copies, waits for them, and re-layouts  30.6 us (11%)
  other arithmetic  16.8 us (6%)
  between operations  14.6 us (5%)
  matrix products  5.08 us (2%)
    ppermute x26, waiting for transfers between devices, shift_by(): lax.ppermute(value, axis, [(i, (i + shift) % count) for i in range(count)])  85.4 us
    pallas_call x5, Pallas kernels, local_call(): pl.pallas_call(body, out_shape=[jax.ShapeDtypeStruct(shape, kind) for sha...  47.8 us
    ppermute x26, starting transfers between devices, shift_by(): lax.ppermute(value, axis, [(i, (i + shift) % count) for i in range(count)])  30.8 us
    unnamed x74, local copies, waits for them, and re-layouts  18.9 us
    all_to_all x1, starting transfers between devices, shards(): lax.all_to_all(outgoing.reshape(16, 16, width), GROUP, 0, 0, tiled=True)  12.4 us
    all_to_all x1, starting transfers between devices, shards(): lax.all_to_all(chunks.reshape(16, 80, width), ('z', 'y'), 0, 0, tiled=True)  7.44 us
    all_to_all x1, waiting for transfers between devices, shards(): plane = lax.all_to_all(plane, GROUP, 0, 0, tiled=True)  6.31 us
  transfers between devices with their start and end apart: 31, of which 12 were waited for; matrix products, arithmetic and copies ran while one was open for 13% of the time, Pallas kernels for 6%

commit v1 on v0

--- a/solution.py
+++ b/solution.py
@@ -58,7 +58,7 @@
     return (place % 4) * 16 + (side + 1) * 4 + place // 4
 
 
-def local_call(body, outs, operands, scratch=(), flops=0, limit=48):
+def local_call(body, outs, operands, scratch=(), flops=0, limit=24):
     return pl.pallas_call(
         body,
         out_shape=[jax.ShapeDtypeStruct(shape, kind) for shape, kind in outs],
@@ -100,11 +100,13 @@
     own_in, own_out,
     m1, m2, m3,
     o1, o2, o3,
-    hidden_sum_ref,
+    own_rel, hidden_sum_ref,
     outgoing_ref, normed_ref, slope_ref, pooled_ref, all_out_ref, route_ref, length_ref, rel_hot_ref,
-    in_ref, pool_ref,
+    rel0_ref, rel1_ref, rel2_ref, rel3_ref,
+    in_ref, pool_ref, rel_ref,
 ):
-    core, my_x = where_ref[1], where_ref[2]
+    core, my_x, my_y = where_ref[1], where_ref[2], where_ref[3]
+    rel_ref[0:64, :] = own_rel[...]
     for s, block in enumerate((b0, b1, b2, b3)):
         normed_ref[s * 256 : (s + 1) * 256, :] = block[0:256, :]
     in_ref[:, 0:256] = own_in[...]
@@ -116,6 +118,8 @@
                 in_ref[rows, t * 256 : (t + 1) * 256] = part[0:256, i * 256 : (i + 1) * 256]
                 rows = pl.ds(pl.multiple_of(t * 256 + half * 128, 128), 128)
                 all_out_ref[rows, i * 512 : (i + 1) * 512] = part[256 + i * 128 : 384 + i * 128, :]
+                rows = pl.ds(pl.multiple_of(t * 64 + half * 32, 32), 32)
+                rel_ref[rows, i * 512 : (i + 1) * 512] = part[512 + i * 32 : 544 + i * 32, :]
 
     wide = (16, 256)
     slot = lanes(wide) % 16
@@ -123,9 +127,19 @@
     bound = (bound // 16 + (bound % 16) // 4 + 15) % 16
     bound_hot = (sublanes((128, 256)) == bound + 16).astype(F32).astype(BF)
     ids = jnp.zeros((16, 64), F32)
+    asked = (rel0_ref, rel1_ref, rel2_ref, rel3_ref)
     for s, block in enumerate((b0, b1, b2, b3)):
         meta = block[256:272, 0:128]
-        length = length_column(meta.astype(F32))
+        values = meta.astype(F32)
+        apart = lanes(meta.shape) - sublanes(meta.shape)
+        wanted = jnp.where(apart == 32, 32.0 * values, jnp.where(apart == 48, values, 0.0))
+        wanted = jnp.sum(wanted, axis=1, keepdims=True)
+        line = lanes(wide)
+        owner_y = (my_y + jnp.where(line < 64, 0, jnp.where(line < 128, 3, line // 64 - 1))) % 4
+        name = (my_x * 4 + owner_y) * 52 + line // 32 % 2 * 26 + line % 32
+        pick = (name.astype(F32) == wanted) & (line % 32 < 26)
+        asked[s][...] = dot(pick.astype(F32).astype(BF), rel_ref[...]).astype(BF)
+        length = length_column(values)
         length_ref[s * 16 : (s + 1) * 16, :] = jnp.broadcast_to(1.0 / length, (16, 128))
         pool_ref[s * 16 : (s + 1) * 16, :] = pool_rows(length, 256)
         sent = dot(meta, bound_hot)
@@ -164,13 +178,16 @@
 
 def graph_kernel(
     where_ref,
-    arrived_ref, base_ref, row_hot_ref, own_hot_t_ref, rel_ref,
+    arrived_ref, base_ref, row_hot_ref, own_hot_t_ref, e0, e1, e2, e3,
     src_hot_ref, dst_hot_ref, dst_hot_t_ref, src_row_hot_ref,
     w_msg_ref, w_self_ref, d_out_ref,
     table_out_ref, blocks_ref, graph_out_ref, aggregate_ref, nodes_ref, pre_ref,
-    ext_ref, sources_ref, edges_ref, agg_grad_ref, sums_ref,
+    ext_ref, sources_ref, edges_ref, agg_grad_ref, sums_ref, rel_ref,
 ):
     scale = (256 / 2048) ** 0.5
+    rel = e0[...].astype(F32) + e1[...].astype(F32) + e2[...].astype(F32) + e3[...].astype(F32)
+    for j in range(16):
+        rel_ref[j] = rel[j : j + 1]
     total = arrived_ref[0:64, :].astype(F32)
     for i in range(1, 4):
         total = total + arrived_ref[i * 64 : (i + 1) * 64, :].astype(F32)
@@ -276,15 +293,6 @@
             rel_ref[pl.ds(pl.multiple_of(half * 32 + z * 8, 8), 8), :] = values[64:72]
 
 
-def scatter_four(chunks, axis):
-    me = lax.axis_index(axis)
-    total = lax.dynamic_index_in_dim(chunks, me, 0, keepdims=False).astype(F32)
-    for shift in SHIFTS:
-        chunk = lax.dynamic_index_in_dim(chunks, (me + shift) % 4, 0, keepdims=False)
-        total = total + shift_by(chunk, axis, shift).astype(F32)
-    return total
-
-
 def shards(
     hidden,
     desc_len,
@@ -310,8 +318,6 @@
     src, dst, rel = edge_src[0], edge_dst[0], edge_rel[0]
     shard_rows = rel_table.shape[0]
 
-    full_table = lax.all_gather(rel_table, GROUP, axis=0, tiled=True)
-
     meta = row_of(jnp.concatenate([desc_len, send_order[0], rel // 32, rel % 32]), width)
     block, hidden_sum = local_call(
         norm_kernel,
@@ -323,11 +329,15 @@
     half_k, half_u = width // 2, units // 2
     in_half = lax.dynamic_slice_in_dim(w_in, my_core * half_k, half_k, 0)
     out_half = lax.dynamic_slice_in_dim(w_out, my_core * half_u, half_u, 0)
+    rel_pad = jnp.pad(rel_table.reshape(2, shard_rows // 2, width), ((0, 0), (0, 32 - shard_rows // 2), (0, 0)))
+    rel_half = lax.dynamic_index_in_dim(rel_pad, my_core, 0, keepdims=False)
     weights = jnp.concatenate(
         [
             jnp.concatenate([in_half[:units], in_half[units:]], axis=1),
             out_half[:, : 2 * units],
             out_half[:, 2 * units :],
+            rel_half[:, : 2 * units],
+            rel_half[:, 2 * units :],
         ],
         axis=0,
     )
@@ -345,8 +355,10 @@
     def edge_of(rows, places):
         return jnp.concatenate([rows, jnp.pad(row_of(places, width), ((0, 15), (0, 0)))], axis=0)
 
-    from_low = shift_by(edge_of(boundary[side:], halo_place[side:]), GROUP, 1)
-    from_high = shift_by(edge_of(boundary[:side], halo_place[:side]), GROUP, 15)
+    to_high, to_low = edge_of(boundary[side:], halo_place[side:]), edge_of(boundary[:side], halo_place[:side])
+    to_high, to_low, *blocks = lax.optimization_barrier((to_high, to_low, *blocks))
+    from_low = shift_by(to_high, GROUP, 1)
+    from_high = shift_by(to_low, GROUP, 15)
     low_place = from_low[side, :side].astype(I32)
     high_place = from_high[side, :side].astype(I32)
     own_row = fresh_row(0, place)
@@ -361,9 +373,8 @@
     block_count = rel.shape[0]
     src_hot = one_hot(src, extended_count)
     src_row_hot = dot_bt(one_hot_t(table_row, 64), src_hot).astype(BF)
-    rel_rows = dot(one_hot(rel, full_table.shape[0]), full_table).reshape(block_count, 1, width)
-
-    outgoing, normed, slope, pooled, all_out, route, inverse, rel_hot = local_call(
+
+    outgoing, normed, slope, pooled, all_out, route, inverse, rel_hot, *asked = local_call(
         encode_kernel,
         [
             ((256, width), BF),
@@ -374,12 +385,18 @@
             ((4 * entities, 256), BF),
             ((4 * entities, 128), F32),
             ((512, 64), BF),
+        ]
+        + [((entities, width), BF)] * 4,
+        [where, *blocks, w_in, w_out, *mine, *other, rel_pad.reshape(64, width), hidden_sum],
+        [
+            pltpu.VMEM((width, 4 * units), BF),
+            pltpu.VMEM((4 * entities, tokens), BF),
+            pltpu.VMEM((256, width), BF),
         ],
-        [where, *blocks, w_in, w_out, *mine, *other, hidden_sum],
-        [pltpu.VMEM((width, 4 * units), BF), pltpu.VMEM((4 * entities, tokens), BF)],
         flops=2 * 4 * tokens * width * 4 * units,
     )
     arrived = lax.all_to_all(outgoing.reshape(16, 16, width), GROUP, 0, 0, tiled=True).reshape(256, width)
+    rel_rows = [asked[0]] + [shift_by(rows, "x", o) for rows, o in zip(asked[1:], ORIGINS[1:])]
     normed_t = normed.T
 
     grad_table, grad_blocks, graph_out, aggregate, nodes, grad_pre = local_call(
@@ -398,7 +415,7 @@
             base,
             row_hot,
             one_hot_t(own_row, 64),
-            rel_rows,
+            *rel_rows,
             src_hot,
             one_hot(dst, node_count),
             one_hot_t(dst, node_count),
@@ -413,6 +430,7 @@
             pltpu.VMEM((edge_count, width), BF),
             pltpu.VMEM((node_count, width), BF),
             pltpu.VMEM((block_count, 1, width), F32),
+            pltpu.VMEM((block_count, 1, width), F32),
         ],
         flops=6 * 10**9,
     )
@@ -422,13 +440,21 @@
     rel_blocks = [grad_blocks] + [shift_by(grad_blocks, "x", s) for s in SHIFTS]
 
     graph_grads = jnp.stack([dot_t(aggregate, grad_pre).astype(BF), dot_t(nodes, grad_pre).astype(BF)])
-    graph_grads = graph_grads.reshape(2, 4, 2, 128, width)
-    graph_kept = lax.dynamic_index_in_dim(graph_grads, my_core, 2, keepdims=False)
-    graph_given = lax.dynamic_index_in_dim(graph_grads, 1 - my_core, 2, keepdims=False)
+    graph_grads = graph_grads.reshape(2, 4, 2, 4, 4, 8, width).transpose(2, 3, 1, 4, 0, 5, 6)
+    graph_grads = graph_grads.reshape(2, 4, 16, 16, width)
+    graph_kept = lax.dynamic_index_in_dim(graph_grads, my_core, 0, keepdims=False)
+    graph_given = lax.dynamic_index_in_dim(graph_grads, 1 - my_core, 0, keepdims=False)
     chip = (graph_kept.astype(F32) + shift_by(graph_given, "core", 1).astype(F32)).astype(BF)
-    line_sum = scatter_four(chip.transpose(1, 0, 2, 3), "z").astype(BF)
-    plane = line_sum.reshape(2, 16, 8, width).transpose(1, 0, 2, 3).reshape(16, 16, width)
-    plane = lax.all_to_all(plane, GROUP, 0, 0, tiled=True)
+    returned, chip = lax.optimization_barrier((returned, chip))
+    my_x = lax.axis_index("x")
+
+    def for_x(shift):
+        return lax.dynamic_index_in_dim(chip, (my_x + shift) % 4, 0, keepdims=False)
+
+    line_sum = for_x(0).astype(F32)
+    for s in SHIFTS:
+        line_sum = line_sum + shift_by(for_x(s), "x", s).astype(F32)
+    plane = lax.all_to_all(line_sum.astype(BF), ("z", "y"), 0, 0, tiled=True)
     weight_rows = jnp.sum(plane.astype(F32), axis=0)
     grad_msg, grad_self = weight_rows[:8], weight_rows[8:]
 

time: 273 us -> 251 us (0.919)
  local copies, waits for them, and re-layouts: 30.6 us -> 49.9 us
  waiting for transfers between devices: 96.3 us -> 77.6 us
  between operations: 14.6 us -> 1.22 us
  Pallas kernels: 47.8 us -> 40.4 us
    ppermute x26 -> x29, waiting for transfers between devices: 85.4 us -> 63.6 us  [shift_by(): lax.ppermute(value, axis, [(i, (i + shift) % count) for i in range(count)])]
    unnamed x74 -> x99, local copies, waits for them, and re-layouts: 18.9 us -> 36.3 us
    all_to_all x1, waiting for transfers between devices: 0.01 us -> 8.86 us  [shards(): lax.all_to_all(chunks.reshape(16, 80, width), ('z', 'y'), 0, 0, tiled=True)]
    all_to_all x1, starting transfers between devices: 12.4 us -> 4.37 us  [shards(): lax.all_to_all(outgoing.reshape(16, 16, width), GROUP, 0, 0, tiled=True)]
    pallas_call x5, Pallas kernels: 47.8 us -> 40.4 us  [local_call(): pl.pallas_call(body, out_shape=[jax.ShapeDtypeStruct(shape, kind) for sha...]
    all_to_all x1, waiting for transfers between devices: 3.95 us -> 0.01 us  [shards(): lax.all_to_all(outgoing.reshape(16, 16, width), GROUP, 0, 0, tiled=True)]
    all_to_all x1, starting transfers between devices: 3.57 us -> 7.04 us  [shards(): lax.all_to_all(back.reshape(16, 16, width), GROUP, 0, 0, tiled=True)]
    ppermute x26 -> x29, starting transfers between devices: 30.8 us -> 33.7 us  [shift_by(): lax.ppermute(value, axis, [(i, (i + shift) % count) for i in range(count)])]
  transfers between devices with their start and end apart: 31 -> 33, of which waited for: 12 -> 13; matrix products, arithmetic and copies ran while one was open for 13% -> 10% of each run, Pallas kernels for 6% -> 0%
where the time goes in v1:
time: 251 us; the launch traced here: 249 us
  waiting for transfers between devices  77.6 us (31%)
  starting transfers between devices  57.2 us (23%)
  local copies, waits for them, and re-layouts  49.9 us (20%)
  Pallas kernels  40.4 us (16%)
  other arithmetic  19.1 us (8%)
  matrix products  3.27 us (1%)
    ppermute x29, waiting for transfers between devices, shift_by(): lax.ppermute(value, axis, [(i, (i + shift) % count) for i in range(count)])  63.6 us
    pallas_call x5, Pallas kernels, local_call(): pl.pallas_call(body, out_shape=[jax.ShapeDtypeStruct(shape, kind) for sha...  40.4 us
    unnamed x99, local copies, waits for them, and re-layouts  36.3 us
    ppermute x29, starting transfers between devices, shift_by(): lax.ppermute(value, axis, [(i, (i + shift) % count) for i in range(count)])  33.7 us
    all_to_all x1, waiting for transfers between devices, shards(): lax.all_to_all(chunks.reshape(16, 80, width), ('z', 'y'), 0, 0, tiled=True)  8.86 us
    all_to_all x1, starting transfers between devices, shards(): lax.all_to_all(chunks.reshape(16, 80, width), ('z', 'y'), 0, 0, tiled=True)  7.82 us
    all_to_all x1, starting transfers between devices, shards(): lax.all_to_all(back.reshape(16, 16, width), GROUP, 0, 0, tiled=True)  7.04 us
    all_to_all x1, waiting for transfers between devices, shards(): plane = lax.all_to_all(line_sum.astype(BF), ('z', 'y'), 0, 0, tiled=True)  5.15 us
  transfers between devices with their start and end apart: 33, of which 13 were waited for; matrix products, arithmetic and copies ran while one was open for 10% of the time, Pallas kernels for 0%

profile of v1, /device:TPU:0, one launch (start us, length us, event | category | flops | bytes accessed | tf_op | source)
XLA Modules:
  0.0 248.7 jit_solution(1599414320574324655)
XLA Ops:
  3.5 1.6 dynamic-slice_dynamic-update-slice_fusion.1
  5.0 1.6 dynamic-slice_dynamic-update-slice_fusion
  7.8 1.7 collective-permute-start.3
  9.5 1.6 collective-permute-start.4
  11.1 2.1 collective-permute-start.5
  14.3 1.6 collective-permute-start
  15.9 1.7 collective-permute-start.1
  18.5 1.2 fusion.5.dst_hot_t_ref
  19.7 9.4 %collective-permute-done.b1 = bf16[272,1024]{1,0:T(8,128)(2,1)S(1)} collective-permute-done((bf16[272,1024]{1,0:T(8,128)(2,1)S(1)}, bf16[272,1024]{1,0:T(8,128)(2,1)S(1)}, u32[]{:S(2)}, u32[]{:S(2)}) %collective-permute-start) | collective-permute-done | bytes 557088 | tf_op jit(solution)/shard_map/ppermute | solution.py:22
  29.1 1.8 collective-permute-start.2
  31.0 1.4 fusion.2.src_hot_ref
  33.1 10.1 %collective-permute-done.2.b3 = bf16[272,1024]{1,0:T(8,128)(2,1)S(1)} collective-permute-done((bf16[272,1024]{1,0:T(8,128)(2,1)S(1)}, bf16[272,1024]{1,0:T(8,128)(2,1)S(1)}, u32[]{:S(2)}, u32[]{:S(2)}) %collective-permute-start.2) | collective-permute-done | bytes 557088 | tf_op jit(solution)/shard_map/ppermute | solution.py:22
  44.0 2.0 collective-permute-start.10
  50.1 9.0 %collective-permute-done.9 = bf16[80,1024]{1,0:T(8,128)(2,1)S(1)} collective-permute-done((bf16[80,1024]{1,0:T(8,128)(2,1)S(1)}, bf16[80,1024]{1,0:T(8,128)(2,1)S(1)}, u32[]{:S(2)}, u32[]{:S(2)}) %collective-permute-start.9) | collective-permute-done | bytes 163872 | tf_op jit(solution)/shard_map/ppermute | solution.py:22
  59.8 1.0 copy-done.6
  60.9 1.0 copy-done.7
  61.9 1.1 copy-done.11
  63.0 1.1 copy-done.13
  64.0 1.1 copy-done.15
  65.1 1.1 copy-done.17
  66.1 1.1 copy-done.19
  67.2 1.1 copy-done.21
  68.2 1.1 copy-done.23
  69.3 11.8 %shard_map.191 = (bf16[256,1024]{1,0:T(8,128)(2,1)S(1)}, bf16[1024,1024]{1,0:T(8,128)(2,1)S(1)}, bf16[1024,1024]{1,0:T(8,128)(2,1)S(1)}, bf16[64,1024]{1,0:T(8,1...) custom-call(s32[4]{0:T(128)S(1)} %pad_add_fusion.1.where_ref, ...), custom_call_target="tpu_custom_call" | custom-call | flops 2147483648 | bytes 1048576 | tf_op jit(solution)/shard_map/pallas_call | solution.py:62
  81.9 1.4 copy-done.25
  83.3 1.3 copy-done.27
  86.6 4.4 %all-to-all-start = ((bf16[16,16,1024]{2,1,0:T(8,128)(2,1)}), bf16[16,16,1024]{2,1,0:T(8,128)(2,1)}, u32[]{:S(2)}, u32[]{:S(2)}) async-start(bf16[16,16,1024]{2,1,0:T(8,128)(2,1)} %bitcast.83), calls=%async_computation | async-start | bytes 1048576 | tf_op jit(solution)/shard_map/all_to_all | solution.py:398
  90.9 1.5 fusion.3.src_row_hot_ref
  93.4 2.1 pad_maximum_fusion.1.base_ref
  95.5 3.0 %collective-permute-start.11 = (bf16[16,1024]{1,0:T(8,128)(2,1)S(1)}, bf16[16,1024]{1,0:T(8,128)(2,1)S(1)}, u32[]{:S(2)}, u32[]{:S(2)}) collective-permute-start(bf16[16,1024]{1,0:T(8,128)(2,1)S(1)} %get-tuple-element.49), channel_id=1, source_target_pairs={{0,12},{4,0},{8,4},{12,8},{1,13},{5,1},{9,5},{13,9},{2,14},{6,2},{... | collective-permute-start | bytes 98312 | tf_op jit(solution)/shard_map/ppermute | solution.py:22
  98.5 2.3 collective-permute-start.13
  100.9 2.7 %collective-permute-done.12.e2 = bf16[16,1024]{1,0:T(8,128)(2,1)S(1)} collective-permute-done((bf16[16,1024]{1,0:T(8,128)(2,1)S(1)}, bf16[16,1024]{1,0:T(8,128)(2,1)S(1)}, u32[]{:S(2)}, u32[]{:S(2)}) %collective-permute-start.12) | collective-permute-done | bytes 32800 | tf_op jit(solution)/shard_map/ppermute | solution.py:22
  104.0 1.4 copy-done.1
  105.4 1.2 copy-done.2
  106.6 1.1 copy-done.3
  107.8 1.6 copy-done.8
  109.4 1.6 copy-done.9
  113.7 18.1 %shard_map.192 = (bf16[64,1024]{1,0:T(8,128)(2,1)S(1)}, bf16[16,1024]{1,0:T(8,128)(2,1)S(1)}, bf16[256,1024]{1,0:T(8,128)(2,1)}, bf16[256,1024]{1,0:T(8,128)(2,1...) custom-call(s32[4]{0:T(128)S(1)} %pad_add_fusion.1.where_ref, ...), custom_call_target="tpu_custom_call" | custom-call | flops 6000000000 | bytes 1048576 | tf_op jit(solution)/shard_map/pallas_call | solution.py:62
  134.4 1.8 dynamic-slice_bitcast_fusion
  137.2 7.0 %all-to-all-start.1 = ((bf16[16,16,1024]{2,1,0:T(8,128)(2,1)}), bf16[16,16,1024]{2,1,0:T(8,128)(2,1)}, u32[]{:S(2)}, u32[]{:S(2)}) async-start(bf16[16,16,1024]{2,1,0:T(8,128)(2,1)} %bitcast.21), calls=%async_computation.1 | async-start | bytes 1048576 | tf_op jit(solution)/shard_map/all_to_all | solution.py:439
  144.3 2.6 %copy.27 = bf16[1024,1024]{0,1:T(8,128)(2,1)} copy(bf16[1024,1024]{1,0:T(8,128)(2,1)S(1)} %get-tuple-element.63) | data formatting | bytes 4194304 | tf_op jit(solution)/shard_map/pallas_call | solution.py:62
  146.8 1.9 collective-permute-start.15
  148.8 1.4 collective-permute-start.16
  150.1 2.2 collective-permute-start.17
  152.3 4.7 %fusion = bf16[4,16,16,1024]{3,2,1,0:T(8,128)(2,1)} fusion(bf16[4,16,16,1024]{3,2,1,0:T(8,128)(2,1)} %collective-permute-done.14, bf16[2,4,16,16,1024]{4,3,2,1,0:T(8,128)(2,1)} %bitcast.87, s32[]{:T(128)S(6)} %select_n.110), kind=kLoop, calls=%fused_computation.3 | loop fusion | flops 4194304 | bytes 6291460 | tf_op jit(solution)/shard_map/convert_element_type | solution.py:447
  157.1 1.6 copy-done.26
  158.6 1.6 copy-done.28
  160.2 7.5 %shard_map.193 = (bf16[4,4,80,1024]{3,2,1,0:T(8,128)(2,1)S(1)}, bf16[4,4,80,1024]{3,2,1,0:T(8,128)(2,1)S(1)}) custom-call(s32[4]{0:T(128)S(1)} %pad_add_fusion.1.where_ref, bf16[256,1024]{1,0:T(8,128)(2,1)} %bitcast.22.returned_ref, bf16[64,256]{1,0:T(8,128)(2,1)S(1)} %get-tuple-element.58.route_ref, f32[64,128]{1,0:T(8,128)S(1)} %copy-done.35, ...), custom_call_target="tpu_custom_call" | custom-call | flops 2147483648 | bytes 1048576 | tf_op jit(solution)/shard_map/pallas_call | solution.py:62
  167.9 4.9 %collective-permute-done.18 = bf16[4,4,80,1024]{3,2,1,0:T(8,128)(2,1)S(1)} collective-permute-done((bf16[4,4,80,1024]{3,2,1,0:T(8,128)(2,1)S(1)}, bf16[4,4,80,1024]{3,2,1,0:T(8,128)(2,1)S(1)}, u32[]{:S(2)}, u32[]{:S(2)}) %collective-permute-start.18) | collective-permute-done | bytes 2621472 | tf_op jit(solution)/shard_map/ppermute | solution.py:22
  172.8 2.8 %add_convert_fusion = bf16[4,4,80,1024]{3,2,1,0:T(8,128)(2,1)} fusion(bf16[4,4,80,1024]{3,2,1,0:T(8,128)(2,1)S(1)} %collective-permute-done.18, bf16[4,4,80,1024]{3,2,1,0:T(8,128)(2,1)S(1)} %get-tuple-element.66), kind=kLoop, calls=%fused_computation | loop fusion | flops 5242880 | bytes 7864320 | tf_op jit(solution)/shard_map/convert_element_type | solution.py:468
  175.5 7.8 %all-to-all-start.2 = ((bf16[16,80,1024]{2,1,0:T(8,128)(2,1)}), bf16[16,80,1024]{2,1,0:T(8,128)(2,1)S(1)}, u32[]{:S(2)}, u32[]{:S(2)}) async-start(bf16[16,80,1024]{2,1,0:T(8,128)(2,1)} %bitcast.88), calls=%async_computation.2 | async-start | bytes 5242880 | tf_op jit(solution)/shard_map/all_to_all | solution.py:469
  183.4 2.6 %dynamic-slice_bitcast_fusion.3 = (bf16[16,16,1024]{2,1,0:T(8,128)(2,1)}, bf16[16,16,1024]{2,1,0:T(8,128)(2,1)}, bf16[16,16,1024]{2,1,0:T(8,128)(2,1)}) fusion(bf16[4,16,16,1024]{3,2,1,0:T(8,128)(2,1)} %fusion, s32[]{:T(128)S(6)} %select_n.125, s32[]{:T(128)S(6)} %select_n.129, s32[]{:T(128)S(6)} %select_n.127), kind=kLoop, calls=%fused_computation.25 | loop fusion | bytes 3145740 | tf_op jit(solution)/shard_map/jit(dynamic_index_in_dim)/squeeze | solution.py:452
  186.5 2.7 %collective-permute-start.27 = (bf16[16,16,1024]{2,1,0:T(8,128)(2,1)}, bf16[16,16,1024]{2,1,0:T(8,128)(2,1)}, u32[]{:S(2)}, u32[]{:S(2)}) collective-permute-start(bf16[16,16,1024]{2,1,0:T(8,128)(2,1)} %get-tuple-element.74), channel_id=1, source_target_pairs={{0,12},{4,0},{8,4},{12,8},{1,13},{5,1},{9,5},{13,9},{2,14},{6,2},{... | collective-permute-start | bytes 1572872 | tf_op jit(solution)/shard_map/ppermute | solution.py:22
  189.8 22.7 %collective-permute-done.26 = bf16[16,16,1024]{2,1,0:T(8,128)(2,1)} collective-permute-done((bf16[16,16,1024]{2,1,0:T(8,128)(2,1)}, bf16[16,16,1024]{2,1,0:T(8,128)(2,1)}, u32[]{:S(2)}, u32[]{:S(2)}) %collective-permute-start.26) | collective-permute-done | bytes 524320 | tf_op jit(solution)/shard_map/ppermute | solution.py:22
  212.4 2.7 %fusion.9 = bf16[16,16,1024]{2,1,0:T(8,128)(2,1)} fusion(bf16[16,16,1024]{2,1,0:T(8,128)(2,1)} %collective-permute-done.28, bf16[16,16,1024]{2,1,0:T(8,128)(2,1)} %collective-permute-done.27, bf16[16,16,1024]{2,1,0:T(8,128)(2,1)} %collective-permute-done.26, bf16[4,16,16,1024]{3,2,1,0:T(8,128)(2,1)} %fusion, s32[]{:T(128)S(6)} %select_n.123), kind=kLoop, calls=%fused_computation.20 | loop fusion | flops 2097152 | bytes 2621444 | tf_op jit(solution)/shard_map/convert_element_type | solution.py:457
  215.1 8.9 %all-to-all-done.2 = bf16[16,80,1024]{2,1,0:T(8,128)(2,1)S(1)} async-done(((bf16[16,80,1024]{2,1,0:T(8,128)(2,1)}), bf16[16,80,1024]{2,1,0:T(8,128)(2,1)S(1)}, u32[]{:S(2)}, u32[]{:S(2)}) %all-to-all-start.2) | async-done | bytes 2621472 | tf_op jit(solution)/shard_map/all_to_all | solution.py:469
  224.0 4.2 %all-to-all-start.3 = ((bf16[16,16,1024]{2,1,0:T(8,128)(2,1)}), bf16[16,16,1024]{2,1,0:T(8,128)(2,1)}, u32[]{:S(2)}, u32[]{:S(2)}) async-start(bf16[16,16,1024]{2,1,0:T(8,128)(2,1)} %fusion.9), calls=%async_computation.3 | async-start | bytes 1048576 | tf_op jit(solution)/shard_map/all_to_all | solution.py:457
  228.7 1.8 collective-permute-start.19
  230.6 1.5 collective-permute-start.20
  232.0 2.1 collective-permute-start.21
  234.1 5.1 %all-to-all-done.3 = bf16[16,16,1024]{2,1,0:T(8,128)(2,1)} async-done(((bf16[16,16,1024]{2,1,0:T(8,128)(2,1)}), bf16[16,16,1024]{2,1,0:T(8,128)(2,1)}, u32[]{:S(2)}, u32[]{:S(2)}) %all-to-all-start.3) | async-done | bytes 524320 | tf_op jit(solution)/shard_map/all_to_all | solution.py:457
  239.3 1.1 convert_reduce_fusion
  241.6 3.0 %collective-permute-done.21.a3 = bf16[80,1024]{1,0:T(8,128)(2,1)S(1)} collective-permute-done((bf16[80,1024]{1,0:T(8,128)(2,1)S(1)}, bf16[80,1024]{1,0:T(8,128)(2,1)S(1)}, u32[]{:S(2)}, u32[]{:S(2)}) %collective-permute-start.21) | collective-permute-done | bytes 163872 | tf_op jit(solution)/shard_map/ppermute | solution.py:22
  245.9 2.0 shard_map.194
  (161 shorter events, 27.7 us)
Async XLA Ops:
  0.6 12.5 %copy-start.44 = (s32[1,16]{1,0:T(1,128)S(1)}, s32[1,16]{1,0:T(1,128)}, u32[]{:S(2)}) copy-start(s32[1,16]{1,0:T(1,128)} %param.25) | copy-start | bytes 196
  0.6 12.5 %copy-start.45 = (s32[16]{0:T(128)S(1)}, s32[16]{0:T(128)}, u32[]{:S(2)}) copy-start(s32[16]{0:T(128)} %param.16) | copy-start | bytes 196
  0.7 12.5 %copy-start.46 = (s32[1,16]{1,0:T(1,128)S(1)}, s32[1,16]{1,0:T(1,128)}, u32[]{:S(2)}) copy-start(s32[1,16]{1,0:T(1,128)} %param.19) | copy-start | bytes 196
  0.7 12.7 %copy-start.4 = (bf16[16,16,1024]{2,1,0:T(8,128)(2,1)S(1)}, bf16[16,16,1024]{2,1,0:T(8,128)(2,1)}, u32[]{:S(2)}) copy-start(bf16[16,16,1024]{2,1,0:T(8,128)(2,1)} %param.15) | copy-start | bytes 1572868
  0.7 16.9 %copy-start.47 = (s32[1,16]{1,0:T(1,128)S(1)}, s32[1,16]{1,0:T(1,128)}, u32[]{:S(2)}) copy-start(s32[1,16]{1,0:T(1,128)} %param.20) | copy-start | bytes 196
  0.7 16.9 %copy-start.43 = (s32[1,128]{1,0:T(1,128)S(1)}, s32[1,128]{1,0:T(1,128)}, u32[]{:S(2)}) copy-start(s32[1,128]{1,0:T(1,128)} %param.22) | copy-start | bytes 1540
  0.7 17.0 %copy-start.39 = (bf16[240,1024]{1,0:T(8,128)(2,1)S(1)}, bf16[240,1024]{1,0:T(8,128)(2,1)}, u32[]{:S(2)}) copy-start(bf16[240,1024]{1,0:T(8,128)(2,1)} %param.21) | copy-start | bytes 1474564
  0.7 17.3 %copy-start.41 = (s32[1,2048]{1,0:T(1,128)S(1)}, s32[1,2048]{1,0:T(1,128)}, u32[]{:S(2)}) copy-start(s32[1,2048]{1,0:T(1,128)} %param.24) | copy-start | bytes 24580
  7.8 38.2 %collective-permute-start.3 = (bf16[576,512]{1,0:T(8,128)(2,1)}, bf16[576,512]{1,0:T(8,128)(2,1)S(1)}, u32[]{:S(2)}, u32[]{:S(2)}) collective-permute-start(bf16[576,512]{1,0:T(8,128)(2,1)} %slice_dynamic-update-slice_fusion), channel_id=1, source_target_pairs={{0,1},{1,2},{2,3},{3,0},{4,5},{5,6},{6,7},{7,4},{8,9},{9,10},{10,1... | collective-permute-start | bytes 1769480 | tf_op jit(solution)/shard_map/ppermute | solution.py:22
  9.5 37.4 %collective-permute-start.4 = (bf16[576,512]{1,0:T(8,128)(2,1)}, bf16[576,512]{1,0:T(8,128)(2,1)S(1)}, u32[]{:S(2)}, u32[]{:S(2)}) collective-permute-start(bf16[576,512]{1,0:T(8,128)(2,1)} %slice_dynamic-update-slice_fusion), channel_id=1, source_target_pairs={{0,3},{1,0},{2,1},{3,2},{4,7},{5,4},{6,5},{7,6},{8,11},{9,8},{10,9... | collective-permute-start | bytes 1769480 | tf_op jit(solution)/shard_map/ppermute | solution.py:22
  11.1 37.2 %collective-permute-start.5 = (bf16[576,512]{1,0:T(8,128)(2,1)}, bf16[576,512]{1,0:T(8,128)(2,1)S(1)}, u32[]{:S(2)}, u32[]{:S(2)}) collective-permute-start(bf16[576,512]{1,0:T(8,128)(2,1)} %slice_dynamic-update-slice_fusion), channel_id=1, source_target_pairs={{0,2},{1,3},{2,0},{3,1},{4,6},{5,7},{6,4},{7,5},{8,10},{9,11},{10,... | collective-permute-start | bytes 1769480 | tf_op jit(solution)/shard_map/ppermute | solution.py:22
  14.3 18.1 %copy-start.16 = (bf16[272,1024]{1,0:T(8,128)(2,1)}, bf16[272,1024]{1,0:T(8,128)(2,1)S(1)}, u32[]{:S(2)}) copy-start(bf16[272,1024]{1,0:T(8,128)(2,1)S(1)} %get-tuple-element.40.b0) | copy-start | bytes 1671172
  14.3 16.7 %copy-start.42 = (s32[1,2048]{1,0:T(1,128)S(1)}, s32[1,2048]{1,0:T(1,128)}, u32[]{:S(2)}) copy-start(s32[1,2048]{1,0:T(1,128)} %param.23) | copy-start | bytes 24580
  14.3 14.8 %collective-permute-start = (bf16[272,1024]{1,0:T(8,128)(2,1)S(1)}, bf16[272,1024]{1,0:T(8,128)(2,1)S(1)}, u32[]{:S(2)}, u32[]{:S(2)}) collective-permute-start(bf16[272,1024]{1,0:T(8,128)(2,1)S(1)} %get-tuple-element.40.b0), channel_id=1, source_target_pairs={{0,4},{4,8},{8,12},{12,0},{1,5},{5,9},{9,13},{13,1},{2,6},{6,10},{... | collective-permute-start | bytes 1671176 | tf_op jit(solution)/shard_map/ppermute | solution.py:22
  15.9 16.5 %collective-permute-start.1 = (bf16[272,1024]{1,0:T(8,128)(2,1)S(1)}, bf16[272,1024]{1,0:T(8,128)(2,1)S(1)}, u32[]{:S(2)}, u32[]{:S(2)}) collective-permute-start(bf16[272,1024]{1,0:T(8,128)(2,1)S(1)} %get-tuple-element.40.b0), channel_id=1, source_target_pairs={{0,12},{4,0},{8,4},{12,8},{1,13},{5,1},{9,5},{13,9},{2,14},{6,2},{... | collective-permute-start | bytes 1671176 | tf_op jit(solution)/shard_map/ppermute | solution.py:22
  29.1 19.2 %copy-start.18 = (bf16[272,1024]{1,0:T(8,128)(2,1)}, bf16[272,1024]{1,0:T(8,128)(2,1)S(1)}, u32[]{:S(2)}) copy-start(bf16[272,1024]{1,0:T(8,128)(2,1)S(1)} %collective-permute-done.b1) | copy-start | bytes 1671172
  29.1 14.1 %collective-permute-start.2 = (bf16[272,1024]{1,0:T(8,128)(2,1)S(1)}, bf16[272,1024]{1,0:T(8,128)(2,1)S(1)}, u32[]{:S(2)}, u32[]{:S(2)}) collective-permute-start(bf16[272,1024]{1,0:T(8,128)(2,1)S(1)} %get-tuple-element.40.b0), channel_id=1, source_target_pairs={{0,8},{4,12},{8,0},{12,4},{1,9},{5,13},{9,1},{13,5},{2,10},{6,14},... | collective-permute-start | bytes 1671176 | tf_op jit(solution)/shard_map/ppermute | solution.py:22
  44.0 5.4 %collective-permute-start.10 = (bf16[80,1024]{1,0:T(8,128)(2,1)S(1)}, bf16[80,1024]{1,0:T(8,128)(2,1)}, u32[]{:S(2)}, u32[]{:S(2)}) collective-permute-start(bf16[80,1024]{1,0:T(8,128)(2,1)S(1)} %get-tuple-element.47), channel_id=1, source_target_pairs={{0,15},{1,0},{2,1},{3,2},{4,3},{5,4},{6,5},{7,6},{8,7},{9,8},{10,9... | collective-permute-start | bytes 491528 | tf_op jit(solution)/shard_map/ppermute | solution.py:22
  46.1 13.2 %collective-permute-start.6 = (bf16[576,512]{1,0:T(8,128)(2,1)S(1)}, bf16[576,512]{1,0:T(8,128)(2,1)}, u32[]{:S(2)}, u32[]{:S(2)}) collective-permute-start(bf16[576,512]{1,0:T(8,128)(2,1)S(1)} %collective-permute-done.3.m1), channel_id=1, source_target_pairs={{0,16},{16,0},{1,17},{17,1},{2,18},{18,2},{3,19},{19,3},{4,20},{20... | collective-permute-start | bytes 1769480 | tf_op jit(solution)/shard_map/ppermute | solution.py:22
  46.9 12.4 %collective-permute-start.7 = (bf16[576,512]{1,0:T(8,128)(2,1)S(1)}, bf16[576,512]{1,0:T(8,128)(2,1)}, u32[]{:S(2)}, u32[]{:S(2)}) collective-permute-start(bf16[576,512]{1,0:T(8,128)(2,1)S(1)} %collective-permute-done.4.m2), channel_id=1, source_target_pairs={{0,16},{16,0},{1,17},{17,1},{2,18},{18,2},{3,19},{19,3},{4,20},{20... | collective-permute-start | bytes 1769480 | tf_op jit(solution)/shard_map/ppermute | solution.py:22
  48.3 11.0 %collective-permute-start.8 = (bf16[576,512]{1,0:T(8,128)(2,1)S(1)}, bf16[576,512]{1,0:T(8,128)(2,1)}, u32[]{:S(2)}, u32[]{:S(2)}) collective-permute-start(bf16[576,512]{1,0:T(8,128)(2,1)S(1)} %collective-permute-done.5.m3), channel_id=1, source_target_pairs={{0,16},{16,0},{1,17},{17,1},{2,18},{18,2},{3,19},{19,3},{4,20},{20... | collective-permute-start | bytes 1769480 | tf_op jit(solution)/shard_map/ppermute | solution.py:22
  49.1 10.0 %collective-permute-start.9 = (bf16[80,1024]{1,0:T(8,128)(2,1)S(1)}, bf16[80,1024]{1,0:T(8,128)(2,1)S(1)}, u32[]{:S(2)}, u32[]{:S(2)}) collective-permute-start(bf16[80,1024]{1,0:T(8,128)(2,1)S(1)} %get-tuple-element.46), channel_id=1, source_target_pairs={{0,1},{1,2},{2,3},{3,4},{4,5},{5,6},{6,7},{7,8},{8,9},{9,10},{10,1... | collective-permute-start | bytes 491528 | tf_op jit(solution)/shard_map/ppermute | solution.py:22
  61.9 1.1 copy-start.11
  63.0 1.1 copy-start.13
  64.0 1.1 copy-start.15
  65.1 1.1 copy-start.17
  81.9 1.4 copy-start.25
  83.3 1.3 copy-start.27
  86.5 8.9 %copy-start.34 = (f32[64,128]{1,0:T(8,128)}, f32[64,128]{1,0:T(8,128)S(1)}, u32[]{:S(2)}) copy-start(f32[64,128]{1,0:T(8,128)S(1)} %get-tuple-element.59.length_ref) | copy-start | bytes 98308
  86.5 6.8 %slice-start = ((bf16[80,1024]{1,0:T(8,128)(2,1)}), bf16[64,1024]{1,0:T(8,128)(2,1)S(1)}, s32[]{:S(2)}) async-start(bf16[80,1024]{1,0:T(8,128)(2,1)} %copy-done.40), calls=%async_computation.4 | async-start | bytes 262144 | tf_op jit(solution)/shard_map/slice | solution.py:369
  86.6 17.4 %all-to-all-start = ((bf16[16,16,1024]{2,1,0:T(8,128)(2,1)}), bf16[16,16,1024]{2,1,0:T(8,128)(2,1)}, u32[]{:S(2)}, u32[]{:S(2)}) async-start(bf16[16,16,1024]{2,1,0:T(8,128)(2,1)} %bitcast.83), calls=%async_computation | async-start | bytes 1048576 | tf_op jit(solution)/shard_map/all_to_all | solution.py:398
  95.5 5.4 %collective-permute-start.11 = (bf16[16,1024]{1,0:T(8,128)(2,1)S(1)}, bf16[16,1024]{1,0:T(8,128)(2,1)S(1)}, u32[]{:S(2)}, u32[]{:S(2)}) collective-permute-start(bf16[16,1024]{1,0:T(8,128)(2,1)S(1)} %get-tuple-element.49), channel_id=1, source_target_pairs={{0,12},{4,0},{8,4},{12,8},{1,13},{5,1},{9,5},{13,9},{2,14},{6,2},{... | collective-permute-start | bytes 98312 | tf_op jit(solution)/shard_map/ppermute | solution.py:22
  98.5 5.1 %collective-permute-start.12 = (bf16[16,1024]{1,0:T(8,128)(2,1)S(1)}, bf16[16,1024]{1,0:T(8,128)(2,1)S(1)}, u32[]{:S(2)}, u32[]{:S(2)}) collective-permute-start(bf16[16,1024]{1,0:T(8,128)(2,1)S(1)} %get-tuple-element.50), channel_id=1, source_target_pairs={{0,4},{4,8},{8,12},{12,0},{1,5},{5,9},{9,13},{13,1},{2,6},{6,10},{... | collective-permute-start | bytes 98312 | tf_op jit(solution)/shard_map/ppermute | solution.py:22
  98.5 5.5 %collective-permute-start.13 = (bf16[16,1024]{1,0:T(8,128)(2,1)S(1)}, bf16[16,1024]{1,0:T(8,128)(2,1)S(1)}, u32[]{:S(2)}, u32[]{:S(2)}) collective-permute-start(bf16[16,1024]{1,0:T(8,128)(2,1)S(1)} %get-tuple-element.51), channel_id=1, source_target_pairs={{0,8},{4,12},{8,0},{12,4},{1,9},{5,13},{9,1},{13,5},{2,10},{6,14},... | collective-permute-start | bytes 98312 | tf_op jit(solution)/shard_map/ppermute | solution.py:22
  104.0 1.4 copy-start.1
  105.4 1.2 copy-start.2
  106.6 1.1 copy-start.3
  107.8 1.6 copy-start.8
  109.4 1.6 copy-start.9
  134.4 2.8 %copy-start.38 = (bf16[2,4,2,4,4,8,1024]{6,5,0,4,1,3,2:T(8,128)(2,1)}, bf16[2,4,2,4,4,8,1024]{6,5,0,4,1,3,2:T(8,128)(2,1)S(1)}, u32[]{:S(2)}) copy-start(bf16[2,4,2,4,4,8,1024]{6,5,0,4,1,3,2:T(8,128)(2,1)S(1)} %copy.28) | copy-start | bytes 12582916
  136.2 16.1 %collective-permute-start.14 = (bf16[4,16,16,1024]{3,2,1,0:T(8,128)(2,1)}, bf16[4,16,16,1024]{3,2,1,0:T(8,128)(2,1)}, u32[]{:S(2)}, u32[]{:S(2)}) collective-permute-start(bf16[4,16,16,1024]{3,2,1,0:T(8,128)(2,1)} %dynamic-slice_bitcast_fusion), channel_id=1, source_target_pairs={{0,16},{16,0},{1,17},{17,1},{2,18},{18,2},{3,19},{19,3},{4,20},{20... | collective-permute-start | bytes 6291464 | tf_op jit(solution)/shard_map/ppermute | solution.py:22
  137.2 19.8 %all-to-all-start.1 = ((bf16[16,16,1024]{2,1,0:T(8,128)(2,1)}), bf16[16,16,1024]{2,1,0:T(8,128)(2,1)}, u32[]{:S(2)}, u32[]{:S(2)}) async-start(bf16[16,16,1024]{2,1,0:T(8,128)(2,1)} %bitcast.21), calls=%async_computation.1 | async-start | bytes 1048576 | tf_op jit(solution)/shard_map/all_to_all | solution.py:439
  146.8 10.2 %copy-start = (bf16[1024,1024]{0,1:T(8,128)(2,1)S(1)}, bf16[1024,1024]{0,1:T(8,128)(2,1)}, u32[]{:S(2)}) copy-start(bf16[1024,1024]{0,1:T(8,128)(2,1)} %copy.27) | copy-start | bytes 6291460
  146.8 10.2 %copy-start.31 = (bf16[64,1024]{1,0:T(8,128)(2,1)S(1)}, bf16[64,1024]{1,0:T(8,128)(2,1)}, u32[]{:S(2)}) copy-start(bf16[64,1024]{1,0:T(8,128)(2,1)} %copy-done.30) | copy-start | bytes 393220
  146.8 10.2 %copy-start.33 = (bf16[512,64]{1,0:T(8,128)(2,1)S(1)}, bf16[512,64]{1,0:T(8,128)(2,1)}, u32[]{:S(2)}) copy-start(bf16[512,64]{1,0:T(8,128)(2,1)} %copy-done.32) | copy-start | bytes 196612
  146.8 10.2 %copy-start.35 = (f32[64,128]{1,0:T(8,128)S(1)}, f32[64,128]{1,0:T(8,128)}, u32[]{:S(2)}) copy-start(f32[64,128]{1,0:T(8,128)} %copy-done.34) | copy-start | bytes 98308
  146.8 10.2 %collective-permute-start.15 = (bf16[16,1024]{1,0:T(8,128)(2,1)S(1)}, bf16[16,1024]{1,0:T(8,128)(2,1)S(1)}, u32[]{:S(2)}, u32[]{:S(2)}) collective-permute-start(bf16[16,1024]{1,0:T(8,128)(2,1)S(1)} %get-tuple-element.65.r0), channel_id=1, source_target_pairs={{0,4},{4,8},{8,12},{12,0},{1,5},{5,9},{9,13},{13,1},{2,6},{6,10},{... | collective-permute-start | bytes 98312 | tf_op jit(solution)/shard_map/ppermute | solution.py:22
  148.8 8.2 %collective-permute-start.16 = (bf16[16,1024]{1,0:T(8,128)(2,1)S(1)}, bf16[16,1024]{1,0:T(8,128)(2,1)S(1)}, u32[]{:S(2)}, u32[]{:S(2)}) collective-permute-start(bf16[16,1024]{1,0:T(8,128)(2,1)S(1)} %get-tuple-element.65.r0), channel_id=1, source_target_pairs={{0,12},{4,0},{8,4},{12,8},{1,13},{5,1},{9,5},{13,9},{2,14},{6,2},{... | collective-permute-start | bytes 98312 | tf_op jit(solution)/shard_map/ppermute | solution.py:22
  150.1 6.9 %collective-permute-start.17 = (bf16[16,1024]{1,0:T(8,128)(2,1)S(1)}, bf16[16,1024]{1,0:T(8,128)(2,1)S(1)}, u32[]{:S(2)}, u32[]{:S(2)}) collective-permute-start(bf16[16,1024]{1,0:T(8,128)(2,1)S(1)} %get-tuple-element.65.r0), channel_id=1, source_target_pairs={{0,8},{4,12},{8,0},{12,4},{1,9},{5,13},{9,1},{13,5},{2,10},{6,14},... | collective-permute-start | bytes 98312 | tf_op jit(solution)/shard_map/ppermute | solution.py:22
  157.0 1.6 copy-start.26
  158.6 1.6 copy-start.28
  167.8 5.0 %collective-permute-start.18 = (bf16[4,4,80,1024]{3,2,1,0:T(8,128)(2,1)S(1)}, bf16[4,4,80,1024]{3,2,1,0:T(8,128)(2,1)S(1)}, u32[]{:S(2)}, u32[]{:S(2)}) collective-permute-start(bf16[4,4,80,1024]{3,2,1,0:T(8,128)(2,1)S(1)} %get-tuple-element.67), channel_id=1, source_target_pairs={{0,16},{16,0},{1,17},{17,1},{2,18},{18,2},{3,19},{19,3},{4,20},{20... | collective-permute-start | bytes 7864328 | tf_op jit(solution)/shard_map/ppermute | solution.py:22
  175.5 48.4 %all-to-all-start.2 = ((bf16[16,80,1024]{2,1,0:T(8,128)(2,1)}), bf16[16,80,1024]{2,1,0:T(8,128)(2,1)S(1)}, u32[]{:S(2)}, u32[]{:S(2)}) async-start(bf16[16,80,1024]{2,1,0:T(8,128)(2,1)} %bitcast.88), calls=%async_computation.2 | async-start | bytes 5242880 | tf_op jit(solution)/shard_map/all_to_all | solution.py:469
  186.0 26.4 %collective-permute-start.26 = (bf16[16,16,1024]{2,1,0:T(8,128)(2,1)}, bf16[16,16,1024]{2,1,0:T(8,128)(2,1)}, u32[]{:S(2)}, u32[]{:S(2)}) collective-permute-start(bf16[16,16,1024]{2,1,0:T(8,128)(2,1)} %get-tuple-element.72), channel_id=1, source_target_pairs={{0,4},{4,8},{8,12},{12,0},{1,5},{5,9},{9,13},{13,1},{2,6},{6,10},{... | collective-permute-start | bytes 1572872 | tf_op jit(solution)/shard_map/ppermute | solution.py:22
  186.5 25.9 %collective-permute-start.27 = (bf16[16,16,1024]{2,1,0:T(8,128)(2,1)}, bf16[16,16,1024]{2,1,0:T(8,128)(2,1)}, u32[]{:S(2)}, u32[]{:S(2)}) collective-permute-start(bf16[16,16,1024]{2,1,0:T(8,128)(2,1)} %get-tuple-element.74), channel_id=1, source_target_pairs={{0,12},{4,0},{8,4},{12,8},{1,13},{5,1},{9,5},{13,9},{2,14},{6,2},{... | collective-permute-start | bytes 1572872 | tf_op jit(solution)/shard_map/ppermute | solution.py:22
  189.2 23.2 %collective-permute-start.28 = (bf16[16,16,1024]{2,1,0:T(8,128)(2,1)}, bf16[16,16,1024]{2,1,0:T(8,128)(2,1)}, u32[]{:S(2)}, u32[]{:S(2)}) collective-permute-start(bf16[16,16,1024]{2,1,0:T(8,128)(2,1)} %get-tuple-element.73), channel_id=1, source_target_pairs={{0,8},{4,12},{8,0},{12,4},{1,9},{5,13},{9,1},{13,5},{2,10},{6,14},... | collective-permute-start | bytes 1572872 | tf_op jit(solution)/shard_map/ppermute | solution.py:22
  224.0 15.3 %all-to-all-start.3 = ((bf16[16,16,1024]{2,1,0:T(8,128)(2,1)}), bf16[16,16,1024]{2,1,0:T(8,128)(2,1)}, u32[]{:S(2)}, u32[]{:S(2)}) async-start(bf16[16,16,1024]{2,1,0:T(8,128)(2,1)} %fusion.9), calls=%async_computation.3 | async-start | bytes 1048576 | tf_op jit(solution)/shard_map/all_to_all | solution.py:457
  228.7 12.3 %collective-permute-start.19 = (bf16[80,1024]{1,0:T(8,128)(2,1)S(1)}, bf16[80,1024]{1,0:T(8,128)(2,1)S(1)}, u32[]{:S(2)}, u32[]{:S(2)}) collective-permute-start(bf16[80,1024]{1,0:T(8,128)(2,1)S(1)} %reduce_sum.31.a0), channel_id=1, source_target_pairs={{0,32},{32,64},{64,96},{96,0},{1,33},{33,65},{65,97},{97,1},{2,34}... | collective-permute-start | bytes 491528 | tf_op jit(solution)/shard_map/ppermute | solution.py:22
  230.6 10.5 %collective-permute-start.20 = (bf16[80,1024]{1,0:T(8,128)(2,1)S(1)}, bf16[80,1024]{1,0:T(8,128)(2,1)S(1)}, u32[]{:S(2)}, u32[]{:S(2)}) collective-permute-start(bf16[80,1024]{1,0:T(8,128)(2,1)S(1)} %reduce_sum.31.a0), channel_id=1, source_target_pairs={{0,96},{32,0},{64,32},{96,64},{1,97},{33,1},{65,33},{97,65},{2,98}... | collective-permute-start | bytes 491528 | tf_op jit(solution)/shard_map/ppermute | solution.py:22
  232.0 12.5 %collective-permute-start.21 = (bf16[80,1024]{1,0:T(8,128)(2,1)S(1)}, bf16[80,1024]{1,0:T(8,128)(2,1)S(1)}, u32[]{:S(2)}, u32[]{:S(2)}) collective-permute-start(bf16[80,1024]{1,0:T(8,128)(2,1)S(1)} %reduce_sum.31.a0), channel_id=1, source_target_pairs={{0,64},{32,96},{64,0},{96,32},{1,65},{33,97},{65,1},{97,33},{2,66}... | collective-permute-start | bytes 491528 | tf_op jit(solution)/shard_map/ppermute | solution.py:22
  240.4 4.8 %collective-permute-start.22 = (bf16[80,1024]{1,0:T(8,128)(2,1)S(1)}, bf16[80,1024]{1,0:T(8,128)(2,1)S(1)}, u32[]{:S(2)}, u32[]{:S(2)}) collective-permute-start(bf16[80,1024]{1,0:T(8,128)(2,1)S(1)} %reduce_sum.31.a0), channel_id=1, source_target_pairs={{0,16},{16,0},{1,17},{17,1},{2,18},{18,2},{3,19},{19,3},{4,20},{20... | collective-permute-start | bytes 491528 | tf_op jit(solution)/shard_map/ppermute | solution.py:22
  241.1 4.1 %collective-permute-start.23 = (bf16[80,1024]{1,0:T(8,128)(2,1)S(1)}, bf16[80,1024]{1,0:T(8,128)(2,1)S(1)}, u32[]{:S(2)}, u32[]{:S(2)}) collective-permute-start(bf16[80,1024]{1,0:T(8,128)(2,1)S(1)} %collective-permute-done.19.a1), channel_id=1, source_target_pairs={{0,16},{16,0},{1,17},{17,1},{2,18},{18,2},{3,19},{19,3},{4,20},{20... | collective-permute-start | bytes 491528 | tf_op jit(solution)/shard_map/ppermute | solution.py:22
  241.1 4.1 %collective-permute-start.24 = (bf16[80,1024]{1,0:T(8,128)(2,1)S(1)}, bf16[80,1024]{1,0:T(8,128)(2,1)S(1)}, u32[]{:S(2)}, u32[]{:S(2)}) collective-permute-start(bf16[80,1024]{1,0:T(8,128)(2,1)S(1)} %collective-permute-done.20.a2), channel_id=1, source_target_pairs={{0,16},{16,0},{1,17},{17,1},{2,18},{18,2},{3,19},{19,3},{4,20},{20... | collective-permute-start | bytes 491528 | tf_op jit(solution)/shard_map/ppermute | solution.py:22
  244.5 1.4 collective-permute-start.25
  (18 other events, 15.5 us)

commit v2 on v1

--- a/solution.py
+++ b/solution.py
@@ -54,21 +54,53 @@
     return jnp.pad(values.astype(BF), (0, width - values.shape[0]))[None, :]
 
 
+def gather_ring(value, axis, cut):
+    low, high = shift_by(value, axis, 1), shift_by(value, axis, 3)
+    return [low, high, shift_by(low[:cut], axis, 1), shift_by(high[cut:], axis, 3)]
+
+
 def fresh_row(side, place):
     return (place % 4) * 16 + (side + 1) * 4 + place // 4
 
 
-def local_call(body, outs, operands, scratch=(), flops=0, limit=24):
+class Copies:
+    def __init__(self, sems):
+        self.sems, self.used = sems, 0
+
+    def start(self, source, target):
+        copy = pltpu.make_async_copy(source, target, self.sems.at[self.used])
+        self.used += 1
+        copy.start()
+        return copy
+
+
+def local_call(body, outs, operands, scratch=(), copies=8, flops=0, limit=44):
+    def kernel(*refs):
+        body(Copies(refs[-1]), *refs[:-1])
+
     return pl.pallas_call(
-        body,
+        kernel,
         out_shape=[jax.ShapeDtypeStruct(shape, kind) for shape, kind in outs],
         in_specs=[pl.BlockSpec(memory_space=pltpu.SMEM)]
-        + [pl.BlockSpec(memory_space=pltpu.VMEM)] * (len(operands) - 1),
-        out_specs=[pl.BlockSpec(memory_space=pltpu.VMEM)] * len(outs),
-        scratch_shapes=list(scratch),
+        + [pl.BlockSpec(memory_space=pl.ANY)] * (len(operands) - 1),
+        out_specs=[pl.BlockSpec(memory_space=pl.ANY)] * len(outs),
+        scratch_shapes=[*scratch, pltpu.SemaphoreType.DMA((copies,))],
         compiler_params=pltpu.CompilerParams(vmem_limit_bytes=limit * 1024 * 1024),
         cost_estimate=pl.CostEstimate(flops=flops, bytes_accessed=1024 * 1024, transcendentals=0),
     )(*operands)
+
+
+def like(arrays):
+    return [pltpu.VMEM(array.shape, array.dtype) for array in arrays]
+
+
+def filled(outs):
+    return [pltpu.VMEM(shape, kind) for shape, kind in outs]
+
+
+def wait_all(copies):
+    for copy in copies:
+        copy.wait()
 
 
 def length_column(meta):
@@ -83,43 +115,86 @@
     return inside.astype(F32).astype(BF)
 
 
-def norm_kernel(where_ref, hidden_ref, meta_ref, block_ref, sum_ref):
+def norm_kernel(
+    copies,
+    where_ref,
+    hidden_hbm, meta_hbm, in_hbm, out_hbm, rel_hbm,
+    block_hbm, sum_hbm, weights_hbm,
+    hidden_ref, meta_ref, block_ref, sum_ref,
+):
+    core = where_ref[1]
+    first = [copies.start(hidden_hbm, hidden_ref), copies.start(meta_hbm, meta_ref)]
+    later = []
+    for i in range(2):
+        cols, wide = pl.ds(i * 256, 256), pl.ds(i * 512, 512)
+        source = in_hbm.at[pl.ds(pl.multiple_of(core * 512 + i * 256, 256), 256), :]
+        later.append(copies.start(source, weights_hbm.at[pl.ds(0, 256), cols]))
+        source = out_hbm.at[pl.ds(pl.multiple_of(core * 128, 128), 128), wide]
+        later.append(copies.start(source, weights_hbm.at[pl.ds(256 + i * 128, 128), :]))
+        source = rel_hbm.at[pl.ds(pl.multiple_of(core * 32, 32), 32), wide]
+        later.append(copies.start(source, weights_hbm.at[pl.ds(512 + i * 32, 32), :]))
+    wait_all(first)
     values = hidden_ref[...].astype(F32)
     center = values - jnp.mean(values, axis=-1, keepdims=True)
     spread = jnp.mean(center * center, axis=-1, keepdims=True)
     tokens = values.shape[0]
     block_ref[0:tokens, :] = (center * lax.rsqrt(spread + 1e-05)).astype(BF)
     block_ref[tokens : tokens + 16, :] = meta_ref[...]
+    later.append(copies.start(block_ref, block_hbm))
     pool = pool_rows(length_column(meta_ref[:, 0:128].astype(F32)), tokens)
     sum_ref[...] = dot(pool, hidden_ref[...])
+    later.append(copies.start(sum_ref, sum_hbm))
+    wait_all(later)
 
 
 def encode_kernel(
+    copies,
     where_ref,
-    b0, b1, b2, b3,
-    own_in, own_out,
-    m1, m2, m3,
-    o1, o2, o3,
-    own_rel, hidden_sum_ref,
+    b0, b1, b2, b3_top, b3_rest,
+    own_in, own_out, own_rel,
+    m1, m2, m3_in, m3_rest,
+    o1, o2, o3_in, o3_rest,
+    hidden_sum_hbm,
+    outgoing_hbm, normed_hbm, slope_hbm, pooled_hbm, all_out_hbm, route_hbm, length_hbm, rel_hot_hbm,
+    rel0_hbm, rel1_hbm, rel2_hbm, rel3_hbm,
     outgoing_ref, normed_ref, slope_ref, pooled_ref, all_out_ref, route_ref, length_ref, rel_hot_ref,
     rel0_ref, rel1_ref, rel2_ref, rel3_ref,
-    in_ref, pool_ref, rel_ref,
+    in_ref, pool_ref, rel_ref, meta_ref, hidden_sum_ref,
 ):
     core, my_x, my_y = where_ref[1], where_ref[2], where_ref[3]
-    rel_ref[0:64, :] = own_rel[...]
-    for s, block in enumerate((b0, b1, b2, b3)):
-        normed_ref[s * 256 : (s + 1) * 256, :] = block[0:256, :]
-    in_ref[:, 0:256] = own_in[...]
-    all_out_ref[0:256, :] = own_out[...]
-    for t, (mine, other) in enumerate(((m1, o1), (m2, o2), (m3, o3)), 1):
-        for part, half in ((mine, core), (other, 1 - core)):
+    metas, tokens, weights, tables = [], [], [[], [], [], []], []
+    for s, (block, row) in enumerate(((b0, 256), (b1, 256), (b2, 256), (b3_rest, 128))):
+        metas.append(copies.start(block.at[pl.ds(row, 16), pl.ds(0, 128)], meta_ref.at[s]))
+    tables.append(copies.start(own_rel, rel_ref.at[pl.ds(0, 64), :]))
+    pieces = []
+    for t, (mine, other) in enumerate(
+        (((m1, m1, 256), (o1, o1, 256)), ((m2, m2, 256), (o2, o2, 256)), ((m3_in, m3_rest, 0), (o3_in, o3_rest, 0))), 1
+    ):
+        for (inner, rest, at), half in ((mine, core), (other, 1 - core)):
+            pieces.append((t, inner, rest, at, half))
             for i in range(2):
-                rows = pl.ds(pl.multiple_of(half * 512 + i * 256, 256), 256)
-                in_ref[rows, t * 256 : (t + 1) * 256] = part[0:256, i * 256 : (i + 1) * 256]
-                rows = pl.ds(pl.multiple_of(t * 256 + half * 128, 128), 128)
-                all_out_ref[rows, i * 512 : (i + 1) * 512] = part[256 + i * 128 : 384 + i * 128, :]
                 rows = pl.ds(pl.multiple_of(t * 64 + half * 32, 32), 32)
-                rel_ref[rows, i * 512 : (i + 1) * 512] = part[512 + i * 32 : 544 + i * 32, :]
+                target = rel_ref.at[rows, pl.ds(i * 512, 512)]
+                tables.append(copies.start(rest.at[pl.ds(at + 256 + i * 32, 32), :], target))
+    for s, (block, row, count) in enumerate(((b0, 0, 256), (b1, 256, 256), (b2, 512, 256), (b3_top, 768, 128), (b3_rest, 896, 128))):
+        tokens.append(copies.start(block.at[pl.ds(0, count), :], normed_ref.at[pl.ds(row, count), :]))
+    weights[0].append(copies.start(own_in, in_ref.at[:, pl.ds(0, 256)]))
+    for t, inner, rest, at, half in pieces:
+        for i in range(2):
+            rows = pl.ds(pl.multiple_of(half * 512 + i * 256, 256), 256)
+            target = in_ref.at[rows, pl.ds(t * 256, 256)]
+            weights[t].append(copies.start(inner.at[pl.ds(0, 256), pl.ds(i * 256, 256)], target))
+    outer = [
+        copies.start(own_out, all_out_ref.at[pl.ds(0, 256), :]),
+        copies.start(hidden_sum_hbm, hidden_sum_ref),
+    ]
+    for t, inner, rest, at, half in pieces:
+        for i in range(2):
+            rows = pl.ds(pl.multiple_of(t * 256 + half * 128, 128), 128)
+            target = all_out_ref.at[rows, pl.ds(i * 512, 512)]
+            outer.append(copies.start(rest.at[pl.ds(at + i * 128, 128), :], target))
+    wait_all(metas)
+    wait_all(tables)
 
     wide = (16, 256)
     slot = lanes(wide) % 16
@@ -128,8 +203,8 @@
     bound_hot = (sublanes((128, 256)) == bound + 16).astype(F32).astype(BF)
     ids = jnp.zeros((16, 64), F32)
     asked = (rel0_ref, rel1_ref, rel2_ref, rel3_ref)
-    for s, block in enumerate((b0, b1, b2, b3)):
-        meta = block[256:272, 0:128]
+    for s in range(4):
+        meta = meta_ref[s]
         values = meta.astype(F32)
         apart = lanes(meta.shape) - sublanes(meta.shape)
         wanted = jnp.where(apart == 32, 32.0 * values, jnp.where(apart == 48, values, 0.0))
@@ -156,28 +231,52 @@
     good = (line % 16 < 8) & (local < 52)
     rel_hot_ref[...] = ((name.astype(F32) == ids[0:1, :]) & good).astype(F32).astype(BF)
 
-    @pl.loop(0, 16)
-    def _(step):
-        s, t = step // 4, step % 4
-        rows = pl.ds(pl.multiple_of(s * 256, 256), 256)
-        cols = pl.ds(pl.multiple_of(t * 256, 256), 256)
-        few = pl.ds(pl.multiple_of(s * 16, 16), 16)
-        pre = dot(normed_ref[rows, :], in_ref[:, cols])
-        square = pre * pre
-        tanh = jnp.tanh(GELU_SCALE * pre * (1.0 + GELU_CUBE * square))
-        upper = 0.5 + 0.5 * tanh
-        slope = upper + (0.5 * GELU_SCALE) * pre * (1.0 - tanh * tanh) * (1.0 + 3.0 * GELU_CUBE * square)
-        slope_ref[rows, cols] = slope.astype(BF)
-        pooled_ref[few, cols] = dot(pool_ref[few, :], (pre * upper).astype(BF)).astype(BF)
-
+    sent_out = [
+        copies.start(rel0_ref, rel0_hbm),
+        copies.start(rel1_ref, rel1_hbm),
+        copies.start(rel2_ref, rel2_hbm),
+        copies.start(rel3_ref, rel3_hbm),
+        copies.start(route_ref, route_hbm),
+        copies.start(length_ref, length_hbm),
+        copies.start(rel_hot_ref, rel_hot_hbm),
+    ]
+    wait_all(tokens)
+    sent_out.append(copies.start(normed_ref, normed_hbm))
+    for t in range(4):
+        cols = slice(t * 256, (t + 1) * 256)
+        wait_all(weights[t])
+
+        @pl.loop(0, 4)
+        def _(s):
+            rows = pl.ds(pl.multiple_of(s * 256, 256), 256)
+            few = pl.ds(pl.multiple_of(s * 16, 16), 16)
+            pre = dot(normed_ref[rows, :], in_ref[:, cols])
+            square = pre * pre
+            tanh = jnp.tanh(GELU_SCALE * pre * (1.0 + GELU_CUBE * square))
+            upper = 0.5 + 0.5 * tanh
+            slope = upper + (0.5 * GELU_SCALE) * pre * (1.0 - tanh * tanh) * (1.0 + 3.0 * GELU_CUBE * square)
+            slope_ref[rows, cols] = slope.astype(BF)
+            pooled_ref[few, cols] = dot(pool_ref[few, :], (pre * upper).astype(BF)).astype(BF)
+
+    sent_out.append(copies.start(slope_ref, slope_hbm))
+    sent_out.append(copies.start(pooled_ref, pooled_hbm))
+    wait_all(outer)
+    sent_out.append(copies.start(all_out_ref, all_out_hbm))
     partial = dot(pooled_ref[...], all_out_ref[...])
     partial = jnp.concatenate([partial[0:16] + hidden_sum_ref[...], partial[16:64]], axis=0)
     partial = (partial * length_ref[:, 0:1]).astype(BF)
     outgoing_ref[...] = dot_t(route_ref[...], partial).astype(BF)
+    sent_out.append(copies.start(outgoing_ref, outgoing_hbm))
+    wait_all(sent_out)
 
 
 def graph_kernel(
+    copies,
     where_ref,
+    arrived_hbm, base_hbm, row_hot_hbm, own_hot_t_hbm, e0_hbm, e1_hbm, e2_hbm, e3_hbm,
+    src_hot_hbm, dst_hot_hbm, dst_hot_t_hbm, src_row_hot_hbm,
+    w_msg_hbm, w_self_hbm, d_out_hbm,
+    table_out_hbm, blocks_hbm, graph_out_hbm, aggregate_hbm, nodes_hbm, pre_hbm,
     arrived_ref, base_ref, row_hot_ref, own_hot_t_ref, e0, e1, e2, e3,
     src_hot_ref, dst_hot_ref, dst_hot_t_ref, src_row_hot_ref,
     w_msg_ref, w_self_ref, d_out_ref,
@@ -185,6 +284,28 @@
     ext_ref, sources_ref, edges_ref, agg_grad_ref, sums_ref, rel_ref,
 ):
     scale = (256 / 2048) ** 0.5
+    first = [
+        copies.start(arrived_hbm, arrived_ref),
+        copies.start(base_hbm, base_ref),
+        copies.start(row_hot_hbm, row_hot_ref),
+        copies.start(e0_hbm, e0),
+        copies.start(e1_hbm, e1),
+        copies.start(e2_hbm, e2),
+        copies.start(e3_hbm, e3),
+        copies.start(src_hot_hbm, src_hot_ref),
+    ]
+    second = [copies.start(dst_hot_t_hbm, dst_hot_t_ref)]
+    third = [
+        copies.start(w_msg_hbm, w_msg_ref),
+        copies.start(w_self_hbm, w_self_ref),
+        copies.start(d_out_hbm, d_out_ref),
+    ]
+    fourth = [
+        copies.start(dst_hot_hbm, dst_hot_ref),
+        copies.start(src_row_hot_hbm, src_row_hot_ref),
+        copies.start(own_hot_t_hbm, own_hot_t_ref),
+    ]
+    wait_all(first)
     rel = e0[...].astype(F32) + e1[...].astype(F32) + e2[...].astype(F32) + e3[...].astype(F32)
     for j in range(16):
         rel_ref[j] = rel[j : j + 1]
@@ -194,6 +315,7 @@
     table = total.astype(BF)
     ext_ref[...] = (base_ref[...].astype(F32) + dot(row_hot_ref[...], table)).astype(BF)
     nodes_ref[...] = ext_ref[0:256, :]
+    sent_out = [copies.start(nodes_ref, nodes_hbm)]
 
     @pl.loop(0, 16)
     def _(j):
@@ -202,10 +324,15 @@
         sources_ref[rows, :] = taken.astype(BF)
         edges_ref[rows, :] = (taken * rel_ref[j]).astype(BF)
 
+    wait_all(second)
+
     @pl.loop(0, 4)
     def _(n):
         cols = pl.ds(pl.multiple_of(n * 256, 256), 256)
         aggregate_ref[:, cols] = (scale * dot(dst_hot_t_ref[...], edges_ref[:, cols])).astype(BF)
+
+    sent_out.append(copies.start(aggregate_ref, aggregate_hbm))
+    wait_all(third)
 
     @pl.loop(0, 4)
     def _(n):
@@ -215,10 +342,15 @@
         graph_out_ref[:, cols] = squashed.astype(BF)
         pre_ref[:, cols] = (d_out_ref[:, cols].astype(F32) * (1.0 - squashed * squashed)).astype(BF)
 
+    sent_out.append(copies.start(graph_out_ref, graph_out_hbm))
+    sent_out.append(copies.start(pre_ref, pre_hbm))
+
     @pl.loop(0, 4)
     def _(n):
         cols = pl.ds(pl.multiple_of(n * 256, 256), 256)
         agg_grad_ref[:, cols] = (scale * dot_bt(pre_ref[...], w_msg_ref[cols, :])).astype(BF)
+
+    wait_all(fourth)
 
     @pl.loop(0, 16)
     def _(j):
@@ -228,6 +360,7 @@
         sums_ref[j] = jnp.sum(at_dest * sources_ref[rows, :].astype(F32), axis=0, keepdims=True)
 
     blocks_ref[...] = jnp.concatenate([sums_ref[j] for j in range(16)], axis=0).astype(BF)
+    sent_out.append(copies.start(blocks_ref, blocks_hbm))
     own_pre = dot(own_hot_t_ref[...], pre_ref[0:16, :]).astype(BF)
 
     @pl.loop(0, 4)
@@ -236,15 +369,69 @@
         grad = dot(src_row_hot_ref[...], edges_ref[:, cols]) + dot_bt(own_pre, w_self_ref[cols, :])
         table_out_ref[:, cols] = grad.astype(BF)
 
+    sent_out.append(copies.start(table_out_ref, table_out_hbm))
+    wait_all(sent_out)
+
+
+def weight_kernel(
+    copies,
+    where_ref,
+    aggregate_hbm, nodes_hbm, pre_hbm,
+    kept_hbm, given_hbm,
+    aggregate_ref, nodes_ref, pre_ref,
+    kept_ref, given_ref,
+):
+    core = where_ref[1]
+    wait_all(
+        [copies.start(aggregate_hbm, aggregate_ref), copies.start(nodes_hbm, nodes_ref), copies.start(pre_hbm, pre_ref)]
+    )
+    sent_out = []
+    for half, chunk_ref, chunk_hbm in ((1 - core, given_ref, given_hbm), (core, kept_ref, kept_hbm)):
+
+        @pl.loop(0, 4)
+        def _(z):
+            rows = pl.ds(pl.multiple_of(z * 256 + half * 128, 128), 128)
+            msg = dot_t(aggregate_ref[:, rows], pre_ref[...])
+            own = dot_t(nodes_ref[:, rows], pre_ref[...])
+            for x in range(4):
+                for y in range(4):
+                    at = (x * 4 + y) * 8
+                    both = jnp.concatenate([msg[at : at + 8], own[at : at + 8]], axis=0)
+                    chunk_ref[x, z * 4 + y] = both.astype(BF)
+
+        sent_out.append(copies.start(chunk_ref, chunk_hbm))
+    wait_all(sent_out)
+
 
 def back_kernel(
+    copies,
     where_ref,
+    returned_hbm, route_hbm, length_hbm, all_out_hbm, slope_hbm, pooled_hbm, normed_t_hbm,
+    rel_hot_hbm, r0_hbm, r1_hbm, r2_hbm, r3_hbm,
+    kept_hbm, given_hbm,
     returned_ref, route_ref, length_ref, all_out_ref, slope_ref, pooled_ref, normed_t_ref,
     rel_hot_ref, r0, r1, r2, r3,
     kept_ref, given_ref,
     scaled_ref, grad_ref,
 ):
     core, my_y = where_ref[1], where_ref[3]
+    first = [
+        copies.start(returned_hbm, returned_ref),
+        copies.start(route_hbm, route_ref),
+        copies.start(length_hbm, length_ref),
+        copies.start(rel_hot_hbm, rel_hot_ref),
+        copies.start(r0_hbm, r0),
+        copies.start(r1_hbm, r1),
+        copies.start(r2_hbm, r2),
+        copies.start(r3_hbm, r3),
+    ]
+    second = [
+        copies.start(all_out_hbm, all_out_ref),
+        copies.start(slope_hbm, slope_ref),
+        copies.start(pooled_hbm, pooled_ref),
+        copies.start(normed_t_hbm, normed_t_ref),
+    ]
+    wait_all(first)
     scaled_ref[...] = (dot(route_ref[...], returned_ref[...]) * length_ref[:, 0:1]).astype(BF)
     blocks = jnp.concatenate([r0[...], r1[...], r2[...], r3[...]], axis=0)
     for half, chunk_ref in ((core, kept_ref), (1 - core, given_ref)):
@@ -253,6 +440,8 @@
             rel = dot(rel_hot_ref[rows, :], blocks).astype(BF)
             for z in range(4):
                 chunk_ref[z, y, 64:80, :] = rel[z * 16 : (z + 1) * 16]
+
+    wait_all(second)
 
     @pl.loop(0, 4)
     def _(t):
@@ -280,7 +469,21 @@
                     chunk_ref[z, owner, 0:32, i * 256 : (i + 1) * 256] = piece
 
 
-def place_kernel(where_ref, a0, a1, a2, a3, c0, c1, c2, c3, in_ref, out_ref, rel_ref):
+    sent_out = [copies.start(given_ref, given_hbm), copies.start(kept_ref, kept_hbm)]
+    wait_all(sent_out)
+
+
+def place_kernel(
+    copies,
+    where_ref,
+    h0, h1, h2, h3, h4, h5, h6, h7,
+    in_hbm, out_hbm, rel_hbm,
+    a0, a1, a2, a3, c0, c1, c2, c3,
+    in_ref, out_ref, rel_ref,
+):
+    sources = (h0, h1, h2, h3, h4, h5, h6, h7)
+    targets = (a0, a1, a2, a3, c0, c1, c2, c3)
+    wait_all([copies.start(source, target) for source, target in zip(sources, targets)])
     my_z, core = where_ref[0], where_ref[1]
     for pieces, half in (((a0, a1, a2, a3), core), ((c0, c1, c2, c3), 1 - core)):
         for piece, origin in zip(pieces, ORIGINS):
@@ -291,6 +494,7 @@
                 in_ref[rows, :] = values[0:32, i * 256 : (i + 1) * 256]
             out_ref[pl.ds(pl.multiple_of(half * 128 + z * 32, 32), 32), :] = values[32:64]
             rel_ref[pl.ds(pl.multiple_of(half * 32 + z * 8, 8), 8), :] = values[64:72]
+    wait_all([copies.start(in_ref, in_hbm), copies.start(out_ref, out_hbm), copies.start(rel_ref, rel_hbm)])
 
 
 def shards(
@@ -319,30 +523,46 @@
     shard_rows = rel_table.shape[0]
 
     meta = row_of(jnp.concatenate([desc_len, send_order[0], rel // 32, rel % 32]), width)
-    block, hidden_sum = local_call(
+    rel_pad = jnp.pad(rel_table.reshape(2, shard_rows // 2, width), ((0, 0), (0, 32 - shard_rows // 2), (0, 0)))
+    rel_pad = rel_pad.reshape(64, width)
+    operands = [hidden.reshape(tokens, width), jnp.broadcast_to(meta, (16, width)), w_in, w_out, rel_pad]
+    outs = [((tokens + 16, width), BF), ((entities, width), F32)]
+    block, hidden_sum, weights = local_call(
         norm_kernel,
-        [((tokens + 16, width), BF), ((entities, width), F32)],
-        [where, hidden.reshape(tokens, width), jnp.broadcast_to(meta, (16, width))],
-    )
-    blocks = [block] + [shift_by(block, "x", s) for s in SHIFTS]
-
-    half_k, half_u = width // 2, units // 2
-    in_half = lax.dynamic_slice_in_dim(w_in, my_core * half_k, half_k, 0)
-    out_half = lax.dynamic_slice_in_dim(w_out, my_core * half_u, half_u, 0)
-    rel_pad = jnp.pad(rel_table.reshape(2, shard_rows // 2, width), ((0, 0), (0, 32 - shard_rows // 2), (0, 0)))
-    rel_half = lax.dynamic_index_in_dim(rel_pad, my_core, 0, keepdims=False)
-    weights = jnp.concatenate(
-        [
-            jnp.concatenate([in_half[:units], in_half[units:]], axis=1),
-            out_half[:, : 2 * units],
-            out_half[:, 2 * units :],
-            rel_half[:, : 2 * units],
-            rel_half[:, 2 * units :],
+        [*outs, ((576, 512), BF)],
+        [where, *operands],
+        like(operands[:2]) + filled(outs),
+        copies=10,
+    )
+    blocks = [block, *gather_ring(block, "x", 128)]
+    mine = gather_ring(weights, "y", 256)
+    other = [shift_by(part, "core", 1) for part in mine]
+
+    outs = [
+        ((256, width), BF),
+        ((4 * tokens, width), BF),
+        ((4 * tokens, 4 * units), BF),
+        ((4 * entities, 4 * units), BF),
+        ((4 * units, width), BF),
+        ((4 * entities, 256), BF),
+        ((4 * entities, 128), F32),
+        ((512, 64), BF),
+    ] + [((entities, width), BF)] * 4
+    outgoing, normed, slope, pooled, all_out, route, inverse, rel_hot, *asked = local_call(
+        encode_kernel,
+        outs,
+        [where, *blocks, w_in, w_out, rel_pad, *mine, *other, hidden_sum],
+        filled(outs)
+        + [
+            pltpu.VMEM((width, 4 * units), BF),
+            pltpu.VMEM((4 * entities, tokens), BF),
+            pltpu.VMEM((256, width), BF),
+            pltpu.VMEM((4, 16, 128), BF),
+            pltpu.VMEM((entities, width), F32),
         ],
-        axis=0,
-    )
-    mine = [shift_by(weights, "y", s) for s in SHIFTS]
-    other = [shift_by(part, "core", 1) for part in mine]
+        copies=64,
+        flops=2 * 4 * tokens * width * 4 * units,
+    )
 
     halo = halo_rows[0]
     place = place_order[0]
@@ -356,7 +576,7 @@
         return jnp.concatenate([rows, jnp.pad(row_of(places, width), ((0, 15), (0, 0)))], axis=0)
 
     to_high, to_low = edge_of(boundary[side:], halo_place[side:]), edge_of(boundary[:side], halo_place[:side])
-    to_high, to_low, *blocks = lax.optimization_barrier((to_high, to_low, *blocks))
+    to_high, to_low, outgoing = lax.optimization_barrier((to_high, to_low, outgoing))
     from_low = shift_by(to_high, GROUP, 1)
     from_high = shift_by(to_low, GROUP, 15)
     low_place = from_low[side, :side].astype(I32)
@@ -374,57 +594,32 @@
     src_hot = one_hot(src, extended_count)
     src_row_hot = dot_bt(one_hot_t(table_row, 64), src_hot).astype(BF)
 
-    outgoing, normed, slope, pooled, all_out, route, inverse, rel_hot, *asked = local_call(
-        encode_kernel,
-        [
-            ((256, width), BF),
-            ((4 * tokens, width), BF),
-            ((4 * tokens, 4 * units), BF),
-            ((4 * entities, 4 * units), BF),
-            ((4 * units, width), BF),
-            ((4 * entities, 256), BF),
-            ((4 * entities, 128), F32),
-            ((512, 64), BF),
-        ]
-        + [((entities, width), BF)] * 4,
-        [where, *blocks, w_in, w_out, *mine, *other, rel_pad.reshape(64, width), hidden_sum],
-        [
-            pltpu.VMEM((width, 4 * units), BF),
-            pltpu.VMEM((4 * entities, tokens), BF),
-            pltpu.VMEM((256, width), BF),
-        ],
-        flops=2 * 4 * tokens * width * 4 * units,
-    )
     arrived = lax.all_to_all(outgoing.reshape(16, 16, width), GROUP, 0, 0, tiled=True).reshape(256, width)
     rel_rows = [asked[0]] + [shift_by(rows, "x", o) for rows, o in zip(asked[1:], ORIGINS[1:])]
     normed_t = normed.T
 
+    outs = [((64, width), BF), ((block_count, width), BF)] + [((node_count, width), BF)] * 4
+    operands = [
+        arrived,
+        base,
+        row_hot,
+        one_hot_t(own_row, 64),
+        *rel_rows,
+        src_hot,
+        one_hot(dst, node_count),
+        one_hot_t(dst, node_count),
+        src_row_hot,
+        w_msg,
+        w_self,
+        d_out,
+    ]
     grad_table, grad_blocks, graph_out, aggregate, nodes, grad_pre = local_call(
         graph_kernel,
-        [
-            ((64, width), BF),
-            ((block_count, width), BF),
-            ((node_count, width), BF),
-            ((node_count, width), BF),
-            ((node_count, width), BF),
-            ((node_count, width), BF),
-        ],
-        [
-            where,
-            arrived,
-            base,
-            row_hot,
-            one_hot_t(own_row, 64),
-            *rel_rows,
-            src_hot,
-            one_hot(dst, node_count),
-            one_hot_t(dst, node_count),
-            src_row_hot,
-            w_msg,
-            w_self,
-            d_out,
-        ],
-        [
+        outs,
+        [where, *operands],
+        like(operands)
+        + filled(outs)
+        + [
             pltpu.VMEM((extended_count, width), BF),
             pltpu.VMEM((edge_count, width), BF),
             pltpu.VMEM((edge_count, width), BF),
@@ -432,6 +627,7 @@
             pltpu.VMEM((block_count, 1, width), F32),
             pltpu.VMEM((block_count, 1, width), F32),
         ],
+        copies=24,
         flops=6 * 10**9,
     )
 
@@ -439,41 +635,40 @@
     returned = lax.all_to_all(back.reshape(16, 16, width), GROUP, 0, 0, tiled=True).reshape(256, width)
     rel_blocks = [grad_blocks] + [shift_by(grad_blocks, "x", s) for s in SHIFTS]
 
-    graph_grads = jnp.stack([dot_t(aggregate, grad_pre).astype(BF), dot_t(nodes, grad_pre).astype(BF)])
-    graph_grads = graph_grads.reshape(2, 4, 2, 4, 4, 8, width).transpose(2, 3, 1, 4, 0, 5, 6)
-    graph_grads = graph_grads.reshape(2, 4, 16, 16, width)
-    graph_kept = lax.dynamic_index_in_dim(graph_grads, my_core, 0, keepdims=False)
-    graph_given = lax.dynamic_index_in_dim(graph_grads, 1 - my_core, 0, keepdims=False)
+    outs = [((4, 16, 16, width), BF)] * 2
+    operands = [aggregate, nodes, grad_pre]
+    graph_kept, graph_given = local_call(
+        weight_kernel, outs, [where, *operands], like(operands) + filled(outs), flops=10**9
+    )
     chip = (graph_kept.astype(F32) + shift_by(graph_given, "core", 1).astype(F32)).astype(BF)
-    returned, chip = lax.optimization_barrier((returned, chip))
-    my_x = lax.axis_index("x")
-
-    def for_x(shift):
-        return lax.dynamic_index_in_dim(chip, (my_x + shift) % 4, 0, keepdims=False)
-
-    line_sum = for_x(0).astype(F32)
-    for s in SHIFTS:
-        line_sum = line_sum + shift_by(for_x(s), "x", s).astype(F32)
-    plane = lax.all_to_all(line_sum.astype(BF), ("z", "y"), 0, 0, tiled=True)
-    weight_rows = jnp.sum(plane.astype(F32), axis=0)
-    grad_msg, grad_self = weight_rows[:8], weight_rows[8:]
-
+    line = lax.all_to_all(chip, "x", 0, 0, tiled=True)
+
+    outs = [((4, 4, 80, width), BF)] * 2
+    operands = [returned, route, inverse, all_out, slope, pooled, normed_t, rel_hot, *rel_blocks]
     kept, given = local_call(
         back_kernel,
-        [((4, 4, 80, width), BF), ((4, 4, 80, width), BF)],
-        [where, returned, route, inverse, all_out, slope, pooled, normed_t, rel_hot, *rel_blocks],
-        [pltpu.VMEM((4 * entities, width), BF), pltpu.VMEM((4 * tokens, units), BF)],
+        outs,
+        [where, *operands],
+        like(operands)
+        + filled(outs)
+        + [pltpu.VMEM((4 * entities, width), BF), pltpu.VMEM((4 * tokens, units), BF)],
+        copies=16,
         flops=2 * 4 * tokens * width * 4 * units,
     )
+    given, line = lax.optimization_barrier((given, line))
+    line_sum = jnp.sum(line.astype(F32), axis=0).astype(BF)
     chunks = (kept.astype(F32) + shift_by(given, "core", 1).astype(F32)).astype(BF)
-    chunks = lax.all_to_all(chunks.reshape(16, 80, width), ("z", "y"), 0, 0, tiled=True)
-    part = jnp.sum(chunks.astype(F32), axis=0).astype(BF)
+    chunks = jnp.concatenate([chunks.reshape(16, 80, width), line_sum], axis=1)
+    chunks = lax.all_to_all(chunks, ("z", "y"), 0, 0, tiled=True)
+    summed = jnp.sum(chunks.astype(F32), axis=0)
+    grad_msg, grad_self = summed[80:88], summed[88:96]
+    part = summed[:80].astype(BF)
     parts = [part] + [shift_by(part, "z", s) for s in SHIFTS]
     others = [shift_by(piece, "core", 1) for piece in parts]
+    outs = [((width, units), F32), ((units, width), F32), ((64, width), F32)]
+    operands = [*parts, *others]
     grad_w_in, grad_w_out, grad_rel = local_call(
-        place_kernel,
-        [((width, units), F32), ((units, width), F32), ((64, width), F32)],
-        [where, *parts, *others],
+        place_kernel, outs, [where, *operands], like(operands) + filled(outs), copies=12
     )
     return (graph_out, grad_w_in, grad_w_out, grad_rel[:shard_rows], grad_msg, grad_self)
 

time: 251 us -> 254 us (1.012)
  blocking collectives: 0 us -> 45.7 us
  local copies, waits for them, and re-layouts: 49.9 us -> 28.9 us
  waiting for transfers between devices: 77.6 us -> 63 us
  starting transfers between devices: 57.2 us -> 43 us
  Pallas kernels: 40.4 us -> 51.3 us
  other arithmetic: 19.1 us -> 16.4 us
    all_to_all x0 -> x1, blocking collectives: none -> 45.7 us  [shards(): chunks = lax.all_to_all(chunks, ('z', 'y'), 0, 0, tiled=True)]
    all_to_all x2 -> x1, waiting for transfers between devices: 14 us -> 0.01 us  [shards(): line = lax.all_to_all(chip, 'x', 0, 0, tiled=True)]
    unnamed x99 -> x74, local copies, waits for them, and re-layouts: 36.3 us -> 22.9 us
    pallas_call x5 -> x6, Pallas kernels: 40.4 us -> 51.3 us  [local_call(): pl.pallas_call(kernel, out_shape=[jax.ShapeDtypeStruct(shape, kind) for s...]
    ppermute x29, waiting for transfers between devices: 63.6 us -> 54.5 us  [shift_by(): lax.ppermute(value, axis, [(i, (i + shift) % count) for i in range(count)])]
    all_to_all x1, waiting for transfers between devices: 0.01 us -> 8.47 us  [shards(): lax.all_to_all(back.reshape(16, 16, width), GROUP, 0, 0, tiled=True)]
    all_to_all x2 -> x1, starting transfers between devices: 12.1 us -> 4.44 us  [shards(): line = lax.all_to_all(chip, 'x', 0, 0, tiled=True)]
    squeeze x3 -> x0, local copies, waits for them, and re-layouts: 4.4 us -> none  [the longest x1 2.56 us: for_x(): return lax.dynamic_index_in_dim(chip, (my_x + shift) % 4, 0, keepdims=False)]
  transfers between devices with their start and end apart: 33 -> 32, of which waited for: 13 -> 16; matrix products, arithmetic and copies ran while one was open for 10% -> 6% of each run, Pallas kernels for 0% -> 4%
where the time goes in v2:
time: 254 us; the launch traced here: 251 us
  waiting for transfers between devices  63 us (25%)
  Pallas kernels  51.3 us (20%)
  blocking collectives  45.7 us (18%)
  starting transfers between devices  43 us (17%)
  local copies, waits for them, and re-layouts  28.9 us (11%)
  other arithmetic  16.4 us (6%)
    ppermute x29, waiting for transfers between devices, shift_by(): lax.ppermute(value, axis, [(i, (i + shift) % count) for i in range(count)])  54.5 us
    pallas_call x6, Pallas kernels, local_call(): pl.pallas_call(kernel, out_shape=[jax.ShapeDtypeStruct(shape, kind) for s...  51.3 us
    all_to_all x1, blocking collectives, shards(): chunks = lax.all_to_all(chunks, ('z', 'y'), 0, 0, tiled=True)  45.7 us
    ppermute x29, starting transfers between devices, shift_by(): lax.ppermute(value, axis, [(i, (i + shift) % count) for i in range(count)])  30.7 us
    unnamed x74, local copies, waits for them, and re-layouts  22.9 us
    all_to_all x1, waiting for transfers between devices, shards(): lax.all_to_all(back.reshape(16, 16, width), GROUP, 0, 0, tiled=True)  8.47 us
  transfers between devices with their start and end apart: 32, of which 16 were waited for; matrix products, arithmetic and copies ran while one was open for 6% of the time, Pallas kernels for 4%

profile of v2, /device:TPU:0, one launch (start us, length us, event | category | flops | bytes accessed | tf_op | source)
XLA Modules:
  0.0 251.2 jit_solution(12740132975740751537)
XLA Ops:
  0.7 0.7 fusion.37
  2.7 0.9 reshape.54
  3.9 1.0 copy-done.4
  4.9 1.0 copy-done.5
  5.9 1.0 copy-done.7
  7.0 1.5 shard_map.190
  8.5 1.6 collective-permute-start
  10.1 1.7 collective-permute-start.1
  11.8 1.7 collective-permute-start.4
  13.4 1.6 collective-permute-start.5
  15.0 1.0 fusion.3.refs_10_
  16.1 1.2 fusion.4.refs_11_
  18.2 5.8 %collective-permute-done.refs_2_ = bf16[272,1024]{1,0:T(8,128)(2,1)S(1)} collective-permute-done((bf16[272,1024]{1,0:T(8,128)(2,1)S(1)}, bf16[272,1024]{1,0:T(8,128)(2,1)S(1)}, u32[]{:S(2)}, u32[]{:S(2)}) %collective-permute-start) | collective-permute-done | bytes 557088 | tf_op jit(solution)/shard_map/ppermute | solution.py:22
  24.6 3.1 %collective-permute-done.4.refs_9_ = bf16[576,512]{1,0:T(8,128)(2,1)S(1)} collective-permute-done((bf16[576,512]{1,0:T(8,128)(2,1)S(1)}, bf16[576,512]{1,0:T(8,128)(2,1)S(1)}, u32[]{:S(2)}, u32[]{:S(2)}) %collective-permute-start.4) | collective-permute-done | bytes 589856 | tf_op jit(solution)/shard_map/ppermute | solution.py:22
  28.1 3.0 %collective-permute-start.7 = (bf16[320,512]{1,0:T(8,128)(2,1)S(1)}, bf16[320,512]{1,0:T(8,128)(2,1)S(1)}, u32[]{:S(2)}, u32[]{:S(2)}) collective-permute-start(bf16[320,512]{1,0:T(8,128)(2,1)S(1)} %slice.72), channel_id=1, source_target_pairs={{0,3},{1,0},{2,1},{3,2},{4,7},{5,4},{6,5},{7,6},{8,11},{9,8},{10,9... | collective-permute-start | bytes 983048 | tf_op jit(solution)/shard_map/ppermute | solution.py:22
  32.3 1.0 collective-permute-start.3
  33.3 2.3 collective-permute-done.6.refs_11_
  35.6 0.8 collective-permute-done.7.refs_12_
  36.5 4.2 %collective-permute-done.3.refs_5_ = bf16[144,1024]{1,0:T(8,128)(2,1)S(1)} collective-permute-done((bf16[144,1024]{1,0:T(8,128)(2,1)S(1)}, bf16[144,1024]{1,0:T(8,128)(2,1)S(1)}, u32[]{:S(2)}, u32[]{:S(2)}) %collective-permute-start.3) | collective-permute-done | bytes 294944 | tf_op jit(solution)/shard_map/ppermute | solution.py:22
  40.7 13.9 %shard_map.191 = (bf16[256,1024]{1,0:T(8,128)(2,1)}, bf16[1024,1024]{1,0:T(8,128)(2,1)S(1)}, bf16[1024,1024]{1,0:T(8,128)(2,1)}, bf16[64,1024]{1,0:T(8,128)(2,1)...) custom-call(s32[4]{0:T(128)S(1)} %pad_add_fusion.1.refs_0_, ...), custom_call_target="tpu_custom_call" | custom-call | flops 2147483648 | bytes 1048576 | tf_op jit(solution)/shard_map/pallas_call | solution.py:81
  54.7 1.3 copy-done
  59.1 2.9 %collective-permute-start.13 = (bf16[80,1024]{1,0:T(8,128)(2,1)S(1)}, bf16[80,1024]{1,0:T(8,128)(2,1)S(1)}, u32[]{:S(2)}, u32[]{:S(2)}) collective-permute-start(bf16[80,1024]{1,0:T(8,128)(2,1)S(1)} %get-tuple-element.45), channel_id=1, source_target_pairs={{0,15},{1,0},{2,1},{3,2},{4,3},{5,4},{6,5},{7,6},{8,7},{9,8},{10,9... | collective-permute-start | bytes 491528 | tf_op jit(solution)/shard_map/ppermute | solution.py:22
  62.1 4.2 %all-to-all-start = ((bf16[16,16,1024]{2,1,0:T(8,128)(2,1)}), bf16[16,16,1024]{2,1,0:T(8,128)(2,1)}, u32[]{:S(2)}, u32[]{:S(2)}) async-start(bf16[16,16,1024]{2,1,0:T(8,128)(2,1)} %bitcast.10), calls=%async_computation | async-start | bytes 1048576 | tf_op jit(solution)/shard_map/all_to_all | solution.py:597
  66.3 1.7 collective-permute-start.12
  68.1 2.8 %collective-permute-start.14 = (bf16[16,1024]{1,0:T(8,128)(2,1)}, bf16[16,1024]{1,0:T(8,128)(2,1)S(1)}, u32[]{:S(2)}, u32[]{:S(2)}) collective-permute-start(bf16[16,1024]{1,0:T(8,128)(2,1)} %get-tuple-element.47), channel_id=1, source_target_pairs={{0,12},{4,0},{8,4},{12,8},{1,13},{5,1},{9,5},{13,9},{2,14},{6,2},{... | collective-permute-start | bytes 98312 | tf_op jit(solution)/shard_map/ppermute | solution.py:22
  70.8 2.3 collective-permute-start.16
  73.2 7.7 %collective-permute-done.12 = bf16[80,1024]{1,0:T(8,128)(2,1)S(1)} collective-permute-done((bf16[80,1024]{1,0:T(8,128)(2,1)S(1)}, bf16[80,1024]{1,0:T(8,128)(2,1)S(1)}, u32[]{:S(2)}, u32[]{:S(2)}) %collective-permute-start.12) | collective-permute-done | bytes 163872 | tf_op jit(solution)/shard_map/ppermute | solution.py:22
  81.0 1.5 fusion.2.refs_12_
  82.5 1.2 pad_maximum_fusion.1.refs_2_
  85.7 1.2 copy-done.3
  86.9 1.6 copy-done.9
  88.5 1.0 copy-done.10
  89.6 0.8 copy-done.14
  90.3 0.8 copy-done.16
  91.1 0.8 copy-done.18
  91.9 0.9 copy-done.21
  92.8 0.8 copy-done.31
  93.6 18.7 %shard_map.192 = (bf16[64,1024]{1,0:T(8,128)(2,1)S(1)}, bf16[16,1024]{1,0:T(8,128)(2,1)S(1)}, bf16[256,1024]{1,0:T(8,128)(2,1)}, bf16[256,1024]{1,0:T(8,128)(2,1...) custom-call(s32[4]{0:T(128)S(1)} %pad_add_fusion.1.refs_0_, bf16[256,1024]{1,0:T(8,128)(2,1)} %bitcast.11.refs_1_, ...), custom_call_target="tpu_custom_call" | custom-call | flops 6000000000 | bytes 1048576 | tf_op jit(solution)/shard_map/pallas_call | solution.py:81
  112.3 3.6 %shard_map.194 = (bf16[4,16,16,1024]{3,2,1,0:T(8,128)(2,1)S(1)}, bf16[4,16,16,1024]{3,2,1,0:T(8,128)(2,1)}) custom-call(s32[4]{0:T(128)S(1)} %pad_add_fusion.1.refs_0_, bf16[256,1024]{1,0:T(8,128)(2,1)S(1)} %get-tuple-element.62.refs_1_, bf16[256,1024]{1,0:T(8,128)(2,1)S(1)} %get-tuple-element.63.refs_2_, bf16[256,1024]{1,0:T(8,128)(2,1)S(1)} %get-tuple-element.64.refs_3_), custom_call_target="tpu_custom_call" | custom-call | flops 1000000000 | bytes 1048576 | tf_op jit(solution)/shard_map/pallas_call | solution.py:81
  116.1 0.9 broadcast_in_dim.65
  116.9 3.6 %all-to-all-start.1 = ((bf16[16,16,1024]{2,1,0:T(8,128)(2,1)}), bf16[16,16,1024]{2,1,0:T(8,128)(2,1)S(1)}, u32[]{:S(2)}, u32[]{:S(2)}) async-start(bf16[16,16,1024]{2,1,0:T(8,128)(2,1)} %bitcast.20), calls=%async_computation.1 | async-start | bytes 1048576 | tf_op jit(solution)/shard_map/all_to_all | solution.py:635
  120.6 3.9 %add_convert_fusion.1 = bf16[4,16,16,1024]{3,2,1,0:T(8,128)(2,1)} fusion(bf16[4,16,16,1024]{3,2,1,0:T(8,128)(2,1)} %collective-permute-done.20, bf16[4,16,16,1024]{3,2,1,0:T(8,128)(2,1)S(1)} %get-tuple-element.65), kind=kLoop, calls=%fused_computation.2 | loop fusion | flops 4194304 | bytes 6291456 | tf_op jit(solution)/shard_map/convert_element_type | solution.py:643
  124.4 8.5 %all-to-all-done.1 = bf16[16,16,1024]{2,1,0:T(8,128)(2,1)S(1)} async-done(((bf16[16,16,1024]{2,1,0:T(8,128)(2,1)}), bf16[16,16,1024]{2,1,0:T(8,128)(2,1)S(1)}, u32[]{:S(2)}, u32[]{:S(2)}) %all-to-all-start.1) | async-done | bytes 524320 | tf_op jit(solution)/shard_map/all_to_all | solution.py:635
  132.9 4.4 %all-to-all-start.2 = ((bf16[4,16,16,1024]{3,2,1,0:T(8,128)(2,1)}), bf16[4,16,16,1024]{3,2,1,0:T(8,128)(2,1)}, u32[]{:S(2)}, u32[]{:S(2)}) async-start(bf16[4,16,16,1024]{3,2,1,0:T(8,128)(2,1)} %add_convert_fusion.1), calls=%async_computation.2 | async-start | bytes 4194304 | tf_op jit(solution)/shard_map/all_to_all | solution.py:644
  137.4 2.0 collective-permute-start.17
  139.4 1.3 collective-permute-start.18
  140.7 2.2 collective-permute-start.19
  142.9 2.6 %copy.23 = bf16[1024,1024]{0,1:T(8,128)(2,1)} copy(bf16[1024,1024]{1,0:T(8,128)(2,1)S(1)} %copy-done.1) | data formatting | bytes 4194304 | tf_op jit(solution)/shard_map/pallas_call | solution.py:81
  145.5 16.5 %collective-permute-done.17.refs_10_ = bf16[16,1024]{1,0:T(8,128)(2,1)S(1)} collective-permute-done((bf16[16,1024]{1,0:T(8,128)(2,1)S(1)}, bf16[16,1024]{1,0:T(8,128)(2,1)S(1)}, u32[]{:S(2)}, u32[]{:S(2)}) %collective-permute-start.17) | collective-permute-done | bytes 32800 | tf_op jit(solution)/shard_map/ppermute | solution.py:22
  162.7 1.9 collective-permute-done.19.refs_12_
  164.6 1.6 copy-done.2
  166.2 1.6 copy-done.19
  167.8 1.6 copy-done.20
  169.4 0.9 copy-done.25
  170.3 9.6 %shard_map.193 = (bf16[4,4,80,1024]{3,2,1,0:T(8,128)(2,1)S(1)}, bf16[4,4,80,1024]{3,2,1,0:T(8,128)(2,1)}) custom-call(s32[4]{0:T(128)S(1)} %pad_add_fusion.1.refs_0_, bf16[256,1024]{1,0:T(8,128)(2,1)S(1)} %bitcast.60, bf16[64,256]{1,0:T(8,128)(2,1)S(1)} %copy-done.27, f32[64,128]{1,0:T(8,128)S(1)} %copy-done.29, bf16[1024,1024]{1,0:T(8,128)(2,1)S(1)} %copy-done.20, ...), custom_call_target="tpu_custom_call" | custom-call | flops 2147483648 | bytes 1048576 | tf_op jit(solution)/shard_map/pallas_call | solution.py:81
  180.1 2.0 reduce_sum.31
  182.1 3.2 %collective-permute-done.21 = bf16[4,4,80,1024]{3,2,1,0:T(8,128)(2,1)} collective-permute-done((bf16[4,4,80,1024]{3,2,1,0:T(8,128)(2,1)}, bf16[4,4,80,1024]{3,2,1,0:T(8,128)(2,1)}, u32[]{:S(2)}, u32[]{:S(2)}) %collective-permute-start.21) | collective-permute-done | bytes 2621472 | tf_op jit(solution)/shard_map/ppermute | solution.py:22
  185.3 3.0 %add_convert_fusion = bf16[4,4,80,1024]{3,2,1,0:T(8,128)(2,1)S(1)} fusion(bf16[4,4,80,1024]{3,2,1,0:T(8,128)(2,1)} %collective-permute-done.21, bf16[4,4,80,1024]{3,2,1,0:T(8,128)(2,1)S(1)} %get-tuple-element.60), kind=kLoop, calls=%fused_computation.1 | loop fusion | flops 5242880 | bytes 7864320 | tf_op jit(solution)/shard_map/convert_element_type | solution.py:660
  188.7 45.7 %all_to_all.20 = bf16[16,96,1024]{2,1,0:T(8,128)(2,1)S(1)} all-to-all(bf16[16,96,1024]{2,1,0:T(8,128)(2,1)S(1)} %pad_maximum_fusion), channel_id=1, replica_groups=mesh['z'=4,'core'=2,'x'=4,'y'=4] {'z','y'}, dimensions={0} | all-to-all | bytes 6291456 | tf_op jit(solution)/shard_map/all_to_all | solution.py:662
  235.2 3.2 %collective-permute-start.23 = (bf16[80,1024]{1,0:T(8,128)(2,1)S(1)}, bf16[80,1024]{1,0:T(8,128)(2,1)S(1)}, u32[]{:S(2)}, u32[]{:S(2)}) collective-permute-start(bf16[80,1024]{1,0:T(8,128)(2,1)S(1)} %slice.91.refs_1_), channel_id=1, source_target_pairs={{0,96},{32,0},{64,32},{96,64},{1,97},{33,1},{65,33},{97,65},{2,98}... | collective-permute-start | bytes 491528 | tf_op jit(solution)/shard_map/ppermute | solution.py:22
  238.4 5.0 %collective-permute-done.22.refs_2_ = bf16[80,1024]{1,0:T(8,128)(2,1)S(1)} collective-permute-done((bf16[80,1024]{1,0:T(8,128)(2,1)S(1)}, bf16[80,1024]{1,0:T(8,128)(2,1)S(1)}, u32[]{:S(2)}, u32[]{:S(2)}) %collective-permute-start.22) | collective-permute-done | bytes 163872 | tf_op jit(solution)/shard_map/ppermute | solution.py:22
  244.0 1.2 collective-permute-done.24.refs_4_
  245.9 0.8 collective-permute-done.28.refs_8_
  246.6 3.8 %shard_map.195 = (f32[1024,256]{1,0:T(8,128)}, f32[256,1024]{1,0:T(8,128)}, f32[64,1024]{1,0:T(8,128)S(1)}) custom-call(s32[4]{0:T(128)S(1)} %pad_add_fusion.1.refs_0_, bf16[80,1024]{1,0:T(8,128)(2,1)S(1)} %slice.91.refs_1_, bf16[80,1024]{1,0:T(8,128)(2,1)S(1)} %collective-permute-done.22.refs_2_, bf16[80,1024]{1,0:T(8,128)(2,1)S(1)} %collective-permute-done.23.refs_3_, ...), custom_call_target="tpu_custom_call" | custom-call | bytes 1048576 | tf_op jit(solution)/shard_map/pallas_call | solution.py:81
  (130 shorter events, 13.8 us)
Async XLA Ops:
  0.6 15.4 %copy-start.33 = (s32[1,2048]{1,0:T(1,128)S(1)}, s32[1,2048]{1,0:T(1,128)}, u32[]{:S(2)}) copy-start(s32[1,2048]{1,0:T(1,128)} %param.24) | copy-start | bytes 24580
  0.6 16.6 %copy-start.36 = (s32[1,16]{1,0:T(1,128)S(1)}, s32[1,16]{1,0:T(1,128)}, u32[]{:S(2)}) copy-start(s32[1,16]{1,0:T(1,128)} %param.20) | copy-start | bytes 196
  0.7 16.6 %copy-start.35 = (s32[1,128]{1,0:T(1,128)S(1)}, s32[1,128]{1,0:T(1,128)}, u32[]{:S(2)}) copy-start(s32[1,128]{1,0:T(1,128)} %param.22) | copy-start | bytes 1540
  0.7 16.7 %copy-start.32 = (bf16[240,1024]{1,0:T(8,128)(2,1)S(1)}, bf16[240,1024]{1,0:T(8,128)(2,1)}, u32[]{:S(2)}) copy-start(bf16[240,1024]{1,0:T(8,128)(2,1)} %param.21) | copy-start | bytes 1474564
  0.7 17.0 %copy-start.34 = (s32[1,2048]{1,0:T(1,128)S(1)}, s32[1,2048]{1,0:T(1,128)}, u32[]{:S(2)}) copy-start(s32[1,2048]{1,0:T(1,128)} %param.23) | copy-start | bytes 24580
  3.9 1.0 copy-start.4
  4.9 1.0 copy-start.5
  5.9 1.0 copy-start.7
  8.5 15.5 %collective-permute-start = (bf16[272,1024]{1,0:T(8,128)(2,1)S(1)}, bf16[272,1024]{1,0:T(8,128)(2,1)S(1)}, u32[]{:S(2)}, u32[]{:S(2)}) collective-permute-start(bf16[272,1024]{1,0:T(8,128)(2,1)S(1)} %get-tuple-element.39.refs_1_), channel_id=1, source_target_pairs={{0,4},{4,8},{8,12},{12,0},{1,5},{5,9},{9,13},{13,1},{2,6},{6,10},{... | collective-permute-start | bytes 1671176 | tf_op jit(solution)/shard_map/ppermute | solution.py:22
  10.1 21.0 %collective-permute-start.1 = (bf16[272,1024]{1,0:T(8,128)(2,1)S(1)}, bf16[272,1024]{1,0:T(8,128)(2,1)S(1)}, u32[]{:S(2)}, u32[]{:S(2)}) collective-permute-start(bf16[272,1024]{1,0:T(8,128)(2,1)S(1)} %get-tuple-element.39.refs_1_), channel_id=1, source_target_pairs={{0,12},{4,0},{8,4},{12,8},{1,13},{5,1},{9,5},{13,9},{2,14},{6,2},{... | collective-permute-start | bytes 1671176 | tf_op jit(solution)/shard_map/ppermute | solution.py:22
  11.8 15.9 %collective-permute-start.4 = (bf16[576,512]{1,0:T(8,128)(2,1)S(1)}, bf16[576,512]{1,0:T(8,128)(2,1)S(1)}, u32[]{:S(2)}, u32[]{:S(2)}) collective-permute-start(bf16[576,512]{1,0:T(8,128)(2,1)S(1)} %get-tuple-element.40), channel_id=1, source_target_pairs={{0,1},{1,2},{2,3},{3,0},{4,5},{5,6},{6,7},{7,4},{8,9},{9,10},{10,1... | collective-permute-start | bytes 1769480 | tf_op jit(solution)/shard_map/ppermute | solution.py:22
  13.4 14.6 %collective-permute-start.5 = (bf16[576,512]{1,0:T(8,128)(2,1)S(1)}, bf16[576,512]{1,0:T(8,128)(2,1)S(1)}, u32[]{:S(2)}, u32[]{:S(2)}) collective-permute-start(bf16[576,512]{1,0:T(8,128)(2,1)S(1)} %get-tuple-element.40), channel_id=1, source_target_pairs={{0,3},{1,0},{2,1},{3,2},{4,7},{5,4},{6,5},{7,6},{8,11},{9,8},{10,9... | collective-permute-start | bytes 1769480 | tf_op jit(solution)/shard_map/ppermute | solution.py:22
  17.6 23.1 %copy-start.6 = (bf16[1024,256]{1,0:T(8,128)(2,1)S(1)}, bf16[1024,256]{1,0:T(8,128)(2,1)}, u32[]{:S(2)}) copy-start(bf16[1024,256]{1,0:T(8,128)(2,1)} %refs_6_.1) | copy-start | bytes 1572868
  17.6 23.1 %copy-start.8 = (bf16[256,1024]{1,0:T(8,128)(2,1)S(1)}, bf16[256,1024]{1,0:T(8,128)(2,1)}, u32[]{:S(2)}) copy-start(bf16[256,1024]{1,0:T(8,128)(2,1)} %refs_7_.1) | copy-start | bytes 1572868
  24.0 8.3 %collective-permute-start.2 = (bf16[128,1024]{1,0:T(8,128)(2,1)S(1)}, bf16[128,1024]{1,0:T(8,128)(2,1)S(1)}, u32[]{:S(2)}, u32[]{:S(2)}) collective-permute-start(bf16[128,1024]{1,0:T(8,128)(2,1)S(1)} %slice.69), channel_id=1, source_target_pairs={{0,4},{4,8},{8,12},{12,0},{1,5},{5,9},{9,13},{13,1},{2,6},{6,10},{... | collective-permute-start | bytes 786440 | tf_op jit(solution)/shard_map/ppermute | solution.py:22
  27.7 8.0 %collective-permute-start.6 = (bf16[256,512]{1,0:T(8,128)(2,1)S(1)}, bf16[256,512]{1,0:T(8,128)(2,1)S(1)}, u32[]{:S(2)}, u32[]{:S(2)}) collective-permute-start(bf16[256,512]{1,0:T(8,128)(2,1)S(1)} %slice.71), channel_id=1, source_target_pairs={{0,1},{1,2},{2,3},{3,0},{4,5},{5,6},{6,7},{7,4},{8,9},{9,10},{10,1... | collective-permute-start | bytes 786440 | tf_op jit(solution)/shard_map/ppermute | solution.py:22
  28.1 8.4 %collective-permute-start.7 = (bf16[320,512]{1,0:T(8,128)(2,1)S(1)}, bf16[320,512]{1,0:T(8,128)(2,1)S(1)}, u32[]{:S(2)}, u32[]{:S(2)}) collective-permute-start(bf16[320,512]{1,0:T(8,128)(2,1)S(1)} %slice.72), channel_id=1, source_target_pairs={{0,3},{1,0},{2,1},{3,2},{4,7},{5,4},{6,5},{7,6},{8,11},{9,8},{10,9... | collective-permute-start | bytes 983048 | tf_op jit(solution)/shard_map/ppermute | solution.py:22
  31.1 9.6 %collective-permute-start.8 = (bf16[576,512]{1,0:T(8,128)(2,1)S(1)}, bf16[576,512]{1,0:T(8,128)(2,1)S(1)}, u32[]{:S(2)}, u32[]{:S(2)}) collective-permute-start(bf16[576,512]{1,0:T(8,128)(2,1)S(1)} %collective-permute-done.4.refs_9_), channel_id=1, source_target_pairs={{0,16},{16,0},{1,17},{17,1},{2,18},{18,2},{3,19},{19,3},{4,20},{20... | collective-permute-start | bytes 1769480 | tf_op jit(solution)/shard_map/ppermute | solution.py:22
  31.1 9.6 %collective-permute-start.9 = (bf16[576,512]{1,0:T(8,128)(2,1)S(1)}, bf16[576,512]{1,0:T(8,128)(2,1)S(1)}, u32[]{:S(2)}, u32[]{:S(2)}) collective-permute-start(bf16[576,512]{1,0:T(8,128)(2,1)S(1)} %collective-permute-done.5.refs_10_), channel_id=1, source_target_pairs={{0,16},{16,0},{1,17},{17,1},{2,18},{18,2},{3,19},{19,3},{4,20},{20... | collective-permute-start | bytes 1769480 | tf_op jit(solution)/shard_map/ppermute | solution.py:22
  32.3 8.3 %collective-permute-start.3 = (bf16[144,1024]{1,0:T(8,128)(2,1)S(1)}, bf16[144,1024]{1,0:T(8,128)(2,1)S(1)}, u32[]{:S(2)}, u32[]{:S(2)}) collective-permute-start(bf16[144,1024]{1,0:T(8,128)(2,1)S(1)} %slice.70), channel_id=1, source_target_pairs={{0,12},{4,0},{8,4},{12,8},{1,13},{5,1},{9,5},{13,9},{2,14},{6,2},{... | collective-permute-start | bytes 884744 | tf_op jit(solution)/shard_map/ppermute | solution.py:22
  35.6 5.1 %collective-permute-start.10 = (bf16[256,512]{1,0:T(8,128)(2,1)S(1)}, bf16[256,512]{1,0:T(8,128)(2,1)S(1)}, u32[]{:S(2)}, u32[]{:S(2)}) collective-permute-start(bf16[256,512]{1,0:T(8,128)(2,1)S(1)} %collective-permute-done.6.refs_11_), channel_id=1, source_target_pairs={{0,16},{16,0},{1,17},{17,1},{2,18},{18,2},{3,19},{19,3},{4,20},{20... | collective-permute-start | bytes 786440 | tf_op jit(solution)/shard_map/ppermute | solution.py:22
  36.4 4.3 %collective-permute-start.11 = (bf16[320,512]{1,0:T(8,128)(2,1)S(1)}, bf16[320,512]{1,0:T(8,128)(2,1)S(1)}, u32[]{:S(2)}, u32[]{:S(2)}) collective-permute-start(bf16[320,512]{1,0:T(8,128)(2,1)S(1)} %collective-permute-done.7.refs_12_), channel_id=1, source_target_pairs={{0,16},{16,0},{1,17},{17,1},{2,18},{18,2},{3,19},{19,3},{4,20},{20... | collective-permute-start | bytes 983048 | tf_op jit(solution)/shard_map/ppermute | solution.py:22
  54.7 1.3 copy-start
  56.0 0.7 copy-start.22
  56.7 0.6 copy-start.24
  59.1 14.0 %collective-permute-start.13 = (bf16[80,1024]{1,0:T(8,128)(2,1)S(1)}, bf16[80,1024]{1,0:T(8,128)(2,1)S(1)}, u32[]{:S(2)}, u32[]{:S(2)}) collective-permute-start(bf16[80,1024]{1,0:T(8,128)(2,1)S(1)} %get-tuple-element.45), channel_id=1, source_target_pairs={{0,15},{1,0},{2,1},{3,2},{4,3},{5,4},{6,5},{7,6},{8,7},{9,8},{10,9... | collective-permute-start | bytes 491528 | tf_op jit(solution)/shard_map/ppermute | solution.py:22
  62.1 23.6 %all-to-all-start = ((bf16[16,16,1024]{2,1,0:T(8,128)(2,1)}), bf16[16,16,1024]{2,1,0:T(8,128)(2,1)}, u32[]{:S(2)}, u32[]{:S(2)}) async-start(bf16[16,16,1024]{2,1,0:T(8,128)(2,1)} %bitcast.10), calls=%async_computation | async-start | bytes 1048576 | tf_op jit(solution)/shard_map/all_to_all | solution.py:597
  66.3 14.5 %collective-permute-start.12 = (bf16[80,1024]{1,0:T(8,128)(2,1)S(1)}, bf16[80,1024]{1,0:T(8,128)(2,1)S(1)}, u32[]{:S(2)}, u32[]{:S(2)}) collective-permute-start(bf16[80,1024]{1,0:T(8,128)(2,1)S(1)} %get-tuple-element.44), channel_id=1, source_target_pairs={{0,1},{1,2},{2,3},{3,4},{4,5},{5,6},{6,7},{7,8},{8,9},{9,10},{10,1... | collective-permute-start | bytes 491528 | tf_op jit(solution)/shard_map/ppermute | solution.py:22
  68.1 15.8 %collective-permute-start.14 = (bf16[16,1024]{1,0:T(8,128)(2,1)}, bf16[16,1024]{1,0:T(8,128)(2,1)S(1)}, u32[]{:S(2)}, u32[]{:S(2)}) collective-permute-start(bf16[16,1024]{1,0:T(8,128)(2,1)} %get-tuple-element.47), channel_id=1, source_target_pairs={{0,12},{4,0},{8,4},{12,8},{1,13},{5,1},{9,5},{13,9},{2,14},{6,2},{... | collective-permute-start | bytes 98312 | tf_op jit(solution)/shard_map/ppermute | solution.py:22
  70.8 13.7 %collective-permute-start.15 = (bf16[16,1024]{1,0:T(8,128)(2,1)}, bf16[16,1024]{1,0:T(8,128)(2,1)S(1)}, u32[]{:S(2)}, u32[]{:S(2)}) collective-permute-start(bf16[16,1024]{1,0:T(8,128)(2,1)} %get-tuple-element.48), channel_id=1, source_target_pairs={{0,4},{4,8},{8,12},{12,0},{1,5},{5,9},{9,13},{13,1},{2,6},{6,10},{... | collective-permute-start | bytes 98312 | tf_op jit(solution)/shard_map/ppermute | solution.py:22
  70.8 14.3 %collective-permute-start.16 = (bf16[16,1024]{1,0:T(8,128)(2,1)}, bf16[16,1024]{1,0:T(8,128)(2,1)S(1)}, u32[]{:S(2)}, u32[]{:S(2)}) collective-permute-start(bf16[16,1024]{1,0:T(8,128)(2,1)} %get-tuple-element.49), channel_id=1, source_target_pairs={{0,8},{4,12},{8,0},{12,4},{1,9},{5,13},{9,1},{13,5},{2,10},{6,14},... | collective-permute-start | bytes 98312 | tf_op jit(solution)/shard_map/ppermute | solution.py:22
  83.9 0.6 copy-start.13
  85.7 1.2 copy-start.3
  86.9 1.6 copy-start.9
  88.5 1.0 copy-start.10
  89.6 0.8 copy-start.14
  90.3 0.8 copy-start.16
  91.1 0.8 copy-start.18
  91.9 0.9 copy-start.21
  92.8 0.8 copy-start.31
  112.3 4.6 %copy-start.11 = (bf16[16,1024]{1,0:T(8,128)(2,1)}, bf16[16,1024]{1,0:T(8,128)(2,1)S(1)}, u32[]{:S(2)}) copy-start(bf16[16,1024]{1,0:T(8,128)(2,1)S(1)} %get-tuple-element.59.refs_9_) | copy-start | bytes 98308
  116.0 4.6 %collective-permute-start.20 = (bf16[4,16,16,1024]{3,2,1,0:T(8,128)(2,1)}, bf16[4,16,16,1024]{3,2,1,0:T(8,128)(2,1)}, u32[]{:S(2)}, u32[]{:S(2)}) collective-permute-start(bf16[4,16,16,1024]{3,2,1,0:T(8,128)(2,1)} %get-tuple-element.66), channel_id=1, source_target_pairs={{0,16},{16,0},{1,17},{17,1},{2,18},{18,2},{3,19},{19,3},{4,20},{20... | collective-permute-start | bytes 6291464 | tf_op jit(solution)/shard_map/ppermute | solution.py:22
  116.9 16.0 %all-to-all-start.1 = ((bf16[16,16,1024]{2,1,0:T(8,128)(2,1)}), bf16[16,16,1024]{2,1,0:T(8,128)(2,1)S(1)}, u32[]{:S(2)}, u32[]{:S(2)}) async-start(bf16[16,16,1024]{2,1,0:T(8,128)(2,1)} %bitcast.20), calls=%async_computation.1 | async-start | bytes 1048576 | tf_op jit(solution)/shard_map/all_to_all | solution.py:635
  124.4 13.0 %copy-start.12 = (bf16[16,1024]{1,0:T(8,128)(2,1)S(1)}, bf16[16,1024]{1,0:T(8,128)(2,1)}, u32[]{:S(2)}) copy-start(bf16[16,1024]{1,0:T(8,128)(2,1)} %copy-done.11) | copy-start | bytes 98308
  124.4 18.5 %copy-start.1 = (bf16[1024,1024]{1,0:T(8,128)(2,1)S(1)}, bf16[1024,1024]{1,0:T(8,128)(2,1)}, u32[]{:S(2)}) copy-start(bf16[1024,1024]{1,0:T(8,128)(2,1)} %copy-done) | copy-start | bytes 6291460
  132.9 47.1 %all-to-all-start.2 = ((bf16[4,16,16,1024]{3,2,1,0:T(8,128)(2,1)}), bf16[4,16,16,1024]{3,2,1,0:T(8,128)(2,1)}, u32[]{:S(2)}, u32[]{:S(2)}) async-start(bf16[4,16,16,1024]{3,2,1,0:T(8,128)(2,1)} %add_convert_fusion.1), calls=%async_computation.2 | async-start | bytes 4194304 | tf_op jit(solution)/shard_map/all_to_all | solution.py:644
  137.3 27.3 %copy-start.23 = (bf16[64,1024]{1,0:T(8,128)(2,1)S(1)}, bf16[64,1024]{1,0:T(8,128)(2,1)}, u32[]{:S(2)}) copy-start(bf16[64,1024]{1,0:T(8,128)(2,1)} %copy-done.22) | copy-start | bytes 393220
  137.4 27.3 %copy-start.27 = (bf16[64,256]{1,0:T(8,128)(2,1)S(1)}, bf16[64,256]{1,0:T(8,128)(2,1)}, u32[]{:S(2)}) copy-start(bf16[64,256]{1,0:T(8,128)(2,1)} %copy-done.26) | copy-start | bytes 98308
  137.4 27.3 %copy-start.29 = (f32[64,128]{1,0:T(8,128)S(1)}, f32[64,128]{1,0:T(8,128)}, u32[]{:S(2)}) copy-start(f32[64,128]{1,0:T(8,128)} %copy-done.28) | copy-start | bytes 98308
  137.4 24.7 %collective-permute-start.17 = (bf16[16,1024]{1,0:T(8,128)(2,1)S(1)}, bf16[16,1024]{1,0:T(8,128)(2,1)S(1)}, u32[]{:S(2)}, u32[]{:S(2)}) collective-permute-start(bf16[16,1024]{1,0:T(8,128)(2,1)S(1)} %copy-done.12), channel_id=1, source_target_pairs={{0,4},{4,8},{8,12},{12,0},{1,5},{5,9},{9,13},{13,1},{2,6},{6,10},{... | collective-permute-start | bytes 98312 | tf_op jit(solution)/shard_map/ppermute | solution.py:22
  139.4 23.3 %collective-permute-start.18 = (bf16[16,1024]{1,0:T(8,128)(2,1)S(1)}, bf16[16,1024]{1,0:T(8,128)(2,1)S(1)}, u32[]{:S(2)}, u32[]{:S(2)}) collective-permute-start(bf16[16,1024]{1,0:T(8,128)(2,1)S(1)} %copy-done.12), channel_id=1, source_target_pairs={{0,12},{4,0},{8,4},{12,8},{1,13},{5,1},{9,5},{13,9},{2,14},{6,2},{... | collective-permute-start | bytes 98312 | tf_op jit(solution)/shard_map/ppermute | solution.py:22
  140.7 23.9 %collective-permute-start.19 = (bf16[16,1024]{1,0:T(8,128)(2,1)S(1)}, bf16[16,1024]{1,0:T(8,128)(2,1)S(1)}, u32[]{:S(2)}, u32[]{:S(2)}) collective-permute-start(bf16[16,1024]{1,0:T(8,128)(2,1)S(1)} %copy-done.12), channel_id=1, source_target_pairs={{0,8},{4,12},{8,0},{12,4},{1,9},{5,13},{9,1},{13,5},{2,10},{6,14},... | collective-permute-start | bytes 98312 | tf_op jit(solution)/shard_map/ppermute | solution.py:22
  164.6 1.6 copy-start.2
  166.2 1.6 copy-start.19
  167.8 1.6 copy-start.20
  169.4 0.9 copy-start.25
  180.0 5.3 %collective-permute-start.21 = (bf16[4,4,80,1024]{3,2,1,0:T(8,128)(2,1)}, bf16[4,4,80,1024]{3,2,1,0:T(8,128)(2,1)}, u32[]{:S(2)}, u32[]{:S(2)}) collective-permute-start(bf16[4,4,80,1024]{3,2,1,0:T(8,128)(2,1)} %get-tuple-element.67), channel_id=1, source_target_pairs={{0,16},{16,0},{1,17},{17,1},{2,18},{18,2},{3,19},{19,3},{4,20},{20... | collective-permute-start | bytes 7864328 | tf_op jit(solution)/shard_map/ppermute | solution.py:22
  235.1 8.4 %collective-permute-start.22 = (bf16[80,1024]{1,0:T(8,128)(2,1)S(1)}, bf16[80,1024]{1,0:T(8,128)(2,1)S(1)}, u32[]{:S(2)}, u32[]{:S(2)}) collective-permute-start(bf16[80,1024]{1,0:T(8,128)(2,1)S(1)} %slice.91.refs_1_), channel_id=1, source_target_pairs={{0,32},{32,64},{64,96},{96,0},{1,33},{33,65},{65,97},{97,1},{2,34}... | collective-permute-start | bytes 491528 | tf_op jit(solution)/shard_map/ppermute | solution.py:22
  235.2 8.8 %collective-permute-start.23 = (bf16[80,1024]{1,0:T(8,128)(2,1)S(1)}, bf16[80,1024]{1,0:T(8,128)(2,1)S(1)}, u32[]{:S(2)}, u32[]{:S(2)}) collective-permute-start(bf16[80,1024]{1,0:T(8,128)(2,1)S(1)} %slice.91.refs_1_), channel_id=1, source_target_pairs={{0,96},{32,0},{64,32},{96,64},{1,97},{33,1},{65,33},{97,65},{2,98}... | collective-permute-start | bytes 491528 | tf_op jit(solution)/shard_map/ppermute | solution.py:22
  238.4 6.8 %collective-permute-start.24 = (bf16[80,1024]{1,0:T(8,128)(2,1)S(1)}, bf16[80,1024]{1,0:T(8,128)(2,1)S(1)}, u32[]{:S(2)}, u32[]{:S(2)}) collective-permute-start(bf16[80,1024]{1,0:T(8,128)(2,1)S(1)} %slice.91.refs_1_), channel_id=1, source_target_pairs={{0,64},{32,96},{64,0},{96,32},{1,65},{33,97},{65,1},{97,33},{2,66}... | collective-permute-start | bytes 491528 | tf_op jit(solution)/shard_map/ppermute | solution.py:22
  238.4 7.5 %collective-permute-start.25 = (bf16[80,1024]{1,0:T(8,128)(2,1)S(1)}, bf16[80,1024]{1,0:T(8,128)(2,1)S(1)}, u32[]{:S(2)}, u32[]{:S(2)}) collective-permute-start(bf16[80,1024]{1,0:T(8,128)(2,1)S(1)} %slice.91.refs_1_), channel_id=1, source_target_pairs={{0,16},{16,0},{1,17},{17,1},{2,18},{18,2},{3,19},{19,3},{4,20},{20... | collective-permute-start | bytes 491528 | tf_op jit(solution)/shard_map/ppermute | solution.py:22
  243.5 2.4 collective-permute-start.26
  244.0 1.9 collective-permute-start.27
  245.2 1.4 collective-permute-start.28
  (5 other events, 3.0 us)

commit v3 on v2

--- a/solution.py
+++ b/solution.py
@@ -74,7 +74,7 @@
         return copy
 
 
-def local_call(body, outs, operands, scratch=(), copies=8, flops=0, limit=44):
+def local_call(body, outs, operands, scratch=(), copies=8, flops=0, limit=60):
     def kernel(*refs):
         body(Copies(refs[-1]), *refs[:-1])
 
@@ -82,8 +82,8 @@
         kernel,
         out_shape=[jax.ShapeDtypeStruct(shape, kind) for shape, kind in outs],
         in_specs=[pl.BlockSpec(memory_space=pltpu.SMEM)]
-        + [pl.BlockSpec(memory_space=pl.ANY)] * (len(operands) - 1),
-        out_specs=[pl.BlockSpec(memory_space=pl.ANY)] * len(outs),
+        + [pl.BlockSpec(memory_space=pltpu.HBM)] * (len(operands) - 1),
+        out_specs=[pl.BlockSpec(memory_space=pltpu.HBM)] * len(outs),
         scratch_shapes=[*scratch, pltpu.SemaphoreType.DMA((copies,))],
         compiler_params=pltpu.CompilerParams(vmem_limit_bytes=limit * 1024 * 1024),
         cost_estimate=pl.CostEstimate(flops=flops, bytes_accessed=1024 * 1024, transcendentals=0),
@@ -246,17 +246,20 @@
         cols = slice(t * 256, (t + 1) * 256)
         wait_all(weights[t])
 
-        @pl.loop(0, 4)
+        @pl.loop(0, 2)
         def _(s):
-            rows = pl.ds(pl.multiple_of(s * 256, 256), 256)
-            few = pl.ds(pl.multiple_of(s * 16, 16), 16)
+            rows = pl.ds(pl.multiple_of(s * 512, 512), 512)
             pre = dot(normed_ref[rows, :], in_ref[:, cols])
             square = pre * pre
             tanh = jnp.tanh(GELU_SCALE * pre * (1.0 + GELU_CUBE * square))
             upper = 0.5 + 0.5 * tanh
             slope = upper + (0.5 * GELU_SCALE) * pre * (1.0 - tanh * tanh) * (1.0 + 3.0 * GELU_CUBE * square)
             slope_ref[rows, cols] = slope.astype(BF)
-            pooled_ref[few, cols] = dot(pool_ref[few, :], (pre * upper).astype(BF)).astype(BF)
+            activation = (pre * upper).astype(BF)
+            for i in range(2):
+                few = pl.ds(pl.multiple_of(s * 32 + i * 16, 16), 16)
+                pooled = dot(pool_ref[few, :], activation[i * 256 : (i + 1) * 256])
+                pooled_ref[few, cols] = pooled.astype(BF)
 
     sent_out.append(copies.start(slope_ref, slope_hbm))
     sent_out.append(copies.start(pooled_ref, pooled_hbm))
@@ -317,12 +320,17 @@
     nodes_ref[...] = ext_ref[0:256, :]
     sent_out = [copies.start(nodes_ref, nodes_hbm)]
 
-    @pl.loop(0, 16)
-    def _(j):
-        rows = pl.ds(pl.multiple_of(j * 128, 128), 128)
-        taken = dot(src_hot_ref[rows, :], ext_ref[...])
-        sources_ref[rows, :] = taken.astype(BF)
-        edges_ref[rows, :] = (taken * rel_ref[j]).astype(BF)
+    for n in range(4):
+        cols = slice(n * 256, (n + 1) * 256)
+
+        @pl.loop(0, 4)
+        def _(k):
+            rows = pl.ds(pl.multiple_of(k * 512, 512), 512)
+            taken = dot(src_hot_ref[rows, :], ext_ref[:, cols])
+            sources_ref[rows, cols] = taken.astype(BF)
+            for i in range(4):
+                few = pl.ds(pl.multiple_of(k * 512 + i * 128, 128), 128)
+                edges_ref[few, cols] = (taken[i * 128 : (i + 1) * 128] * rel_ref[k * 4 + i, :, cols]).astype(BF)
 
     wait_all(second)
 
@@ -352,12 +360,19 @@
 
     wait_all(fourth)
 
-    @pl.loop(0, 16)
-    def _(j):
-        rows = pl.ds(pl.multiple_of(j * 128, 128), 128)
-        at_dest = dot(dst_hot_ref[rows, :], agg_grad_ref[...])
-        edges_ref[rows, :] = (at_dest * rel_ref[j]).astype(BF)
-        sums_ref[j] = jnp.sum(at_dest * sources_ref[rows, :].astype(F32), axis=0, keepdims=True)
+    for n in range(4):
+        cols = slice(n * 256, (n + 1) * 256)
+
+        @pl.loop(0, 4)
+        def _(k):
+            rows = pl.ds(pl.multiple_of(k * 512, 512), 512)
+            at_dest = dot(dst_hot_ref[rows, :], agg_grad_ref[:, cols])
+            for i in range(4):
+                few = pl.ds(pl.multiple_of(k * 512 + i * 128, 128), 128)
+                part = at_dest[i * 128 : (i + 1) * 128]
+                edges_ref[few, cols] = (part * rel_ref[k * 4 + i, :, cols]).astype(BF)
+                product = part * sources_ref[few, cols].astype(F32)
+                sums_ref[k * 4 + i, :, cols] = jnp.sum(product, axis=0, keepdims=True)
 
     blocks_ref[...] = jnp.concatenate([sums_ref[j] for j in range(16)], axis=0).astype(BF)
     sent_out.append(copies.start(blocks_ref, blocks_hbm))
@@ -403,16 +418,39 @@
     wait_all(sent_out)
 
 
+def encoder_grads(half, my_y, chunk_ref, blocks, rel_hot_ref, pooled_ref, scaled_ref, normed_t_ref, grad_ref, prepare):
+    for y in range(4):
+        rel = dot(rel_hot_ref[pl.ds(pl.multiple_of(y * 128 + half * 64, 64), 64), :], blocks).astype(BF)
+        for z in range(4):
+            chunk_ref[z, y, 64:80, :] = rel[z * 16 : (z + 1) * 16]
+
+    prepare(None)
+
+    @pl.loop(0, 4)
+    def _(t):
+        cols = pl.ds(pl.multiple_of(t * 256, 256), 256)
+        origin = jnp.where(t == 0, 0, jnp.where(t == 1, 3, t - 1))
+        owner = lax.rem(my_y + origin, 4)
+        prepare(cols)
+        units = pl.ds(pl.multiple_of(t * 256 + half * 128, 128), 128)
+        out = dot_t(pooled_ref[:, units], scaled_ref[...]).astype(BF)
+        inner = dot(normed_t_ref[pl.ds(pl.multiple_of(half * 512, 512), 512), :], grad_ref[:, cols]).astype(BF)
+        for z in range(4):
+            chunk_ref[z, owner, 32:64, :] = out[z * 32 : (z + 1) * 32]
+            for i in range(4):
+                piece = inner[z * 128 + i * 32 : z * 128 + (i + 1) * 32]
+                chunk_ref[z, owner, 0:32, i * 256 : (i + 1) * 256] = piece
+
+
 def back_kernel(
     copies,
     where_ref,
     returned_hbm, route_hbm, length_hbm, all_out_hbm, slope_hbm, pooled_hbm, normed_t_hbm,
     rel_hot_hbm, r0_hbm, r1_hbm, r2_hbm, r3_hbm,
-    kept_hbm, given_hbm,
+    given_hbm, scaled_hbm, grad_hbm,
     returned_ref, route_ref, length_ref, all_out_ref, slope_ref, pooled_ref, normed_t_ref,
     rel_hot_ref, r0, r1, r2, r3,
-    kept_ref, given_ref,
-    scaled_ref, grad_ref,
+    given_ref, scaled_ref, grad_ref,
 ):
     core, my_y = where_ref[1], where_ref[3]
     first = [
@@ -434,43 +472,62 @@
     wait_all(first)
     scaled_ref[...] = (dot(route_ref[...], returned_ref[...]) * length_ref[:, 0:1]).astype(BF)
     blocks = jnp.concatenate([r0[...], r1[...], r2[...], r3[...]], axis=0)
-    for half, chunk_ref in ((core, kept_ref), (1 - core, given_ref)):
-        for y in range(4):
-            rows = pl.ds(pl.multiple_of(y * 128 + half * 64, 64), 64)
-            rel = dot(rel_hot_ref[rows, :], blocks).astype(BF)
-            for z in range(4):
-                chunk_ref[z, y, 64:80, :] = rel[z * 16 : (z + 1) * 16]
-
-    wait_all(second)
-
-    @pl.loop(0, 4)
-    def _(t):
-        cols = pl.ds(pl.multiple_of(t * 256, 256), 256)
-        origin = jnp.where(t == 0, 0, jnp.where(t == 1, 3, t - 1))
-        owner = lax.rem(my_y + origin, 4)
+
+    def prepare(cols):
+        if cols is None:
+            wait_all(second)
+            return
         upstream = dot_bt(scaled_ref[...], all_out_ref[cols, :]).astype(BF)
         for s in range(4):
             rows = slice(s * 256, (s + 1) * 256)
-            shape = (16, 256)
-            line = lanes(shape)
+            line = lanes((16, 256))
             length = 1.0 / length_ref[s * 16 : (s + 1) * 16, 0:1]
-            inside = (line // 16 == sublanes(shape)) & ((line % 16).astype(F32) + 0.5 < length)
+            inside = (line // 16 == sublanes((16, 256))) & ((line % 16).astype(F32) + 0.5 < length)
             pool = inside.astype(F32).astype(BF)
             at_tokens = dot_t(pool, upstream[s * 16 : (s + 1) * 16])
-            grad_ref[rows, :] = (slope_ref[rows, cols].astype(F32) * at_tokens).astype(BF)
-        for half, chunk_ref in ((1 - core, given_ref), (core, kept_ref)):
-            units = pl.ds(pl.multiple_of(t * 256 + half * 128, 128), 128)
-            out = dot_t(pooled_ref[:, units], scaled_ref[...]).astype(BF)
-            inner = dot(normed_t_ref[pl.ds(pl.multiple_of(half * 512, 512), 512), :], grad_ref[...]).astype(BF)
-            for z in range(4):
-                chunk_ref[z, owner, 32:64, :] = out[z * 32 : (z + 1) * 32]
-                for i in range(4):
-                    piece = inner[z * 128 + i * 32 : z * 128 + (i + 1) * 32]
-                    chunk_ref[z, owner, 0:32, i * 256 : (i + 1) * 256] = piece
-
-
-    sent_out = [copies.start(given_ref, given_hbm), copies.start(kept_ref, kept_hbm)]
-    wait_all(sent_out)
+            grad_ref[rows, cols] = (slope_ref[rows, cols].astype(F32) * at_tokens).astype(BF)
+
+    encoder_grads(
+        1 - core, my_y, given_ref, blocks, rel_hot_ref, pooled_ref, scaled_ref, normed_t_ref, grad_ref, prepare
+    )
+    wait_all(
+        [copies.start(given_ref, given_hbm), copies.start(scaled_ref, scaled_hbm), copies.start(grad_ref, grad_hbm)]
+    )
+
+
+def rest_kernel(
+    copies,
+    where_ref,
+    scaled_hbm, grad_hbm, pooled_hbm, normed_t_hbm, rel_hot_hbm, r0_hbm, r1_hbm, r2_hbm, r3_hbm,
+    kept_hbm,
+    scaled_ref, grad_ref, pooled_ref, normed_t_ref, rel_hot_ref, r0, r1, r2, r3,
+    kept_ref,
+):
+    core, my_y = where_ref[1], where_ref[3]
+    first = [
+        copies.start(rel_hot_hbm, rel_hot_ref),
+        copies.start(r0_hbm, r0),
+        copies.start(r1_hbm, r1),
+        copies.start(r2_hbm, r2),
+        copies.start(r3_hbm, r3),
+    ]
+    second = [
+        copies.start(grad_hbm, grad_ref),
+        copies.start(normed_t_hbm, normed_t_ref),
+        copies.start(pooled_hbm, pooled_ref),
+        copies.start(scaled_hbm, scaled_ref),
+    ]
+    wait_all(first)
+    blocks = jnp.concatenate([r0[...], r1[...], r2[...], r3[...]], axis=0)
+
+    def prepare(cols):
+        if cols is None:
+            wait_all(second)
+
+    encoder_grads(
+        core, my_y, kept_ref, blocks, rel_hot_ref, pooled_ref, scaled_ref, normed_t_ref, grad_ref, prepare
+    )
+    wait_all([copies.start(kept_ref, kept_hbm)])
 
 
 def place_kernel(
@@ -641,21 +698,29 @@
         weight_kernel, outs, [where, *operands], like(operands) + filled(outs), flops=10**9
     )
     chip = (graph_kept.astype(F32) + shift_by(graph_given, "core", 1).astype(F32)).astype(BF)
+    chip, *rel_blocks = lax.optimization_barrier((chip, *rel_blocks))
     line = lax.all_to_all(chip, "x", 0, 0, tiled=True)
 
-    outs = [((4, 4, 80, width), BF)] * 2
+    outs = [((4, 4, 80, width), BF), ((4 * entities, width), BF), ((4 * tokens, 4 * units), BF)]
     operands = [returned, route, inverse, all_out, slope, pooled, normed_t, rel_hot, *rel_blocks]
-    kept, given = local_call(
+    given, scaled, grad_tokens = local_call(
         back_kernel,
         outs,
         [where, *operands],
-        like(operands)
-        + filled(outs)
-        + [pltpu.VMEM((4 * entities, width), BF), pltpu.VMEM((4 * tokens, units), BF)],
+        like(operands) + filled(outs),
         copies=16,
-        flops=2 * 4 * tokens * width * 4 * units,
-    )
-    given, line = lax.optimization_barrier((given, line))
+        flops=3 * 2 * tokens * width * 4 * units,
+    )
+    outs = [((4, 4, 80, width), BF)]
+    operands = [scaled, grad_tokens, pooled, normed_t, rel_hot, *rel_blocks]
+    (kept,) = local_call(
+        rest_kernel,
+        outs,
+        [where, *operands],
+        like(operands) + filled(outs),
+        copies=12,
+        flops=2 * 2 * tokens * width * 4 * units,
+    )
     line_sum = jnp.sum(line.astype(F32), axis=0).astype(BF)
     chunks = (kept.astype(F32) + shift_by(given, "core", 1).astype(F32)).astype(BF)
     chunks = jnp.concatenate([chunks.reshape(16, 80, width), line_sum], axis=1)

time: 254 us -> 257 us (1.012)
  Pallas kernels: 51.3 us -> 79.1 us
  local copies, waits for them, and re-layouts: 28.9 us -> 13.7 us
  waiting for transfers between devices: 63 us -> 49.3 us
  other arithmetic: 16.4 us -> 20.1 us
    pallas_call x6 -> x7, Pallas kernels: 51.3 us -> 79.1 us  [local_call(): pl.pallas_call(kernel, out_shape=[jax.ShapeDtypeStruct(shape, kind) for s...]
    ppermute x29, waiting for transfers between devices: 54.5 us -> 29.1 us  [shift_by(): lax.ppermute(value, axis, [(i, (i + shift) % count) for i in range(count)])]
    all_to_all x1, waiting for transfers between devices: 0.01 us -> 20.2 us  [shards(): line = lax.all_to_all(chip, 'x', 0, 0, tiled=True)]
    unnamed x74, local copies, waits for them, and re-layouts: 22.9 us -> 4.07 us
    all_to_all x1, waiting for transfers between devices: 8.47 us -> 0.01 us  [shards(): lax.all_to_all(back.reshape(16, 16, width), GROUP, 0, 0, tiled=True)]
    convert_element_type x3, other arithmetic: 1.58 us -> 4.21 us  [one_hot(): return (index[:, None] == jnp.arange(count, dtype=I32)[None, :]).astype(BF)]
  transfers between devices with their start and end apart: 32 -> 32, of which waited for: 16 -> 12; matrix products, arithmetic and copies ran while one was open for 6% -> 8% of each run, Pallas kernels for 4% -> 3%
where the time goes in v3:
time: 257 us; the launch traced here: 255 us
  Pallas kernels  79.1 us (31%)
  waiting for transfers between devices  49.3 us (19%)
  blocking collectives  47.1 us (18%)
  starting transfers between devices  42.7 us (17%)
  other arithmetic  20.1 us (8%)
  local copies, waits for them, and re-layouts  13.7 us (5%)
    pallas_call x7, Pallas kernels, local_call(): pl.pallas_call(kernel, out_shape=[jax.ShapeDtypeStruct(shape, kind) for s...  79.1 us
    all_to_all x1, blocking collectives, shards(): chunks = lax.all_to_all(chunks, ('z', 'y'), 0, 0, tiled=True)  47.1 us
    ppermute x29, starting transfers between devices, shift_by(): lax.ppermute(value, axis, [(i, (i + shift) % count) for i in range(count)])  30.8 us
    ppermute x29, waiting for transfers between devices, shift_by(): lax.ppermute(value, axis, [(i, (i + shift) % count) for i in range(count)])  29.1 us
    all_to_all x1, waiting for transfers between devices, shards(): line = lax.all_to_all(chip, 'x', 0, 0, tiled=True)  20.2 us
  transfers between devices with their start and end apart: 32, of which 12 were waited for; matrix products, arithmetic and copies ran while one was open for 8% of the time, Pallas kernels for 3%

profile of v3, /device:TPU:0, one launch (start us, length us, event | category | flops | bytes accessed | tf_op | source)
XLA Modules:
  0.0 255.0 jit_solution(16106419692443894132)
XLA Ops:
  0.7 0.7 fusion.37
  1.4 0.7 convert_bitcast_fusion
  2.1 0.7 convert.24
  2.7 0.9 reshape.54
  3.7 0.7 pad.26
  4.3 0.7 pad_add_fusion.1.refs_0_
  5.1 0.6 broadcast_in_dim.61.refs_2_
  5.7 19.7 %shard_map.190 = (bf16[272,1024]{1,0:T(8,128)(2,1)}, f32[16,1024]{1,0:T(8,128)}, bf16[576,512]{1,0:T(8,128)(2,1)}) custom-call(s32[4]{0:T(128)} %pad_add_fusion.1.refs_0_, bf16[256,1024]{1,0:T(8,128)(2,1)} %bitcast.62, bf16[16,1024]{1,0:T(8,128)(2,1)} %broadcast_in_dim.61.refs_2_, bf16[1024,256]{1,0:T(8,128)(2,1)} %refs_6_.1, bf16[256,1024]{1,0:T(8,128)(2,1)} %refs_7_.1, ...), custom_call_target="tpu_custom_call" | custom-call | bytes 1048576 | tf_op jit(solution)/shard_map/pallas_call | solution.py:81
  25.4 1.6 collective-permute-start
  27.1 1.7 collective-permute-start.1
  28.7 1.7 collective-permute-start.4
  30.4 1.6 collective-permute-start.5
  32.0 2.0 fusion.3.refs_10_
  34.0 1.2 fusion.4.refs_11_
  35.6 1.5 fusion.1.refs_9_
  37.1 4.1 %collective-permute-done.refs_2_ = bf16[272,1024]{1,0:T(8,128)(2,1)S(1)} collective-permute-done((bf16[272,1024]{1,0:T(8,128)(2,1)}, bf16[272,1024]{1,0:T(8,128)(2,1)S(1)}, u32[]{:S(2)}, u32[]{:S(2)}) %collective-permute-start) | collective-permute-done | bytes 557088 | tf_op jit(solution)/shard_map/ppermute | solution.py:22
  41.2 0.5 collective-permute-start.2
  41.7 3.1 %collective-permute-done.4.refs_9_ = bf16[576,512]{1,0:T(8,128)(2,1)S(1)} collective-permute-done((bf16[576,512]{1,0:T(8,128)(2,1)}, bf16[576,512]{1,0:T(8,128)(2,1)S(1)}, u32[]{:S(2)}, u32[]{:S(2)}) %collective-permute-start.4) | collective-permute-done | bytes 589856 | tf_op jit(solution)/shard_map/ppermute | solution.py:22
  45.2 3.0 %collective-permute-start.7 = (bf16[320,512]{1,0:T(8,128)(2,1)S(1)}, bf16[320,512]{1,0:T(8,128)(2,1)S(1)}, u32[]{:S(2)}, u32[]{:S(2)}) collective-permute-start(bf16[320,512]{1,0:T(8,128)(2,1)S(1)} %slice.72), channel_id=1, source_target_pairs={{0,3},{1,0},{2,1},{3,2},{4,7},{5,4},{6,5},{7,6},{8,11},{9,8},{10,9... | collective-permute-start | bytes 983048 | tf_op jit(solution)/shard_map/ppermute | solution.py:22
  48.9 0.7 collective-permute-done.2.refs_4_
  49.5 1.0 collective-permute-start.3
  50.5 2.3 collective-permute-done.6.refs_11_
  52.8 0.8 collective-permute-done.7.refs_12_
  53.6 0.6 fusion.13.refs_4_
  54.3 3.7 %collective-permute-done.3.refs_5_ = bf16[144,1024]{1,0:T(8,128)(2,1)S(1)} collective-permute-done((bf16[144,1024]{1,0:T(8,128)(2,1)S(1)}, bf16[144,1024]{1,0:T(8,128)(2,1)S(1)}, u32[]{:S(2)}, u32[]{:S(2)}) %collective-permute-start.3) | collective-permute-done | bytes 294944 | tf_op jit(solution)/shard_map/ppermute | solution.py:22
  58.0 0.8 copy-done.26
  59.0 0.7 copy-done.28
  59.7 11.8 %shard_map.191 = (bf16[256,1024]{1,0:T(8,128)(2,1)}, bf16[1024,1024]{1,0:T(8,128)(2,1)}, bf16[1024,1024]{1,0:T(8,128)(2,1)}, bf16[64,1024]{1,0:T(8,128)(2,1)}, b...) custom-call(s32[4]{0:T(128)} %pad_add_fusion.1.refs_0_, ...), custom_call_target="tpu_custom_call" | custom-call | flops 2147483648 | bytes 1048576 | tf_op jit(solution)/shard_map/pallas_call | solution.py:81
  71.5 2.9 %collective-permute-start.13 = (bf16[80,1024]{1,0:T(8,128)(2,1)S(1)}, bf16[80,1024]{1,0:T(8,128)(2,1)S(1)}, u32[]{:S(2)}, u32[]{:S(2)}) collective-permute-start(bf16[80,1024]{1,0:T(8,128)(2,1)S(1)} %get-tuple-element.49), channel_id=1, source_target_pairs={{0,15},{1,0},{2,1},{3,2},{4,3},{5,4},{6,5},{7,6},{8,7},{9,8},{10,9... | collective-permute-start | bytes 491528 | tf_op jit(solution)/shard_map/ppermute | solution.py:22
  74.5 3.6 %all-to-all-start = ((bf16[16,16,1024]{2,1,0:T(8,128)(2,1)}), bf16[16,16,1024]{2,1,0:T(8,128)(2,1)S(1)}, u32[]{:S(2)}, u32[]{:S(2)}) async-start(bf16[16,16,1024]{2,1,0:T(8,128)(2,1)} %bitcast.63), calls=%async_computation | async-start | bytes 1048576 | tf_op jit(solution)/shard_map/all_to_all | solution.py:654
  78.1 1.8 collective-permute-start.12
  79.9 2.8 %collective-permute-start.14 = (bf16[16,1024]{1,0:T(8,128)(2,1)}, bf16[16,1024]{1,0:T(8,128)(2,1)S(1)}, u32[]{:S(2)}, u32[]{:S(2)}) collective-permute-start(bf16[16,1024]{1,0:T(8,128)(2,1)} %get-tuple-element.51), channel_id=1, source_target_pairs={{0,12},{4,0},{8,4},{12,8},{1,13},{5,1},{9,5},{13,9},{2,14},{6,2},{... | collective-permute-start | bytes 98312 | tf_op jit(solution)/shard_map/ppermute | solution.py:22
  82.6 2.3 collective-permute-start.16
  84.9 7.2 %collective-permute-done.12 = bf16[80,1024]{1,0:T(8,128)(2,1)S(1)} collective-permute-done((bf16[80,1024]{1,0:T(8,128)(2,1)S(1)}, bf16[80,1024]{1,0:T(8,128)(2,1)S(1)}, u32[]{:S(2)}, u32[]{:S(2)}) %collective-permute-start.12) | collective-permute-done | bytes 163872 | tf_op jit(solution)/shard_map/ppermute | solution.py:22
  92.2 1.5 fusion.2.refs_12_
  93.8 1.1 pad_maximum_fusion.1.refs_2_
  94.8 0.8 fusion.8.refs_3_
  95.7 0.5 copy-done.33
  96.4 19.8 %shard_map.192 = (bf16[64,1024]{1,0:T(8,128)(2,1)}, bf16[16,1024]{1,0:T(8,128)(2,1)}, bf16[256,1024]{1,0:T(8,128)(2,1)}, bf16[256,1024]{1,0:T(8,128)(2,1)}, bf16...) custom-call(s32[4]{0:T(128)} %pad_add_fusion.1.refs_0_, bf16[256,1024]{1,0:T(8,128)(2,1)} %bitcast.64, ...), custom_call_target="tpu_custom_call" | custom-call | flops 6000000000 | bytes 1048576 | tf_op jit(solution)/shard_map/pallas_call | solution.py:81
  116.2 6.4 %shard_map.193 = (bf16[4,16,16,1024]{3,2,1,0:T(8,128)(2,1)}, bf16[4,16,16,1024]{3,2,1,0:T(8,128)(2,1)}) custom-call(s32[4]{0:T(128)} %pad_add_fusion.1.refs_0_, bf16[256,1024]{1,0:T(8,128)(2,1)} %get-tuple-element.63.refs_1_, bf16[256,1024]{1,0:T(8,128)(2,1)} %get-tuple-element.64.refs_2_, bf16[256,1024]{1,0:T(8,128)(2,1)} %get-tuple-element.65.refs_3_), custom_call_target="tpu_custom_call" | custom-call | flops 1000000000 | bytes 1048576 | tf_op jit(solution)/shard_map/pallas_call | solution.py:81
  122.7 0.9 broadcast_in_dim.65
  123.6 3.7 %all-to-all-start.1 = ((bf16[16,16,1024]{2,1,0:T(8,128)(2,1)}), bf16[16,16,1024]{2,1,0:T(8,128)(2,1)S(1)}, u32[]{:S(2)}, u32[]{:S(2)}) async-start(bf16[16,16,1024]{2,1,0:T(8,128)(2,1)} %bitcast.20), calls=%async_computation.1 | async-start | bytes 1048576 | tf_op jit(solution)/shard_map/all_to_all | solution.py:692
  127.3 4.0 %copy.23 = bf16[1024,1024]{0,1:T(8,128)(2,1)} copy(bf16[1024,1024]{1,0:T(8,128)(2,1)} %get-tuple-element.61) | data formatting | bytes 4194304 | tf_op jit(solution)/shard_map/pallas_call | solution.py:81
  131.2 1.8 collective-permute-start.18
  133.1 1.4 collective-permute-start.19
  134.5 2.1 collective-permute-start.20
  136.6 3.9 %add_convert_fusion.1 = bf16[4,16,16,1024]{3,2,1,0:T(8,128)(2,1)} fusion(bf16[4,16,16,1024]{3,2,1,0:T(8,128)(2,1)} %collective-permute-done.17, bf16[4,16,16,1024]{3,2,1,0:T(8,128)(2,1)S(1)} %copy-done.2), kind=kLoop, calls=%fused_computation.2 | loop fusion | flops 4194304 | bytes 6291456 | tf_op jit(solution)/shard_map/convert_element_type | solution.py:700
  140.6 0.6 copy-done.16
  141.4 10.9 %shard_map.194 = (bf16[4,4,80,1024]{3,2,1,0:T(8,128)(2,1)}, bf16[64,1024]{1,0:T(8,128)(2,1)}, bf16[1024,1024]{1,0:T(8,128)(2,1)}) custom-call(s32[4]{0:T(128)} %pad_add_fusion.1.refs_0_, bf16[256,1024]{1,0:T(8,128)(2,1)} %bitcast.59, bf16[64,256]{1,0:T(8,128)(2,1)} %get-tuple-element.56.refs_2_, f32[64,128]{1,0:T(8,128)} %get-tuple-element.57.refs_3_, ...), custom_call_target="tpu_custom_call" | custom-call | flops 1610612736 | bytes 1048576 | tf_op jit(solution)/shard_map/pallas_call | solution.py:81
  152.4 4.7 %all-to-all-start.2 = ((bf16[4,16,16,1024]{3,2,1,0:T(8,128)(2,1)}), bf16[4,16,16,1024]{3,2,1,0:T(8,128)(2,1)}, u32[]{:S(2)}, u32[]{:S(2)}) async-start(bf16[4,16,16,1024]{3,2,1,0:T(8,128)(2,1)} %add_convert_fusion.1), calls=%async_computation.2 | async-start | bytes 4194304 | tf_op jit(solution)/shard_map/all_to_all | solution.py:702
  157.0 6.9 %shard_map.195 = bf16[4,4,80,1024]{3,2,1,0:T(8,128)(2,1)} custom-call(s32[4]{0:T(128)} %pad_add_fusion.1.refs_0_, bf16[64,1024]{1,0:T(8,128)(2,1)} %get-tuple-element.73.refs_1_, bf16[1024,1024]{1,0:T(8,128)(2,1)} %get-tuple-element.74.refs_2_, bf16[64,1024]{1,0:T(8,128)(2,1)} %get-tuple-element.60.refs_6_.refs_3_, bf16[1024,1024]{1,0:T(8,128)(2,1)} %bitcast.57, ...), custom_call_target="tpu_custom_call" | custom-call | flops 1073741824 | bytes 1048576 | tf_op jit(solution)/shard_map/pallas_call | solution.py:81
  164.0 20.2 %all-to-all-done.2 = bf16[4,16,16,1024]{3,2,1,0:T(8,128)(2,1)} async-done(((bf16[4,16,16,1024]{3,2,1,0:T(8,128)(2,1)}), bf16[4,16,16,1024]{3,2,1,0:T(8,128)(2,1)}, u32[]{:S(2)}, u32[]{:S(2)}) %all-to-all-start.2) | async-done | bytes 2097184 | tf_op jit(solution)/shard_map/all_to_all | solution.py:702
  184.1 2.0 reduce_sum.31
  186.2 3.0 %add_convert_fusion = bf16[4,4,80,1024]{3,2,1,0:T(8,128)(2,1)S(1)} fusion(bf16[4,4,80,1024]{3,2,1,0:T(8,128)(2,1)} %collective-permute-done.21, bf16[4,4,80,1024]{3,2,1,0:T(8,128)(2,1)S(1)} %copy-done), kind=kLoop, calls=%fused_computation.1 | loop fusion | flops 5242880 | bytes 7864320 | tf_op jit(solution)/shard_map/convert_element_type | solution.py:725
  189.6 47.1 %all_to_all.20 = bf16[16,96,1024]{2,1,0:T(8,128)(2,1)S(1)} all-to-all(bf16[16,96,1024]{2,1,0:T(8,128)(2,1)S(1)} %pad_maximum_fusion), channel_id=1, replica_groups=mesh['z'=4,'core'=2,'x'=4,'y'=4] {'z','y'}, dimensions={0} | all-to-all | bytes 6291456 | tf_op jit(solution)/shard_map/all_to_all | solution.py:727
  236.7 0.6 convert_reduce_fusion
  237.5 3.2 %collective-permute-start.23 = (bf16[80,1024]{1,0:T(8,128)(2,1)S(1)}, bf16[80,1024]{1,0:T(8,128)(2,1)S(1)}, u32[]{:S(2)}, u32[]{:S(2)}) collective-permute-start(bf16[80,1024]{1,0:T(8,128)(2,1)S(1)} %slice.91.refs_1_), channel_id=1, source_target_pairs={{0,96},{32,0},{64,32},{96,64},{1,97},{33,1},{65,33},{97,65},{2,98}... | collective-permute-start | bytes 491528 | tf_op jit(solution)/shard_map/ppermute | solution.py:22
  240.7 5.0 %collective-permute-done.22.refs_2_ = bf16[80,1024]{1,0:T(8,128)(2,1)S(1)} collective-permute-done((bf16[80,1024]{1,0:T(8,128)(2,1)S(1)}, bf16[80,1024]{1,0:T(8,128)(2,1)S(1)}, u32[]{:S(2)}, u32[]{:S(2)}) %collective-permute-start.22) | collective-permute-done | bytes 163872 | tf_op jit(solution)/shard_map/ppermute | solution.py:22
  246.3 1.3 collective-permute-done.24.refs_4_
  247.5 0.7 fusion.38
  248.2 0.7 collective-permute-done.28.refs_8_
  249.0 0.7 copy-done.13
  249.7 3.7 %shard_map.196 = (f32[1024,256]{1,0:T(8,128)}, f32[256,1024]{1,0:T(8,128)}, f32[64,1024]{1,0:T(8,128)}) custom-call(s32[4]{0:T(128)} %pad_add_fusion.1.refs_0_, bf16[80,1024]{1,0:T(8,128)(2,1)} %copy-done.4, bf16[80,1024]{1,0:T(8,128)(2,1)} %copy-done.7, bf16[80,1024]{1,0:T(8,128)(2,1)} %copy-done.8, bf16[80,1024]{1,0:T(8,128)(2,1)} %copy-done.9, ...), custom_call_target="tpu_custom_call" | custom-call | bytes 1048576 | tf_op jit(solution)/shard_map/pallas_call | solution.py:81
  253.4 1.6 slice.64
  (131 shorter events, 3.7 us)
Async XLA Ops:
  0.6 33.3 %copy-start.22 = (s32[1,2048]{1,0:T(1,128)S(1)}, s32[1,2048]{1,0:T(1,128)}, u32[]{:S(2)}) copy-start(s32[1,2048]{1,0:T(1,128)} %param.24) | copy-start | bytes 24580
  0.6 34.5 %copy-start.36 = (s32[1,16]{1,0:T(1,128)S(1)}, s32[1,16]{1,0:T(1,128)}, u32[]{:S(2)}) copy-start(s32[1,16]{1,0:T(1,128)} %param.20) | copy-start | bytes 196
  0.7 34.5 %copy-start.24 = (s32[1,128]{1,0:T(1,128)S(1)}, s32[1,128]{1,0:T(1,128)}, u32[]{:S(2)}) copy-start(s32[1,128]{1,0:T(1,128)} %param.22) | copy-start | bytes 1540
  0.7 34.6 %copy-start.3 = (bf16[240,1024]{1,0:T(8,128)(2,1)S(1)}, bf16[240,1024]{1,0:T(8,128)(2,1)}, u32[]{:S(2)}) copy-start(bf16[240,1024]{1,0:T(8,128)(2,1)} %param.21) | copy-start | bytes 1474564
  0.7 34.9 %copy-start.23 = (s32[1,2048]{1,0:T(1,128)S(1)}, s32[1,2048]{1,0:T(1,128)}, u32[]{:S(2)}) copy-start(s32[1,2048]{1,0:T(1,128)} %param.23) | copy-start | bytes 24580
  25.4 15.7 %collective-permute-start = (bf16[272,1024]{1,0:T(8,128)(2,1)}, bf16[272,1024]{1,0:T(8,128)(2,1)S(1)}, u32[]{:S(2)}, u32[]{:S(2)}) collective-permute-start(bf16[272,1024]{1,0:T(8,128)(2,1)} %get-tuple-element.43.refs_1_), channel_id=1, source_target_pairs={{0,4},{4,8},{8,12},{12,0},{1,5},{5,9},{9,13},{13,1},{2,6},{6,10},{... | collective-permute-start | bytes 1671176 | tf_op jit(solution)/shard_map/ppermute | solution.py:22
  27.1 21.2 %collective-permute-start.1 = (bf16[272,1024]{1,0:T(8,128)(2,1)}, bf16[272,1024]{1,0:T(8,128)(2,1)S(1)}, u32[]{:S(2)}, u32[]{:S(2)}) collective-permute-start(bf16[272,1024]{1,0:T(8,128)(2,1)} %get-tuple-element.43.refs_1_), channel_id=1, source_target_pairs={{0,12},{4,0},{8,4},{12,8},{1,13},{5,1},{9,5},{13,9},{2,14},{6,2},{... | collective-permute-start | bytes 1671176 | tf_op jit(solution)/shard_map/ppermute | solution.py:22
  28.7 16.1 %collective-permute-start.4 = (bf16[576,512]{1,0:T(8,128)(2,1)}, bf16[576,512]{1,0:T(8,128)(2,1)S(1)}, u32[]{:S(2)}, u32[]{:S(2)}) collective-permute-start(bf16[576,512]{1,0:T(8,128)(2,1)} %get-tuple-element.44), channel_id=1, source_target_pairs={{0,1},{1,2},{2,3},{3,0},{4,5},{5,6},{6,7},{7,4},{8,9},{9,10},{10,1... | collective-permute-start | bytes 1769480 | tf_op jit(solution)/shard_map/ppermute | solution.py:22
  30.4 14.8 %collective-permute-start.5 = (bf16[576,512]{1,0:T(8,128)(2,1)}, bf16[576,512]{1,0:T(8,128)(2,1)S(1)}, u32[]{:S(2)}, u32[]{:S(2)}) collective-permute-start(bf16[576,512]{1,0:T(8,128)(2,1)} %get-tuple-element.44), channel_id=1, source_target_pairs={{0,3},{1,0},{2,1},{3,2},{4,7},{5,4},{6,5},{7,6},{8,11},{9,8},{10,9... | collective-permute-start | bytes 1769480 | tf_op jit(solution)/shard_map/ppermute | solution.py:22
  41.2 18.5 %copy-start.20 = (bf16[272,1024]{1,0:T(8,128)(2,1)}, bf16[272,1024]{1,0:T(8,128)(2,1)S(1)}, u32[]{:S(2)}) copy-start(bf16[272,1024]{1,0:T(8,128)(2,1)S(1)} %collective-permute-done.refs_2_) | copy-start | bytes 1671172
  41.2 8.3 %collective-permute-start.2 = (bf16[128,1024]{1,0:T(8,128)(2,1)S(1)}, bf16[128,1024]{1,0:T(8,128)(2,1)S(1)}, u32[]{:S(2)}, u32[]{:S(2)}) collective-permute-start(bf16[128,1024]{1,0:T(8,128)(2,1)S(1)} %slice.69), channel_id=1, source_target_pairs={{0,4},{4,8},{8,12},{12,0},{1,5},{5,9},{9,13},{13,1},{2,6},{6,10},{... | collective-permute-start | bytes 786440 | tf_op jit(solution)/shard_map/ppermute | solution.py:22
  44.8 14.9 %copy-start.21 = (bf16[576,512]{1,0:T(8,128)(2,1)}, bf16[576,512]{1,0:T(8,128)(2,1)S(1)}, u32[]{:S(2)}) copy-start(bf16[576,512]{1,0:T(8,128)(2,1)S(1)} %collective-permute-done.4.refs_9_) | copy-start | bytes 1769476
  44.8 8.0 %collective-permute-start.6 = (bf16[256,512]{1,0:T(8,128)(2,1)S(1)}, bf16[256,512]{1,0:T(8,128)(2,1)S(1)}, u32[]{:S(2)}, u32[]{:S(2)}) collective-permute-start(bf16[256,512]{1,0:T(8,128)(2,1)S(1)} %slice.71), channel_id=1, source_target_pairs={{0,1},{1,2},{2,3},{3,0},{4,5},{5,6},{6,7},{7,4},{8,9},{9,10},{10,1... | collective-permute-start | bytes 786440 | tf_op jit(solution)/shard_map/ppermute | solution.py:22
  45.2 14.5 %copy-start.6 = (bf16[576,512]{1,0:T(8,128)(2,1)}, bf16[576,512]{1,0:T(8,128)(2,1)S(1)}, u32[]{:S(2)}) copy-start(bf16[576,512]{1,0:T(8,128)(2,1)S(1)} %collective-permute-done.5.refs_10_) | copy-start | bytes 1769476
  45.2 8.4 %collective-permute-start.7 = (bf16[320,512]{1,0:T(8,128)(2,1)S(1)}, bf16[320,512]{1,0:T(8,128)(2,1)S(1)}, u32[]{:S(2)}, u32[]{:S(2)}) collective-permute-start(bf16[320,512]{1,0:T(8,128)(2,1)S(1)} %slice.72), channel_id=1, source_target_pairs={{0,3},{1,0},{2,1},{3,2},{4,7},{5,4},{6,5},{7,6},{8,11},{9,8},{10,9... | collective-permute-start | bytes 983048 | tf_op jit(solution)/shard_map/ppermute | solution.py:22
  48.2 9.7 %collective-permute-start.8 = (bf16[576,512]{1,0:T(8,128)(2,1)S(1)}, bf16[576,512]{1,0:T(8,128)(2,1)S(1)}, u32[]{:S(2)}, u32[]{:S(2)}) collective-permute-start(bf16[576,512]{1,0:T(8,128)(2,1)S(1)} %collective-permute-done.4.refs_9_), channel_id=1, source_target_pairs={{0,16},{16,0},{1,17},{17,1},{2,18},{18,2},{3,19},{19,3},{4,20},{20... | collective-permute-start | bytes 1769480 | tf_op jit(solution)/shard_map/ppermute | solution.py:22
  48.2 11.5 %copy-start.14 = (bf16[272,1024]{1,0:T(8,128)(2,1)}, bf16[272,1024]{1,0:T(8,128)(2,1)S(1)}, u32[]{:S(2)}) copy-start(bf16[272,1024]{1,0:T(8,128)(2,1)S(1)} %collective-permute-done.1.refs_3_) | copy-start | bytes 1671172
  48.2 9.7 %collective-permute-start.9 = (bf16[576,512]{1,0:T(8,128)(2,1)S(1)}, bf16[576,512]{1,0:T(8,128)(2,1)S(1)}, u32[]{:S(2)}, u32[]{:S(2)}) collective-permute-start(bf16[576,512]{1,0:T(8,128)(2,1)S(1)} %collective-permute-done.5.refs_10_), channel_id=1, source_target_pairs={{0,16},{16,0},{1,17},{17,1},{2,18},{18,2},{3,19},{19,3},{4,20},{20... | collective-permute-start | bytes 1769480 | tf_op jit(solution)/shard_map/ppermute | solution.py:22
  49.5 4.1 %copy-start.30 = (bf16[128,1024]{1,0:T(8,128)(2,1)}, bf16[128,1024]{1,0:T(8,128)(2,1)S(1)}, u32[]{:S(2)}) copy-start(bf16[128,1024]{1,0:T(8,128)(2,1)S(1)} %collective-permute-done.2.refs_4_) | copy-start | bytes 786436
  49.5 8.4 %collective-permute-start.3 = (bf16[144,1024]{1,0:T(8,128)(2,1)S(1)}, bf16[144,1024]{1,0:T(8,128)(2,1)S(1)}, u32[]{:S(2)}, u32[]{:S(2)}) collective-permute-start(bf16[144,1024]{1,0:T(8,128)(2,1)S(1)} %slice.70), channel_id=1, source_target_pairs={{0,12},{4,0},{8,4},{12,8},{1,13},{5,1},{9,5},{13,9},{2,14},{6,2},{... | collective-permute-start | bytes 884744 | tf_op jit(solution)/shard_map/ppermute | solution.py:22
  52.8 6.0 %copy-start.31 = (bf16[256,512]{1,0:T(8,128)(2,1)}, bf16[256,512]{1,0:T(8,128)(2,1)S(1)}, u32[]{:S(2)}) copy-start(bf16[256,512]{1,0:T(8,128)(2,1)S(1)} %collective-permute-done.6.refs_11_) | copy-start | bytes 786436
  52.8 5.1 %collective-permute-start.10 = (bf16[256,512]{1,0:T(8,128)(2,1)S(1)}, bf16[256,512]{1,0:T(8,128)(2,1)S(1)}, u32[]{:S(2)}, u32[]{:S(2)}) collective-permute-start(bf16[256,512]{1,0:T(8,128)(2,1)S(1)} %collective-permute-done.6.refs_11_), channel_id=1, source_target_pairs={{0,16},{16,0},{1,17},{17,1},{2,18},{18,2},{3,19},{19,3},{4,20},{20... | collective-permute-start | bytes 786440 | tf_op jit(solution)/shard_map/ppermute | solution.py:22
  53.6 6.1 %copy-start.27 = (bf16[320,512]{1,0:T(8,128)(2,1)}, bf16[320,512]{1,0:T(8,128)(2,1)S(1)}, u32[]{:S(2)}) copy-start(bf16[320,512]{1,0:T(8,128)(2,1)S(1)} %collective-permute-done.7.refs_12_) | copy-start | bytes 983044
  53.6 5.3 %collective-permute-start.11 = (bf16[320,512]{1,0:T(8,128)(2,1)S(1)}, bf16[320,512]{1,0:T(8,128)(2,1)S(1)}, u32[]{:S(2)}, u32[]{:S(2)}) collective-permute-start(bf16[320,512]{1,0:T(8,128)(2,1)S(1)} %collective-permute-done.7.refs_12_), channel_id=1, source_target_pairs={{0,16},{16,0},{1,17},{17,1},{2,18},{18,2},{3,19},{19,3},{4,20},{20... | collective-permute-start | bytes 983048 | tf_op jit(solution)/shard_map/ppermute | solution.py:22
  58.0 0.9 copy-start.29
  58.0 1.0 copy-start.32
  58.0 1.7 copy-start.25
  58.0 0.9 copy-start.26
  59.0 0.7 copy-start.28
  71.5 13.4 %collective-permute-start.13 = (bf16[80,1024]{1,0:T(8,128)(2,1)S(1)}, bf16[80,1024]{1,0:T(8,128)(2,1)S(1)}, u32[]{:S(2)}, u32[]{:S(2)}) collective-permute-start(bf16[80,1024]{1,0:T(8,128)(2,1)S(1)} %get-tuple-element.49), channel_id=1, source_target_pairs={{0,15},{1,0},{2,1},{3,2},{4,3},{5,4},{6,5},{7,6},{8,7},{9,8},{10,9... | collective-permute-start | bytes 491528 | tf_op jit(solution)/shard_map/ppermute | solution.py:22
  74.5 21.2 %all-to-all-start = ((bf16[16,16,1024]{2,1,0:T(8,128)(2,1)}), bf16[16,16,1024]{2,1,0:T(8,128)(2,1)S(1)}, u32[]{:S(2)}, u32[]{:S(2)}) async-start(bf16[16,16,1024]{2,1,0:T(8,128)(2,1)} %bitcast.63), calls=%async_computation | async-start | bytes 1048576 | tf_op jit(solution)/shard_map/all_to_all | solution.py:654
  78.1 14.1 %collective-permute-start.12 = (bf16[80,1024]{1,0:T(8,128)(2,1)S(1)}, bf16[80,1024]{1,0:T(8,128)(2,1)S(1)}, u32[]{:S(2)}, u32[]{:S(2)}) collective-permute-start(bf16[80,1024]{1,0:T(8,128)(2,1)S(1)} %get-tuple-element.48), channel_id=1, source_target_pairs={{0,1},{1,2},{2,3},{3,4},{4,5},{5,6},{6,7},{7,8},{8,9},{9,10},{10,1... | collective-permute-start | bytes 491528 | tf_op jit(solution)/shard_map/ppermute | solution.py:22
  79.9 15.7 %collective-permute-start.14 = (bf16[16,1024]{1,0:T(8,128)(2,1)}, bf16[16,1024]{1,0:T(8,128)(2,1)S(1)}, u32[]{:S(2)}, u32[]{:S(2)}) collective-permute-start(bf16[16,1024]{1,0:T(8,128)(2,1)} %get-tuple-element.51), channel_id=1, source_target_pairs={{0,12},{4,0},{8,4},{12,8},{1,13},{5,1},{9,5},{13,9},{2,14},{6,2},{... | collective-permute-start | bytes 98312 | tf_op jit(solution)/shard_map/ppermute | solution.py:22
  82.6 13.0 %collective-permute-start.15 = (bf16[16,1024]{1,0:T(8,128)(2,1)}, bf16[16,1024]{1,0:T(8,128)(2,1)S(1)}, u32[]{:S(2)}, u32[]{:S(2)}) collective-permute-start(bf16[16,1024]{1,0:T(8,128)(2,1)} %get-tuple-element.52), channel_id=1, source_target_pairs={{0,4},{4,8},{8,12},{12,0},{1,5},{5,9},{9,13},{13,1},{2,6},{6,10},{... | collective-permute-start | bytes 98312 | tf_op jit(solution)/shard_map/ppermute | solution.py:22
  82.6 13.0 %collective-permute-start.16 = (bf16[16,1024]{1,0:T(8,128)(2,1)}, bf16[16,1024]{1,0:T(8,128)(2,1)S(1)}, u32[]{:S(2)}, u32[]{:S(2)}) collective-permute-start(bf16[16,1024]{1,0:T(8,128)(2,1)} %get-tuple-element.53), channel_id=1, source_target_pairs={{0,8},{4,12},{8,0},{12,4},{1,9},{5,13},{9,1},{13,5},{2,10},{6,14},... | collective-permute-start | bytes 98312 | tf_op jit(solution)/shard_map/ppermute | solution.py:22
  95.6 0.6 copy-start.34
  95.7 0.8 copy-start.5
  116.2 6.5 %copy-start.19 = (bf16[64,1024]{1,0:T(8,128)(2,1)S(1)}, bf16[64,1024]{1,0:T(8,128)(2,1)}, u32[]{:S(2)}) copy-start(bf16[64,1024]{1,0:T(8,128)(2,1)} %get-tuple-element.55) | copy-start | bytes 393220
  122.6 14.0 %collective-permute-start.17 = (bf16[4,16,16,1024]{3,2,1,0:T(8,128)(2,1)}, bf16[4,16,16,1024]{3,2,1,0:T(8,128)(2,1)}, u32[]{:S(2)}, u32[]{:S(2)}) collective-permute-start(bf16[4,16,16,1024]{3,2,1,0:T(8,128)(2,1)} %get-tuple-element.67), channel_id=1, source_target_pairs={{0,16},{16,0},{1,17},{17,1},{2,18},{18,2},{3,19},{19,3},{4,20},{20... | collective-permute-start | bytes 6291464 | tf_op jit(solution)/shard_map/ppermute | solution.py:22
  123.6 7.7 %copy-start.15 = (bf16[16,1024]{1,0:T(8,128)(2,1)S(1)}, bf16[16,1024]{1,0:T(8,128)(2,1)}, u32[]{:S(2)}) copy-start(bf16[16,1024]{1,0:T(8,128)(2,1)} %get-tuple-element.69.refs_9_.refs_6_) | copy-start | bytes 98308
  123.6 13.1 %copy-start.2 = (bf16[4,16,16,1024]{3,2,1,0:T(8,128)(2,1)S(1)}, bf16[4,16,16,1024]{3,2,1,0:T(8,128)(2,1)}, u32[]{:S(2)}) copy-start(bf16[4,16,16,1024]{3,2,1,0:T(8,128)(2,1)} %get-tuple-element.66) | copy-start | bytes 6291460
  123.6 17.0 %all-to-all-start.1 = ((bf16[16,16,1024]{2,1,0:T(8,128)(2,1)}), bf16[16,16,1024]{2,1,0:T(8,128)(2,1)S(1)}, u32[]{:S(2)}, u32[]{:S(2)}) async-start(bf16[16,16,1024]{2,1,0:T(8,128)(2,1)} %bitcast.20), calls=%async_computation.1 | async-start | bytes 1048576 | tf_op jit(solution)/shard_map/all_to_all | solution.py:692
  131.2 9.3 %collective-permute-start.18 = (bf16[16,1024]{1,0:T(8,128)(2,1)S(1)}, bf16[16,1024]{1,0:T(8,128)(2,1)S(1)}, u32[]{:S(2)}, u32[]{:S(2)}) collective-permute-start(bf16[16,1024]{1,0:T(8,128)(2,1)S(1)} %copy-done.15), channel_id=1, source_target_pairs={{0,4},{4,8},{8,12},{12,0},{1,5},{5,9},{9,13},{13,1},{2,6},{6,10},{... | collective-permute-start | bytes 98312 | tf_op jit(solution)/shard_map/ppermute | solution.py:22
  133.1 7.5 %collective-permute-start.19 = (bf16[16,1024]{1,0:T(8,128)(2,1)S(1)}, bf16[16,1024]{1,0:T(8,128)(2,1)S(1)}, u32[]{:S(2)}, u32[]{:S(2)}) collective-permute-start(bf16[16,1024]{1,0:T(8,128)(2,1)S(1)} %copy-done.15), channel_id=1, source_target_pairs={{0,12},{4,0},{8,4},{12,8},{1,13},{5,1},{9,5},{13,9},{2,14},{6,2},{... | collective-permute-start | bytes 98312 | tf_op jit(solution)/shard_map/ppermute | solution.py:22
  134.5 6.1 %collective-permute-start.20 = (bf16[16,1024]{1,0:T(8,128)(2,1)S(1)}, bf16[16,1024]{1,0:T(8,128)(2,1)S(1)}, u32[]{:S(2)}, u32[]{:S(2)}) collective-permute-start(bf16[16,1024]{1,0:T(8,128)(2,1)S(1)} %copy-done.15), channel_id=1, source_target_pairs={{0,8},{4,12},{8,0},{12,4},{1,9},{5,13},{9,1},{13,5},{2,10},{6,14},... | collective-permute-start | bytes 98312 | tf_op jit(solution)/shard_map/ppermute | solution.py:22
  140.6 0.8 copy-start.1
  152.3 33.9 %collective-permute-start.21 = (bf16[4,4,80,1024]{3,2,1,0:T(8,128)(2,1)}, bf16[4,4,80,1024]{3,2,1,0:T(8,128)(2,1)}, u32[]{:S(2)}, u32[]{:S(2)}) collective-permute-start(bf16[4,4,80,1024]{3,2,1,0:T(8,128)(2,1)} %get-tuple-element.75), channel_id=1, source_target_pairs={{0,16},{16,0},{1,17},{17,1},{2,18},{18,2},{3,19},{19,3},{4,20},{20... | collective-permute-start | bytes 7864328 | tf_op jit(solution)/shard_map/ppermute | solution.py:22
  152.4 31.8 %all-to-all-start.2 = ((bf16[4,16,16,1024]{3,2,1,0:T(8,128)(2,1)}), bf16[4,16,16,1024]{3,2,1,0:T(8,128)(2,1)}, u32[]{:S(2)}, u32[]{:S(2)}) async-start(bf16[4,16,16,1024]{3,2,1,0:T(8,128)(2,1)} %add_convert_fusion.1), calls=%async_computation.2 | async-start | bytes 4194304 | tf_op jit(solution)/shard_map/all_to_all | solution.py:702
  164.0 22.2 %copy-start = (bf16[4,4,80,1024]{3,2,1,0:T(8,128)(2,1)S(1)}, bf16[4,4,80,1024]{3,2,1,0:T(8,128)(2,1)}, u32[]{:S(2)}) copy-start(bf16[4,4,80,1024]{3,2,1,0:T(8,128)(2,1)} %shard_map.195) | copy-start | bytes 7864324
  237.4 11.5 %copy-start.4 = (bf16[80,1024]{1,0:T(8,128)(2,1)}, bf16[80,1024]{1,0:T(8,128)(2,1)S(1)}, u32[]{:S(2)}) copy-start(bf16[80,1024]{1,0:T(8,128)(2,1)S(1)} %slice.91.refs_1_) | copy-start | bytes 491524
  237.4 8.4 %collective-permute-start.22 = (bf16[80,1024]{1,0:T(8,128)(2,1)S(1)}, bf16[80,1024]{1,0:T(8,128)(2,1)S(1)}, u32[]{:S(2)}, u32[]{:S(2)}) collective-permute-start(bf16[80,1024]{1,0:T(8,128)(2,1)S(1)} %slice.91.refs_1_), channel_id=1, source_target_pairs={{0,32},{32,64},{64,96},{96,0},{1,33},{33,65},{65,97},{97,1},{2,34}... | collective-permute-start | bytes 491528 | tf_op jit(solution)/shard_map/ppermute | solution.py:22
  237.5 8.6 %collective-permute-start.23 = (bf16[80,1024]{1,0:T(8,128)(2,1)S(1)}, bf16[80,1024]{1,0:T(8,128)(2,1)S(1)}, u32[]{:S(2)}, u32[]{:S(2)}) collective-permute-start(bf16[80,1024]{1,0:T(8,128)(2,1)S(1)} %slice.91.refs_1_), channel_id=1, source_target_pairs={{0,96},{32,0},{64,32},{96,64},{1,97},{33,1},{65,33},{97,65},{2,98}... | collective-permute-start | bytes 491528 | tf_op jit(solution)/shard_map/ppermute | solution.py:22
  240.7 6.8 %collective-permute-start.24 = (bf16[80,1024]{1,0:T(8,128)(2,1)S(1)}, bf16[80,1024]{1,0:T(8,128)(2,1)S(1)}, u32[]{:S(2)}, u32[]{:S(2)}) collective-permute-start(bf16[80,1024]{1,0:T(8,128)(2,1)S(1)} %slice.91.refs_1_), channel_id=1, source_target_pairs={{0,64},{32,96},{64,0},{96,32},{1,65},{33,97},{65,1},{97,33},{2,66}... | collective-permute-start | bytes 491528 | tf_op jit(solution)/shard_map/ppermute | solution.py:22
  240.7 7.5 %collective-permute-start.25 = (bf16[80,1024]{1,0:T(8,128)(2,1)S(1)}, bf16[80,1024]{1,0:T(8,128)(2,1)S(1)}, u32[]{:S(2)}, u32[]{:S(2)}) collective-permute-start(bf16[80,1024]{1,0:T(8,128)(2,1)S(1)} %slice.91.refs_1_), channel_id=1, source_target_pairs={{0,16},{16,0},{1,17},{17,1},{2,18},{18,2},{3,19},{19,3},{4,20},{20... | collective-permute-start | bytes 491528 | tf_op jit(solution)/shard_map/ppermute | solution.py:22
  245.8 3.2 %copy-start.7 = (bf16[80,1024]{1,0:T(8,128)(2,1)}, bf16[80,1024]{1,0:T(8,128)(2,1)S(1)}, u32[]{:S(2)}) copy-start(bf16[80,1024]{1,0:T(8,128)(2,1)S(1)} %collective-permute-done.22.refs_2_) | copy-start | bytes 491524
  245.8 2.4 collective-permute-start.26
  246.1 2.8 %copy-start.8 = (bf16[80,1024]{1,0:T(8,128)(2,1)}, bf16[80,1024]{1,0:T(8,128)(2,1)S(1)}, u32[]{:S(2)}) copy-start(bf16[80,1024]{1,0:T(8,128)(2,1)S(1)} %collective-permute-done.23.refs_3_) | copy-start | bytes 491524
  246.1 2.1 collective-permute-start.27
  247.5 1.4 copy-start.9
  247.5 1.4 collective-permute-start.28
  248.2 0.8 copy-start.10
  248.2 0.8 copy-start.11
  248.2 0.8 copy-start.12
  249.0 0.7 copy-start.13
  (5 other events, 3.0 us)

commit v4 on v2

--- a/solution.py
+++ b/solution.py
@@ -59,6 +59,13 @@
     return [low, high, shift_by(low[:cut], axis, 1), shift_by(high[cut:], axis, 3)]
 
 
+def reduce_ring(chunks, axis):
+    total = chunks[0].astype(F32)
+    for chunk, origin in zip(chunks[1:], ORIGINS[1:]):
+        total = total + shift_by(chunk, axis, origin).astype(F32)
+    return total.astype(BF)
+
+
 def fresh_row(side, place):
     return (place % 4) * 16 + (side + 1) * 4 + place // 4
 
@@ -74,7 +81,7 @@
         return copy
 
 
-def local_call(body, outs, operands, scratch=(), copies=8, flops=0, limit=44):
+def local_call(body, outs, operands, scratch=(), copies=8, flops=0, limit=60):
     def kernel(*refs):
         body(Copies(refs[-1]), *refs[:-1])
 
@@ -82,8 +89,8 @@
         kernel,
         out_shape=[jax.ShapeDtypeStruct(shape, kind) for shape, kind in outs],
         in_specs=[pl.BlockSpec(memory_space=pltpu.SMEM)]
-        + [pl.BlockSpec(memory_space=pl.ANY)] * (len(operands) - 1),
-        out_specs=[pl.BlockSpec(memory_space=pl.ANY)] * len(outs),
+        + [pl.BlockSpec(memory_space=pltpu.HBM)] * (len(operands) - 1),
+        out_specs=[pl.BlockSpec(memory_space=pltpu.HBM)] * len(outs),
         scratch_shapes=[*scratch, pltpu.SemaphoreType.DMA((copies,))],
         compiler_params=pltpu.CompilerParams(vmem_limit_bytes=limit * 1024 * 1024),
         cost_estimate=pl.CostEstimate(flops=flops, bytes_accessed=1024 * 1024, transcendentals=0),
@@ -118,31 +125,45 @@
 def norm_kernel(
     copies,
     where_ref,
-    hidden_hbm, meta_hbm, in_hbm, out_hbm, rel_hbm,
+    hidden_hbm, lens_hbm, order_hbm, rel_hbm, in_hbm, out_hbm, table_hbm,
     block_hbm, sum_hbm, weights_hbm,
-    hidden_ref, meta_ref, block_ref, sum_ref,
+    hidden_ref, lens_ref, order_ref, rel_ref,
+    block_ref, sum_ref, weights_ref,
 ):
     core = where_ref[1]
-    first = [copies.start(hidden_hbm, hidden_ref), copies.start(meta_hbm, meta_ref)]
-    later = []
+    packed = []
     for i in range(2):
         cols, wide = pl.ds(i * 256, 256), pl.ds(i * 512, 512)
         source = in_hbm.at[pl.ds(pl.multiple_of(core * 512 + i * 256, 256), 256), :]
-        later.append(copies.start(source, weights_hbm.at[pl.ds(0, 256), cols]))
+        packed.append(copies.start(source, weights_ref.at[pl.ds(0, 256), cols]))
         source = out_hbm.at[pl.ds(pl.multiple_of(core * 128, 128), 128), wide]
-        later.append(copies.start(source, weights_hbm.at[pl.ds(256 + i * 128, 128), :]))
-        source = rel_hbm.at[pl.ds(pl.multiple_of(core * 32, 32), 32), wide]
-        later.append(copies.start(source, weights_hbm.at[pl.ds(512 + i * 32, 32), :]))
+        packed.append(copies.start(source, weights_ref.at[pl.ds(256 + i * 128, 128), :]))
+        source = table_hbm.at[pl.ds(pl.multiple_of(core * 32, 32), 32), wide]
+        packed.append(copies.start(source, weights_ref.at[pl.ds(512 + i * 32, 32), :]))
+    first = [
+        copies.start(hidden_hbm, hidden_ref),
+        copies.start(lens_hbm, lens_ref),
+        copies.start(order_hbm, order_ref),
+        copies.start(rel_hbm, rel_ref),
+    ]
+    wait_all(packed)
+    later = [copies.start(weights_ref, weights_hbm)]
     wait_all(first)
+    meta = jnp.zeros((16, 128), F32)
+    high = rel_ref[...] // 32
+    for i, row in enumerate((lens_ref[...], order_ref[...], high, rel_ref[...] - 32 * high)):
+        values = jnp.broadcast_to(row.astype(F32), (16, 16)).astype(BF)
+        select = (lanes((16, 128)) == sublanes((16, 128)) + 16 * i).astype(F32).astype(BF)
+        meta = meta + dot(values, select)
     values = hidden_ref[...].astype(F32)
     center = values - jnp.mean(values, axis=-1, keepdims=True)
     spread = jnp.mean(center * center, axis=-1, keepdims=True)
     tokens = values.shape[0]
     block_ref[0:tokens, :] = (center * lax.rsqrt(spread + 1e-05)).astype(BF)
-    block_ref[tokens : tokens + 16, :] = meta_ref[...]
+    block_ref[tokens : tokens + 16, :] = jnp.zeros((16, values.shape[1]), BF)
+    block_ref[tokens : tokens + 16, 0:128] = meta.astype(BF)
     later.append(copies.start(block_ref, block_hbm))
-    pool = pool_rows(length_column(meta_ref[:, 0:128].astype(F32)), tokens)
-    sum_ref[...] = dot(pool, hidden_ref[...])
+    sum_ref[...] = dot(pool_rows(length_column(meta), tokens), hidden_ref[...])
     later.append(copies.start(sum_ref, sum_hbm))
     wait_all(later)
 
@@ -211,8 +232,8 @@
         wanted = jnp.sum(wanted, axis=1, keepdims=True)
         line = lanes(wide)
         owner_y = (my_y + jnp.where(line < 64, 0, jnp.where(line < 128, 3, line // 64 - 1))) % 4
-        name = (my_x * 4 + owner_y) * 52 + line // 32 % 2 * 26 + line % 32
-        pick = (name.astype(F32) == wanted) & (line % 32 < 26)
+        name = (my_x * 4 + owner_y) * 52 + line % 64
+        pick = (name.astype(F32) == wanted) & (line % 64 < 52)
         asked[s][...] = dot(pick.astype(F32).astype(BF), rel_ref[...]).astype(BF)
         length = length_column(values)
         length_ref[s * 16 : (s + 1) * 16, :] = jnp.broadcast_to(1.0 / length, (16, 128))
@@ -246,17 +267,20 @@
         cols = slice(t * 256, (t + 1) * 256)
         wait_all(weights[t])
 
-        @pl.loop(0, 4)
+        @pl.loop(0, 2)
         def _(s):
-            rows = pl.ds(pl.multiple_of(s * 256, 256), 256)
-            few = pl.ds(pl.multiple_of(s * 16, 16), 16)
+            rows = pl.ds(pl.multiple_of(s * 512, 512), 512)
             pre = dot(normed_ref[rows, :], in_ref[:, cols])
             square = pre * pre
             tanh = jnp.tanh(GELU_SCALE * pre * (1.0 + GELU_CUBE * square))
             upper = 0.5 + 0.5 * tanh
             slope = upper + (0.5 * GELU_SCALE) * pre * (1.0 - tanh * tanh) * (1.0 + 3.0 * GELU_CUBE * square)
             slope_ref[rows, cols] = slope.astype(BF)
-            pooled_ref[few, cols] = dot(pool_ref[few, :], (pre * upper).astype(BF)).astype(BF)
+            activation = (pre * upper).astype(BF)
+            for i in range(2):
+                few = pl.ds(pl.multiple_of(s * 32 + i * 16, 16), 16)
+                pooled = dot(pool_ref[few, :], activation[i * 256 : (i + 1) * 256])
+                pooled_ref[few, cols] = pooled.astype(BF)
 
     sent_out.append(copies.start(slope_ref, slope_hbm))
     sent_out.append(copies.start(pooled_ref, pooled_hbm))
@@ -273,21 +297,27 @@
 def graph_kernel(
     copies,
     where_ref,
-    arrived_hbm, base_hbm, row_hot_hbm, own_hot_t_hbm, e0_hbm, e1_hbm, e2_hbm, e3_hbm,
-    src_hot_hbm, dst_hot_hbm, dst_hot_t_hbm, src_row_hot_hbm,
+    arrived_hbm, own_hot_t_hbm, e0_hbm, e1_hbm, e2_hbm, e3_hbm,
+    src_hot_hbm, dst_hot_hbm, dst_hot_t_hbm,
     w_msg_hbm, w_self_hbm, d_out_hbm,
+    cache_hbm, low_hbm, high_hbm,
     table_out_hbm, blocks_hbm, graph_out_hbm, aggregate_hbm, nodes_hbm, pre_hbm,
-    arrived_ref, base_ref, row_hot_ref, own_hot_t_ref, e0, e1, e2, e3,
-    src_hot_ref, dst_hot_ref, dst_hot_t_ref, src_row_hot_ref,
+    arrived_ref, own_hot_t_ref, e0, e1, e2, e3,
+    src_hot_ref, dst_hot_ref, dst_hot_t_ref,
     w_msg_ref, w_self_ref, d_out_ref,
     table_out_ref, blocks_ref, graph_out_ref, aggregate_ref, nodes_ref, pre_ref,
+    base_ref, places_ref, row_hot_t_ref, src_row_hot_ref,
     ext_ref, sources_ref, edges_ref, agg_grad_ref, sums_ref, rel_ref,
 ):
     scale = (256 / 2048) ** 0.5
     first = [
+        copies.start(low_hbm.at[pl.ds(64, 16), pl.ds(0, 128)], places_ref.at[0]),
+        copies.start(high_hbm.at[pl.ds(64, 16), pl.ds(0, 128)], places_ref.at[1]),
+        copies.start(own_hot_t_hbm, own_hot_t_ref),
         copies.start(arrived_hbm, arrived_ref),
-        copies.start(base_hbm, base_ref),
-        copies.start(row_hot_hbm, row_hot_ref),
+        copies.start(cache_hbm, base_ref.at[pl.ds(16, 240), :]),
+        copies.start(low_hbm.at[pl.ds(0, 64), :], base_ref.at[pl.ds(256, 64), :]),
+        copies.start(high_hbm.at[pl.ds(0, 64), :], base_ref.at[pl.ds(320, 64), :]),
         copies.start(e0_hbm, e0),
         copies.start(e1_hbm, e1),
         copies.start(e2_hbm, e2),
@@ -300,29 +330,42 @@
         copies.start(w_self_hbm, w_self_ref),
         copies.start(d_out_hbm, d_out_ref),
     ]
-    fourth = [
-        copies.start(dst_hot_hbm, dst_hot_ref),
-        copies.start(src_row_hot_hbm, src_row_hot_ref),
-        copies.start(own_hot_t_hbm, own_hot_t_ref),
-    ]
+    fourth = [copies.start(dst_hot_hbm, dst_hot_ref)]
+    base_ref[0:16, :] = jnp.zeros((16, 1024), BF)
     wait_all(first)
     rel = e0[...].astype(F32) + e1[...].astype(F32) + e2[...].astype(F32) + e3[...].astype(F32)
     for j in range(16):
         rel_ref[j] = rel[j : j + 1]
+
+    to = lanes((128, 128)) - sublanes((128, 128))
+    inside = sublanes((128, 128)) < 64
+    low_move = ((to == 0) & inside).astype(F32).astype(BF)
+    high_move = ((to == 64) & inside).astype(F32).astype(BF)
+    places = (dot(places_ref[0], low_move) + dot(places_ref[1], high_move))[0:1].astype(I32)
+    upper = (lax.broadcasted_iota(I32, (1, 128), 1) >= 64).astype(I32)
+    table_row = jnp.where(places < 16, (places % 4) * 16 + upper * 8 + places // 4, -1)
+    row_hot_t_ref[:, 0:256] = own_hot_t_ref[...]
+    row_hot_t_ref[:, 256:384] = (sublanes((64, 128)) == table_row).astype(F32).astype(BF)
+    src_row_hot_ref[...] = dot_bt(row_hot_t_ref[...], src_hot_ref[...]).astype(BF)
     total = arrived_ref[0:64, :].astype(F32)
     for i in range(1, 4):
         total = total + arrived_ref[i * 64 : (i + 1) * 64, :].astype(F32)
     table = total.astype(BF)
-    ext_ref[...] = (base_ref[...].astype(F32) + dot(row_hot_ref[...], table)).astype(BF)
+    ext_ref[...] = (base_ref[...].astype(F32) + dot_t(row_hot_t_ref[...], table)).astype(BF)
     nodes_ref[...] = ext_ref[0:256, :]
     sent_out = [copies.start(nodes_ref, nodes_hbm)]
 
-    @pl.loop(0, 16)
-    def _(j):
-        rows = pl.ds(pl.multiple_of(j * 128, 128), 128)
-        taken = dot(src_hot_ref[rows, :], ext_ref[...])
-        sources_ref[rows, :] = taken.astype(BF)
-        edges_ref[rows, :] = (taken * rel_ref[j]).astype(BF)
+    for n in range(4):
+        cols = slice(n * 256, (n + 1) * 256)
+
+        @pl.loop(0, 4)
+        def _(k):
+            rows = pl.ds(pl.multiple_of(k * 512, 512), 512)
+            taken = dot(src_hot_ref[rows, :], ext_ref[:, cols])
+            sources_ref[rows, cols] = taken.astype(BF)
+            for i in range(4):
+                few = pl.ds(pl.multiple_of(k * 512 + i * 128, 128), 128)
+                edges_ref[few, cols] = (taken[i * 128 : (i + 1) * 128] * rel_ref[k * 4 + i, :, cols]).astype(BF)
 
     wait_all(second)
 
@@ -352,16 +395,23 @@
 
     wait_all(fourth)
 
-    @pl.loop(0, 16)
-    def _(j):
-        rows = pl.ds(pl.multiple_of(j * 128, 128), 128)
-        at_dest = dot(dst_hot_ref[rows, :], agg_grad_ref[...])
-        edges_ref[rows, :] = (at_dest * rel_ref[j]).astype(BF)
-        sums_ref[j] = jnp.sum(at_dest * sources_ref[rows, :].astype(F32), axis=0, keepdims=True)
+    for n in range(4):
+        cols = slice(n * 256, (n + 1) * 256)
+
+        @pl.loop(0, 4)
+        def _(k):
+            rows = pl.ds(pl.multiple_of(k * 512, 512), 512)
+            at_dest = dot(dst_hot_ref[rows, :], agg_grad_ref[:, cols])
+            for i in range(4):
+                few = pl.ds(pl.multiple_of(k * 512 + i * 128, 128), 128)
+                part = at_dest[i * 128 : (i + 1) * 128]
+                edges_ref[few, cols] = (part * rel_ref[k * 4 + i, :, cols]).astype(BF)
+                product = part * sources_ref[few, cols].astype(F32)
+                sums_ref[k * 4 + i, :, cols] = jnp.sum(product, axis=0, keepdims=True)
 
     blocks_ref[...] = jnp.concatenate([sums_ref[j] for j in range(16)], axis=0).astype(BF)
     sent_out.append(copies.start(blocks_ref, blocks_hbm))
-    own_pre = dot(own_hot_t_ref[...], pre_ref[0:16, :]).astype(BF)
+    own_pre = dot(own_hot_t_ref[...], pre_ref[...]).astype(BF)
 
     @pl.loop(0, 4)
     def _(n):
@@ -408,13 +458,13 @@
     where_ref,
     returned_hbm, route_hbm, length_hbm, all_out_hbm, slope_hbm, pooled_hbm, normed_t_hbm,
     rel_hot_hbm, r0_hbm, r1_hbm, r2_hbm, r3_hbm,
-    kept_hbm, given_hbm,
+    out_kept_hbm, out_given_hbm, in_kept_hbm, in_given_hbm,
     returned_ref, route_ref, length_ref, all_out_ref, slope_ref, pooled_ref, normed_t_ref,
     rel_hot_ref, r0, r1, r2, r3,
-    kept_ref, given_ref,
+    out_kept_ref, out_given_ref, in_kept_ref, in_given_ref,
     scaled_ref, grad_ref,
 ):
-    core, my_y = where_ref[1], where_ref[3]
+    my_z, core, my_y = where_ref[0], where_ref[1], where_ref[3]
     first = [
         copies.start(returned_hbm, returned_ref),
         copies.start(route_hbm, route_ref),
@@ -427,20 +477,17 @@
     ]
     second = [
         copies.start(all_out_hbm, all_out_ref),
+        copies.start(pooled_hbm, pooled_ref),
         copies.start(slope_hbm, slope_ref),
-        copies.start(pooled_hbm, pooled_ref),
         copies.start(normed_t_hbm, normed_t_ref),
     ]
     wait_all(first)
     scaled_ref[...] = (dot(route_ref[...], returned_ref[...]) * length_ref[:, 0:1]).astype(BF)
     blocks = jnp.concatenate([r0[...], r1[...], r2[...], r3[...]], axis=0)
-    for half, chunk_ref in ((core, kept_ref), (1 - core, given_ref)):
-        for y in range(4):
-            rows = pl.ds(pl.multiple_of(y * 128 + half * 64, 64), 64)
-            rel = dot(rel_hot_ref[rows, :], blocks).astype(BF)
-            for z in range(4):
-                chunk_ref[z, y, 64:80, :] = rel[z * 16 : (z + 1) * 16]
-
+    places = []
+    for z in range(4):
+        ahead = lax.rem(z - my_z + 4, 4)
+        places.append(jnp.where(ahead == 0, 0, jnp.where(ahead == 3, 1, ahead + 1)))
     wait_all(second)
 
     @pl.loop(0, 4)
@@ -451,26 +498,33 @@
         upstream = dot_bt(scaled_ref[...], all_out_ref[cols, :]).astype(BF)
         for s in range(4):
             rows = slice(s * 256, (s + 1) * 256)
-            shape = (16, 256)
-            line = lanes(shape)
+            line = lanes((16, 256))
             length = 1.0 / length_ref[s * 16 : (s + 1) * 16, 0:1]
-            inside = (line // 16 == sublanes(shape)) & ((line % 16).astype(F32) + 0.5 < length)
+            inside = (line // 16 == sublanes((16, 256))) & ((line % 16).astype(F32) + 0.5 < length)
             pool = inside.astype(F32).astype(BF)
             at_tokens = dot_t(pool, upstream[s * 16 : (s + 1) * 16])
             grad_ref[rows, :] = (slope_ref[rows, cols].astype(F32) * at_tokens).astype(BF)
-        for half, chunk_ref in ((1 - core, given_ref), (core, kept_ref)):
+        for half, out_ref, in_ref in ((1 - core, out_given_ref, in_given_ref), (core, out_kept_ref, in_kept_ref)):
             units = pl.ds(pl.multiple_of(t * 256 + half * 128, 128), 128)
             out = dot_t(pooled_ref[:, units], scaled_ref[...]).astype(BF)
+            rel_rows = pl.ds(pl.multiple_of(owner * 128 + half * 64, 64), 64)
+            rel = dot(rel_hot_ref[rel_rows, :], blocks).astype(BF)
             inner = dot(normed_t_ref[pl.ds(pl.multiple_of(half * 512, 512), 512), :], grad_ref[...]).astype(BF)
             for z in range(4):
-                chunk_ref[z, owner, 32:64, :] = out[z * 32 : (z + 1) * 32]
+                out_ref[t, places[z], 0:32, :] = out[z * 32 : (z + 1) * 32]
+                out_ref[t, places[z], 32:48, :] = rel[z * 16 : (z + 1) * 16]
                 for i in range(4):
                     piece = inner[z * 128 + i * 32 : z * 128 + (i + 1) * 32]
-                    chunk_ref[z, owner, 0:32, i * 256 : (i + 1) * 256] = piece
-
-
-    sent_out = [copies.start(given_ref, given_hbm), copies.start(kept_ref, kept_hbm)]
-    wait_all(sent_out)
+                    in_ref[places[z], t, :, i * 256 : (i + 1) * 256] = piece
+
+    wait_all(
+        [
+            copies.start(out_given_ref, out_given_hbm),
+            copies.start(in_given_ref, in_given_hbm),
+            copies.start(out_kept_ref, out_kept_hbm),
+            copies.start(in_kept_ref, in_kept_hbm),
+        ]
+    )
 
 
 def place_kernel(
@@ -479,7 +533,7 @@
     h0, h1, h2, h3, h4, h5, h6, h7,
     in_hbm, out_hbm, rel_hbm,
     a0, a1, a2, a3, c0, c1, c2, c3,
-    in_ref, out_ref, rel_ref,
+    in_ref, out_ref, owned_ref, rel_ref,
 ):
     sources = (h0, h1, h2, h3, h4, h5, h6, h7)
     targets = (a0, a1, a2, a3, c0, c1, c2, c3)
@@ -494,7 +548,8 @@
                 in_ref[rows, :] = values[0:32, i * 256 : (i + 1) * 256]
             out_ref[pl.ds(pl.multiple_of(half * 128 + z * 32, 32), 32), :] = values[32:64]
             rel_ref[pl.ds(pl.multiple_of(half * 32 + z * 8, 8), 8), :] = values[64:72]
-    wait_all([copies.start(in_ref, in_hbm), copies.start(out_ref, out_hbm), copies.start(rel_ref, rel_hbm)])
+    owned_ref[...] = rel_ref[0:52, :]
+    wait_all([copies.start(in_ref, in_hbm), copies.start(out_ref, out_hbm), copies.start(owned_ref, rel_hbm)])
 
 
 def shards(
@@ -522,17 +577,15 @@
     src, dst, rel = edge_src[0], edge_dst[0], edge_rel[0]
     shard_rows = rel_table.shape[0]
 
-    meta = row_of(jnp.concatenate([desc_len, send_order[0], rel // 32, rel % 32]), width)
-    rel_pad = jnp.pad(rel_table.reshape(2, shard_rows // 2, width), ((0, 0), (0, 32 - shard_rows // 2), (0, 0)))
-    rel_pad = rel_pad.reshape(64, width)
-    operands = [hidden.reshape(tokens, width), jnp.broadcast_to(meta, (16, width)), w_in, w_out, rel_pad]
-    outs = [((tokens + 16, width), BF), ((entities, width), F32)]
+    rel_pad = jnp.pad(rel_table, ((0, 64 - shard_rows), (0, 0)))
+    operands = [hidden.reshape(tokens, width), desc_len[None, :], send_order, edge_rel]
+    outs = [((tokens + 16, width), BF), ((entities, width), F32), ((576, 512), BF)]
     block, hidden_sum, weights = local_call(
         norm_kernel,
-        [*outs, ((576, 512), BF)],
-        [where, *operands],
-        like(operands[:2]) + filled(outs),
-        copies=10,
+        outs,
+        [where, *operands, w_in, w_out, rel_pad],
+        like(operands) + filled(outs),
+        copies=14,
     )
     blocks = [block, *gather_ring(block, "x", 128)]
     mine = gather_ring(weights, "y", 256)
@@ -579,21 +632,12 @@
     to_high, to_low, outgoing = lax.optimization_barrier((to_high, to_low, outgoing))
     from_low = shift_by(to_high, GROUP, 1)
     from_high = shift_by(to_low, GROUP, 15)
-    low_place = from_low[side, :side].astype(I32)
-    high_place = from_high[side, :side].astype(I32)
-    own_row = fresh_row(0, place)
-    low_row = jnp.where(low_place < 16, fresh_row(-1, low_place), -1)
-    high_row = jnp.where(high_place < 16, fresh_row(1, high_place), -1)
-    table_row = jnp.concatenate([own_row, jnp.full((cache_count,), -1, I32), low_row, high_row])
-    row_hot = one_hot(table_row, 64)
-    base = jnp.concatenate([jnp.zeros((entities, width), BF), cache, from_low[:side], from_high[:side]], axis=0)
+    own_row = jnp.concatenate([fresh_row(0, place), jnp.full((cache_count,), -1, I32)])
     node_count = entities + cache_count
     extended_count = node_count + 2 * side
     edge_count = src.shape[0]
     block_count = rel.shape[0]
     src_hot = one_hot(src, extended_count)
-    src_row_hot = dot_bt(one_hot_t(table_row, 64), src_hot).astype(BF)
-
     arrived = lax.all_to_all(outgoing.reshape(16, 16, width), GROUP, 0, 0, tiled=True).reshape(256, width)
     rel_rows = [asked[0]] + [shift_by(rows, "x", o) for rows, o in zip(asked[1:], ORIGINS[1:])]
     normed_t = normed.T
@@ -601,14 +645,11 @@
     outs = [((64, width), BF), ((block_count, width), BF)] + [((node_count, width), BF)] * 4
     operands = [
         arrived,
-        base,
-        row_hot,
         one_hot_t(own_row, 64),
         *rel_rows,
         src_hot,
         one_hot(dst, node_count),
         one_hot_t(dst, node_count),
-        src_row_hot,
         w_msg,
         w_self,
         d_out,
@@ -616,10 +657,14 @@
     grad_table, grad_blocks, graph_out, aggregate, nodes, grad_pre = local_call(
         graph_kernel,
         outs,
-        [where, *operands],
+        [where, *operands, cache, from_low, from_high],
         like(operands)
         + filled(outs)
         + [
+            pltpu.VMEM((extended_count, width), BF),
+            pltpu.VMEM((2, 16, 128), BF),
+            pltpu.VMEM((64, extended_count), BF),
+            pltpu.VMEM((64, edge_count), BF),
             pltpu.VMEM((extended_count, width), BF),
             pltpu.VMEM((edge_count, width), BF),
             pltpu.VMEM((edge_count, width), BF),
@@ -627,7 +672,7 @@
             pltpu.VMEM((block_count, 1, width), F32),
             pltpu.VMEM((block_count, 1, width), F32),
         ],
-        copies=24,
+        copies=26,
         flops=6 * 10**9,
     )
 
@@ -636,16 +681,20 @@
     rel_blocks = [grad_blocks] + [shift_by(grad_blocks, "x", s) for s in SHIFTS]
 
     outs = [((4, 16, 16, width), BF)] * 2
+    grad_pre, *rel_blocks = lax.optimization_barrier((grad_pre, *rel_blocks))
     operands = [aggregate, nodes, grad_pre]
     graph_kept, graph_given = local_call(
         weight_kernel, outs, [where, *operands], like(operands) + filled(outs), flops=10**9
     )
     chip = (graph_kept.astype(F32) + shift_by(graph_given, "core", 1).astype(F32)).astype(BF)
     line = lax.all_to_all(chip, "x", 0, 0, tiled=True)
-
-    outs = [((4, 4, 80, width), BF)] * 2
+    plane = lax.all_to_all(jnp.sum(line.astype(F32), axis=0).astype(BF), ("z", "y"), 0, 0, tiled=True)
+    weight_rows = jnp.sum(plane.astype(F32), axis=0)
+    grad_msg, grad_self = weight_rows[:8], weight_rows[8:]
+
+    outs = [((4, 4, 48, width), BF)] * 2 + [((4, 4, 32, width), BF)] * 2
     operands = [returned, route, inverse, all_out, slope, pooled, normed_t, rel_hot, *rel_blocks]
-    kept, given = local_call(
+    out_kept, out_given, in_kept, in_given = local_call(
         back_kernel,
         outs,
         [where, *operands],
@@ -655,22 +704,25 @@
         copies=16,
         flops=2 * 4 * tokens * width * 4 * units,
     )
-    given, line = lax.optimization_barrier((given, line))
-    line_sum = jnp.sum(line.astype(F32), axis=0).astype(BF)
-    chunks = (kept.astype(F32) + shift_by(given, "core", 1).astype(F32)).astype(BF)
-    chunks = jnp.concatenate([chunks.reshape(16, 80, width), line_sum], axis=1)
-    chunks = lax.all_to_all(chunks, ("z", "y"), 0, 0, tiled=True)
-    summed = jnp.sum(chunks.astype(F32), axis=0)
-    grad_msg, grad_self = summed[80:88], summed[88:96]
-    part = summed[:80].astype(BF)
+    out_chip = (out_kept.astype(F32) + shift_by(out_given, "core", 1).astype(F32)).astype(BF)
+    in_chip = (in_kept.astype(F32) + shift_by(in_given, "core", 1).astype(F32)).astype(BF)
+    out_part = reduce_ring([out_chip[i].reshape(192, width) for i in range(4)], "y").reshape(4, 48, width)
+    in_part = reduce_ring([in_chip[i].reshape(128, width) for i in range(4)], "z").reshape(4, 32, width)
+    out_part = reduce_ring([out_part[i] for i in range(4)], "z")
+    in_part = reduce_ring([in_part[i] for i in range(4)], "y")
+    part = jnp.concatenate([in_part, out_part], axis=0)
     parts = [part] + [shift_by(part, "z", s) for s in SHIFTS]
     others = [shift_by(piece, "core", 1) for piece in parts]
-    outs = [((width, units), F32), ((units, width), F32), ((64, width), F32)]
+    outs = [((width, units), F32), ((units, width), F32), ((shard_rows, width), F32)]
     operands = [*parts, *others]
     grad_w_in, grad_w_out, grad_rel = local_call(
-        place_kernel, outs, [where, *operands], like(operands) + filled(outs), copies=12
-    )
-    return (graph_out, grad_w_in, grad_w_out, grad_rel[:shard_rows], grad_msg, grad_self)
+        place_kernel,
+        outs,
+        [where, *operands],
+        like(operands) + filled(outs) + [pltpu.VMEM((64, width), F32)],
+        copies=12,
+    )
+    return (graph_out, grad_w_in, grad_w_out, grad_rel, grad_msg, grad_self)
 
 
 def solution(mesh):

time: 254 us -> 214 us (0.84)
  blocking collectives: 45.7 us -> 0 us
  starting transfers between devices: 43 us -> 69.5 us
  local copies, waits for them, and re-layouts: 28.9 us -> 13.3 us
  waiting for transfers between devices: 63 us -> 55.5 us
  Pallas kernels: 51.3 us -> 58 us
    all_to_all x1 -> x0, blocking collectives: 45.7 us -> none  [shards(): chunks = lax.all_to_all(chunks, ('z', 'y'), 0, 0, tiled=True)]
    ppermute x29 -> x42, starting transfers between devices: 30.7 us -> 50 us  [shift_by(): lax.ppermute(value, axis, [(i, (i + shift) % count) for i in range(count)])]
    unnamed x74 -> x76, local copies, waits for them, and re-layouts: 22.9 us -> 4.12 us
    all_to_all x1, waiting for transfers between devices: 8.47 us -> 0.01 us  [shards(): lax.all_to_all(back.reshape(16, 16, width), GROUP, 0, 0, tiled=True)]
    pallas_call x6, Pallas kernels: 51.3 us -> 58 us  [local_call(): pl.pallas_call(kernel, out_shape=[jax.ShapeDtypeStruct(shape, kind) for s...]
    all_to_all x0 -> x1, starting transfers between devices: none -> 4.59 us  [shards(): lax.all_to_all(jnp.sum(line.astype(F32), axis=0).astype(BF), ('z', 'y'),...]
    all_to_all x1, starting transfers between devices: 4.25 us -> 7.37 us  [shards(): lax.all_to_all(outgoing.reshape(16, 16, width), GROUP, 0, 0, tiled=True)]
    ppermute x29 -> x42, waiting for transfers between devices: 54.5 us -> 55.4 us  [shift_by(): lax.ppermute(value, axis, [(i, (i + shift) % count) for i in range(count)])]
  transfers between devices with their start and end apart: 32 -> 46, of which waited for: 16 -> 16; matrix products, arithmetic and copies ran while one was open for 6% -> 9% of each run, Pallas kernels for 4% -> 11%
where the time goes in v4:
time: 214 us; the launch traced here: 213 us
  starting transfers between devices  69.5 us (32%)
  Pallas kernels  58 us (27%)
  waiting for transfers between devices  55.5 us (26%)
  other arithmetic  14.7 us (7%)
  local copies, waits for them, and re-layouts  13.3 us (6%)
    pallas_call x6, Pallas kernels, local_call(): pl.pallas_call(kernel, out_shape=[jax.ShapeDtypeStruct(shape, kind) for s...  58 us
    ppermute x42, waiting for transfers between devices, shift_by(): lax.ppermute(value, axis, [(i, (i + shift) % count) for i in range(count)])  55.4 us
    ppermute x42, starting transfers between devices, shift_by(): lax.ppermute(value, axis, [(i, (i + shift) % count) for i in range(count)])  50 us
    all_to_all x1, starting transfers between devices, shards(): lax.all_to_all(outgoing.reshape(16, 16, width), GROUP, 0, 0, tiled=True)  7.37 us
    all_to_all x1, starting transfers between devices, shards(): lax.all_to_all(jnp.sum(line.astype(F32), axis=0).astype(BF), ('z', 'y'),...  4.59 us
  transfers between devices with their start and end apart: 46, of which 16 were waited for; matrix products, arithmetic and copies ran while one was open for 9% of the time, Pallas kernels for 11%

profile of v4, /device:TPU:0, one launch (start us, length us, event | category | flops | bytes accessed | tf_op | source)
XLA Modules:
  0.0 212.5 jit_solution(8317693433243008742)
XLA Ops:
  0.6 1.6 pad.23.refs_7_.refs_8_
  2.2 0.6 pad_add_fusion.refs_0_
  2.8 3.5 %shard_map.190 = (bf16[272,1024]{1,0:T(8,128)(2,1)}, f32[16,1024]{1,0:T(8,128)}, bf16[576,512]{1,0:T(8,128)(2,1)}) custom-call(s32[4]{0:T(128)} %pad_add_fusion.refs_0_, bf16[256,1024]{1,0:T(8,128)(2,1)} %bitcast.36, s32[1,16]{1,0:T(1,128)} %bitcast.45, s32[1,16]{1,0:T(1,128)} %refs_3_.1, s32[1,16]{1,0:T(1,128)} %refs_4_.1, bf16[1024,256]{1,0:T(8,128)(2,1)} %refs_6_.3, ...), custom_call_target="tpu_custom_call" | custom-call | bytes 1048576 | tf_op jit(solution)/shard_map/pallas_call | solution.py:88
  6.3 3.2 %collective-permute-start.5 = (bf16[576,512]{1,0:T(8,128)(2,1)}, bf16[576,512]{1,0:T(8,128)(2,1)S(1)}, u32[]{:S(2)}, u32[]{:S(2)}) collective-permute-start(bf16[576,512]{1,0:T(8,128)(2,1)} %get-tuple-element.45), channel_id=1, source_target_pairs={{0,3},{1,0},{2,1},{3,2},{4,7},{5,4},{6,5},{7,6},{8,11},{9,8},{10,9... | collective-permute-start | bytes 1769480 | tf_op jit(solution)/shard_map/ppermute | solution.py:22
  9.5 2.8 %collective-permute-start.1 = (bf16[272,1024]{1,0:T(8,128)(2,1)}, bf16[272,1024]{1,0:T(8,128)(2,1)S(1)}, u32[]{:S(2)}, u32[]{:S(2)}) collective-permute-start(bf16[272,1024]{1,0:T(8,128)(2,1)} %get-tuple-element.44.refs_1_), channel_id=1, source_target_pairs={{0,12},{4,0},{8,4},{12,8},{1,13},{5,1},{9,5},{13,9},{2,14},{6,2},{... | collective-permute-start | bytes 1671176 | tf_op jit(solution)/shard_map/ppermute | solution.py:22
  12.3 2.2 %fusion.refs_7_ = bf16[2048,384]{1,0:T(8,128)(2,1)} fusion(s32[2048]{0:T(1024)} %bitcast.44), kind=kLoop, calls=%fused_computation.3 | loop fusion | flops 1572864 | bytes 1581056 | tf_op jit(solution)/shard_map/convert_element_type | solution.py:38
  14.4 1.3 fusion.1.refs_8_
  15.9 11.5 %collective-permute-done.refs_2_ = bf16[272,1024]{1,0:T(8,128)(2,1)S(1)} collective-permute-done((bf16[272,1024]{1,0:T(8,128)(2,1)}, bf16[272,1024]{1,0:T(8,128)(2,1)S(1)}, u32[]{:S(2)}, u32[]{:S(2)}) %collective-permute-start) | collective-permute-done | bytes 557088 | tf_op jit(solution)/shard_map/ppermute | solution.py:22
  27.6 3.0 %collective-permute-start.7 = (bf16[320,512]{1,0:T(8,128)(2,1)S(1)}, bf16[320,512]{1,0:T(8,128)(2,1)S(1)}, u32[]{:S(2)}, u32[]{:S(2)}) collective-permute-start(bf16[320,512]{1,0:T(8,128)(2,1)S(1)} %slice.119), channel_id=1, source_target_pairs={{0,3},{1,0},{2,1},{3,2},{4,7},{5,4},{6,5},{7,6},{8,11},{9,8},{10,9... | collective-permute-start | bytes 983048 | tf_op jit(solution)/shard_map/ppermute | solution.py:22
  31.8 3.6 %collective-permute-done.2.refs_4_ = bf16[128,1024]{1,0:T(8,128)(2,1)S(1)} collective-permute-done((bf16[128,1024]{1,0:T(8,128)(2,1)S(1)}, bf16[128,1024]{1,0:T(8,128)(2,1)S(1)}, u32[]{:S(2)}, u32[]{:S(2)}) %collective-permute-start.2) | collective-permute-done | bytes 262176 | tf_op jit(solution)/shard_map/ppermute | solution.py:22
  35.3 3.0 %collective-permute-done.6.refs_11_ = bf16[256,512]{1,0:T(8,128)(2,1)S(1)} collective-permute-done((bf16[256,512]{1,0:T(8,128)(2,1)S(1)}, bf16[256,512]{1,0:T(8,128)(2,1)S(1)}, u32[]{:S(2)}, u32[]{:S(2)}) %collective-permute-start.6) | collective-permute-done | bytes 262176 | tf_op jit(solution)/shard_map/ppermute | solution.py:22
  38.9 3.1 %collective-permute-done.3.refs_5_ = bf16[144,1024]{1,0:T(8,128)(2,1)S(1)} collective-permute-done((bf16[144,1024]{1,0:T(8,128)(2,1)S(1)}, bf16[144,1024]{1,0:T(8,128)(2,1)S(1)}, u32[]{:S(2)}, u32[]{:S(2)}) %collective-permute-start.3) | collective-permute-done | bytes 294944 | tf_op jit(solution)/shard_map/ppermute | solution.py:22
  42.1 0.9 copy-done.19
  43.1 0.8 copy-done.21
  43.9 11.8 %shard_map.191 = (bf16[256,1024]{1,0:T(8,128)(2,1)}, bf16[1024,1024]{1,0:T(8,128)(2,1)}, bf16[1024,1024]{1,0:T(8,128)(2,1)}, bf16[64,1024]{1,0:T(8,128)(2,1)}, b...) custom-call(s32[4]{0:T(128)} %pad_add_fusion.refs_0_, ...), custom_call_target="tpu_custom_call" | custom-call | flops 2147483648 | bytes 1048576 | tf_op jit(solution)/shard_map/pallas_call | solution.py:88
  55.7 7.4 %all-to-all-start = ((bf16[16,16,1024]{2,1,0:T(8,128)(2,1)}), bf16[16,16,1024]{2,1,0:T(8,128)(2,1)S(1)}, u32[]{:S(2)}, u32[]{:S(2)}) async-start(bf16[16,16,1024]{2,1,0:T(8,128)(2,1)} %bitcast.33), calls=%async_computation | async-start | bytes 1048576 | tf_op jit(solution)/shard_map/all_to_all | solution.py:641
  63.1 1.2 fusion.2.refs_9_
  64.3 1.9 collective-permute-start.15
  66.2 3.4 %collective-permute-start.16 = (bf16[80,1024]{1,0:T(8,128)(2,1)S(1)}, bf16[80,1024]{1,0:T(8,128)(2,1)S(1)}, u32[]{:S(2)}, u32[]{:S(2)}) collective-permute-start(bf16[80,1024]{1,0:T(8,128)(2,1)S(1)} %get-tuple-element.54), channel_id=1, source_target_pairs={{0,15},{1,0},{2,1},{3,2},{4,3},{5,4},{6,5},{7,6},{8,7},{9,8},{10,9... | collective-permute-start | bytes 491528 | tf_op jit(solution)/shard_map/ppermute | solution.py:22
  69.6 1.9 collective-permute-start.12
  71.6 2.2 %collective-permute-start.14 = (bf16[16,1024]{1,0:T(8,128)(2,1)S(1)}, bf16[16,1024]{1,0:T(8,128)(2,1)S(1)}, u32[]{:S(2)}, u32[]{:S(2)}) collective-permute-start(bf16[16,1024]{1,0:T(8,128)(2,1)S(1)} %copy-done.28), channel_id=1, source_target_pairs={{0,8},{4,12},{8,0},{12,4},{1,9},{5,13},{9,1},{13,5},{2,10},{6,14},... | collective-permute-start | bytes 98312 | tf_op jit(solution)/shard_map/ppermute | solution.py:22
  73.9 0.6 fusion.14.refs_2_
  74.5 1.9 collective-permute-done.12.refs_4_
  77.2 0.7 collective-permute-done.15.refs_14_
  78.0 0.6 copy-done.26
  78.8 20.3 %shard_map.192 = (bf16[64,1024]{1,0:T(8,128)(2,1)}, bf16[16,1024]{1,0:T(8,128)(2,1)}, bf16[256,1024]{1,0:T(8,128)(2,1)}, bf16[256,1024]{1,0:T(8,128)(2,1)}, bf16...) custom-call(s32[4]{0:T(128)} %pad_add_fusion.refs_0_, bf16[256,1024]{1,0:T(8,128)(2,1)} %bitcast.34, ...), custom_call_target="tpu_custom_call" | custom-call | flops 6000000000 | bytes 1048576 | tf_op jit(solution)/shard_map/pallas_call | solution.py:88
  99.1 1.8 broadcast_in_dim.48
  100.9 3.9 %all-to-all-start.1 = ((bf16[16,16,1024]{2,1,0:T(8,128)(2,1)}), bf16[16,16,1024]{2,1,0:T(8,128)(2,1)S(1)}, u32[]{:S(2)}, u32[]{:S(2)}) async-start(bf16[16,16,1024]{2,1,0:T(8,128)(2,1)} %bitcast.13), calls=%async_computation.1 | async-start | bytes 1048576 | tf_op jit(solution)/shard_map/all_to_all | solution.py:680
  104.9 1.9 collective-permute-start.17
  106.8 1.4 collective-permute-start.18
  108.2 2.2 %collective-permute-start.19 = (bf16[16,1024]{1,0:T(8,128)(2,1)}, bf16[16,1024]{1,0:T(8,128)(2,1)S(1)}, u32[]{:S(2)}, u32[]{:S(2)}) collective-permute-start(bf16[16,1024]{1,0:T(8,128)(2,1)} %get-tuple-element.66.refs_9_), channel_id=1, source_target_pairs={{0,8},{4,12},{8,0},{12,4},{1,9},{5,13},{9,1},{13,5},{2,10},{6,14},... | collective-permute-start | bytes 98312 | tf_op jit(solution)/shard_map/ppermute | solution.py:22
  110.3 3.1 %collective-permute-done.17.refs_10_ = bf16[16,1024]{1,0:T(8,128)(2,1)S(1)} collective-permute-done((bf16[16,1024]{1,0:T(8,128)(2,1)}, bf16[16,1024]{1,0:T(8,128)(2,1)S(1)}, u32[]{:S(2)}, u32[]{:S(2)}) %collective-permute-start.17) | collective-permute-done | bytes 32800 | tf_op jit(solution)/shard_map/ppermute | solution.py:22
  113.4 0.6 collective-permute-done.19.refs_12_
  114.0 6.3 %shard_map.195 = (bf16[4,16,16,1024]{3,2,1,0:T(8,128)(2,1)}, bf16[4,16,16,1024]{3,2,1,0:T(8,128)(2,1)}) custom-call(s32[4]{0:T(128)} %pad_add_fusion.refs_0_, bf16[256,1024]{1,0:T(8,128)(2,1)} %get-tuple-element.77.refs_1_, bf16[256,1024]{1,0:T(8,128)(2,1)} %get-tuple-element.78.refs_2_, bf16[256,1024]{1,0:T(8,128)(2,1)} %get-tuple-element.79.refs_3_), custom_call_target="tpu_custom_call" | custom-call | flops 1000000000 | bytes 1048576 | tf_op jit(solution)/shard_map/pallas_call | solution.py:88
  120.4 3.9 %copy.22 = bf16[1024,1024]{0,1:T(8,128)(2,1)} copy(bf16[1024,1024]{1,0:T(8,128)(2,1)} %get-tuple-element.62) | data formatting | bytes 4194304 | tf_op jit(solution)/shard_map/pallas_call | solution.py:88
  124.4 0.8 copy-done.3
  125.1 12.5 %shard_map.193 = (bf16[4,4,48,1024]{3,2,1,0:T(8,128)(2,1)}, bf16[4,4,48,1024]{3,2,1,0:T(8,128)(2,1)}, bf16[4,4,32,1024]{3,2,1,0:T(8,128)(2,1)}, bf16[4,4,32,1024]{3,2,1,0:T(8,128)(2,1)}) custom-call(s32[4]{0:T(128)} %pad_add_fusion.refs_0_, bf16[256,1024]{1,0:T(8,128)(2,1)} %bitcast.35, bf16[64,256]{1,0:T(8,128)(2,1)} %get-tuple-element.57.refs_2_, ...), custom_call_target="tpu_custom_call" | custom-call | flops 2147483648 | bytes 1048576 | tf_op jit(solution)/shard_map/pallas_call | solution.py:88
  138.3 3.0 %collective-permute-done.20 = bf16[4,4,32,1024]{3,2,1,0:T(8,128)(2,1)S(1)} collective-permute-done((bf16[4,4,32,1024]{3,2,1,0:T(8,128)(2,1)}, bf16[4,4,32,1024]{3,2,1,0:T(8,128)(2,1)S(1)}, u32[]{:S(2)}, u32[]{:S(2)}) %collective-permute-start.20) | collective-permute-done | bytes 1048608 | tf_op jit(solution)/shard_map/ppermute | solution.py:22
  141.3 1.8 add_convert_fusion.2
  143.0 0.9 fusion.20
  143.9 4.0 %collective-permute-start.21 = (bf16[128,1024]{1,0:T(8,128)(2,1)}, bf16[128,1024]{1,0:T(8,128)(2,1)S(1)}, u32[]{:S(2)}, u32[]{:S(2)}) collective-permute-start(bf16[128,1024]{1,0:T(8,128)(2,1)} %bitcast.17), channel_id=1, source_target_pairs={{0,96},{32,0},{64,32},{96,64},{1,97},{33,1},{65,33},{97,65},{2,98}... | collective-permute-start | bytes 786440 | tf_op jit(solution)/shard_map/ppermute | solution.py:22
  148.0 1.9 collective-permute-start.23
  149.9 2.3 %add_convert_fusion = bf16[4,16,16,1024]{3,2,1,0:T(8,128)(2,1)} fusion(bf16[4,16,16,1024]{3,2,1,0:T(8,128)(2,1)S(1)} %collective-permute-done.41, bf16[4,16,16,1024]{3,2,1,0:T(8,128)(2,1)S(1)} %copy-done), kind=kLoop, calls=%fused_computation | loop fusion | flops 4194304 | bytes 6291456 | tf_op jit(solution)/shard_map/convert_element_type | solution.py:689
  152.1 3.6 %all-to-all-start.2 = ((bf16[4,16,16,1024]{3,2,1,0:T(8,128)(2,1)}), bf16[4,16,16,1024]{3,2,1,0:T(8,128)(2,1)S(1)}, u32[]{:S(2)}, u32[]{:S(2)}) async-start(bf16[4,16,16,1024]{3,2,1,0:T(8,128)(2,1)} %add_convert_fusion), calls=%async_computation.2 | async-start | bytes 4194304 | tf_op jit(solution)/shard_map/all_to_all | solution.py:690
  155.8 2.6 %add_convert_fusion.1 = bf16[4,4,48,1024]{3,2,1,0:T(8,128)(2,1)S(1)} fusion(bf16[4,4,48,1024]{3,2,1,0:T(8,128)(2,1)} %collective-permute-done.27, bf16[4,4,48,1024]{3,2,1,0:T(8,128)(2,1)} %get-tuple-element.72), kind=kLoop, calls=%fused_computation.1 | loop fusion | flops 3145728 | bytes 4718592 | tf_op jit(solution)/shard_map/convert_element_type | solution.py:707
  158.5 2.9 %collective-permute-start.28 = (bf16[192,1024]{1,0:T(8,128)(2,1)S(1)}, bf16[192,1024]{1,0:T(8,128)(2,1)S(1)}, u32[]{:S(2)}, u32[]{:S(2)}) collective-permute-start(bf16[192,1024]{1,0:T(8,128)(2,1)S(1)} %bitcast.39), channel_id=1, source_target_pairs={{0,3},{1,0},{2,1},{3,2},{4,7},{5,4},{6,5},{7,6},{8,11},{9,8},{10,9... | collective-permute-start | bytes 1179656 | tf_op jit(solution)/shard_map/ppermute | solution.py:22
  161.4 2.3 %collective-permute-start.30 = (bf16[192,1024]{1,0:T(8,128)(2,1)S(1)}, bf16[192,1024]{1,0:T(8,128)(2,1)S(1)}, u32[]{:S(2)}, u32[]{:S(2)}) collective-permute-start(bf16[192,1024]{1,0:T(8,128)(2,1)S(1)} %bitcast.37), channel_id=1, source_target_pairs={{0,2},{1,3},{2,0},{3,1},{4,6},{5,7},{6,4},{7,5},{8,10},{9,11},{10,... | collective-permute-start | bytes 1179656 | tf_op jit(solution)/shard_map/ppermute | solution.py:22
  164.0 2.5 %collective-permute-start.24 = (bf16[32,1024]{1,0:T(8,128)(2,1)S(1)}, bf16[32,1024]{1,0:T(8,128)(2,1)S(1)}, u32[]{:S(2)}, u32[]{:S(2)}) collective-permute-start(bf16[32,1024]{1,0:T(8,128)(2,1)S(1)} %get-tuple-element.93), channel_id=1, source_target_pairs={{0,3},{1,0},{2,1},{3,2},{4,7},{5,4},{6,5},{7,6},{8,11},{9,8},{10,9... | collective-permute-start | bytes 196616 | tf_op jit(solution)/shard_map/ppermute | solution.py:22
  166.5 12.9 %collective-permute-done.28 = bf16[192,1024]{1,0:T(8,128)(2,1)S(1)} collective-permute-done((bf16[192,1024]{1,0:T(8,128)(2,1)S(1)}, bf16[192,1024]{1,0:T(8,128)(2,1)S(1)}, u32[]{:S(2)}, u32[]{:S(2)}) %collective-permute-start.28) | collective-permute-done | bytes 393248 | tf_op jit(solution)/shard_map/ppermute | solution.py:22
  179.3 3.4 %collective-permute-done.29 = bf16[192,1024]{1,0:T(8,128)(2,1)S(1)} collective-permute-done((bf16[192,1024]{1,0:T(8,128)(2,1)S(1)}, bf16[192,1024]{1,0:T(8,128)(2,1)S(1)}, u32[]{:S(2)}, u32[]{:S(2)}) %collective-permute-start.29) | collective-permute-done | bytes 393248 | tf_op jit(solution)/shard_map/ppermute | solution.py:22
  183.1 1.7 collective-permute-start.31
  184.8 0.7 collective-permute-start.32
  185.5 2.0 collective-permute-start.33
  187.5 1.3 reduce_sum.31
  188.9 4.6 %all-to-all-start.3 = ((bf16[16,16,1024]{2,1,0:T(8,128)(2,1)}), bf16[16,16,1024]{2,1,0:T(8,128)(2,1)S(1)}, u32[]{:S(2)}, u32[]{:S(2)}) async-start(bf16[16,16,1024]{2,1,0:T(8,128)(2,1)} %reduce_sum.31), calls=%async_computation.3 | async-start | bytes 1048576 | tf_op jit(solution)/shard_map/all_to_all | solution.py:691
  193.6 2.0 collective-permute-start.34
  195.6 1.3 collective-permute-start.35
  196.9 2.2 %collective-permute-start.36 = (bf16[80,1024]{1,0:T(8,128)(2,1)S(1)}, bf16[80,1024]{1,0:T(8,128)(2,1)S(1)}, u32[]{:S(2)}, u32[]{:S(2)}) collective-permute-start(bf16[80,1024]{1,0:T(8,128)(2,1)S(1)} %pad_maximum_fusion.refs_1_), channel_id=1, source_target_pairs={{0,64},{32,96},{64,0},{96,32},{1,65},{33,97},{65,1},{97,33},{2,66}... | collective-permute-start | bytes 491528 | tf_op jit(solution)/shard_map/ppermute | solution.py:22
  199.1 5.2 %collective-permute-done.34.refs_2_ = bf16[80,1024]{1,0:T(8,128)(2,1)S(1)} collective-permute-done((bf16[80,1024]{1,0:T(8,128)(2,1)S(1)}, bf16[80,1024]{1,0:T(8,128)(2,1)S(1)}, u32[]{:S(2)}, u32[]{:S(2)}) %collective-permute-start.34) | collective-permute-done | bytes 163872 | tf_op jit(solution)/shard_map/ppermute | solution.py:22
  204.8 1.2 collective-permute-done.36.refs_4_
  206.1 1.3 collective-permute-done.40.refs_8_
  207.5 0.6 copy-done.12
  208.1 3.7 %shard_map.194 = (f32[1024,256]{1,0:T(8,128)}, f32[256,1024]{1,0:T(8,128)}, f32[52,1024]{1,0:T(8,128)}) custom-call(s32[4]{0:T(128)} %pad_add_fusion.refs_0_, bf16[80,1024]{1,0:T(8,128)(2,1)} %copy-done.1, bf16[80,1024]{1,0:T(8,128)(2,1)} %copy-done.6, bf16[80,1024]{1,0:T(8,128)(2,1)} %copy-done.7, bf16[80,1024]{1,0:T(8,128)(2,1)} %copy-done.8, ...), custom_call_target="tpu_custom_call" | custom-call | bytes 1048576 | tf_op jit(solution)/shard_map/pallas_call | solution.py:88
  211.9 0.6 fusion.24
  (149 shorter events, 5.4 us)
Async XLA Ops:
  0.6 13.8 %copy-start.16 = (s32[1,2048]{1,0:T(1,128)S(1)}, s32[1,2048]{1,0:T(1,128)}, u32[]{:S(2)}) copy-start(s32[1,2048]{1,0:T(1,128)} %param.24) | copy-start | bytes 24580
  2.8 12.9 %copy-start.17 = (s32[1,128]{1,0:T(1,128)S(1)}, s32[1,128]{1,0:T(1,128)}, u32[]{:S(2)}) copy-start(s32[1,128]{1,0:T(1,128)} %param.22) | copy-start | bytes 1540
  2.8 12.9 %copy-start.37 = (s32[1,16]{1,0:T(1,128)S(1)}, s32[1,16]{1,0:T(1,128)}, u32[]{:S(2)}) copy-start(s32[1,16]{1,0:T(1,128)} %param.20) | copy-start | bytes 196
  6.3 21.3 %collective-permute-start.5 = (bf16[576,512]{1,0:T(8,128)(2,1)}, bf16[576,512]{1,0:T(8,128)(2,1)S(1)}, u32[]{:S(2)}, u32[]{:S(2)}) collective-permute-start(bf16[576,512]{1,0:T(8,128)(2,1)} %get-tuple-element.45), channel_id=1, source_target_pairs={{0,3},{1,0},{2,1},{3,2},{4,7},{5,4},{6,5},{7,6},{8,11},{9,8},{10,9... | collective-permute-start | bytes 1769480 | tf_op jit(solution)/shard_map/ppermute | solution.py:22
  9.5 21.2 %collective-permute-start.4 = (bf16[576,512]{1,0:T(8,128)(2,1)}, bf16[576,512]{1,0:T(8,128)(2,1)S(1)}, u32[]{:S(2)}, u32[]{:S(2)}) collective-permute-start(bf16[576,512]{1,0:T(8,128)(2,1)} %get-tuple-element.45), channel_id=1, source_target_pairs={{0,1},{1,2},{2,3},{3,0},{4,5},{5,6},{6,7},{7,4},{8,9},{9,10},{10,1... | collective-permute-start | bytes 1769480 | tf_op jit(solution)/shard_map/ppermute | solution.py:22
  9.5 21.5 %collective-permute-start.1 = (bf16[272,1024]{1,0:T(8,128)(2,1)}, bf16[272,1024]{1,0:T(8,128)(2,1)S(1)}, u32[]{:S(2)}, u32[]{:S(2)}) collective-permute-start(bf16[272,1024]{1,0:T(8,128)(2,1)} %get-tuple-element.44.refs_1_), channel_id=1, source_target_pairs={{0,12},{4,0},{8,4},{12,8},{1,13},{5,1},{9,5},{13,9},{2,14},{6,2},{... | collective-permute-start | bytes 1671176 | tf_op jit(solution)/shard_map/ppermute | solution.py:22
  12.3 15.2 %collective-permute-start = (bf16[272,1024]{1,0:T(8,128)(2,1)}, bf16[272,1024]{1,0:T(8,128)(2,1)S(1)}, u32[]{:S(2)}, u32[]{:S(2)}) collective-permute-start(bf16[272,1024]{1,0:T(8,128)(2,1)} %get-tuple-element.44.refs_1_), channel_id=1, source_target_pairs={{0,4},{4,8},{8,12},{12,0},{1,5},{5,9},{9,13},{13,1},{2,6},{6,10},{... | collective-permute-start | bytes 1671176 | tf_op jit(solution)/shard_map/ppermute | solution.py:22
  12.3 19.2 %copy-start.4 = (bf16[240,1024]{1,0:T(8,128)(2,1)S(1)}, bf16[240,1024]{1,0:T(8,128)(2,1)}, u32[]{:S(2)}) copy-start(bf16[240,1024]{1,0:T(8,128)(2,1)} %refs_13_.1) | copy-start | bytes 1474564
  27.5 11.4 %copy-start.14 = (bf16[272,1024]{1,0:T(8,128)(2,1)}, bf16[272,1024]{1,0:T(8,128)(2,1)S(1)}, u32[]{:S(2)}) copy-start(bf16[272,1024]{1,0:T(8,128)(2,1)S(1)} %collective-permute-done.refs_2_) | copy-start | bytes 1671172
  27.5 7.8 %collective-permute-start.2 = (bf16[128,1024]{1,0:T(8,128)(2,1)S(1)}, bf16[128,1024]{1,0:T(8,128)(2,1)S(1)}, u32[]{:S(2)}, u32[]{:S(2)}) collective-permute-start(bf16[128,1024]{1,0:T(8,128)(2,1)S(1)} %slice.116), channel_id=1, source_target_pairs={{0,4},{4,8},{8,12},{12,0},{1,5},{5,9},{9,13},{13,1},{2,6},{6,10},{... | collective-permute-start | bytes 786440 | tf_op jit(solution)/shard_map/ppermute | solution.py:22
  27.6 16.2 %copy-start.5 = (bf16[576,512]{1,0:T(8,128)(2,1)}, bf16[576,512]{1,0:T(8,128)(2,1)S(1)}, u32[]{:S(2)}) copy-start(bf16[576,512]{1,0:T(8,128)(2,1)S(1)} %collective-permute-done.5.refs_10_) | copy-start | bytes 1769476
  27.6 10.7 %collective-permute-start.7 = (bf16[320,512]{1,0:T(8,128)(2,1)S(1)}, bf16[320,512]{1,0:T(8,128)(2,1)S(1)}, u32[]{:S(2)}, u32[]{:S(2)}) collective-permute-start(bf16[320,512]{1,0:T(8,128)(2,1)S(1)} %slice.119), channel_id=1, source_target_pairs={{0,3},{1,0},{2,1},{3,2},{4,7},{5,4},{6,5},{7,6},{8,11},{9,8},{10,9... | collective-permute-start | bytes 983048 | tf_op jit(solution)/shard_map/ppermute | solution.py:22
  30.7 13.2 %copy-start.15 = (bf16[576,512]{1,0:T(8,128)(2,1)}, bf16[576,512]{1,0:T(8,128)(2,1)S(1)}, u32[]{:S(2)}) copy-start(bf16[576,512]{1,0:T(8,128)(2,1)S(1)} %collective-permute-done.4.refs_9_) | copy-start | bytes 1769476
  30.7 7.7 %collective-permute-start.6 = (bf16[256,512]{1,0:T(8,128)(2,1)S(1)}, bf16[256,512]{1,0:T(8,128)(2,1)S(1)}, u32[]{:S(2)}, u32[]{:S(2)}) collective-permute-start(bf16[256,512]{1,0:T(8,128)(2,1)S(1)} %slice.118), channel_id=1, source_target_pairs={{0,1},{1,2},{2,3},{3,0},{4,5},{5,6},{6,7},{7,4},{8,9},{9,10},{10,1... | collective-permute-start | bytes 786440 | tf_op jit(solution)/shard_map/ppermute | solution.py:22
  30.9 11.2 %collective-permute-start.8 = (bf16[576,512]{1,0:T(8,128)(2,1)S(1)}, bf16[576,512]{1,0:T(8,128)(2,1)S(1)}, u32[]{:S(2)}, u32[]{:S(2)}) collective-permute-start(bf16[576,512]{1,0:T(8,128)(2,1)S(1)} %collective-permute-done.4.refs_9_), channel_id=1, source_target_pairs={{0,16},{16,0},{1,17},{17,1},{2,18},{18,2},{3,19},{19,3},{4,20},{20... | collective-permute-start | bytes 1769480 | tf_op jit(solution)/shard_map/ppermute | solution.py:22
  31.0 12.9 %copy-start.13 = (bf16[272,1024]{1,0:T(8,128)(2,1)}, bf16[272,1024]{1,0:T(8,128)(2,1)S(1)}, u32[]{:S(2)}) copy-start(bf16[272,1024]{1,0:T(8,128)(2,1)S(1)} %collective-permute-done.1.refs_3_) | copy-start | bytes 1671172
  31.0 11.1 %collective-permute-start.9 = (bf16[576,512]{1,0:T(8,128)(2,1)S(1)}, bf16[576,512]{1,0:T(8,128)(2,1)S(1)}, u32[]{:S(2)}, u32[]{:S(2)}) collective-permute-start(bf16[576,512]{1,0:T(8,128)(2,1)S(1)} %collective-permute-done.5.refs_10_), channel_id=1, source_target_pairs={{0,16},{16,0},{1,17},{17,1},{2,18},{18,2},{3,19},{19,3},{4,20},{20... | collective-permute-start | bytes 1769480 | tf_op jit(solution)/shard_map/ppermute | solution.py:22
  35.3 7.6 %copy-start.23 = (bf16[128,1024]{1,0:T(8,128)(2,1)}, bf16[128,1024]{1,0:T(8,128)(2,1)S(1)}, u32[]{:S(2)}) copy-start(bf16[128,1024]{1,0:T(8,128)(2,1)S(1)} %collective-permute-done.2.refs_4_) | copy-start | bytes 786436
  35.3 6.7 %collective-permute-start.3 = (bf16[144,1024]{1,0:T(8,128)(2,1)S(1)}, bf16[144,1024]{1,0:T(8,128)(2,1)S(1)}, u32[]{:S(2)}, u32[]{:S(2)}) collective-permute-start(bf16[144,1024]{1,0:T(8,128)(2,1)S(1)} %slice.117), channel_id=1, source_target_pairs={{0,12},{4,0},{8,4},{12,8},{1,13},{5,1},{9,5},{13,9},{2,14},{6,2},{... | collective-permute-start | bytes 884744 | tf_op jit(solution)/shard_map/ppermute | solution.py:22
  38.3 3.7 %collective-permute-start.10 = (bf16[256,512]{1,0:T(8,128)(2,1)S(1)}, bf16[256,512]{1,0:T(8,128)(2,1)S(1)}, u32[]{:S(2)}, u32[]{:S(2)}) collective-permute-start(bf16[256,512]{1,0:T(8,128)(2,1)S(1)} %collective-permute-done.6.refs_11_), channel_id=1, source_target_pairs={{0,16},{16,0},{1,17},{17,1},{2,18},{18,2},{3,19},{19,3},{4,20},{20... | collective-permute-start | bytes 786440 | tf_op jit(solution)/shard_map/ppermute | solution.py:22
  38.3 5.5 %copy-start.20 = (bf16[320,512]{1,0:T(8,128)(2,1)}, bf16[320,512]{1,0:T(8,128)(2,1)S(1)}, u32[]{:S(2)}) copy-start(bf16[320,512]{1,0:T(8,128)(2,1)S(1)} %collective-permute-done.7.refs_12_) | copy-start | bytes 983044
  38.4 4.6 %collective-permute-start.11 = (bf16[320,512]{1,0:T(8,128)(2,1)S(1)}, bf16[320,512]{1,0:T(8,128)(2,1)S(1)}, u32[]{:S(2)}, u32[]{:S(2)}) collective-permute-start(bf16[320,512]{1,0:T(8,128)(2,1)S(1)} %collective-permute-done.7.refs_12_), channel_id=1, source_target_pairs={{0,16},{16,0},{1,17},{17,1},{2,18},{18,2},{3,19},{19,3},{4,20},{20... | collective-permute-start | bytes 983048 | tf_op jit(solution)/shard_map/ppermute | solution.py:22
  55.7 14.0 %copy-start.30 = (bf16[16,1024]{1,0:T(8,128)(2,1)S(1)}, bf16[16,1024]{1,0:T(8,128)(2,1)}, u32[]{:S(2)}) copy-start(bf16[16,1024]{1,0:T(8,128)(2,1)} %get-tuple-element.50) | copy-start | bytes 98308
  55.7 15.9 %copy-start.29 = (bf16[16,1024]{1,0:T(8,128)(2,1)S(1)}, bf16[16,1024]{1,0:T(8,128)(2,1)}, u32[]{:S(2)}) copy-start(bf16[16,1024]{1,0:T(8,128)(2,1)} %get-tuple-element.51) | copy-start | bytes 98308
  55.7 16.0 %copy-start.28 = (bf16[16,1024]{1,0:T(8,128)(2,1)S(1)}, bf16[16,1024]{1,0:T(8,128)(2,1)}, u32[]{:S(2)}) copy-start(bf16[16,1024]{1,0:T(8,128)(2,1)} %get-tuple-element.52) | copy-start | bytes 98308
  55.7 22.2 %all-to-all-start = ((bf16[16,16,1024]{2,1,0:T(8,128)(2,1)}), bf16[16,16,1024]{2,1,0:T(8,128)(2,1)S(1)}, u32[]{:S(2)}, u32[]{:S(2)}) async-start(bf16[16,16,1024]{2,1,0:T(8,128)(2,1)} %bitcast.33), calls=%async_computation | async-start | bytes 1048576 | tf_op jit(solution)/shard_map/all_to_all | solution.py:641
  64.3 13.7 %collective-permute-start.15 = (bf16[80,1024]{1,0:T(8,128)(2,1)S(1)}, bf16[80,1024]{1,0:T(8,128)(2,1)S(1)}, u32[]{:S(2)}, u32[]{:S(2)}) collective-permute-start(bf16[80,1024]{1,0:T(8,128)(2,1)S(1)} %get-tuple-element.53), channel_id=1, source_target_pairs={{0,1},{1,2},{2,3},{3,4},{4,5},{5,6},{6,7},{7,8},{8,9},{9,10},{10,1... | collective-permute-start | bytes 491528 | tf_op jit(solution)/shard_map/ppermute | solution.py:22
  66.2 11.7 %collective-permute-start.16 = (bf16[80,1024]{1,0:T(8,128)(2,1)S(1)}, bf16[80,1024]{1,0:T(8,128)(2,1)S(1)}, u32[]{:S(2)}, u32[]{:S(2)}) collective-permute-start(bf16[80,1024]{1,0:T(8,128)(2,1)S(1)} %get-tuple-element.54), channel_id=1, source_target_pairs={{0,15},{1,0},{2,1},{3,2},{4,3},{5,4},{6,5},{7,6},{8,7},{9,8},{10,9... | collective-permute-start | bytes 491528 | tf_op jit(solution)/shard_map/ppermute | solution.py:22
  69.6 6.8 %collective-permute-start.12 = (bf16[16,1024]{1,0:T(8,128)(2,1)S(1)}, bf16[16,1024]{1,0:T(8,128)(2,1)S(1)}, u32[]{:S(2)}, u32[]{:S(2)}) collective-permute-start(bf16[16,1024]{1,0:T(8,128)(2,1)S(1)} %copy-done.30), channel_id=1, source_target_pairs={{0,12},{4,0},{8,4},{12,8},{1,13},{5,1},{9,5},{13,9},{2,14},{6,2},{... | collective-permute-start | bytes 98312 | tf_op jit(solution)/shard_map/ppermute | solution.py:22
  71.5 5.1 %collective-permute-start.13 = (bf16[16,1024]{1,0:T(8,128)(2,1)S(1)}, bf16[16,1024]{1,0:T(8,128)(2,1)S(1)}, u32[]{:S(2)}, u32[]{:S(2)}) collective-permute-start(bf16[16,1024]{1,0:T(8,128)(2,1)S(1)} %copy-done.29), channel_id=1, source_target_pairs={{0,4},{4,8},{8,12},{12,0},{1,5},{5,9},{9,13},{13,1},{2,6},{6,10},{... | collective-permute-start | bytes 98312 | tf_op jit(solution)/shard_map/ppermute | solution.py:22
  71.6 5.6 %collective-permute-start.14 = (bf16[16,1024]{1,0:T(8,128)(2,1)S(1)}, bf16[16,1024]{1,0:T(8,128)(2,1)S(1)}, u32[]{:S(2)}, u32[]{:S(2)}) collective-permute-start(bf16[16,1024]{1,0:T(8,128)(2,1)S(1)} %copy-done.28), channel_id=1, source_target_pairs={{0,8},{4,12},{8,0},{12,4},{1,9},{5,13},{9,1},{13,5},{2,10},{6,14},... | collective-permute-start | bytes 98312 | tf_op jit(solution)/shard_map/ppermute | solution.py:22
  100.9 23.4 %all-to-all-start.1 = ((bf16[16,16,1024]{2,1,0:T(8,128)(2,1)}), bf16[16,16,1024]{2,1,0:T(8,128)(2,1)S(1)}, u32[]{:S(2)}, u32[]{:S(2)}) async-start(bf16[16,16,1024]{2,1,0:T(8,128)(2,1)} %bitcast.13), calls=%async_computation.1 | async-start | bytes 1048576 | tf_op jit(solution)/shard_map/all_to_all | solution.py:680
  104.9 8.5 %collective-permute-start.17 = (bf16[16,1024]{1,0:T(8,128)(2,1)}, bf16[16,1024]{1,0:T(8,128)(2,1)S(1)}, u32[]{:S(2)}, u32[]{:S(2)}) collective-permute-start(bf16[16,1024]{1,0:T(8,128)(2,1)} %get-tuple-element.66.refs_9_), channel_id=1, source_target_pairs={{0,4},{4,8},{8,12},{12,0},{1,5},{5,9},{9,13},{13,1},{2,6},{6,10},{... | collective-permute-start | bytes 98312 | tf_op jit(solution)/shard_map/ppermute | solution.py:22
  106.8 6.6 %collective-permute-start.18 = (bf16[16,1024]{1,0:T(8,128)(2,1)}, bf16[16,1024]{1,0:T(8,128)(2,1)S(1)}, u32[]{:S(2)}, u32[]{:S(2)}) collective-permute-start(bf16[16,1024]{1,0:T(8,128)(2,1)} %get-tuple-element.66.refs_9_), channel_id=1, source_target_pairs={{0,12},{4,0},{8,4},{12,8},{1,13},{5,1},{9,5},{13,9},{2,14},{6,2},{... | collective-permute-start | bytes 98312 | tf_op jit(solution)/shard_map/ppermute | solution.py:22
  108.2 5.9 %collective-permute-start.19 = (bf16[16,1024]{1,0:T(8,128)(2,1)}, bf16[16,1024]{1,0:T(8,128)(2,1)S(1)}, u32[]{:S(2)}, u32[]{:S(2)}) collective-permute-start(bf16[16,1024]{1,0:T(8,128)(2,1)} %get-tuple-element.66.refs_9_), channel_id=1, source_target_pairs={{0,8},{4,12},{8,0},{12,4},{1,9},{5,13},{9,1},{13,5},{2,10},{6,14},... | collective-permute-start | bytes 98312 | tf_op jit(solution)/shard_map/ppermute | solution.py:22
  113.4 11.0 %copy-start.32 = (bf16[16,1024]{1,0:T(8,128)(2,1)}, bf16[16,1024]{1,0:T(8,128)(2,1)S(1)}, u32[]{:S(2)}) copy-start(bf16[16,1024]{1,0:T(8,128)(2,1)S(1)} %collective-permute-done.17.refs_10_) | copy-start | bytes 98308
  113.4 11.0 %copy-start.34 = (bf16[16,1024]{1,0:T(8,128)(2,1)}, bf16[16,1024]{1,0:T(8,128)(2,1)S(1)}, u32[]{:S(2)}) copy-start(bf16[16,1024]{1,0:T(8,128)(2,1)S(1)} %collective-permute-done.18.refs_11_) | copy-start | bytes 98308
  114.0 10.3 %copy-start.36 = (bf16[16,1024]{1,0:T(8,128)(2,1)}, bf16[16,1024]{1,0:T(8,128)(2,1)S(1)}, u32[]{:S(2)}) copy-start(bf16[16,1024]{1,0:T(8,128)(2,1)S(1)} %collective-permute-done.19.refs_12_) | copy-start | bytes 98308
  120.3 29.6 %collective-permute-start.41 = (bf16[4,16,16,1024]{3,2,1,0:T(8,128)(2,1)}, bf16[4,16,16,1024]{3,2,1,0:T(8,128)(2,1)S(1)}, u32[]{:S(2)}, u32[]{:S(2)}) collective-permute-start(bf16[4,16,16,1024]{3,2,1,0:T(8,128)(2,1)} %get-tuple-element.81), channel_id=1, source_target_pairs={{0,16},{16,0},{1,17},{17,1},{2,18},{18,2},{3,19},{19,3},{4,20},{20... | collective-permute-start | bytes 6291464 | tf_op jit(solution)/shard_map/ppermute | solution.py:22
  137.6 3.6 %collective-permute-start.20 = (bf16[4,4,32,1024]{3,2,1,0:T(8,128)(2,1)}, bf16[4,4,32,1024]{3,2,1,0:T(8,128)(2,1)S(1)}, u32[]{:S(2)}, u32[]{:S(2)}) collective-permute-start(bf16[4,4,32,1024]{3,2,1,0:T(8,128)(2,1)} %get-tuple-element.71), channel_id=1, source_target_pairs={{0,16},{16,0},{1,17},{17,1},{2,18},{18,2},{3,19},{19,3},{4,20},{20... | collective-permute-start | bytes 3145736 | tf_op jit(solution)/shard_map/ppermute | solution.py:22
  138.2 17.6 %collective-permute-start.27 = (bf16[4,4,48,1024]{3,2,1,0:T(8,128)(2,1)}, bf16[4,4,48,1024]{3,2,1,0:T(8,128)(2,1)}, u32[]{:S(2)}, u32[]{:S(2)}) collective-permute-start(bf16[4,4,48,1024]{3,2,1,0:T(8,128)(2,1)} %get-tuple-element.73), channel_id=1, source_target_pairs={{0,16},{16,0},{1,17},{17,1},{2,18},{18,2},{3,19},{19,3},{4,20},{20... | collective-permute-start | bytes 4718600 | tf_op jit(solution)/shard_map/ppermute | solution.py:22
  141.3 8.6 %copy-start = (bf16[4,16,16,1024]{3,2,1,0:T(8,128)(2,1)S(1)}, bf16[4,16,16,1024]{3,2,1,0:T(8,128)(2,1)}, u32[]{:S(2)}) copy-start(bf16[4,16,16,1024]{3,2,1,0:T(8,128)(2,1)} %get-tuple-element.80) | copy-start | bytes 6291460
  143.9 17.5 %collective-permute-start.21 = (bf16[128,1024]{1,0:T(8,128)(2,1)}, bf16[128,1024]{1,0:T(8,128)(2,1)S(1)}, u32[]{:S(2)}, u32[]{:S(2)}) collective-permute-start(bf16[128,1024]{1,0:T(8,128)(2,1)} %bitcast.17), channel_id=1, source_target_pairs={{0,96},{32,0},{64,32},{96,64},{1,97},{33,1},{65,33},{97,65},{2,98}... | collective-permute-start | bytes 786440 | tf_op jit(solution)/shard_map/ppermute | solution.py:22
  148.0 15.8 %collective-permute-start.22 = (bf16[128,1024]{1,0:T(8,128)(2,1)}, bf16[128,1024]{1,0:T(8,128)(2,1)S(1)}, u32[]{:S(2)}, u32[]{:S(2)}) collective-permute-start(bf16[128,1024]{1,0:T(8,128)(2,1)} %bitcast.18), channel_id=1, source_target_pairs={{0,32},{32,64},{64,96},{96,0},{1,33},{33,65},{65,97},{97,1},{2,34}... | collective-permute-start | bytes 786440 | tf_op jit(solution)/shard_map/ppermute | solution.py:22
  148.0 15.8 %collective-permute-start.23 = (bf16[128,1024]{1,0:T(8,128)(2,1)S(1)}, bf16[128,1024]{1,0:T(8,128)(2,1)S(1)}, u32[]{:S(2)}, u32[]{:S(2)}) collective-permute-start(bf16[128,1024]{1,0:T(8,128)(2,1)S(1)} %bitcast.40), channel_id=1, source_target_pairs={{0,64},{32,96},{64,0},{96,32},{1,65},{33,97},{65,1},{97,33},{2,66}... | collective-permute-start | bytes 786440 | tf_op jit(solution)/shard_map/ppermute | solution.py:22
  152.1 35.4 %all-to-all-start.2 = ((bf16[4,16,16,1024]{3,2,1,0:T(8,128)(2,1)}), bf16[4,16,16,1024]{3,2,1,0:T(8,128)(2,1)S(1)}, u32[]{:S(2)}, u32[]{:S(2)}) async-start(bf16[4,16,16,1024]{3,2,1,0:T(8,128)(2,1)} %add_convert_fusion), calls=%async_computation.2 | async-start | bytes 4194304 | tf_op jit(solution)/shard_map/all_to_all | solution.py:690
  158.5 20.8 %collective-permute-start.28 = (bf16[192,1024]{1,0:T(8,128)(2,1)S(1)}, bf16[192,1024]{1,0:T(8,128)(2,1)S(1)}, u32[]{:S(2)}, u32[]{:S(2)}) collective-permute-start(bf16[192,1024]{1,0:T(8,128)(2,1)S(1)} %bitcast.39), channel_id=1, source_target_pairs={{0,3},{1,0},{2,1},{3,2},{4,7},{5,4},{6,5},{7,6},{8,11},{9,8},{10,9... | collective-permute-start | bytes 1179656 | tf_op jit(solution)/shard_map/ppermute | solution.py:22
  161.4 21.3 %collective-permute-start.29 = (bf16[192,1024]{1,0:T(8,128)(2,1)S(1)}, bf16[192,1024]{1,0:T(8,128)(2,1)S(1)}, u32[]{:S(2)}, u32[]{:S(2)}) collective-permute-start(bf16[192,1024]{1,0:T(8,128)(2,1)S(1)} %bitcast.38), channel_id=1, source_target_pairs={{0,1},{1,2},{2,3},{3,0},{4,5},{5,6},{6,7},{7,4},{8,9},{9,10},{10,1... | collective-permute-start | bytes 1179656 | tf_op jit(solution)/shard_map/ppermute | solution.py:22
  161.4 21.3 %collective-permute-start.30 = (bf16[192,1024]{1,0:T(8,128)(2,1)S(1)}, bf16[192,1024]{1,0:T(8,128)(2,1)S(1)}, u32[]{:S(2)}, u32[]{:S(2)}) collective-permute-start(bf16[192,1024]{1,0:T(8,128)(2,1)S(1)} %bitcast.37), channel_id=1, source_target_pairs={{0,2},{1,3},{2,0},{3,1},{4,6},{5,7},{6,4},{7,5},{8,10},{9,11},{10,... | collective-permute-start | bytes 1179656 | tf_op jit(solution)/shard_map/ppermute | solution.py:22
  164.0 21.5 %collective-permute-start.24 = (bf16[32,1024]{1,0:T(8,128)(2,1)S(1)}, bf16[32,1024]{1,0:T(8,128)(2,1)S(1)}, u32[]{:S(2)}, u32[]{:S(2)}) collective-permute-start(bf16[32,1024]{1,0:T(8,128)(2,1)S(1)} %get-tuple-element.93), channel_id=1, source_target_pairs={{0,3},{1,0},{2,1},{3,2},{4,7},{5,4},{6,5},{7,6},{8,11},{9,8},{10,9... | collective-permute-start | bytes 196616 | tf_op jit(solution)/shard_map/ppermute | solution.py:22
  166.5 21.0 %collective-permute-start.25 = (bf16[32,1024]{1,0:T(8,128)(2,1)S(1)}, bf16[32,1024]{1,0:T(8,128)(2,1)S(1)}, u32[]{:S(2)}, u32[]{:S(2)}) collective-permute-start(bf16[32,1024]{1,0:T(8,128)(2,1)S(1)} %get-tuple-element.95), channel_id=1, source_target_pairs={{0,1},{1,2},{2,3},{3,0},{4,5},{5,6},{6,7},{7,4},{8,9},{9,10},{10,1... | collective-permute-start | bytes 196616 | tf_op jit(solution)/shard_map/ppermute | solution.py:22
  179.3 8.1 %collective-permute-start.26 = (bf16[32,1024]{1,0:T(8,128)(2,1)S(1)}, bf16[32,1024]{1,0:T(8,128)(2,1)S(1)}, u32[]{:S(2)}, u32[]{:S(2)}) collective-permute-start(bf16[32,1024]{1,0:T(8,128)(2,1)S(1)} %get-tuple-element.94), channel_id=1, source_target_pairs={{0,2},{1,3},{2,0},{3,1},{4,6},{5,7},{6,4},{7,5},{8,10},{9,11},{10,... | collective-permute-start | bytes 196616 | tf_op jit(solution)/shard_map/ppermute | solution.py:22
  183.1 10.4 %collective-permute-start.31 = (bf16[48,1024]{1,0:T(8,128)(2,1)S(1)}, bf16[48,1024]{1,0:T(8,128)(2,1)S(1)}, u32[]{:S(2)}, u32[]{:S(2)}) collective-permute-start(bf16[48,1024]{1,0:T(8,128)(2,1)S(1)} %get-tuple-element.90), channel_id=1, source_target_pairs={{0,96},{32,0},{64,32},{96,64},{1,97},{33,1},{65,33},{97,65},{2,98}... | collective-permute-start | bytes 294920 | tf_op jit(solution)/shard_map/ppermute | solution.py:22
  184.8 8.7 %collective-permute-start.32 = (bf16[48,1024]{1,0:T(8,128)(2,1)S(1)}, bf16[48,1024]{1,0:T(8,128)(2,1)S(1)}, u32[]{:S(2)}, u32[]{:S(2)}) collective-permute-start(bf16[48,1024]{1,0:T(8,128)(2,1)S(1)} %get-tuple-element.92), channel_id=1, source_target_pairs={{0,32},{32,64},{64,96},{96,0},{1,33},{33,65},{65,97},{97,1},{2,34}... | collective-permute-start | bytes 294920 | tf_op jit(solution)/shard_map/ppermute | solution.py:22
  185.5 8.0 %collective-permute-start.33 = (bf16[48,1024]{1,0:T(8,128)(2,1)S(1)}, bf16[48,1024]{1,0:T(8,128)(2,1)S(1)}, u32[]{:S(2)}, u32[]{:S(2)}) collective-permute-start(bf16[48,1024]{1,0:T(8,128)(2,1)S(1)} %get-tuple-element.91), channel_id=1, source_target_pairs={{0,64},{32,96},{64,0},{96,32},{1,65},{33,97},{65,1},{97,33},{2,66}... | collective-permute-start | bytes 294920 | tf_op jit(solution)/shard_map/ppermute | solution.py:22
  188.9 23.0 %all-to-all-start.3 = ((bf16[16,16,1024]{2,1,0:T(8,128)(2,1)}), bf16[16,16,1024]{2,1,0:T(8,128)(2,1)S(1)}, u32[]{:S(2)}, u32[]{:S(2)}) async-start(bf16[16,16,1024]{2,1,0:T(8,128)(2,1)} %reduce_sum.31), calls=%async_computation.3 | async-start | bytes 1048576 | tf_op jit(solution)/shard_map/all_to_all | solution.py:691
  193.6 13.9 %copy-start.1 = (bf16[80,1024]{1,0:T(8,128)(2,1)}, bf16[80,1024]{1,0:T(8,128)(2,1)S(1)}, u32[]{:S(2)}) copy-start(bf16[80,1024]{1,0:T(8,128)(2,1)S(1)} %pad_maximum_fusion.refs_1_) | copy-start | bytes 491524
  193.6 10.7 %collective-permute-start.34 = (bf16[80,1024]{1,0:T(8,128)(2,1)S(1)}, bf16[80,1024]{1,0:T(8,128)(2,1)S(1)}, u32[]{:S(2)}, u32[]{:S(2)}) collective-permute-start(bf16[80,1024]{1,0:T(8,128)(2,1)S(1)} %pad_maximum_fusion.refs_1_), channel_id=1, source_target_pairs={{0,32},{32,64},{64,96},{96,0},{1,33},{33,65},{65,97},{97,1},{2,34}... | collective-permute-start | bytes 491528 | tf_op jit(solution)/shard_map/ppermute | solution.py:22
  195.6 8.7 %collective-permute-start.35 = (bf16[80,1024]{1,0:T(8,128)(2,1)S(1)}, bf16[80,1024]{1,0:T(8,128)(2,1)S(1)}, u32[]{:S(2)}, u32[]{:S(2)}) collective-permute-start(bf16[80,1024]{1,0:T(8,128)(2,1)S(1)} %pad_maximum_fusion.refs_1_), channel_id=1, source_target_pairs={{0,96},{32,0},{64,32},{96,64},{1,97},{33,1},{65,33},{97,65},{2,98}... | collective-permute-start | bytes 491528 | tf_op jit(solution)/shard_map/ppermute | solution.py:22
  196.9 9.1 %collective-permute-start.36 = (bf16[80,1024]{1,0:T(8,128)(2,1)S(1)}, bf16[80,1024]{1,0:T(8,128)(2,1)S(1)}, u32[]{:S(2)}, u32[]{:S(2)}) collective-permute-start(bf16[80,1024]{1,0:T(8,128)(2,1)S(1)} %pad_maximum_fusion.refs_1_), channel_id=1, source_target_pairs={{0,64},{32,96},{64,0},{96,32},{1,65},{33,97},{65,1},{97,33},{2,66}... | collective-permute-start | bytes 491528 | tf_op jit(solution)/shard_map/ppermute | solution.py:22
  199.1 6.9 %collective-permute-start.37 = (bf16[80,1024]{1,0:T(8,128)(2,1)S(1)}, bf16[80,1024]{1,0:T(8,128)(2,1)S(1)}, u32[]{:S(2)}, u32[]{:S(2)}) collective-permute-start(bf16[80,1024]{1,0:T(8,128)(2,1)S(1)} %pad_maximum_fusion.refs_1_), channel_id=1, source_target_pairs={{0,16},{16,0},{1,17},{17,1},{2,18},{18,2},{3,19},{19,3},{4,20},{20... | collective-permute-start | bytes 491528 | tf_op jit(solution)/shard_map/ppermute | solution.py:22
  204.3 1.8 collective-permute-start.38
  204.3 1.8 collective-permute-start.39
  206.0 1.4 collective-permute-start.40
  (20 other events, 29.2 us)

commit v5 on v4

--- a/solution.py
+++ b/solution.py
@@ -362,10 +362,11 @@
         def _(k):
             rows = pl.ds(pl.multiple_of(k * 512, 512), 512)
             taken = dot(src_hot_ref[rows, :], ext_ref[:, cols])
-            sources_ref[rows, cols] = taken.astype(BF)
+            taken = taken.astype(BF)
+            sources_ref[rows, cols] = taken
             for i in range(4):
                 few = pl.ds(pl.multiple_of(k * 512 + i * 128, 128), 128)
-                edges_ref[few, cols] = (taken[i * 128 : (i + 1) * 128] * rel_ref[k * 4 + i, :, cols]).astype(BF)
+                edges_ref[few, cols] = taken[i * 128 : (i + 1) * 128] * rel_ref[k * 4 + i, :, cols].astype(BF)
 
     wait_all(second)
 
@@ -405,7 +406,7 @@
             for i in range(4):
                 few = pl.ds(pl.multiple_of(k * 512 + i * 128, 128), 128)
                 part = at_dest[i * 128 : (i + 1) * 128]
-                edges_ref[few, cols] = (part * rel_ref[k * 4 + i, :, cols]).astype(BF)
+                edges_ref[few, cols] = part.astype(BF) * rel_ref[k * 4 + i, :, cols].astype(BF)
                 product = part * sources_ref[few, cols].astype(F32)
                 sums_ref[k * 4 + i, :, cols] = jnp.sum(product, axis=0, keepdims=True)
 
@@ -419,7 +420,8 @@
         grad = dot(src_row_hot_ref[...], edges_ref[:, cols]) + dot_bt(own_pre, w_self_ref[cols, :])
         table_out_ref[:, cols] = grad.astype(BF)
 
-    sent_out.append(copies.start(table_out_ref, table_out_hbm))
+    for x in range(4):
+        sent_out.append(copies.start(table_out_ref, table_out_hbm.at[pl.ds(x * 64, 64), :]))
     wait_all(sent_out)
 
 
@@ -432,6 +434,7 @@
     kept_ref, given_ref,
 ):
     core = where_ref[1]
+    places = ring_places(where_ref[2])
     wait_all(
         [copies.start(aggregate_hbm, aggregate_ref), copies.start(nodes_hbm, nodes_ref), copies.start(pre_hbm, pre_ref)]
     )
@@ -447,84 +450,110 @@
                 for y in range(4):
                     at = (x * 4 + y) * 8
                     both = jnp.concatenate([msg[at : at + 8], own[at : at + 8]], axis=0)
-                    chunk_ref[x, z * 4 + y] = both.astype(BF)
+                    chunk_ref[places[x], z * 4 + y] = both.astype(BF)
 
         sent_out.append(copies.start(chunk_ref, chunk_hbm))
     wait_all(sent_out)
 
 
-def back_kernel(
+def out_kernel(
     copies,
     where_ref,
-    returned_hbm, route_hbm, length_hbm, all_out_hbm, slope_hbm, pooled_hbm, normed_t_hbm,
-    rel_hot_hbm, r0_hbm, r1_hbm, r2_hbm, r3_hbm,
-    out_kept_hbm, out_given_hbm, in_kept_hbm, in_given_hbm,
-    returned_ref, route_ref, length_ref, all_out_ref, slope_ref, pooled_ref, normed_t_ref,
-    rel_hot_ref, r0, r1, r2, r3,
-    out_kept_ref, out_given_ref, in_kept_ref, in_given_ref,
-    scaled_ref, grad_ref,
+    returned_hbm, route_hbm, length_hbm, rel_hot_hbm, pooled_hbm, r0_hbm, r1_hbm, r2_hbm, r3_hbm,
+    given_hbm, kept_hbm, scaled_hbm,
+    returned_ref, route_ref, length_ref, rel_hot_ref, pooled_ref, r0, r1, r2, r3,
+    given_ref, kept_ref, scaled_ref,
 ):
     my_z, core, my_y = where_ref[0], where_ref[1], where_ref[3]
-    first = [
-        copies.start(returned_hbm, returned_ref),
-        copies.start(route_hbm, route_ref),
-        copies.start(length_hbm, length_ref),
-        copies.start(rel_hot_hbm, rel_hot_ref),
-        copies.start(r0_hbm, r0),
-        copies.start(r1_hbm, r1),
-        copies.start(r2_hbm, r2),
-        copies.start(r3_hbm, r3),
-    ]
-    second = [
-        copies.start(all_out_hbm, all_out_ref),
-        copies.start(pooled_hbm, pooled_ref),
-        copies.start(slope_hbm, slope_ref),
-        copies.start(normed_t_hbm, normed_t_ref),
-    ]
-    wait_all(first)
+    wait_all(
+        [
+            copies.start(returned_hbm, returned_ref),
+            copies.start(route_hbm, route_ref),
+            copies.start(length_hbm, length_ref),
+            copies.start(rel_hot_hbm, rel_hot_ref),
+            copies.start(pooled_hbm, pooled_ref),
+            copies.start(r0_hbm, r0),
+            copies.start(r1_hbm, r1),
+            copies.start(r2_hbm, r2),
+            copies.start(r3_hbm, r3),
+        ]
+    )
     scaled_ref[...] = (dot(route_ref[...], returned_ref[...]) * length_ref[:, 0:1]).astype(BF)
+    sent_out = [copies.start(scaled_ref, scaled_hbm)]
     blocks = jnp.concatenate([r0[...], r1[...], r2[...], r3[...]], axis=0)
-    places = []
-    for z in range(4):
-        ahead = lax.rem(z - my_z + 4, 4)
-        places.append(jnp.where(ahead == 0, 0, jnp.where(ahead == 3, 1, ahead + 1)))
-    wait_all(second)
-
-    @pl.loop(0, 4)
-    def _(t):
-        cols = pl.ds(pl.multiple_of(t * 256, 256), 256)
-        origin = jnp.where(t == 0, 0, jnp.where(t == 1, 3, t - 1))
-        owner = lax.rem(my_y + origin, 4)
-        upstream = dot_bt(scaled_ref[...], all_out_ref[cols, :]).astype(BF)
-        for s in range(4):
-            rows = slice(s * 256, (s + 1) * 256)
-            line = lanes((16, 256))
-            length = 1.0 / length_ref[s * 16 : (s + 1) * 16, 0:1]
-            inside = (line // 16 == sublanes((16, 256))) & ((line % 16).astype(F32) + 0.5 < length)
-            pool = inside.astype(F32).astype(BF)
-            at_tokens = dot_t(pool, upstream[s * 16 : (s + 1) * 16])
-            grad_ref[rows, :] = (slope_ref[rows, cols].astype(F32) * at_tokens).astype(BF)
-        for half, out_ref, in_ref in ((1 - core, out_given_ref, in_given_ref), (core, out_kept_ref, in_kept_ref)):
+    places = ring_places(my_z)
+    for half, out_ref, out_hbm in ((1 - core, given_ref, given_hbm), (core, kept_ref, kept_hbm)):
+        for t in range(4):
+            owner = lax.rem(my_y + ORIGINS[t], 4)
             units = pl.ds(pl.multiple_of(t * 256 + half * 128, 128), 128)
             out = dot_t(pooled_ref[:, units], scaled_ref[...]).astype(BF)
             rel_rows = pl.ds(pl.multiple_of(owner * 128 + half * 64, 64), 64)
             rel = dot(rel_hot_ref[rel_rows, :], blocks).astype(BF)
-            inner = dot(normed_t_ref[pl.ds(pl.multiple_of(half * 512, 512), 512), :], grad_ref[...]).astype(BF)
             for z in range(4):
-                out_ref[t, places[z], 0:32, :] = out[z * 32 : (z + 1) * 32]
-                out_ref[t, places[z], 32:48, :] = rel[z * 16 : (z + 1) * 16]
+                out_ref[owner, places[z], 0:32, :] = out[z * 32 : (z + 1) * 32]
+                out_ref[owner, places[z], 32:48, :] = rel[z * 16 : (z + 1) * 16]
+        sent_out.append(copies.start(out_ref, out_hbm))
+    wait_all(sent_out)
+
+
+def ring_places(mine):
+    places = []
+    for at in range(4):
+        ahead = lax.rem(at - mine + 4, 4)
+        places.append(jnp.where(ahead == 0, 0, jnp.where(ahead == 3, 1, ahead + 1)))
+    return places
+
+
+def in_kernel(
+    copies,
+    where_ref,
+    scaled_hbm, length_hbm, all_out_hbm, slope_hbm, normed_t_hbm,
+    given_hbm, kept_hbm,
+    scaled_ref, length_ref, all_out_ref, slope_ref, normed_t_ref,
+    given_ref, kept_ref,
+    grad_ref,
+):
+    my_z, core = where_ref[0], where_ref[1]
+    wait_first = [
+        copies.start(scaled_hbm, scaled_ref),
+        copies.start(length_hbm, length_ref),
+        copies.start(all_out_hbm, all_out_ref),
+        copies.start(slope_hbm, slope_ref),
+    ]
+    wait_next = [copies.start(normed_t_hbm, normed_t_ref)]
+    places = ring_places(my_z)
+    wait_all(wait_first)
+    pools = []
+    for s in range(4):
+        line = lanes((16, 256))
+        length = 1.0 / length_ref[s * 16 : (s + 1) * 16, 0:1]
+        inside = (line // 16 == sublanes((16, 256))) & ((line % 16).astype(F32) + 0.5 < length)
+        pools.append(inside.astype(F32).astype(BF))
+
+    @pl.loop(0, 4)
+    def _(t):
+        cols = pl.ds(pl.multiple_of(t * 256, 256), 256)
+        upstream = dot_bt(scaled_ref[...], all_out_ref[cols, :]).astype(BF)
+        for s in range(4):
+            rows = slice(s * 256, (s + 1) * 256)
+            at_tokens = dot_t(pools[s], upstream[s * 16 : (s + 1) * 16])
+            grad_ref[rows, cols] = (slope_ref[rows, cols].astype(F32) * at_tokens).astype(BF)
+
+    wait_all(wait_next)
+    sent_out = []
+    for half, in_ref, in_hbm in ((1 - core, given_ref, given_hbm), (core, kept_ref, kept_hbm)):
+
+        @pl.loop(0, 4)
+        def _(t):
+            cols = pl.ds(pl.multiple_of(t * 256, 256), 256)
+            inner = dot(normed_t_ref[pl.ds(pl.multiple_of(half * 512, 512), 512), :], grad_ref[:, cols]).astype(BF)
+            for z in range(4):
                 for i in range(4):
                     piece = inner[z * 128 + i * 32 : z * 128 + (i + 1) * 32]
                     in_ref[places[z], t, :, i * 256 : (i + 1) * 256] = piece
 
-    wait_all(
-        [
-            copies.start(out_given_ref, out_given_hbm),
-            copies.start(in_given_ref, in_given_hbm),
-            copies.start(out_kept_ref, out_kept_hbm),
-            copies.start(in_kept_ref, in_kept_hbm),
-        ]
-    )
+        sent_out.append(copies.start(in_ref, in_hbm))
+    wait_all(sent_out)
 
 
 def place_kernel(
@@ -640,9 +669,9 @@
     src_hot = one_hot(src, extended_count)
     arrived = lax.all_to_all(outgoing.reshape(16, 16, width), GROUP, 0, 0, tiled=True).reshape(256, width)
     rel_rows = [asked[0]] + [shift_by(rows, "x", o) for rows, o in zip(asked[1:], ORIGINS[1:])]
-    normed_t = normed.T
-
-    outs = [((64, width), BF), ((block_count, width), BF)] + [((node_count, width), BF)] * 4
+    arrived, normed_t = lax.optimization_barrier((arrived, normed.T))
+
+    outs = [((256, width), BF), ((block_count, width), BF)] + [((node_count, width), BF)] * 4
     operands = [
         arrived,
         one_hot_t(own_row, 64),
@@ -659,7 +688,7 @@
         outs,
         [where, *operands, cache, from_low, from_high],
         like(operands)
-        + filled(outs)
+        + filled([((64, width), BF), *outs[1:]])
         + [
             pltpu.VMEM((extended_count, width), BF),
             pltpu.VMEM((2, 16, 128), BF),
@@ -672,12 +701,11 @@
             pltpu.VMEM((block_count, 1, width), F32),
             pltpu.VMEM((block_count, 1, width), F32),
         ],
-        copies=26,
+        copies=30,
         flops=6 * 10**9,
     )
 
-    back = jnp.broadcast_to(grad_table.reshape(1, 4, 16, width), (4, 4, 16, width))
-    returned = lax.all_to_all(back.reshape(16, 16, width), GROUP, 0, 0, tiled=True).reshape(256, width)
+    returned = lax.all_to_all(grad_table.reshape(16, 16, width), GROUP, 0, 0, tiled=True).reshape(256, width)
     rel_blocks = [grad_blocks] + [shift_by(grad_blocks, "x", s) for s in SHIFTS]
 
     outs = [((4, 16, 16, width), BF)] * 2
@@ -687,26 +715,30 @@
         weight_kernel, outs, [where, *operands], like(operands) + filled(outs), flops=10**9
     )
     chip = (graph_kept.astype(F32) + shift_by(graph_given, "core", 1).astype(F32)).astype(BF)
-    line = lax.all_to_all(chip, "x", 0, 0, tiled=True)
-    plane = lax.all_to_all(jnp.sum(line.astype(F32), axis=0).astype(BF), ("z", "y"), 0, 0, tiled=True)
+    outs = [((4, 4, 48, width), BF)] * 2 + [((4 * entities, width), BF)]
+    operands = [returned, route, inverse, rel_hot, pooled, *rel_blocks]
+    out_given, out_kept, scaled = local_call(
+        out_kernel, outs, [where, *operands], like(operands) + filled(outs), copies=12, flops=10**9
+    )
+    out_chip = (out_kept.astype(F32) + shift_by(out_given, "core", 1).astype(F32)).astype(BF)
+    scaled, out_chip, chip = lax.optimization_barrier((scaled, out_chip, chip))
+    out_lines = lax.all_to_all(out_chip, "y", 0, 0, tiled=True)
+    outs = [((4, 4, 32, width), BF)] * 2
+    operands = [scaled, inverse, all_out, slope, normed_t]
+    in_given, in_kept = local_call(
+        in_kernel,
+        outs,
+        [where, *operands],
+        like(operands) + filled(outs) + [pltpu.VMEM((4 * tokens, 4 * units), BF)],
+        flops=10 * 4 * tokens * width * 4 * units,
+    )
+
+    line = reduce_ring([chip[i] for i in range(4)], "x")
+    plane = lax.all_to_all(line, ("z", "y"), 0, 0, tiled=True)
     weight_rows = jnp.sum(plane.astype(F32), axis=0)
     grad_msg, grad_self = weight_rows[:8], weight_rows[8:]
-
-    outs = [((4, 4, 48, width), BF)] * 2 + [((4, 4, 32, width), BF)] * 2
-    operands = [returned, route, inverse, all_out, slope, pooled, normed_t, rel_hot, *rel_blocks]
-    out_kept, out_given, in_kept, in_given = local_call(
-        back_kernel,
-        outs,
-        [where, *operands],
-        like(operands)
-        + filled(outs)
-        + [pltpu.VMEM((4 * entities, width), BF), pltpu.VMEM((4 * tokens, units), BF)],
-        copies=16,
-        flops=2 * 4 * tokens * width * 4 * units,
-    )
-    out_chip = (out_kept.astype(F32) + shift_by(out_given, "core", 1).astype(F32)).astype(BF)
     in_chip = (in_kept.astype(F32) + shift_by(in_given, "core", 1).astype(F32)).astype(BF)
-    out_part = reduce_ring([out_chip[i].reshape(192, width) for i in range(4)], "y").reshape(4, 48, width)
+    out_part = jnp.sum(out_lines.astype(F32), axis=0).astype(BF)
     in_part = reduce_ring([in_chip[i].reshape(128, width) for i in range(4)], "z").reshape(4, 32, width)
     out_part = reduce_ring([out_part[i] for i in range(4)], "z")
     in_part = reduce_ring([in_part[i] for i in range(4)], "y")

time: 214 us -> 223 us (1.042)
  starting transfers between devices: 69.5 us -> 77.6 us
  Pallas kernels: 58 us -> 61.2 us
    all_to_all x3, starting transfers between devices: 12.1 us -> 16.4 us  [the longest x1 7.54 us: shards(): plane = lax.all_to_all(line, ('z', 'y'), 0, 0, tiled=True)]
    ppermute x42, starting transfers between devices: 50 us -> 53.9 us  [shift_by(): lax.ppermute(value, axis, [(i, (i + shift) % count) for i in range(count)])]
    pallas_call x6 -> x7, Pallas kernels: 58 us -> 61.2 us  [local_call(): pl.pallas_call(kernel, out_shape=[jax.ShapeDtypeStruct(shape, kind) for s...]
    unnamed x76 -> x74, local copies, waits for them, and re-layouts: 4.12 us -> 5.22 us
  transfers between devices with their start and end apart: 46 -> 46, of which waited for: 16 -> 15; matrix products, arithmetic and copies ran while one was open for 9% -> 8% of each run, Pallas kernels for 11% -> 5%
where the time goes in v5:
time: 223 us; the launch traced here: 221 us
  starting transfers between devices  77.6 us (35%)
  Pallas kernels  61.2 us (27%)
  waiting for transfers between devices  53.4 us (24%)
  other arithmetic  15.7 us (7%)
  local copies, waits for them, and re-layouts  11.3 us (5%)
    pallas_call x7, Pallas kernels, local_call(): pl.pallas_call(kernel, out_shape=[jax.ShapeDtypeStruct(shape, kind) for s...  61.2 us
    ppermute x42, starting transfers between devices, shift_by(): lax.ppermute(value, axis, [(i, (i + shift) % count) for i in range(count)])  53.9 us
    ppermute x42, waiting for transfers between devices, shift_by(): lax.ppermute(value, axis, [(i, (i + shift) % count) for i in range(count)])  53.4 us
    all_to_all x1, starting transfers between devices, shards(): plane = lax.all_to_all(line, ('z', 'y'), 0, 0, tiled=True)  7.54 us
    all_to_all x1, starting transfers between devices, shards(): lax.all_to_all(outgoing.reshape(16, 16, width), GROUP, 0, 0, tiled=True)  7.29 us
    unnamed x74, local copies, waits for them, and re-layouts  5.22 us
    all_to_all x1, starting transfers between devices, shards(): out_lines = lax.all_to_all(out_chip, 'y', 0, 0, tiled=True)  4.63 us
  transfers between devices with their start and end apart: 46, of which 15 were waited for; matrix products, arithmetic and copies ran while one was open for 8% of the time, Pallas kernels for 5%

profile of v5, /device:TPU:0, one launch (start us, length us, event | category | flops | bytes accessed | tf_op | source)
XLA Modules:
  0.0 220.9 jit_solution(7180716378660387793)
XLA Ops:
  0.6 1.6 pad.23.refs_7_.refs_8_
  2.2 0.6 pad_add_fusion.refs_0_
  2.8 3.5 %shard_map.190 = (bf16[272,1024]{1,0:T(8,128)(2,1)}, f32[16,1024]{1,0:T(8,128)}, bf16[576,512]{1,0:T(8,128)(2,1)}) custom-call(s32[4]{0:T(128)} %pad_add_fusion.refs_0_, bf16[256,1024]{1,0:T(8,128)(2,1)} %bitcast.50, s32[1,16]{1,0:T(1,128)} %bitcast.55, s32[1,16]{1,0:T(1,128)} %refs_3_.1, s32[1,16]{1,0:T(1,128)} %refs_4_.1, bf16[1024,256]{1,0:T(8,128)(2,1)} %refs_6_.3, ...), custom_call_target="tpu_custom_call" | custom-call | bytes 1048576 | tf_op jit(solution)/shard_map/pallas_call | solution.py:88
  6.3 3.2 %collective-permute-start.5 = (bf16[576,512]{1,0:T(8,128)(2,1)}, bf16[576,512]{1,0:T(8,128)(2,1)S(1)}, u32[]{:S(2)}, u32[]{:S(2)}) collective-permute-start(bf16[576,512]{1,0:T(8,128)(2,1)} %get-tuple-element.51), channel_id=1, source_target_pairs={{0,3},{1,0},{2,1},{3,2},{4,7},{5,4},{6,5},{7,6},{8,11},{9,8},{10,9... | collective-permute-start | bytes 1769480 | tf_op jit(solution)/shard_map/ppermute | solution.py:22
  9.5 2.8 %collective-permute-start.1 = (bf16[272,1024]{1,0:T(8,128)(2,1)}, bf16[272,1024]{1,0:T(8,128)(2,1)S(1)}, u32[]{:S(2)}, u32[]{:S(2)}) collective-permute-start(bf16[272,1024]{1,0:T(8,128)(2,1)} %get-tuple-element.50.refs_1_), channel_id=1, source_target_pairs={{0,12},{4,0},{8,4},{12,8},{1,13},{5,1},{9,5},{13,9},{2,14},{6,2},{... | collective-permute-start | bytes 1671176 | tf_op jit(solution)/shard_map/ppermute | solution.py:22
  12.2 2.2 fusion.refs_7_
  14.4 1.3 fusion.1.refs_8_
  15.9 11.5 %collective-permute-done.refs_2_ = bf16[272,1024]{1,0:T(8,128)(2,1)S(1)} collective-permute-done((bf16[272,1024]{1,0:T(8,128)(2,1)}, bf16[272,1024]{1,0:T(8,128)(2,1)S(1)}, u32[]{:S(2)}, u32[]{:S(2)}) %collective-permute-start) | collective-permute-done | bytes 557088 | tf_op jit(solution)/shard_map/ppermute | solution.py:22
  27.6 3.0 %collective-permute-start.7 = (bf16[320,512]{1,0:T(8,128)(2,1)S(1)}, bf16[320,512]{1,0:T(8,128)(2,1)S(1)}, u32[]{:S(2)}, u32[]{:S(2)}) collective-permute-start(bf16[320,512]{1,0:T(8,128)(2,1)S(1)} %slice.115), channel_id=1, source_target_pairs={{0,3},{1,0},{2,1},{3,2},{4,7},{5,4},{6,5},{7,6},{8,11},{9,8},{10,9... | collective-permute-start | bytes 983048 | tf_op jit(solution)/shard_map/ppermute | solution.py:22
  31.7 3.7 %collective-permute-done.2.refs_4_ = bf16[128,1024]{1,0:T(8,128)(2,1)} collective-permute-done((bf16[128,1024]{1,0:T(8,128)(2,1)S(1)}, bf16[128,1024]{1,0:T(8,128)(2,1)}, u32[]{:S(2)}, u32[]{:S(2)}) %collective-permute-start.2) | collective-permute-done | bytes 262176 | tf_op jit(solution)/shard_map/ppermute | solution.py:22
  35.4 2.9 %collective-permute-done.6.refs_11_ = bf16[256,512]{1,0:T(8,128)(2,1)S(1)} collective-permute-done((bf16[256,512]{1,0:T(8,128)(2,1)S(1)}, bf16[256,512]{1,0:T(8,128)(2,1)S(1)}, u32[]{:S(2)}, u32[]{:S(2)}) %collective-permute-start.6) | collective-permute-done | bytes 262176 | tf_op jit(solution)/shard_map/ppermute | solution.py:22
  38.9 3.2 %collective-permute-done.3.refs_5_ = bf16[144,1024]{1,0:T(8,128)(2,1)S(1)} collective-permute-done((bf16[144,1024]{1,0:T(8,128)(2,1)S(1)}, bf16[144,1024]{1,0:T(8,128)(2,1)S(1)}, u32[]{:S(2)}, u32[]{:S(2)}) %collective-permute-start.3) | collective-permute-done | bytes 294944 | tf_op jit(solution)/shard_map/ppermute | solution.py:22
  42.2 0.9 copy-done.22
  43.1 0.8 copy-done.24
  43.9 11.8 %shard_map.191 = (bf16[256,1024]{1,0:T(8,128)(2,1)}, bf16[1024,1024]{1,0:T(8,128)(2,1)}, bf16[1024,1024]{1,0:T(8,128)(2,1)}, bf16[64,1024]{1,0:T(8,128)(2,1)}, b...) custom-call(s32[4]{0:T(128)} %pad_add_fusion.refs_0_, ...), custom_call_target="tpu_custom_call" | custom-call | flops 2147483648 | bytes 1048576 | tf_op jit(solution)/shard_map/pallas_call | solution.py:88
  55.7 7.3 %all-to-all-start = ((bf16[16,16,1024]{2,1,0:T(8,128)(2,1)}), bf16[16,16,1024]{2,1,0:T(8,128)(2,1)S(1)}, u32[]{:S(2)}, u32[]{:S(2)}) async-start(bf16[16,16,1024]{2,1,0:T(8,128)(2,1)} %bitcast.47), calls=%async_computation | async-start | bytes 1048576 | tf_op jit(solution)/shard_map/all_to_all | solution.py:670
  63.0 1.2 fusion.2.refs_9_
  64.2 1.9 collective-permute-start.15
  66.1 3.4 %collective-permute-start.16 = (bf16[80,1024]{1,0:T(8,128)(2,1)S(1)}, bf16[80,1024]{1,0:T(8,128)(2,1)S(1)}, u32[]{:S(2)}, u32[]{:S(2)}) collective-permute-start(bf16[80,1024]{1,0:T(8,128)(2,1)S(1)} %get-tuple-element.62), channel_id=1, source_target_pairs={{0,15},{1,0},{2,1},{3,2},{4,3},{5,4},{6,5},{7,6},{8,7},{9,8},{10,9... | collective-permute-start | bytes 491528 | tf_op jit(solution)/shard_map/ppermute | solution.py:22
  69.5 1.9 collective-permute-start.12
  71.5 2.2 %collective-permute-start.14 = (bf16[16,1024]{1,0:T(8,128)(2,1)}, bf16[16,1024]{1,0:T(8,128)(2,1)S(1)}, u32[]{:S(2)}, u32[]{:S(2)}) collective-permute-start(bf16[16,1024]{1,0:T(8,128)(2,1)} %get-tuple-element.60), channel_id=1, source_target_pairs={{0,8},{4,12},{8,0},{12,4},{1,9},{5,13},{9,1},{13,5},{2,10},{6,14},... | collective-permute-start | bytes 98312 | tf_op jit(solution)/shard_map/ppermute | solution.py:22
  73.8 0.6 fusion.17.refs_2_
  74.4 2.6 %copy.22 = bf16[1024,1024]{0,1:T(8,128)(2,1)} copy(bf16[1024,1024]{1,0:T(8,128)(2,1)S(1)} %copy-done.2) | data formatting | bytes 4194304 | tf_op jit(solution)/shard_map/pallas_call | solution.py:88
  77.2 0.6 collective-permute-done.15.refs_14_
  77.9 0.6 copy-done.28
  78.5 20.6 %shard_map.192 = (bf16[256,1024]{1,0:T(8,128)(2,1)}, bf16[16,1024]{1,0:T(8,128)(2,1)}, bf16[256,1024]{1,0:T(8,128)(2,1)}, bf16[256,1024]{1,0:T(8,128)(2,1)}, bf1...) custom-call(s32[4]{0:T(128)} %pad_add_fusion.refs_0_, bf16[256,1024]{1,0:T(8,128)(2,1)} %bitcast.46, ...), custom_call_target="tpu_custom_call" | custom-call | flops 6000000000 | bytes 1048576 | tf_op jit(solution)/shard_map/pallas_call | solution.py:88
  99.1 4.2 %all-to-all-start.1 = ((bf16[16,16,1024]{2,1,0:T(8,128)(2,1)}), bf16[16,16,1024]{2,1,0:T(8,128)(2,1)S(1)}, u32[]{:S(2)}, u32[]{:S(2)}) async-start(bf16[16,16,1024]{2,1,0:T(8,128)(2,1)} %bitcast.48), calls=%async_computation.1 | async-start | bytes 1048576 | tf_op jit(solution)/shard_map/all_to_all | solution.py:708
  103.3 1.9 collective-permute-start.17
  105.2 1.4 collective-permute-start.18
  106.6 2.2 collective-permute-start.19
  108.8 2.9 %collective-permute-done.17.refs_7_ = bf16[16,1024]{1,0:T(8,128)(2,1)S(1)} collective-permute-done((bf16[16,1024]{1,0:T(8,128)(2,1)}, bf16[16,1024]{1,0:T(8,128)(2,1)S(1)}, u32[]{:S(2)}, u32[]{:S(2)}) %collective-permute-start.17) | collective-permute-done | bytes 32800 | tf_op jit(solution)/shard_map/ppermute | solution.py:22
  112.2 6.3 %shard_map.194 = (bf16[4,16,16,1024]{3,2,1,0:T(8,128)(2,1)}, bf16[4,16,16,1024]{3,2,1,0:T(8,128)(2,1)}) custom-call(s32[4]{0:T(128)} %pad_add_fusion.refs_0_, bf16[256,1024]{1,0:T(8,128)(2,1)} %get-tuple-element.78.refs_1_, bf16[256,1024]{1,0:T(8,128)(2,1)} %get-tuple-element.79.refs_2_, bf16[256,1024]{1,0:T(8,128)(2,1)} %get-tuple-element.80.refs_3_), custom_call_target="tpu_custom_call" | custom-call | flops 1000000000 | bytes 1048576 | tf_op jit(solution)/shard_map/pallas_call | solution.py:88
  118.7 0.8 copy-done.6
  119.4 4.6 %shard_map.193 = (bf16[4,4,48,1024]{3,2,1,0:T(8,128)(2,1)}, bf16[4,4,48,1024]{3,2,1,0:T(8,128)(2,1)}, bf16[64,1024]{1,0:T(8,128)(2,1)}) custom-call(s32[4]{0:T(128)} %pad_add_fusion.refs_0_, bf16[256,1024]{1,0:T(8,128)(2,1)} %bitcast.49, bf16[64,256]{1,0:T(8,128)(2,1)} %get-tuple-element.65.refs_2_, f32[64,128]{1,0:T(8,128)} %get-tuple-element.66.refs_3_.refs_2_, ...), custom_call_target="tpu_custom_call" | custom-call | flops 1000000000 | bytes 1048576 | tf_op jit(solution)/shard_map/pallas_call | solution.py:88
  124.6 3.2 %collective-permute-done.20 = bf16[4,4,48,1024]{3,2,1,0:T(8,128)(2,1)S(1)} collective-permute-done((bf16[4,4,48,1024]{3,2,1,0:T(8,128)(2,1)}, bf16[4,4,48,1024]{3,2,1,0:T(8,128)(2,1)S(1)}, u32[]{:S(2)}, u32[]{:S(2)}) %collective-permute-start.20) | collective-permute-done | bytes 1572896 | tf_op jit(solution)/shard_map/ppermute | solution.py:22
  127.8 3.5 %add_convert_fusion.1 = bf16[4,4,48,1024]{3,2,1,0:T(8,128)(2,1)} fusion(bf16[4,4,48,1024]{3,2,1,0:T(8,128)(2,1)S(1)} %collective-permute-done.20, bf16[4,4,48,1024]{3,2,1,0:T(8,128)(2,1)} %get-tuple-element.76), kind=kLoop, calls=%fused_computation.1 | loop fusion | flops 3145728 | bytes 4718592 | tf_op jit(solution)/shard_map/convert_element_type | solution.py:723
  131.3 1.3 copy-done.1
  132.6 2.5 %add_convert_fusion = bf16[4,16,16,1024]{3,2,1,0:T(8,128)(2,1)S(1)} fusion(bf16[4,16,16,1024]{3,2,1,0:T(8,128)(2,1)} %copy-done.1, bf16[4,16,16,1024]{3,2,1,0:T(8,128)(2,1)S(1)} %copy-done), kind=kLoop, calls=%fused_computation | loop fusion | flops 4194304 | bytes 6291456 | tf_op jit(solution)/shard_map/convert_element_type | solution.py:717
  135.2 10.9 %shard_map.195 = (bf16[4,4,32,1024]{3,2,1,0:T(8,128)(2,1)}, bf16[4,4,32,1024]{3,2,1,0:T(8,128)(2,1)}) custom-call(s32[4]{0:T(128)} %pad_add_fusion.refs_0_, bf16[64,1024]{1,0:T(8,128)(2,1)} %get-tuple-element.83.refs_1_, f32[64,128]{1,0:T(8,128)} %get-tuple-element.66.refs_3_.refs_2_, bf16[1024,1024]{1,0:T(8,128)(2,1)} %get-tuple-element.84.refs_3_, ...), custom_call_target="tpu_custom_call" | custom-call | flops 10737418240 | bytes 1048576 | tf_op jit(solution)/shard_map/pallas_call | solution.py:88
  146.5 4.6 %all-to-all-start.2 = ((bf16[4,4,48,1024]{3,2,1,0:T(8,128)(2,1)}), bf16[4,4,48,1024]{3,2,1,0:T(8,128)(2,1)}, u32[]{:S(2)}, u32[]{:S(2)}) async-start(bf16[4,4,48,1024]{3,2,1,0:T(8,128)(2,1)} %add_convert_fusion.1), calls=%async_computation.2 | async-start | bytes 3145728 | tf_op jit(solution)/shard_map/all_to_all | solution.py:725
  151.3 1.6 collective-permute-start.39
  153.4 1.9 collective-permute-start.41
  155.7 0.9 fusion.22
  156.6 4.0 %collective-permute-start.23 = (bf16[128,1024]{1,0:T(8,128)(2,1)}, bf16[128,1024]{1,0:T(8,128)(2,1)S(1)}, u32[]{:S(2)}, u32[]{:S(2)}) collective-permute-start(bf16[128,1024]{1,0:T(8,128)(2,1)} %bitcast.16), channel_id=1, source_target_pairs={{0,96},{32,0},{64,32},{96,64},{1,97},{33,1},{65,33},{97,65},{2,98}... | collective-permute-start | bytes 786440 | tf_op jit(solution)/shard_map/ppermute | solution.py:22
  160.6 15.1 %collective-permute-done.39 = bf16[16,16,1024]{2,1,0:T(8,128)(2,1)S(1)} collective-permute-done((bf16[16,16,1024]{2,1,0:T(8,128)(2,1)S(1)}, bf16[16,16,1024]{2,1,0:T(8,128)(2,1)S(1)}, u32[]{:S(2)}, u32[]{:S(2)}) %collective-permute-start.39) | collective-permute-done | bytes 524320 | tf_op jit(solution)/shard_map/ppermute | solution.py:22
  175.7 3.9 %collective-permute-start.25 = (bf16[128,1024]{1,0:T(8,128)(2,1)S(1)}, bf16[128,1024]{1,0:T(8,128)(2,1)S(1)}, u32[]{:S(2)}, u32[]{:S(2)}) collective-permute-start(bf16[128,1024]{1,0:T(8,128)(2,1)S(1)} %bitcast.51), channel_id=1, source_target_pairs={{0,64},{32,96},{64,0},{96,32},{1,65},{33,97},{65,1},{97,33},{2,66}... | collective-permute-start | bytes 786440 | tf_op jit(solution)/shard_map/ppermute | solution.py:22
  179.6 1.2 fusion.5
  180.7 7.5 %all-to-all-start.3 = ((bf16[16,16,1024]{2,1,0:T(8,128)(2,1)}), bf16[16,16,1024]{2,1,0:T(8,128)(2,1)S(1)}, u32[]{:S(2)}, u32[]{:S(2)}) async-start(bf16[16,16,1024]{2,1,0:T(8,128)(2,1)} %fusion.5), calls=%async_computation.3 | async-start | bytes 1048576 | tf_op jit(solution)/shard_map/all_to_all | solution.py:737
  188.3 1.7 reduce_sum.31
  190.0 3.2 %collective-permute-start.29 = (bf16[48,1024]{1,0:T(8,128)(2,1)S(1)}, bf16[48,1024]{1,0:T(8,128)(2,1)S(1)}, u32[]{:S(2)}, u32[]{:S(2)}) collective-permute-start(bf16[48,1024]{1,0:T(8,128)(2,1)S(1)} %get-tuple-element.101), channel_id=1, source_target_pairs={{0,96},{32,0},{64,32},{96,64},{1,97},{33,1},{65,33},{97,65},{2,98}... | collective-permute-start | bytes 294920 | tf_op jit(solution)/shard_map/ppermute | solution.py:22
  193.3 2.3 %collective-permute-start.31 = (bf16[48,1024]{1,0:T(8,128)(2,1)S(1)}, bf16[48,1024]{1,0:T(8,128)(2,1)S(1)}, u32[]{:S(2)}, u32[]{:S(2)}) collective-permute-start(bf16[48,1024]{1,0:T(8,128)(2,1)S(1)} %get-tuple-element.102), channel_id=1, source_target_pairs={{0,64},{32,96},{64,0},{96,32},{1,65},{33,97},{65,1},{97,33},{2,66}... | collective-permute-start | bytes 294920 | tf_op jit(solution)/shard_map/ppermute | solution.py:22
  195.8 2.7 %collective-permute-start.26 = (bf16[32,1024]{1,0:T(8,128)(2,1)S(1)}, bf16[32,1024]{1,0:T(8,128)(2,1)S(1)}, u32[]{:S(2)}, u32[]{:S(2)}) collective-permute-start(bf16[32,1024]{1,0:T(8,128)(2,1)S(1)} %get-tuple-element.104), channel_id=1, source_target_pairs={{0,3},{1,0},{2,1},{3,2},{4,7},{5,4},{6,5},{7,6},{8,11},{9,8},{10,9... | collective-permute-start | bytes 196616 | tf_op jit(solution)/shard_map/ppermute | solution.py:22
  198.5 2.3 %collective-permute-start.28 = (bf16[32,1024]{1,0:T(8,128)(2,1)S(1)}, bf16[32,1024]{1,0:T(8,128)(2,1)S(1)}, u32[]{:S(2)}, u32[]{:S(2)}) collective-permute-start(bf16[32,1024]{1,0:T(8,128)(2,1)S(1)} %get-tuple-element.105), channel_id=1, source_target_pairs={{0,2},{1,3},{2,0},{3,1},{4,6},{5,7},{6,4},{7,5},{8,10},{9,11},{10,... | collective-permute-start | bytes 196616 | tf_op jit(solution)/shard_map/ppermute | solution.py:22
  200.9 0.6 collective-permute-done.30
  201.5 3.2 %collective-permute-done.27 = bf16[32,1024]{1,0:T(8,128)(2,1)S(1)} collective-permute-done((bf16[32,1024]{1,0:T(8,128)(2,1)S(1)}, bf16[32,1024]{1,0:T(8,128)(2,1)S(1)}, u32[]{:S(2)}, u32[]{:S(2)}) %collective-permute-start.27) | collective-permute-done | bytes 65568 | tf_op jit(solution)/shard_map/ppermute | solution.py:22
  204.8 1.8 collective-permute-start.32
  206.6 1.5 collective-permute-start.33
  208.1 1.2 collective-permute-start.34
  209.5 2.9 %collective-permute-done.32.refs_2_ = bf16[80,1024]{1,0:T(8,128)(2,1)S(1)} collective-permute-done((bf16[80,1024]{1,0:T(8,128)(2,1)S(1)}, bf16[80,1024]{1,0:T(8,128)(2,1)S(1)}, u32[]{:S(2)}, u32[]{:S(2)}) %collective-permute-start.32) | collective-permute-done | bytes 163872 | tf_op jit(solution)/shard_map/ppermute | solution.py:22
  212.8 2.1 collective-permute-done.34.refs_4_
  214.9 0.7 fusion.25
  215.7 0.7 collective-permute-done.38.refs_8_
  216.4 0.7 copy-done.15
  217.1 3.7 %shard_map.196 = (f32[1024,256]{1,0:T(8,128)}, f32[256,1024]{1,0:T(8,128)}, f32[52,1024]{1,0:T(8,128)}) custom-call(s32[4]{0:T(128)} %pad_add_fusion.refs_0_, bf16[80,1024]{1,0:T(8,128)(2,1)} %copy-done.4, bf16[80,1024]{1,0:T(8,128)(2,1)} %copy-done.9, bf16[80,1024]{1,0:T(8,128)(2,1)} %copy-done.10, bf16[80,1024]{1,0:T(8,128)(2,1)} %copy-done.11, ...), custom_call_target="tpu_custom_call" | custom-call | bytes 1048576 | tf_op jit(solution)/shard_map/pallas_call | solution.py:88
  (147 shorter events, 6.1 us)
Async XLA Ops:
  0.6 13.8 %copy-start.19 = (s32[1,2048]{1,0:T(1,128)S(1)}, s32[1,2048]{1,0:T(1,128)}, u32[]{:S(2)}) copy-start(s32[1,2048]{1,0:T(1,128)} %param.24) | copy-start | bytes 24580
  2.8 12.9 %copy-start.20 = (s32[1,128]{1,0:T(1,128)S(1)}, s32[1,128]{1,0:T(1,128)}, u32[]{:S(2)}) copy-start(s32[1,128]{1,0:T(1,128)} %param.22) | copy-start | bytes 1540
  2.8 12.9 %copy-start.36 = (s32[1,16]{1,0:T(1,128)S(1)}, s32[1,16]{1,0:T(1,128)}, u32[]{:S(2)}) copy-start(s32[1,16]{1,0:T(1,128)} %param.20) | copy-start | bytes 196
  6.3 21.3 %collective-permute-start.5 = (bf16[576,512]{1,0:T(8,128)(2,1)}, bf16[576,512]{1,0:T(8,128)(2,1)S(1)}, u32[]{:S(2)}, u32[]{:S(2)}) collective-permute-start(bf16[576,512]{1,0:T(8,128)(2,1)} %get-tuple-element.51), channel_id=1, source_target_pairs={{0,3},{1,0},{2,1},{3,2},{4,7},{5,4},{6,5},{7,6},{8,11},{9,8},{10,9... | collective-permute-start | bytes 1769480 | tf_op jit(solution)/shard_map/ppermute | solution.py:22
  9.5 21.2 %collective-permute-start.4 = (bf16[576,512]{1,0:T(8,128)(2,1)}, bf16[576,512]{1,0:T(8,128)(2,1)S(1)}, u32[]{:S(2)}, u32[]{:S(2)}) collective-permute-start(bf16[576,512]{1,0:T(8,128)(2,1)} %get-tuple-element.51), channel_id=1, source_target_pairs={{0,1},{1,2},{2,3},{3,0},{4,5},{5,6},{6,7},{7,4},{8,9},{9,10},{10,1... | collective-permute-start | bytes 1769480 | tf_op jit(solution)/shard_map/ppermute | solution.py:22
  9.5 21.5 %collective-permute-start.1 = (bf16[272,1024]{1,0:T(8,128)(2,1)}, bf16[272,1024]{1,0:T(8,128)(2,1)S(1)}, u32[]{:S(2)}, u32[]{:S(2)}) collective-permute-start(bf16[272,1024]{1,0:T(8,128)(2,1)} %get-tuple-element.50.refs_1_), channel_id=1, source_target_pairs={{0,12},{4,0},{8,4},{12,8},{1,13},{5,1},{9,5},{13,9},{2,14},{6,2},{... | collective-permute-start | bytes 1671176 | tf_op jit(solution)/shard_map/ppermute | solution.py:22
  12.2 15.2 %collective-permute-start = (bf16[272,1024]{1,0:T(8,128)(2,1)}, bf16[272,1024]{1,0:T(8,128)(2,1)S(1)}, u32[]{:S(2)}, u32[]{:S(2)}) collective-permute-start(bf16[272,1024]{1,0:T(8,128)(2,1)} %get-tuple-element.50.refs_1_), channel_id=1, source_target_pairs={{0,4},{4,8},{8,12},{12,0},{1,5},{5,9},{9,13},{13,1},{2,6},{6,10},{... | collective-permute-start | bytes 1671176 | tf_op jit(solution)/shard_map/ppermute | solution.py:22
  12.2 19.2 %copy-start.7 = (bf16[240,1024]{1,0:T(8,128)(2,1)S(1)}, bf16[240,1024]{1,0:T(8,128)(2,1)}, u32[]{:S(2)}) copy-start(bf16[240,1024]{1,0:T(8,128)(2,1)} %refs_13_.1) | copy-start | bytes 1474564
  27.5 11.4 %copy-start.17 = (bf16[272,1024]{1,0:T(8,128)(2,1)}, bf16[272,1024]{1,0:T(8,128)(2,1)S(1)}, u32[]{:S(2)}) copy-start(bf16[272,1024]{1,0:T(8,128)(2,1)S(1)} %collective-permute-done.refs_2_) | copy-start | bytes 1671172
  27.5 7.9 %collective-permute-start.2 = (bf16[128,1024]{1,0:T(8,128)(2,1)S(1)}, bf16[128,1024]{1,0:T(8,128)(2,1)}, u32[]{:S(2)}, u32[]{:S(2)}) collective-permute-start(bf16[128,1024]{1,0:T(8,128)(2,1)S(1)} %slice.112), channel_id=1, source_target_pairs={{0,4},{4,8},{8,12},{12,0},{1,5},{5,9},{9,13},{13,1},{2,6},{6,10},{... | collective-permute-start | bytes 786440 | tf_op jit(solution)/shard_map/ppermute | solution.py:22
  27.6 16.3 %copy-start.8 = (bf16[576,512]{1,0:T(8,128)(2,1)}, bf16[576,512]{1,0:T(8,128)(2,1)S(1)}, u32[]{:S(2)}) copy-start(bf16[576,512]{1,0:T(8,128)(2,1)S(1)} %collective-permute-done.5.refs_10_) | copy-start | bytes 1769476
  27.6 10.7 %collective-permute-start.7 = (bf16[320,512]{1,0:T(8,128)(2,1)S(1)}, bf16[320,512]{1,0:T(8,128)(2,1)S(1)}, u32[]{:S(2)}, u32[]{:S(2)}) collective-permute-start(bf16[320,512]{1,0:T(8,128)(2,1)S(1)} %slice.115), channel_id=1, source_target_pairs={{0,3},{1,0},{2,1},{3,2},{4,7},{5,4},{6,5},{7,6},{8,11},{9,8},{10,9... | collective-permute-start | bytes 983048 | tf_op jit(solution)/shard_map/ppermute | solution.py:22
  30.6 13.2 %copy-start.18 = (bf16[576,512]{1,0:T(8,128)(2,1)}, bf16[576,512]{1,0:T(8,128)(2,1)S(1)}, u32[]{:S(2)}) copy-start(bf16[576,512]{1,0:T(8,128)(2,1)S(1)} %collective-permute-done.4.refs_9_) | copy-start | bytes 1769476
  30.7 7.7 %collective-permute-start.6 = (bf16[256,512]{1,0:T(8,128)(2,1)S(1)}, bf16[256,512]{1,0:T(8,128)(2,1)S(1)}, u32[]{:S(2)}, u32[]{:S(2)}) collective-permute-start(bf16[256,512]{1,0:T(8,128)(2,1)S(1)} %slice.114), channel_id=1, source_target_pairs={{0,1},{1,2},{2,3},{3,0},{4,5},{5,6},{6,7},{7,4},{8,9},{9,10},{10,1... | collective-permute-start | bytes 786440 | tf_op jit(solution)/shard_map/ppermute | solution.py:22
  30.8 11.3 %collective-permute-start.8 = (bf16[576,512]{1,0:T(8,128)(2,1)S(1)}, bf16[576,512]{1,0:T(8,128)(2,1)S(1)}, u32[]{:S(2)}, u32[]{:S(2)}) collective-permute-start(bf16[576,512]{1,0:T(8,128)(2,1)S(1)} %collective-permute-done.4.refs_9_), channel_id=1, source_target_pairs={{0,16},{16,0},{1,17},{17,1},{2,18},{18,2},{3,19},{19,3},{4,20},{20... | collective-permute-start | bytes 1769480 | tf_op jit(solution)/shard_map/ppermute | solution.py:22
  30.9 12.9 %copy-start.16 = (bf16[272,1024]{1,0:T(8,128)(2,1)}, bf16[272,1024]{1,0:T(8,128)(2,1)S(1)}, u32[]{:S(2)}) copy-start(bf16[272,1024]{1,0:T(8,128)(2,1)S(1)} %collective-permute-done.1.refs_3_) | copy-start | bytes 1671172
  30.9 11.2 %collective-permute-start.9 = (bf16[576,512]{1,0:T(8,128)(2,1)S(1)}, bf16[576,512]{1,0:T(8,128)(2,1)S(1)}, u32[]{:S(2)}, u32[]{:S(2)}) collective-permute-start(bf16[576,512]{1,0:T(8,128)(2,1)S(1)} %collective-permute-done.5.refs_10_), channel_id=1, source_target_pairs={{0,16},{16,0},{1,17},{17,1},{2,18},{18,2},{3,19},{19,3},{4,20},{20... | collective-permute-start | bytes 1769480 | tf_op jit(solution)/shard_map/ppermute | solution.py:22
  35.4 6.7 %collective-permute-start.3 = (bf16[144,1024]{1,0:T(8,128)(2,1)S(1)}, bf16[144,1024]{1,0:T(8,128)(2,1)S(1)}, u32[]{:S(2)}, u32[]{:S(2)}) collective-permute-start(bf16[144,1024]{1,0:T(8,128)(2,1)S(1)} %slice.113), channel_id=1, source_target_pairs={{0,12},{4,0},{8,4},{12,8},{1,13},{5,1},{9,5},{13,9},{2,14},{6,2},{... | collective-permute-start | bytes 884744 | tf_op jit(solution)/shard_map/ppermute | solution.py:22
  38.3 4.7 %copy-start.26 = (bf16[256,512]{1,0:T(8,128)(2,1)}, bf16[256,512]{1,0:T(8,128)(2,1)S(1)}, u32[]{:S(2)}) copy-start(bf16[256,512]{1,0:T(8,128)(2,1)S(1)} %collective-permute-done.6.refs_11_) | copy-start | bytes 786436
  38.3 3.8 %collective-permute-start.10 = (bf16[256,512]{1,0:T(8,128)(2,1)S(1)}, bf16[256,512]{1,0:T(8,128)(2,1)S(1)}, u32[]{:S(2)}, u32[]{:S(2)}) collective-permute-start(bf16[256,512]{1,0:T(8,128)(2,1)S(1)} %collective-permute-done.6.refs_11_), channel_id=1, source_target_pairs={{0,16},{16,0},{1,17},{17,1},{2,18},{18,2},{3,19},{19,3},{4,20},{20... | collective-permute-start | bytes 786440 | tf_op jit(solution)/shard_map/ppermute | solution.py:22
  38.3 5.5 %copy-start.23 = (bf16[320,512]{1,0:T(8,128)(2,1)}, bf16[320,512]{1,0:T(8,128)(2,1)S(1)}, u32[]{:S(2)}) copy-start(bf16[320,512]{1,0:T(8,128)(2,1)S(1)} %collective-permute-done.7.refs_12_) | copy-start | bytes 983044
  38.3 4.7 %collective-permute-start.11 = (bf16[320,512]{1,0:T(8,128)(2,1)S(1)}, bf16[320,512]{1,0:T(8,128)(2,1)S(1)}, u32[]{:S(2)}, u32[]{:S(2)}) collective-permute-start(bf16[320,512]{1,0:T(8,128)(2,1)S(1)} %collective-permute-done.7.refs_12_), channel_id=1, source_target_pairs={{0,16},{16,0},{1,17},{17,1},{2,18},{18,2},{3,19},{19,3},{4,20},{20... | collective-permute-start | bytes 983048 | tf_op jit(solution)/shard_map/ppermute | solution.py:22
  55.7 18.7 %copy-start.2 = (bf16[1024,1024]{1,0:T(8,128)(2,1)S(1)}, bf16[1024,1024]{1,0:T(8,128)(2,1)}, u32[]{:S(2)}) copy-start(bf16[1024,1024]{1,0:T(8,128)(2,1)} %get-tuple-element.55) | copy-start | bytes 6291460
  55.7 21.3 %all-to-all-start = ((bf16[16,16,1024]{2,1,0:T(8,128)(2,1)}), bf16[16,16,1024]{2,1,0:T(8,128)(2,1)S(1)}, u32[]{:S(2)}, u32[]{:S(2)}) async-start(bf16[16,16,1024]{2,1,0:T(8,128)(2,1)} %bitcast.47), calls=%async_computation | async-start | bytes 1048576 | tf_op jit(solution)/shard_map/all_to_all | solution.py:670
  64.2 13.6 %collective-permute-start.15 = (bf16[80,1024]{1,0:T(8,128)(2,1)S(1)}, bf16[80,1024]{1,0:T(8,128)(2,1)S(1)}, u32[]{:S(2)}, u32[]{:S(2)}) collective-permute-start(bf16[80,1024]{1,0:T(8,128)(2,1)S(1)} %get-tuple-element.61), channel_id=1, source_target_pairs={{0,1},{1,2},{2,3},{3,4},{4,5},{5,6},{6,7},{7,8},{8,9},{9,10},{10,1... | collective-permute-start | bytes 491528 | tf_op jit(solution)/shard_map/ppermute | solution.py:22
  66.1 11.7 %collective-permute-start.16 = (bf16[80,1024]{1,0:T(8,128)(2,1)S(1)}, bf16[80,1024]{1,0:T(8,128)(2,1)S(1)}, u32[]{:S(2)}, u32[]{:S(2)}) collective-permute-start(bf16[80,1024]{1,0:T(8,128)(2,1)S(1)} %get-tuple-element.62), channel_id=1, source_target_pairs={{0,15},{1,0},{2,1},{3,2},{4,3},{5,4},{6,5},{7,6},{8,7},{9,8},{10,9... | collective-permute-start | bytes 491528 | tf_op jit(solution)/shard_map/ppermute | solution.py:22
  69.5 7.4 %collective-permute-start.12 = (bf16[16,1024]{1,0:T(8,128)(2,1)}, bf16[16,1024]{1,0:T(8,128)(2,1)S(1)}, u32[]{:S(2)}, u32[]{:S(2)}) collective-permute-start(bf16[16,1024]{1,0:T(8,128)(2,1)} %get-tuple-element.58), channel_id=1, source_target_pairs={{0,12},{4,0},{8,4},{12,8},{1,13},{5,1},{9,5},{13,9},{2,14},{6,2},{... | collective-permute-start | bytes 98312 | tf_op jit(solution)/shard_map/ppermute | solution.py:22
  71.4 5.5 %collective-permute-start.13 = (bf16[16,1024]{1,0:T(8,128)(2,1)}, bf16[16,1024]{1,0:T(8,128)(2,1)S(1)}, u32[]{:S(2)}, u32[]{:S(2)}) collective-permute-start(bf16[16,1024]{1,0:T(8,128)(2,1)} %get-tuple-element.59), channel_id=1, source_target_pairs={{0,4},{4,8},{8,12},{12,0},{1,5},{5,9},{9,13},{13,1},{2,6},{6,10},{... | collective-permute-start | bytes 98312 | tf_op jit(solution)/shard_map/ppermute | solution.py:22
  71.5 5.6 %collective-permute-start.14 = (bf16[16,1024]{1,0:T(8,128)(2,1)}, bf16[16,1024]{1,0:T(8,128)(2,1)S(1)}, u32[]{:S(2)}, u32[]{:S(2)}) collective-permute-start(bf16[16,1024]{1,0:T(8,128)(2,1)} %get-tuple-element.60), channel_id=1, source_target_pairs={{0,8},{4,12},{8,0},{12,4},{1,9},{5,13},{9,1},{13,5},{2,10},{6,14},... | collective-permute-start | bytes 98312 | tf_op jit(solution)/shard_map/ppermute | solution.py:22
  99.1 19.5 %all-to-all-start.1 = ((bf16[16,16,1024]{2,1,0:T(8,128)(2,1)}), bf16[16,16,1024]{2,1,0:T(8,128)(2,1)S(1)}, u32[]{:S(2)}, u32[]{:S(2)}) async-start(bf16[16,16,1024]{2,1,0:T(8,128)(2,1)} %bitcast.48), calls=%async_computation.1 | async-start | bytes 1048576 | tf_op jit(solution)/shard_map/all_to_all | solution.py:708
  103.3 8.4 %collective-permute-start.17 = (bf16[16,1024]{1,0:T(8,128)(2,1)}, bf16[16,1024]{1,0:T(8,128)(2,1)S(1)}, u32[]{:S(2)}, u32[]{:S(2)}) collective-permute-start(bf16[16,1024]{1,0:T(8,128)(2,1)} %get-tuple-element.71.refs_6_), channel_id=1, source_target_pairs={{0,4},{4,8},{8,12},{12,0},{1,5},{5,9},{9,13},{13,1},{2,6},{6,10},{... | collective-permute-start | bytes 98312 | tf_op jit(solution)/shard_map/ppermute | solution.py:22
  105.2 6.5 %collective-permute-start.18 = (bf16[16,1024]{1,0:T(8,128)(2,1)}, bf16[16,1024]{1,0:T(8,128)(2,1)S(1)}, u32[]{:S(2)}, u32[]{:S(2)}) collective-permute-start(bf16[16,1024]{1,0:T(8,128)(2,1)} %get-tuple-element.71.refs_6_), channel_id=1, source_target_pairs={{0,12},{4,0},{8,4},{12,8},{1,13},{5,1},{9,5},{13,9},{2,14},{6,2},{... | collective-permute-start | bytes 98312 | tf_op jit(solution)/shard_map/ppermute | solution.py:22
  106.6 5.6 %collective-permute-start.19 = (bf16[16,1024]{1,0:T(8,128)(2,1)}, bf16[16,1024]{1,0:T(8,128)(2,1)S(1)}, u32[]{:S(2)}, u32[]{:S(2)}) collective-permute-start(bf16[16,1024]{1,0:T(8,128)(2,1)} %get-tuple-element.71.refs_6_), channel_id=1, source_target_pairs={{0,8},{4,12},{8,0},{12,4},{1,9},{5,13},{9,1},{13,5},{2,10},{6,14},... | collective-permute-start | bytes 98312 | tf_op jit(solution)/shard_map/ppermute | solution.py:22
  111.7 6.9 %copy-start.33 = (bf16[16,1024]{1,0:T(8,128)(2,1)}, bf16[16,1024]{1,0:T(8,128)(2,1)S(1)}, u32[]{:S(2)}) copy-start(bf16[16,1024]{1,0:T(8,128)(2,1)S(1)} %collective-permute-done.17.refs_7_) | copy-start | bytes 98308
  111.7 6.9 %copy-start.34 = (bf16[16,1024]{1,0:T(8,128)(2,1)}, bf16[16,1024]{1,0:T(8,128)(2,1)S(1)}, u32[]{:S(2)}) copy-start(bf16[16,1024]{1,0:T(8,128)(2,1)S(1)} %collective-permute-done.18.refs_8_) | copy-start | bytes 98308
  112.2 6.4 %copy-start.35 = (bf16[16,1024]{1,0:T(8,128)(2,1)}, bf16[16,1024]{1,0:T(8,128)(2,1)S(1)}, u32[]{:S(2)}) copy-start(bf16[16,1024]{1,0:T(8,128)(2,1)S(1)} %collective-permute-done.19.refs_9_) | copy-start | bytes 98308
  118.5 12.8 %collective-permute-start.21 = (bf16[4,16,16,1024]{3,2,1,0:T(8,128)(2,1)}, bf16[4,16,16,1024]{3,2,1,0:T(8,128)(2,1)S(1)}, u32[]{:S(2)}, u32[]{:S(2)}) collective-permute-start(bf16[4,16,16,1024]{3,2,1,0:T(8,128)(2,1)} %get-tuple-element.82), channel_id=1, source_target_pairs={{0,16},{16,0},{1,17},{17,1},{2,18},{18,2},{3,19},{19,3},{4,20},{20... | collective-permute-start | bytes 6291464 | tf_op jit(solution)/shard_map/ppermute | solution.py:22
  124.0 3.8 %collective-permute-start.20 = (bf16[4,4,48,1024]{3,2,1,0:T(8,128)(2,1)}, bf16[4,4,48,1024]{3,2,1,0:T(8,128)(2,1)S(1)}, u32[]{:S(2)}, u32[]{:S(2)}) collective-permute-start(bf16[4,4,48,1024]{3,2,1,0:T(8,128)(2,1)} %get-tuple-element.77), channel_id=1, source_target_pairs={{0,16},{16,0},{1,17},{17,1},{2,18},{18,2},{3,19},{19,3},{4,20},{20... | collective-permute-start | bytes 4718600 | tf_op jit(solution)/shard_map/ppermute | solution.py:22
  127.8 4.8 %copy-start = (bf16[4,16,16,1024]{3,2,1,0:T(8,128)(2,1)S(1)}, bf16[4,16,16,1024]{3,2,1,0:T(8,128)(2,1)}, u32[]{:S(2)}) copy-start(bf16[4,16,16,1024]{3,2,1,0:T(8,128)(2,1)} %get-tuple-element.81) | copy-start | bytes 6291460
  146.1 9.2 %collective-permute-start.22 = (bf16[4,4,32,1024]{3,2,1,0:T(8,128)(2,1)}, bf16[4,4,32,1024]{3,2,1,0:T(8,128)(2,1)S(1)}, u32[]{:S(2)}, u32[]{:S(2)}) collective-permute-start(bf16[4,4,32,1024]{3,2,1,0:T(8,128)(2,1)} %get-tuple-element.88), channel_id=1, source_target_pairs={{0,16},{16,0},{1,17},{17,1},{2,18},{18,2},{3,19},{19,3},{4,20},{20... | collective-permute-start | bytes 3145736 | tf_op jit(solution)/shard_map/ppermute | solution.py:22
  146.5 34.2 %all-to-all-start.2 = ((bf16[4,4,48,1024]{3,2,1,0:T(8,128)(2,1)}), bf16[4,4,48,1024]{3,2,1,0:T(8,128)(2,1)}, u32[]{:S(2)}, u32[]{:S(2)}) async-start(bf16[4,4,48,1024]{3,2,1,0:T(8,128)(2,1)} %add_convert_fusion.1), calls=%async_computation.2 | async-start | bytes 3145728 | tf_op jit(solution)/shard_map/all_to_all | solution.py:725
  151.1 4.1 %copy-start.3 = (bf16[4,4,32,1024]{3,2,1,0:T(8,128)(2,1)S(1)}, bf16[4,4,32,1024]{3,2,1,0:T(8,128)(2,1)}, u32[]{:S(2)}) copy-start(bf16[4,4,32,1024]{3,2,1,0:T(8,128)(2,1)} %get-tuple-element.87) | copy-start | bytes 3145732
  151.3 24.4 %collective-permute-start.39 = (bf16[16,16,1024]{2,1,0:T(8,128)(2,1)S(1)}, bf16[16,16,1024]{2,1,0:T(8,128)(2,1)S(1)}, u32[]{:S(2)}, u32[]{:S(2)}) collective-permute-start(bf16[16,16,1024]{2,1,0:T(8,128)(2,1)S(1)} %get-tuple-element.94), channel_id=1, source_target_pairs={{0,12},{4,0},{8,4},{12,8},{1,13},{5,1},{9,5},{13,9},{2,14},{6,2},{... | collective-permute-start | bytes 1572872 | tf_op jit(solution)/shard_map/ppermute | solution.py:22
  152.9 26.6 %collective-permute-start.40 = (bf16[16,16,1024]{2,1,0:T(8,128)(2,1)S(1)}, bf16[16,16,1024]{2,1,0:T(8,128)(2,1)S(1)}, u32[]{:S(2)}, u32[]{:S(2)}) collective-permute-start(bf16[16,16,1024]{2,1,0:T(8,128)(2,1)S(1)} %get-tuple-element.96), channel_id=1, source_target_pairs={{0,4},{4,8},{8,12},{12,0},{1,5},{5,9},{9,13},{13,1},{2,6},{6,10},{... | collective-permute-start | bytes 1572872 | tf_op jit(solution)/shard_map/ppermute | solution.py:22
  153.4 26.2 %collective-permute-start.41 = (bf16[16,16,1024]{2,1,0:T(8,128)(2,1)S(1)}, bf16[16,16,1024]{2,1,0:T(8,128)(2,1)S(1)}, u32[]{:S(2)}, u32[]{:S(2)}) collective-permute-start(bf16[16,16,1024]{2,1,0:T(8,128)(2,1)S(1)} %get-tuple-element.95), channel_id=1, source_target_pairs={{0,8},{4,12},{8,0},{12,4},{1,9},{5,13},{9,1},{13,5},{2,10},{6,14},... | collective-permute-start | bytes 1572872 | tf_op jit(solution)/shard_map/ppermute | solution.py:22
  156.6 36.7 %collective-permute-start.23 = (bf16[128,1024]{1,0:T(8,128)(2,1)}, bf16[128,1024]{1,0:T(8,128)(2,1)S(1)}, u32[]{:S(2)}, u32[]{:S(2)}) collective-permute-start(bf16[128,1024]{1,0:T(8,128)(2,1)} %bitcast.16), channel_id=1, source_target_pairs={{0,96},{32,0},{64,32},{96,64},{1,97},{33,1},{65,33},{97,65},{2,98}... | collective-permute-start | bytes 786440 | tf_op jit(solution)/shard_map/ppermute | solution.py:22
  160.6 35.0 %collective-permute-start.24 = (bf16[128,1024]{1,0:T(8,128)(2,1)}, bf16[128,1024]{1,0:T(8,128)(2,1)S(1)}, u32[]{:S(2)}, u32[]{:S(2)}) collective-permute-start(bf16[128,1024]{1,0:T(8,128)(2,1)} %bitcast.17), channel_id=1, source_target_pairs={{0,32},{32,64},{64,96},{96,0},{1,33},{33,65},{65,97},{97,1},{2,34}... | collective-permute-start | bytes 786440 | tf_op jit(solution)/shard_map/ppermute | solution.py:22
  175.7 19.9 %collective-permute-start.25 = (bf16[128,1024]{1,0:T(8,128)(2,1)S(1)}, bf16[128,1024]{1,0:T(8,128)(2,1)S(1)}, u32[]{:S(2)}, u32[]{:S(2)}) collective-permute-start(bf16[128,1024]{1,0:T(8,128)(2,1)S(1)} %bitcast.51), channel_id=1, source_target_pairs={{0,64},{32,96},{64,0},{96,32},{1,65},{33,97},{65,1},{97,33},{2,66}... | collective-permute-start | bytes 786440 | tf_op jit(solution)/shard_map/ppermute | solution.py:22
  180.7 28.6 %all-to-all-start.3 = ((bf16[16,16,1024]{2,1,0:T(8,128)(2,1)}), bf16[16,16,1024]{2,1,0:T(8,128)(2,1)S(1)}, u32[]{:S(2)}, u32[]{:S(2)}) async-start(bf16[16,16,1024]{2,1,0:T(8,128)(2,1)} %fusion.5), calls=%async_computation.3 | async-start | bytes 1048576 | tf_op jit(solution)/shard_map/all_to_all | solution.py:737
  190.0 8.5 %collective-permute-start.29 = (bf16[48,1024]{1,0:T(8,128)(2,1)S(1)}, bf16[48,1024]{1,0:T(8,128)(2,1)S(1)}, u32[]{:S(2)}, u32[]{:S(2)}) collective-permute-start(bf16[48,1024]{1,0:T(8,128)(2,1)S(1)} %get-tuple-element.101), channel_id=1, source_target_pairs={{0,96},{32,0},{64,32},{96,64},{1,97},{33,1},{65,33},{97,65},{2,98}... | collective-permute-start | bytes 294920 | tf_op jit(solution)/shard_map/ppermute | solution.py:22
  193.3 8.2 %collective-permute-start.30 = (bf16[48,1024]{1,0:T(8,128)(2,1)S(1)}, bf16[48,1024]{1,0:T(8,128)(2,1)S(1)}, u32[]{:S(2)}, u32[]{:S(2)}) collective-permute-start(bf16[48,1024]{1,0:T(8,128)(2,1)S(1)} %get-tuple-element.103), channel_id=1, source_target_pairs={{0,32},{32,64},{64,96},{96,0},{1,33},{33,65},{65,97},{97,1},{2,34}... | collective-permute-start | bytes 294920 | tf_op jit(solution)/shard_map/ppermute | solution.py:22
  193.3 8.2 %collective-permute-start.31 = (bf16[48,1024]{1,0:T(8,128)(2,1)S(1)}, bf16[48,1024]{1,0:T(8,128)(2,1)S(1)}, u32[]{:S(2)}, u32[]{:S(2)}) collective-permute-start(bf16[48,1024]{1,0:T(8,128)(2,1)S(1)} %get-tuple-element.102), channel_id=1, source_target_pairs={{0,64},{32,96},{64,0},{96,32},{1,65},{33,97},{65,1},{97,33},{2,66}... | collective-permute-start | bytes 294920 | tf_op jit(solution)/shard_map/ppermute | solution.py:22
  195.8 5.7 %collective-permute-start.26 = (bf16[32,1024]{1,0:T(8,128)(2,1)S(1)}, bf16[32,1024]{1,0:T(8,128)(2,1)S(1)}, u32[]{:S(2)}, u32[]{:S(2)}) collective-permute-start(bf16[32,1024]{1,0:T(8,128)(2,1)S(1)} %get-tuple-element.104), channel_id=1, source_target_pairs={{0,3},{1,0},{2,1},{3,2},{4,7},{5,4},{6,5},{7,6},{8,11},{9,8},{10,9... | collective-permute-start | bytes 196616 | tf_op jit(solution)/shard_map/ppermute | solution.py:22
  198.5 6.2 %collective-permute-start.27 = (bf16[32,1024]{1,0:T(8,128)(2,1)S(1)}, bf16[32,1024]{1,0:T(8,128)(2,1)S(1)}, u32[]{:S(2)}, u32[]{:S(2)}) collective-permute-start(bf16[32,1024]{1,0:T(8,128)(2,1)S(1)} %get-tuple-element.106), channel_id=1, source_target_pairs={{0,1},{1,2},{2,3},{3,0},{4,5},{5,6},{6,7},{7,4},{8,9},{9,10},{10,1... | collective-permute-start | bytes 196616 | tf_op jit(solution)/shard_map/ppermute | solution.py:22
  198.5 6.2 %collective-permute-start.28 = (bf16[32,1024]{1,0:T(8,128)(2,1)S(1)}, bf16[32,1024]{1,0:T(8,128)(2,1)S(1)}, u32[]{:S(2)}, u32[]{:S(2)}) collective-permute-start(bf16[32,1024]{1,0:T(8,128)(2,1)S(1)} %get-tuple-element.105), channel_id=1, source_target_pairs={{0,2},{1,3},{2,0},{3,1},{4,6},{5,7},{6,4},{7,5},{8,10},{9,11},{10,... | collective-permute-start | bytes 196616 | tf_op jit(solution)/shard_map/ppermute | solution.py:22
  204.8 11.5 %copy-start.4 = (bf16[80,1024]{1,0:T(8,128)(2,1)}, bf16[80,1024]{1,0:T(8,128)(2,1)S(1)}, u32[]{:S(2)}) copy-start(bf16[80,1024]{1,0:T(8,128)(2,1)S(1)} %pad_maximum_fusion.refs_1_) | copy-start | bytes 491524
  204.8 7.5 %collective-permute-start.32 = (bf16[80,1024]{1,0:T(8,128)(2,1)S(1)}, bf16[80,1024]{1,0:T(8,128)(2,1)S(1)}, u32[]{:S(2)}, u32[]{:S(2)}) collective-permute-start(bf16[80,1024]{1,0:T(8,128)(2,1)S(1)} %pad_maximum_fusion.refs_1_), channel_id=1, source_target_pairs={{0,32},{32,64},{64,96},{96,0},{1,33},{33,65},{65,97},{97,1},{2,34}... | collective-permute-start | bytes 491528 | tf_op jit(solution)/shard_map/ppermute | solution.py:22
  206.6 5.7 %collective-permute-start.33 = (bf16[80,1024]{1,0:T(8,128)(2,1)S(1)}, bf16[80,1024]{1,0:T(8,128)(2,1)S(1)}, u32[]{:S(2)}, u32[]{:S(2)}) collective-permute-start(bf16[80,1024]{1,0:T(8,128)(2,1)S(1)} %pad_maximum_fusion.refs_1_), channel_id=1, source_target_pairs={{0,96},{32,0},{64,32},{96,64},{1,97},{33,1},{65,33},{97,65},{2,98}... | collective-permute-start | bytes 491528 | tf_op jit(solution)/shard_map/ppermute | solution.py:22
  208.1 6.8 %collective-permute-start.34 = (bf16[80,1024]{1,0:T(8,128)(2,1)S(1)}, bf16[80,1024]{1,0:T(8,128)(2,1)S(1)}, u32[]{:S(2)}, u32[]{:S(2)}) collective-permute-start(bf16[80,1024]{1,0:T(8,128)(2,1)S(1)} %pad_maximum_fusion.refs_1_), channel_id=1, source_target_pairs={{0,64},{32,96},{64,0},{96,32},{1,65},{33,97},{65,1},{97,33},{2,66}... | collective-permute-start | bytes 491528 | tf_op jit(solution)/shard_map/ppermute | solution.py:22
  209.4 6.3 %collective-permute-start.35 = (bf16[80,1024]{1,0:T(8,128)(2,1)S(1)}, bf16[80,1024]{1,0:T(8,128)(2,1)S(1)}, u32[]{:S(2)}, u32[]{:S(2)}) collective-permute-start(bf16[80,1024]{1,0:T(8,128)(2,1)S(1)} %pad_maximum_fusion.refs_1_), channel_id=1, source_target_pairs={{0,16},{16,0},{1,17},{17,1},{2,18},{18,2},{3,19},{19,3},{4,20},{20... | collective-permute-start | bytes 491528 | tf_op jit(solution)/shard_map/ppermute | solution.py:22
  212.3 4.0 %copy-start.9 = (bf16[80,1024]{1,0:T(8,128)(2,1)}, bf16[80,1024]{1,0:T(8,128)(2,1)S(1)}, u32[]{:S(2)}) copy-start(bf16[80,1024]{1,0:T(8,128)(2,1)S(1)} %collective-permute-done.32.refs_2_) | copy-start | bytes 491524
  212.3 3.3 %collective-permute-start.36 = (bf16[80,1024]{1,0:T(8,128)(2,1)S(1)}, bf16[80,1024]{1,0:T(8,128)(2,1)S(1)}, u32[]{:S(2)}, u32[]{:S(2)}) collective-permute-start(bf16[80,1024]{1,0:T(8,128)(2,1)S(1)} %collective-permute-done.32.refs_2_), channel_id=1, source_target_pairs={{0,16},{16,0},{1,17},{17,1},{2,18},{18,2},{3,19},{19,3},{4,20},{20... | collective-permute-start | bytes 491528 | tf_op jit(solution)/shard_map/ppermute | solution.py:22
  212.3 3.3 %collective-permute-start.37 = (bf16[80,1024]{1,0:T(8,128)(2,1)S(1)}, bf16[80,1024]{1,0:T(8,128)(2,1)S(1)}, u32[]{:S(2)}, u32[]{:S(2)}) collective-permute-start(bf16[80,1024]{1,0:T(8,128)(2,1)S(1)} %collective-permute-done.33.refs_3_), channel_id=1, source_target_pairs={{0,16},{16,0},{1,17},{17,1},{2,18},{18,2},{3,19},{19,3},{4,20},{20... | collective-permute-start | bytes 491528 | tf_op jit(solution)/shard_map/ppermute | solution.py:22
  214.9 1.4 collective-permute-start.38
  (19 other events, 21.0 us)

commit v6 on v5

--- a/solution.py
+++ b/solution.py
@@ -125,9 +125,9 @@
 def norm_kernel(
     copies,
     where_ref,
-    hidden_hbm, lens_hbm, order_hbm, rel_hbm, in_hbm, out_hbm, table_hbm,
+    hidden_hbm, lens_hbm, order_hbm, in_hbm, out_hbm, table_hbm,
     block_hbm, sum_hbm, weights_hbm,
-    hidden_ref, lens_ref, order_ref, rel_ref,
+    hidden_ref, lens_ref, order_ref,
     block_ref, sum_ref, weights_ref,
 ):
     core = where_ref[1]
@@ -144,14 +144,12 @@
         copies.start(hidden_hbm, hidden_ref),
         copies.start(lens_hbm, lens_ref),
         copies.start(order_hbm, order_ref),
-        copies.start(rel_hbm, rel_ref),
     ]
     wait_all(packed)
     later = [copies.start(weights_ref, weights_hbm)]
     wait_all(first)
     meta = jnp.zeros((16, 128), F32)
-    high = rel_ref[...] // 32
-    for i, row in enumerate((lens_ref[...], order_ref[...], high, rel_ref[...] - 32 * high)):
+    for i, row in enumerate((lens_ref[...], order_ref[...])):
         values = jnp.broadcast_to(row.astype(F32), (16, 16)).astype(BF)
         select = (lanes((16, 128)) == sublanes((16, 128)) + 16 * i).astype(F32).astype(BF)
         meta = meta + dot(values, select)
@@ -175,18 +173,17 @@
     own_in, own_out, own_rel,
     m1, m2, m3_in, m3_rest,
     o1, o2, o3_in, o3_rest,
-    hidden_sum_hbm,
+    hidden_sum_hbm, numbers_hbm,
     outgoing_hbm, normed_hbm, slope_hbm, pooled_hbm, all_out_hbm, route_hbm, length_hbm, rel_hot_hbm,
-    rel0_hbm, rel1_hbm, rel2_hbm, rel3_hbm,
     outgoing_ref, normed_ref, slope_ref, pooled_ref, all_out_ref, route_ref, length_ref, rel_hot_ref,
-    rel0_ref, rel1_ref, rel2_ref, rel3_ref,
-    in_ref, pool_ref, rel_ref, meta_ref, hidden_sum_ref,
+    in_ref, pool_ref, rel_ref, meta_ref, hidden_sum_ref, numbers_ref,
 ):
     core, my_x, my_y = where_ref[1], where_ref[2], where_ref[3]
     metas, tokens, weights, tables = [], [], [[], [], [], []], []
     for s, (block, row) in enumerate(((b0, 256), (b1, 256), (b2, 256), (b3_rest, 128))):
         metas.append(copies.start(block.at[pl.ds(row, 16), pl.ds(0, 128)], meta_ref.at[s]))
     tables.append(copies.start(own_rel, rel_ref.at[pl.ds(0, 64), :]))
+    tables.append(copies.start(numbers_hbm, numbers_ref))
     pieces = []
     for t, (mine, other) in enumerate(
         (((m1, m1, 256), (o1, o1, 256)), ((m2, m2, 256), (o2, o2, 256)), ((m3_in, m3_rest, 0), (o3_in, o3_rest, 0))), 1
@@ -222,19 +219,9 @@
     bound = lanes((128, 256))
     bound = (bound // 16 + (bound % 16) // 4 + 15) % 16
     bound_hot = (sublanes((128, 256)) == bound + 16).astype(F32).astype(BF)
-    ids = jnp.zeros((16, 64), F32)
-    asked = (rel0_ref, rel1_ref, rel2_ref, rel3_ref)
     for s in range(4):
         meta = meta_ref[s]
         values = meta.astype(F32)
-        apart = lanes(meta.shape) - sublanes(meta.shape)
-        wanted = jnp.where(apart == 32, 32.0 * values, jnp.where(apart == 48, values, 0.0))
-        wanted = jnp.sum(wanted, axis=1, keepdims=True)
-        line = lanes(wide)
-        owner_y = (my_y + jnp.where(line < 64, 0, jnp.where(line < 128, 3, line // 64 - 1))) % 4
-        name = (my_x * 4 + owner_y) * 52 + line % 64
-        pick = (name.astype(F32) == wanted) & (line % 64 < 52)
-        asked[s][...] = dot(pick.astype(F32).astype(BF), rel_ref[...]).astype(BF)
         length = length_column(values)
         length_ref[s * 16 : (s + 1) * 16, :] = jnp.broadcast_to(1.0 / length, (16, 128))
         pool_ref[s * 16 : (s + 1) * 16, :] = pool_rows(length, 256)
@@ -242,21 +229,28 @@
         encoder = lax.rem(my_x + ORIGINS[s], 4)
         chosen = (sent == sublanes(wide).astype(F32)) & (slot % 4 == encoder) & (slot < 12)
         route_ref[s * 16 : (s + 1) * 16, :] = chosen.astype(F32).astype(BF)
-        at, to = sublanes((128, 64)), lanes((128, 64)) - s * 16
-        inside = (to >= 0) & (to < 16)
-        select = jnp.where(inside & (at == 32 + to), 32.0, jnp.where(inside & (at == 48 + to), 1.0, 0.0))
-        ids = ids + dot(meta, select.astype(BF))
-    line = sublanes((512, 64))
+
+    high = numbers_ref[...] // 32
+    digits = (high.astype(F32).astype(BF), (numbers_ref[...] - 32 * high).astype(F32).astype(BF))
+    tall, flat = (256, 128), (16, 256)
+    chosen = lanes(tall) == sublanes(tall) % 16 - 12
+    source_hot = (sublanes((256, 16)) // 16 == lanes((256, 16))).astype(F32).astype(BF)
+    column = [jnp.sum(jnp.where(chosen, dot(source_hot, part), 0.0), axis=1, keepdims=True) for part in digits]
+    line = lanes((256, 256))
+    owner_y = (my_y + jnp.where(line < 64, 0, jnp.where(line < 128, 3, line // 64 - 1))) % 4
+    name = ((my_x * 4 + owner_y) * 52 + line % 64).astype(F32)
+    served = (name == 32.0 * column[0] + column[1]) & (line % 64 < 52) & (sublanes((256, 256)) % 16 >= 12)
+    slot_hot = (sublanes((128, 256)) == lanes((128, 256)) % 16 - 12).astype(F32).astype(BF)
+    own = sublanes(flat) == lanes(flat) // 16
+    row = [jnp.sum(jnp.where(own, dot(part, slot_hot), 0.0), axis=0, keepdims=True) for part in digits]
+    line = sublanes((512, 256))
     local = (line // 64) % 2 * 32 + (line // 16) % 4 * 8 + line % 16
-    name = (my_x * 4 + line // 128) * 52 + local
-    good = (line % 16 < 8) & (local < 52)
-    rel_hot_ref[...] = ((name.astype(F32) == ids[0:1, :]) & good).astype(F32).astype(BF)
+    name = ((my_x * 4 + line // 128) * 52 + local).astype(F32)
+    good = (line % 16 < 8) & (local < 52) & (lanes((512, 256)) % 16 >= 12)
+    rel_hot_ref[...] = ((name == 32.0 * row[0] + row[1]) & good).astype(F32).astype(BF)
+    relations = dot(served.astype(F32).astype(BF), rel_ref[...])
 
     sent_out = [
-        copies.start(rel0_ref, rel0_hbm),
-        copies.start(rel1_ref, rel1_hbm),
-        copies.start(rel2_ref, rel2_hbm),
-        copies.start(rel3_ref, rel3_hbm),
         copies.start(route_ref, route_hbm),
         copies.start(length_ref, length_hbm),
         copies.start(rel_hot_ref, rel_hot_hbm),
@@ -289,7 +283,7 @@
     partial = dot(pooled_ref[...], all_out_ref[...])
     partial = jnp.concatenate([partial[0:16] + hidden_sum_ref[...], partial[16:64]], axis=0)
     partial = (partial * length_ref[:, 0:1]).astype(BF)
-    outgoing_ref[...] = dot_t(route_ref[...], partial).astype(BF)
+    outgoing_ref[...] = (dot_t(route_ref[...], partial) + relations).astype(BF)
     sent_out.append(copies.start(outgoing_ref, outgoing_hbm))
     wait_all(sent_out)
 
@@ -297,17 +291,17 @@
 def graph_kernel(
     copies,
     where_ref,
-    arrived_hbm, own_hot_t_hbm, e0_hbm, e1_hbm, e2_hbm, e3_hbm,
+    arrived_hbm, own_hot_t_hbm,
     src_hot_hbm, dst_hot_hbm, dst_hot_t_hbm,
     w_msg_hbm, w_self_hbm, d_out_hbm,
     cache_hbm, low_hbm, high_hbm,
-    table_out_hbm, blocks_hbm, graph_out_hbm, aggregate_hbm, nodes_hbm, pre_hbm,
-    arrived_ref, own_hot_t_ref, e0, e1, e2, e3,
+    table_out_hbm, graph_out_hbm, aggregate_hbm, nodes_hbm, pre_hbm,
+    arrived_ref, own_hot_t_ref,
     src_hot_ref, dst_hot_ref, dst_hot_t_ref,
     w_msg_ref, w_self_ref, d_out_ref,
-    table_out_ref, blocks_ref, graph_out_ref, aggregate_ref, nodes_ref, pre_ref,
+    table_out_ref, graph_out_ref, aggregate_ref, nodes_ref, pre_ref,
     base_ref, places_ref, row_hot_t_ref, src_row_hot_ref,
-    ext_ref, sources_ref, edges_ref, agg_grad_ref, sums_ref, rel_ref,
+    ext_ref, sources_ref, edges_ref, agg_grad_ref, sums_ref, rel_ref, blocks_ref,
 ):
     scale = (256 / 2048) ** 0.5
     first = [
@@ -318,10 +312,6 @@
         copies.start(cache_hbm, base_ref.at[pl.ds(16, 240), :]),
         copies.start(low_hbm.at[pl.ds(0, 64), :], base_ref.at[pl.ds(256, 64), :]),
         copies.start(high_hbm.at[pl.ds(0, 64), :], base_ref.at[pl.ds(320, 64), :]),
-        copies.start(e0_hbm, e0),
-        copies.start(e1_hbm, e1),
-        copies.start(e2_hbm, e2),
-        copies.start(e3_hbm, e3),
         copies.start(src_hot_hbm, src_hot_ref),
     ]
     second = [copies.start(dst_hot_t_hbm, dst_hot_t_ref)]
@@ -333,10 +323,6 @@
     fourth = [copies.start(dst_hot_hbm, dst_hot_ref)]
     base_ref[0:16, :] = jnp.zeros((16, 1024), BF)
     wait_all(first)
-    rel = e0[...].astype(F32) + e1[...].astype(F32) + e2[...].astype(F32) + e3[...].astype(F32)
-    for j in range(16):
-        rel_ref[j] = rel[j : j + 1]
-
     to = lanes((128, 128)) - sublanes((128, 128))
     inside = sublanes((128, 128)) < 64
     low_move = ((to == 0) & inside).astype(F32).astype(BF)
@@ -350,6 +336,9 @@
     total = arrived_ref[0:64, :].astype(F32)
     for i in range(1, 4):
         total = total + arrived_ref[i * 64 : (i + 1) * 64, :].astype(F32)
+    for j in range(16):
+        at = j // 4 * 16 + 12 + j % 4
+        rel_ref[j] = total[at : at + 1]
     table = total.astype(BF)
     ext_ref[...] = (base_ref[...].astype(F32) + dot_t(row_hot_t_ref[...], table)).astype(BF)
     nodes_ref[...] = ext_ref[0:256, :]
@@ -411,13 +400,15 @@
                 sums_ref[k * 4 + i, :, cols] = jnp.sum(product, axis=0, keepdims=True)
 
     blocks_ref[...] = jnp.concatenate([sums_ref[j] for j in range(16)], axis=0).astype(BF)
-    sent_out.append(copies.start(blocks_ref, blocks_hbm))
+    block = lanes((64, 16))
+    block_hot = (sublanes((64, 16)) == block // 4 * 16 + 12 + block % 4).astype(F32).astype(BF)
     own_pre = dot(own_hot_t_ref[...], pre_ref[...]).astype(BF)
 
     @pl.loop(0, 4)
     def _(n):
         cols = pl.ds(pl.multiple_of(n * 256, 256), 256)
         grad = dot(src_row_hot_ref[...], edges_ref[:, cols]) + dot_bt(own_pre, w_self_ref[cols, :])
+        grad = grad + dot(block_hot, blocks_ref[:, cols])
         table_out_ref[:, cols] = grad.astype(BF)
 
     for x in range(4):
@@ -434,7 +425,6 @@
     kept_ref, given_ref,
 ):
     core = where_ref[1]
-    places = ring_places(where_ref[2])
     wait_all(
         [copies.start(aggregate_hbm, aggregate_ref), copies.start(nodes_hbm, nodes_ref), copies.start(pre_hbm, pre_ref)]
     )
@@ -450,49 +440,9 @@
                 for y in range(4):
                     at = (x * 4 + y) * 8
                     both = jnp.concatenate([msg[at : at + 8], own[at : at + 8]], axis=0)
-                    chunk_ref[places[x], z * 4 + y] = both.astype(BF)
+                    chunk_ref[z * 16 + x * 4 + y] = both.astype(BF)
 
         sent_out.append(copies.start(chunk_ref, chunk_hbm))
-    wait_all(sent_out)
-
-
-def out_kernel(
-    copies,
-    where_ref,
-    returned_hbm, route_hbm, length_hbm, rel_hot_hbm, pooled_hbm, r0_hbm, r1_hbm, r2_hbm, r3_hbm,
-    given_hbm, kept_hbm, scaled_hbm,
-    returned_ref, route_ref, length_ref, rel_hot_ref, pooled_ref, r0, r1, r2, r3,
-    given_ref, kept_ref, scaled_ref,
-):
-    my_z, core, my_y = where_ref[0], where_ref[1], where_ref[3]
-    wait_all(
-        [
-            copies.start(returned_hbm, returned_ref),
-            copies.start(route_hbm, route_ref),
-            copies.start(length_hbm, length_ref),
-            copies.start(rel_hot_hbm, rel_hot_ref),
-            copies.start(pooled_hbm, pooled_ref),
-            copies.start(r0_hbm, r0),
-            copies.start(r1_hbm, r1),
-            copies.start(r2_hbm, r2),
-            copies.start(r3_hbm, r3),
-        ]
-    )
-    scaled_ref[...] = (dot(route_ref[...], returned_ref[...]) * length_ref[:, 0:1]).astype(BF)
-    sent_out = [copies.start(scaled_ref, scaled_hbm)]
-    blocks = jnp.concatenate([r0[...], r1[...], r2[...], r3[...]], axis=0)
-    places = ring_places(my_z)
-    for half, out_ref, out_hbm in ((1 - core, given_ref, given_hbm), (core, kept_ref, kept_hbm)):
-        for t in range(4):
-            owner = lax.rem(my_y + ORIGINS[t], 4)
-            units = pl.ds(pl.multiple_of(t * 256 + half * 128, 128), 128)
-            out = dot_t(pooled_ref[:, units], scaled_ref[...]).astype(BF)
-            rel_rows = pl.ds(pl.multiple_of(owner * 128 + half * 64, 64), 64)
-            rel = dot(rel_hot_ref[rel_rows, :], blocks).astype(BF)
-            for z in range(4):
-                out_ref[owner, places[z], 0:32, :] = out[z * 32 : (z + 1) * 32]
-                out_ref[owner, places[z], 32:48, :] = rel[z * 16 : (z + 1) * 16]
-        sent_out.append(copies.start(out_ref, out_hbm))
     wait_all(sent_out)
 
 
@@ -504,31 +454,35 @@
     return places
 
 
-def in_kernel(
+def back_kernel(
     copies,
     where_ref,
-    scaled_hbm, length_hbm, all_out_hbm, slope_hbm, normed_t_hbm,
+    returned_hbm, route_hbm, length_hbm, rel_hot_hbm, pooled_hbm, all_out_hbm, slope_hbm, normed_t_hbm,
     given_hbm, kept_hbm,
-    scaled_ref, length_ref, all_out_ref, slope_ref, normed_t_ref,
+    returned_ref, route_ref, length_ref, rel_hot_ref, pooled_ref, all_out_ref, slope_ref, normed_t_ref,
     given_ref, kept_ref,
-    grad_ref,
+    scaled_ref, grad_ref,
 ):
-    my_z, core = where_ref[0], where_ref[1]
-    wait_first = [
-        copies.start(scaled_hbm, scaled_ref),
+    my_z, core, my_y = where_ref[0], where_ref[1], where_ref[3]
+    first = [
+        copies.start(returned_hbm, returned_ref),
+        copies.start(route_hbm, route_ref),
         copies.start(length_hbm, length_ref),
-        copies.start(all_out_hbm, all_out_ref),
-        copies.start(slope_hbm, slope_ref),
+        copies.start(rel_hot_hbm, rel_hot_ref),
+        copies.start(pooled_hbm, pooled_ref),
     ]
-    wait_next = [copies.start(normed_t_hbm, normed_t_ref)]
+    second = [copies.start(all_out_hbm, all_out_ref), copies.start(slope_hbm, slope_ref)]
+    third = [copies.start(normed_t_hbm, normed_t_ref)]
     places = ring_places(my_z)
-    wait_all(wait_first)
     pools = []
+    wait_all(first)
+    scaled_ref[...] = (dot(route_ref[...], returned_ref[...]) * length_ref[:, 0:1]).astype(BF)
     for s in range(4):
         line = lanes((16, 256))
         length = 1.0 / length_ref[s * 16 : (s + 1) * 16, 0:1]
         inside = (line // 16 == sublanes((16, 256))) & ((line % 16).astype(F32) + 0.5 < length)
         pools.append(inside.astype(F32).astype(BF))
+    wait_all(second)
 
     @pl.loop(0, 4)
     def _(t):
@@ -539,20 +493,28 @@
             at_tokens = dot_t(pools[s], upstream[s * 16 : (s + 1) * 16])
             grad_ref[rows, cols] = (slope_ref[rows, cols].astype(F32) * at_tokens).astype(BF)
 
-    wait_all(wait_next)
+    wait_all(third)
     sent_out = []
-    for half, in_ref, in_hbm in ((1 - core, given_ref, given_hbm), (core, kept_ref, kept_hbm)):
+    for half, chunk_ref, chunk_hbm in ((1 - core, given_ref, given_hbm), (core, kept_ref, kept_hbm)):
 
         @pl.loop(0, 4)
         def _(t):
             cols = pl.ds(pl.multiple_of(t * 256, 256), 256)
+            origin = jnp.where(t == 0, 0, jnp.where(t == 1, 3, t - 1))
+            owner = lax.rem(my_y + origin, 4)
+            units = pl.ds(pl.multiple_of(t * 256 + half * 128, 128), 128)
+            out = dot_t(pooled_ref[:, units], scaled_ref[...]).astype(BF)
+            rel_rows = pl.ds(pl.multiple_of(owner * 128 + half * 64, 64), 64)
+            rel = dot(rel_hot_ref[rel_rows, :], returned_ref[...]).astype(BF)
             inner = dot(normed_t_ref[pl.ds(pl.multiple_of(half * 512, 512), 512), :], grad_ref[:, cols]).astype(BF)
             for z in range(4):
+                chunk_ref[t, places[z], 32:64, :] = out[z * 32 : (z + 1) * 32]
+                chunk_ref[t, places[z], 64:80, :] = rel[z * 16 : (z + 1) * 16]
                 for i in range(4):
                     piece = inner[z * 128 + i * 32 : z * 128 + (i + 1) * 32]
-                    in_ref[places[z], t, :, i * 256 : (i + 1) * 256] = piece
-
-        sent_out.append(copies.start(in_ref, in_hbm))
+                    chunk_ref[t, places[z], 0:32, i * 256 : (i + 1) * 256] = piece
+
+        sent_out.append(copies.start(chunk_ref, chunk_hbm))
     wait_all(sent_out)
 
 
@@ -606,8 +568,11 @@
     src, dst, rel = edge_src[0], edge_dst[0], edge_rel[0]
     shard_rows = rel_table.shape[0]
 
+    numbers = jnp.broadcast_to(rel.reshape(1, 4, 4), (4, 4, 4)).reshape(16, 4)
+    numbers = lax.all_to_all(jnp.pad(numbers, ((0, 0), (0, 124))), GROUP, 0, 0, tiled=True)
+
     rel_pad = jnp.pad(rel_table, ((0, 64 - shard_rows), (0, 0)))
-    operands = [hidden.reshape(tokens, width), desc_len[None, :], send_order, edge_rel]
+    operands = [hidden.reshape(tokens, width), desc_len[None, :], send_order]
     outs = [((tokens + 16, width), BF), ((entities, width), F32), ((576, 512), BF)]
     block, hidden_sum, weights = local_call(
         norm_kernel,
@@ -628,12 +593,12 @@
         ((4 * units, width), BF),
         ((4 * entities, 256), BF),
         ((4 * entities, 128), F32),
-        ((512, 64), BF),
-    ] + [((entities, width), BF)] * 4
-    outgoing, normed, slope, pooled, all_out, route, inverse, rel_hot, *asked = local_call(
+        ((512, 256), BF),
+    ]
+    outgoing, normed, slope, pooled, all_out, route, inverse, rel_hot = local_call(
         encode_kernel,
         outs,
-        [where, *blocks, w_in, w_out, rel_pad, *mine, *other, hidden_sum],
+        [where, *blocks, w_in, w_out, rel_pad, *mine, *other, hidden_sum, numbers],
         filled(outs)
         + [
             pltpu.VMEM((width, 4 * units), BF),
@@ -641,6 +606,7 @@
             pltpu.VMEM((256, width), BF),
             pltpu.VMEM((4, 16, 128), BF),
             pltpu.VMEM((entities, width), F32),
+            pltpu.VMEM((16, 128), I32),
         ],
         copies=64,
         flops=2 * 4 * tokens * width * 4 * units,
@@ -668,14 +634,12 @@
     block_count = rel.shape[0]
     src_hot = one_hot(src, extended_count)
     arrived = lax.all_to_all(outgoing.reshape(16, 16, width), GROUP, 0, 0, tiled=True).reshape(256, width)
-    rel_rows = [asked[0]] + [shift_by(rows, "x", o) for rows, o in zip(asked[1:], ORIGINS[1:])]
     arrived, normed_t = lax.optimization_barrier((arrived, normed.T))
 
-    outs = [((256, width), BF), ((block_count, width), BF)] + [((node_count, width), BF)] * 4
+    outs = [((256, width), BF)] + [((node_count, width), BF)] * 4
     operands = [
         arrived,
         one_hot_t(own_row, 64),
-        *rel_rows,
         src_hot,
         one_hot(dst, node_count),
         one_hot_t(dst, node_count),
@@ -683,7 +647,7 @@
         w_self,
         d_out,
     ]
-    grad_table, grad_blocks, graph_out, aggregate, nodes, grad_pre = local_call(
+    grad_table, graph_out, aggregate, nodes, grad_pre = local_call(
         graph_kernel,
         outs,
         [where, *operands, cache, from_low, from_high],
@@ -700,49 +664,40 @@
             pltpu.VMEM((node_count, width), BF),
             pltpu.VMEM((block_count, 1, width), F32),
             pltpu.VMEM((block_count, 1, width), F32),
+            pltpu.VMEM((block_count, width), BF),
         ],
         copies=30,
         flops=6 * 10**9,
     )
 
     returned = lax.all_to_all(grad_table.reshape(16, 16, width), GROUP, 0, 0, tiled=True).reshape(256, width)
-    rel_blocks = [grad_blocks] + [shift_by(grad_blocks, "x", s) for s in SHIFTS]
-
-    outs = [((4, 16, 16, width), BF)] * 2
-    grad_pre, *rel_blocks = lax.optimization_barrier((grad_pre, *rel_blocks))
+
+    outs = [((64, 16, width), BF)] * 2
     operands = [aggregate, nodes, grad_pre]
     graph_kept, graph_given = local_call(
         weight_kernel, outs, [where, *operands], like(operands) + filled(outs), flops=10**9
     )
+    returned, graph_kept, graph_given = lax.optimization_barrier((returned, graph_kept, graph_given))
     chip = (graph_kept.astype(F32) + shift_by(graph_given, "core", 1).astype(F32)).astype(BF)
-    outs = [((4, 4, 48, width), BF)] * 2 + [((4 * entities, width), BF)]
-    operands = [returned, route, inverse, rel_hot, pooled, *rel_blocks]
-    out_given, out_kept, scaled = local_call(
-        out_kernel, outs, [where, *operands], like(operands) + filled(outs), copies=12, flops=10**9
-    )
-    out_chip = (out_kept.astype(F32) + shift_by(out_given, "core", 1).astype(F32)).astype(BF)
-    scaled, out_chip, chip = lax.optimization_barrier((scaled, out_chip, chip))
-    out_lines = lax.all_to_all(out_chip, "y", 0, 0, tiled=True)
-    outs = [((4, 4, 32, width), BF)] * 2
-    operands = [scaled, inverse, all_out, slope, normed_t]
-    in_given, in_kept = local_call(
-        in_kernel,
+    plane = lax.all_to_all(chip, ("z", "x", "y"), 0, 0, tiled=True)
+    weight_rows = jnp.sum(plane.astype(F32), axis=0)
+    grad_msg, grad_self = weight_rows[:8], weight_rows[8:]
+
+    outs = [((4, 4, 80, width), BF)] * 2
+    operands = [returned, route, inverse, rel_hot, pooled, all_out, slope, normed_t]
+    given, kept = local_call(
+        back_kernel,
         outs,
         [where, *operands],
-        like(operands) + filled(outs) + [pltpu.VMEM((4 * tokens, 4 * units), BF)],
-        flops=10 * 4 * tokens * width * 4 * units,
-    )
-
-    line = reduce_ring([chip[i] for i in range(4)], "x")
-    plane = lax.all_to_all(line, ("z", "y"), 0, 0, tiled=True)
-    weight_rows = jnp.sum(plane.astype(F32), axis=0)
-    grad_msg, grad_self = weight_rows[:8], weight_rows[8:]
-    in_chip = (in_kept.astype(F32) + shift_by(in_given, "core", 1).astype(F32)).astype(BF)
-    out_part = jnp.sum(out_lines.astype(F32), axis=0).astype(BF)
-    in_part = reduce_ring([in_chip[i].reshape(128, width) for i in range(4)], "z").reshape(4, 32, width)
-    out_part = reduce_ring([out_part[i] for i in range(4)], "z")
-    in_part = reduce_ring([in_part[i] for i in range(4)], "y")
-    part = jnp.concatenate([in_part, out_part], axis=0)
+        like(operands)
+        + filled(outs)
+        + [pltpu.VMEM((4 * entities, width), BF), pltpu.VMEM((4 * tokens, 4 * units), BF)],
+        copies=12,
+        flops=2 * 4 * tokens * width * 4 * units,
+    )
+    mixed = (kept.astype(F32) + shift_by(given, "core", 1).astype(F32)).astype(BF)
+    part = reduce_ring([mixed[i].reshape(320, width) for i in range(4)], "y").reshape(4, 80, width)
+    part = reduce_ring([part[i] for i in range(4)], "z")
     parts = [part] + [shift_by(part, "z", s) for s in SHIFTS]
     others = [shift_by(piece, "core", 1) for piece in parts]
     outs = [((width, units), F32), ((units, width), F32), ((shard_rows, width), F32)]

time: 223 us -> 230 us (1.031)
  waiting for transfers between devices: 53.4 us -> 88 us
  starting transfers between devices: 77.6 us -> 56.1 us
  Pallas kernels: 61.2 us -> 58.9 us
    ppermute x42 -> x29, waiting for transfers between devices: 53.4 us -> 81.4 us  [shift_by(): lax.ppermute(value, axis, [(i, (i + shift) % count) for i in range(count)])]
    ppermute x42 -> x29, starting transfers between devices: 53.9 us -> 30.3 us  [shift_by(): lax.ppermute(value, axis, [(i, (i + shift) % count) for i in range(count)])]
    all_to_all x1, waiting for transfers between devices: 0.01 us -> 4.45 us  [shards(): lax.all_to_all(grad_table.reshape(16, 16, width), GROUP, 0, 0, tiled=True)]
    all_to_all x2, starting transfers between devices: 12.2 us -> 15.1 us  [the longest x1 7.83 us: shards(): plane = lax.all_to_all(chip, ('z', 'x', 'y'), 0, 0, tiled=True)]
    pallas_call x7 -> x6, Pallas kernels: 61.2 us -> 58.9 us  [local_call(): pl.pallas_call(kernel, out_shape=[jax.ShapeDtypeStruct(shape, kind) for s...]
    unnamed x74 -> x53, local copies, waits for them, and re-layouts: 5.22 us -> 4.15 us
  transfers between devices with their start and end apart: 46 -> 33, of which waited for: 15 -> 16; matrix products, arithmetic and copies ran while one was open for 8% -> 8% of each run, Pallas kernels for 5% -> 4%
where the time goes in v6:
time: 230 us; the launch traced here: 229 us
  waiting for transfers between devices  88 us (38%)
  Pallas kernels  58.9 us (26%)
  starting transfers between devices  56.1 us (24%)
  other arithmetic  13.7 us (6%)
  local copies, waits for them, and re-layouts  10.4 us (5%)
    ppermute x29, waiting for transfers between devices, shift_by(): lax.ppermute(value, axis, [(i, (i + shift) % count) for i in range(count)])  81.4 us
    pallas_call x6, Pallas kernels, local_call(): pl.pallas_call(kernel, out_shape=[jax.ShapeDtypeStruct(shape, kind) for s...  58.9 us
    ppermute x29, starting transfers between devices, shift_by(): lax.ppermute(value, axis, [(i, (i + shift) % count) for i in range(count)])  30.3 us
    all_to_all x1, starting transfers between devices, shards(): plane = lax.all_to_all(chip, ('z', 'x', 'y'), 0, 0, tiled=True)  7.83 us
    all_to_all x1, starting transfers between devices, shards(): lax.all_to_all(jnp.pad(numbers, ((0, 0), (0, 124))), GROUP, 0, 0, tiled=T...  7.28 us
    all_to_all x1, starting transfers between devices, shards(): lax.all_to_all(outgoing.reshape(16, 16, width), GROUP, 0, 0, tiled=True)  7.13 us
  transfers between devices with their start and end apart: 33, of which 16 were waited for; matrix products, arithmetic and copies ran while one was open for 8% of the time, Pallas kernels for 4%

profile of v6, /device:TPU:0, one launch (start us, length us, event | category | flops | bytes accessed | tf_op | source)
XLA Modules:
  0.0 228.7 jit_solution(7028241186582327969)
XLA Ops:
  0.7 1.6 pad.27.refs_6_.refs_8_
  2.3 0.7 pad_add_fusion.refs_0_
  3.0 3.3 %shard_map.190 = (bf16[272,1024]{1,0:T(8,128)(2,1)}, f32[16,1024]{1,0:T(8,128)}, bf16[576,512]{1,0:T(8,128)(2,1)}) custom-call(s32[4]{0:T(128)} %pad_add_fusion.refs_0_, bf16[256,1024]{1,0:T(8,128)(2,1)} %bitcast.34, s32[1,16]{1,0:T(1,128)} %bitcast.43, s32[1,16]{1,0:T(1,128)} %refs_3_.1, bf16[1024,256]{1,0:T(8,128)(2,1)} %refs_6_.2, ...), custom_call_target="tpu_custom_call" | custom-call | bytes 1048576 | tf_op jit(solution)/shard_map/pallas_call | solution.py:88
  6.3 3.2 %collective-permute-start.5 = (bf16[576,512]{1,0:T(8,128)(2,1)}, bf16[576,512]{1,0:T(8,128)(2,1)S(1)}, u32[]{:S(2)}, u32[]{:S(2)}) collective-permute-start(bf16[576,512]{1,0:T(8,128)(2,1)} %get-tuple-element.38), channel_id=1, source_target_pairs={{0,3},{1,0},{2,1},{3,2},{4,7},{5,4},{6,5},{7,6},{8,11},{9,8},{10,9... | collective-permute-start | bytes 1769480 | tf_op jit(solution)/shard_map/ppermute | solution.py:22
  9.5 2.8 %collective-permute-start.1 = (bf16[272,1024]{1,0:T(8,128)(2,1)}, bf16[272,1024]{1,0:T(8,128)(2,1)S(1)}, u32[]{:S(2)}, u32[]{:S(2)}) collective-permute-start(bf16[272,1024]{1,0:T(8,128)(2,1)} %get-tuple-element.37.refs_1_), channel_id=1, source_target_pairs={{0,12},{4,0},{8,4},{12,8},{1,13},{5,1},{9,5},{13,9},{2,14},{6,2},{... | collective-permute-start | bytes 1671176 | tf_op jit(solution)/shard_map/ppermute | solution.py:22
  12.2 0.5 broadcast.63
  12.7 1.3 reduce.3
  14.1 0.1 copy.27
  14.3 0.7 copy.28
  15.0 7.3 %all-to-all-start = ((s32[16,1,128]{2,1,0:T(1,128)}), s32[16,1,128]{2,1,0:T(1,128)S(1)}, u32[]{:S(2)}, u32[]{:S(2)}) async-start(s32[16,1,128]{2,1,0:T(1,128)} %copy.28), calls=%async_computation | async-start | bytes 16384 | tf_op jit(solution)/shard_map/all_to_all | solution.py:572
  22.4 1.3 fusion.1.refs_4_
  23.7 0.3 convolution_convert_fusion
  24.0 1.4 fusion.refs_3_
  25.4 2.1 collective-permute-done.refs_2_
  27.7 3.0 %collective-permute-start.7 = (bf16[320,512]{1,0:T(8,128)(2,1)S(1)}, bf16[320,512]{1,0:T(8,128)(2,1)}, u32[]{:S(2)}, u32[]{:S(2)}) collective-permute-start(bf16[320,512]{1,0:T(8,128)(2,1)S(1)} %slice.83), channel_id=1, source_target_pairs={{0,3},{1,0},{2,1},{3,2},{4,7},{5,4},{6,5},{7,6},{8,11},{9,8},{10,9... | collective-permute-start | bytes 983048 | tf_op jit(solution)/shard_map/ppermute | solution.py:22
  30.9 0.5 collective-permute-start.9
  31.6 3.8 %collective-permute-done.2.refs_4_ = bf16[128,1024]{1,0:T(8,128)(2,1)S(1)} collective-permute-done((bf16[128,1024]{1,0:T(8,128)(2,1)S(1)}, bf16[128,1024]{1,0:T(8,128)(2,1)S(1)}, u32[]{:S(2)}, u32[]{:S(2)}) %collective-permute-start.2) | collective-permute-done | bytes 262176 | tf_op jit(solution)/shard_map/ppermute | solution.py:22
  35.3 3.1 %collective-permute-done.6.refs_11_ = bf16[256,512]{1,0:T(8,128)(2,1)} collective-permute-done((bf16[256,512]{1,0:T(8,128)(2,1)S(1)}, bf16[256,512]{1,0:T(8,128)(2,1)}, u32[]{:S(2)}, u32[]{:S(2)}) %collective-permute-start.6) | collective-permute-done | bytes 262176 | tf_op jit(solution)/shard_map/ppermute | solution.py:22
  38.5 0.5 collective-permute-start.11
  39.1 3.1 %collective-permute-done.3.refs_5_ = bf16[144,1024]{1,0:T(8,128)(2,1)} collective-permute-done((bf16[144,1024]{1,0:T(8,128)(2,1)S(1)}, bf16[144,1024]{1,0:T(8,128)(2,1)}, u32[]{:S(2)}, u32[]{:S(2)}) %collective-permute-start.3) | collective-permute-done | bytes 294944 | tf_op jit(solution)/shard_map/ppermute | solution.py:22
  42.3 0.8 copy-done.21
  43.0 11.8 %shard_map.191 = (bf16[256,1024]{1,0:T(8,128)(2,1)}, bf16[1024,1024]{1,0:T(8,128)(2,1)}, bf16[1024,1024]{1,0:T(8,128)(2,1)}, bf16[64,1024]{1,0:T(8,128)(2,1)}, b...) custom-call(s32[4]{0:T(128)} %pad_add_fusion.refs_0_, ...), custom_call_target="tpu_custom_call" | custom-call | flops 2147483648 | bytes 1048576 | tf_op jit(solution)/shard_map/pallas_call | solution.py:88
  54.8 7.1 %all-to-all-start.1 = ((bf16[16,16,1024]{2,1,0:T(8,128)(2,1)}), bf16[16,16,1024]{2,1,0:T(8,128)(2,1)S(1)}, u32[]{:S(2)}, u32[]{:S(2)}) async-start(bf16[16,16,1024]{2,1,0:T(8,128)(2,1)} %bitcast.35), calls=%async_computation.1 | async-start | bytes 1048576 | tf_op jit(solution)/shard_map/all_to_all | solution.py:636
  62.0 1.2 fusion.2.refs_5_
  63.2 1.9 collective-permute-start.12
  65.1 3.4 %collective-permute-start.13 = (bf16[80,1024]{1,0:T(8,128)(2,1)S(1)}, bf16[80,1024]{1,0:T(8,128)(2,1)S(1)}, u32[]{:S(2)}, u32[]{:S(2)}) collective-permute-start(bf16[80,1024]{1,0:T(8,128)(2,1)S(1)} %get-tuple-element.45), channel_id=1, source_target_pairs={{0,15},{1,0},{2,1},{3,2},{4,3},{5,4},{6,5},{7,6},{8,7},{9,8},{10,9... | collective-permute-start | bytes 491528 | tf_op jit(solution)/shard_map/ppermute | solution.py:22
  68.5 0.6 fusion.11.refs_2_
  69.1 2.5 %copy.29 = bf16[1024,1024]{0,1:T(8,128)(2,1)} copy(bf16[1024,1024]{1,0:T(8,128)(2,1)S(1)} %copy-done.1) | data formatting | bytes 4194304 | tf_op jit(solution)/shard_map/pallas_call | solution.py:88
  71.7 2.2 all-to-all-done.1
  73.9 2.1 collective-permute-done.12.refs_10_
  75.9 0.7 copy-done.23
  76.6 0.7 copy-done.24
  77.2 20.8 %shard_map.192 = (bf16[256,1024]{1,0:T(8,128)(2,1)}, bf16[256,1024]{1,0:T(8,128)(2,1)}, bf16[256,1024]{1,0:T(8,128)(2,1)}, bf16[256,1024]{1,0:T(8,128)(2,1)}, bf16[256,1024]{1,0:T(8,128)(2,1)}) custom-call(s32[4]{0:T(128)} %pad_add_fusion.refs_0_, bf16[256,1024]{1,0:T(8,128)(2,1)} %bitcast.36, bf16[64,256]{1,0:T(8,128)(2,1)} %fusion.11.refs_2_, ...), custom_call_target="tpu_custom_call" | custom-call | flops 6000000000 | bytes 1048576 | tf_op jit(solution)/shard_map/pallas_call | solution.py:88
  98.0 3.6 %all-to-all-start.2 = ((bf16[16,16,1024]{2,1,0:T(8,128)(2,1)}), bf16[16,16,1024]{2,1,0:T(8,128)(2,1)S(1)}, u32[]{:S(2)}, u32[]{:S(2)}) async-start(bf16[16,16,1024]{2,1,0:T(8,128)(2,1)} %bitcast.38), calls=%async_computation.2 | async-start | bytes 1048576 | tf_op jit(solution)/shard_map/all_to_all | solution.py:673
  101.6 6.2 %shard_map.193 = (bf16[64,16,1024]{2,1,0:T(8,128)(2,1)}, bf16[64,16,1024]{2,1,0:T(8,128)(2,1)}) custom-call(s32[4]{0:T(128)} %pad_add_fusion.refs_0_, bf16[256,1024]{1,0:T(8,128)(2,1)} %get-tuple-element.48.refs_1_, bf16[256,1024]{1,0:T(8,128)(2,1)} %get-tuple-element.49.refs_2_, bf16[256,1024]{1,0:T(8,128)(2,1)} %get-tuple-element.50.refs_3_), custom_call_target="tpu_custom_call" | custom-call | flops 1000000000 | bytes 1048576 | tf_op jit(solution)/shard_map/pallas_call | solution.py:88
  107.8 4.5 %all-to-all-done.2 = bf16[16,16,1024]{2,1,0:T(8,128)(2,1)S(1)} async-done(((bf16[16,16,1024]{2,1,0:T(8,128)(2,1)}), bf16[16,16,1024]{2,1,0:T(8,128)(2,1)S(1)}, u32[]{:S(2)}, u32[]{:S(2)}) %all-to-all-start.2) | async-done | bytes 524320 | tf_op jit(solution)/shard_map/all_to_all | solution.py:673
  112.3 0.8 copy-done.4
  113.1 13.2 %shard_map.194 = (bf16[4,4,80,1024]{3,2,1,0:T(8,128)(2,1)}, bf16[4,4,80,1024]{3,2,1,0:T(8,128)(2,1)}) custom-call(s32[4]{0:T(128)} %pad_add_fusion.refs_0_, bf16[256,1024]{1,0:T(8,128)(2,1)} %bitcast.37, bf16[64,256]{1,0:T(8,128)(2,1)} %get-tuple-element.54.refs_2_, f32[64,128]{1,0:T(8,128)} %get-tuple-element.55.refs_3_, ...), custom_call_target="tpu_custom_call" | custom-call | flops 2147483648 | bytes 1048576 | tf_op jit(solution)/shard_map/pallas_call | solution.py:88
  126.4 0.5 collective-permute-start.28
  126.9 7.6 %collective-permute-done.28 = bf16[64,16,1024]{2,1,0:T(8,128)(2,1)S(1)} collective-permute-done((bf16[64,16,1024]{2,1,0:T(8,128)(2,1)}, bf16[64,16,1024]{2,1,0:T(8,128)(2,1)S(1)}, u32[]{:S(2)}, u32[]{:S(2)}) %collective-permute-start.28) | collective-permute-done | bytes 2097184 | tf_op jit(solution)/shard_map/ppermute | solution.py:22
  134.5 2.4 %add_convert_fusion.1 = bf16[64,16,1024]{2,1,0:T(8,128)(2,1)} fusion(bf16[64,16,1024]{2,1,0:T(8,128)(2,1)S(1)} %collective-permute-done.28, bf16[64,16,1024]{2,1,0:T(8,128)(2,1)S(1)} %copy-done), kind=kLoop, calls=%fused_computation.2 | loop fusion | flops 4194304 | bytes 6291456 | tf_op jit(solution)/shard_map/convert_element_type | solution.py:681
  136.9 7.8 %all-to-all-start.3 = ((bf16[64,16,1024]{2,1,0:T(8,128)(2,1)}), bf16[64,16,1024]{2,1,0:T(8,128)(2,1)S(1)}, u32[]{:S(2)}, u32[]{:S(2)}) async-start(bf16[64,16,1024]{2,1,0:T(8,128)(2,1)} %add_convert_fusion.1), calls=%async_computation.3 | async-start | bytes 4194304 | tf_op jit(solution)/shard_map/all_to_all | solution.py:682
  144.8 3.8 %add_convert_fusion = bf16[4,4,80,1024]{3,2,1,0:T(8,128)(2,1)S(1)} fusion(bf16[4,4,80,1024]{3,2,1,0:T(8,128)(2,1)} %collective-permute-done.14, bf16[4,4,80,1024]{3,2,1,0:T(8,128)(2,1)} %get-tuple-element.61), kind=kLoop, calls=%fused_computation | loop fusion | flops 5242880 | bytes 7864320 | tf_op jit(solution)/shard_map/convert_element_type | solution.py:698
  148.6 0.3 fusion.16
  148.9 2.9 %collective-permute-start.15 = (bf16[320,1024]{1,0:T(8,128)(2,1)S(1)}, bf16[320,1024]{1,0:T(8,128)(2,1)S(1)}, u32[]{:S(2)}, u32[]{:S(2)}) collective-permute-start(bf16[320,1024]{1,0:T(8,128)(2,1)S(1)} %bitcast.33), channel_id=1, source_target_pairs={{0,3},{1,0},{2,1},{3,2},{4,7},{5,4},{6,5},{7,6},{8,11},{9,8},{10,9... | collective-permute-start | bytes 1966088 | tf_op jit(solution)/shard_map/ppermute | solution.py:22
  151.7 2.3 %collective-permute-start.17 = (bf16[320,1024]{1,0:T(8,128)(2,1)S(1)}, bf16[320,1024]{1,0:T(8,128)(2,1)S(1)}, u32[]{:S(2)}, u32[]{:S(2)}) collective-permute-start(bf16[320,1024]{1,0:T(8,128)(2,1)S(1)} %bitcast.31), channel_id=1, source_target_pairs={{0,2},{1,3},{2,0},{3,1},{4,6},{5,7},{6,4},{7,5},{8,10},{9,11},{10,... | collective-permute-start | bytes 1966088 | tf_op jit(solution)/shard_map/ppermute | solution.py:22
  154.0 30.4 %collective-permute-done.15 = bf16[320,1024]{1,0:T(8,128)(2,1)S(1)} collective-permute-done((bf16[320,1024]{1,0:T(8,128)(2,1)S(1)}, bf16[320,1024]{1,0:T(8,128)(2,1)S(1)}, u32[]{:S(2)}, u32[]{:S(2)}) %collective-permute-start.15) | collective-permute-done | bytes 655392 | tf_op jit(solution)/shard_map/ppermute | solution.py:22
  184.4 0.7 collective-permute-done.16
  185.1 13.5 %collective-permute-done.17 = bf16[320,1024]{1,0:T(8,128)(2,1)S(1)} collective-permute-done((bf16[320,1024]{1,0:T(8,128)(2,1)S(1)}, bf16[320,1024]{1,0:T(8,128)(2,1)S(1)}, u32[]{:S(2)}, u32[]{:S(2)}) %collective-permute-start.17) | collective-permute-done | bytes 655392 | tf_op jit(solution)/shard_map/ppermute | solution.py:22
  198.6 0.4 fusion.5
  199.1 3.0 %collective-permute-start.18 = (bf16[80,1024]{1,0:T(8,128)(2,1)S(1)}, bf16[80,1024]{1,0:T(8,128)(2,1)S(1)}, u32[]{:S(2)}, u32[]{:S(2)}) collective-permute-start(bf16[80,1024]{1,0:T(8,128)(2,1)S(1)} %get-tuple-element.72), channel_id=1, source_target_pairs={{0,96},{32,0},{64,32},{96,64},{1,97},{33,1},{65,33},{97,65},{2,98}... | collective-permute-start | bytes 491528 | tf_op jit(solution)/shard_map/ppermute | solution.py:22
  202.1 2.2 collective-permute-start.20
  204.3 2.4 %collective-permute-done.18 = bf16[80,1024]{1,0:T(8,128)(2,1)S(1)} collective-permute-done((bf16[80,1024]{1,0:T(8,128)(2,1)S(1)}, bf16[80,1024]{1,0:T(8,128)(2,1)S(1)}, u32[]{:S(2)}, u32[]{:S(2)}) %collective-permute-start.18) | collective-permute-done | bytes 163872 | tf_op jit(solution)/shard_map/ppermute | solution.py:22
  206.7 4.9 %collective-permute-done.19 = bf16[80,1024]{1,0:T(8,128)(2,1)S(1)} collective-permute-done((bf16[80,1024]{1,0:T(8,128)(2,1)S(1)}, bf16[80,1024]{1,0:T(8,128)(2,1)S(1)}, u32[]{:S(2)}, u32[]{:S(2)}) %collective-permute-start.19) | collective-permute-done | bytes 163872 | tf_op jit(solution)/shard_map/ppermute | solution.py:22
  211.6 0.1 add_convert_fusion.2.refs_1_
  211.8 3.2 %collective-permute-start.22 = (bf16[80,1024]{1,0:T(8,128)(2,1)S(1)}, bf16[80,1024]{1,0:T(8,128)(2,1)S(1)}, u32[]{:S(2)}, u32[]{:S(2)}) collective-permute-start(bf16[80,1024]{1,0:T(8,128)(2,1)S(1)} %add_convert_fusion.2.refs_1_), channel_id=1, source_target_pairs={{0,96},{32,0},{64,32},{96,64},{1,97},{33,1},{65,33},{97,65},{2,98}... | collective-permute-start | bytes 491528 | tf_op jit(solution)/shard_map/ppermute | solution.py:22
  215.0 4.6 %collective-permute-done.21.refs_2_ = bf16[80,1024]{1,0:T(8,128)(2,1)S(1)} collective-permute-done((bf16[80,1024]{1,0:T(8,128)(2,1)S(1)}, bf16[80,1024]{1,0:T(8,128)(2,1)S(1)}, u32[]{:S(2)}, u32[]{:S(2)}) %collective-permute-start.21) | collective-permute-done | bytes 163872 | tf_op jit(solution)/shard_map/ppermute | solution.py:22
  219.6 0.5 collective-permute-start.26
  220.1 1.7 collective-permute-done.23.refs_4_
  221.9 1.3 collective-permute-done.27.refs_8_
  223.3 0.7 copy-done.13
  224.0 3.7 %shard_map.195 = (f32[1024,256]{1,0:T(8,128)}, f32[256,1024]{1,0:T(8,128)}, f32[52,1024]{1,0:T(8,128)}) custom-call(s32[4]{0:T(128)} %pad_add_fusion.refs_0_, bf16[80,1024]{1,0:T(8,128)(2,1)} %copy-done.2, bf16[80,1024]{1,0:T(8,128)(2,1)} %copy-done.7, bf16[80,1024]{1,0:T(8,128)(2,1)} %copy-done.8, bf16[80,1024]{1,0:T(8,128)(2,1)} %copy-done.9, ...), custom_call_target="tpu_custom_call" | custom-call | bytes 1048576 | tf_op jit(solution)/shard_map/pallas_call | solution.py:88
  227.7 0.4 convert_reduce_fusion
  228.0 0.6 fusion.19
  (99 shorter events, 1.1 us)
Async XLA Ops:
  0.6 21.7 %copy-start.20 = (s32[1,128]{1,0:T(1,128)S(1)}, s32[1,128]{1,0:T(1,128)}, u32[]{:S(2)}) copy-start(s32[1,128]{1,0:T(1,128)} %param.22) | copy-start | bytes 1540
  0.6 21.7 %copy-start.25 = (s32[1,16]{1,0:T(1,128)S(1)}, s32[1,16]{1,0:T(1,128)}, u32[]{:S(2)}) copy-start(s32[1,16]{1,0:T(1,128)} %param.20) | copy-start | bytes 196
  0.7 21.8 %copy-start.17 = (s32[1,2048]{1,0:T(1,128)S(1)}, s32[1,2048]{1,0:T(1,128)}, u32[]{:S(2)}) copy-start(s32[1,2048]{1,0:T(1,128)} %param.24) | copy-start | bytes 24580
  0.7 23.1 %copy-start.5 = (bf16[240,1024]{1,0:T(8,128)(2,1)S(1)}, bf16[240,1024]{1,0:T(8,128)(2,1)}, u32[]{:S(2)}) copy-start(bf16[240,1024]{1,0:T(8,128)(2,1)} %refs_9_.1) | copy-start | bytes 1474564
  0.7 23.3 %copy-start.18 = (s32[1,2048]{1,0:T(1,128)S(1)}, s32[1,2048]{1,0:T(1,128)}, u32[]{:S(2)}) copy-start(s32[1,2048]{1,0:T(1,128)} %param.23) | copy-start | bytes 24580
  6.3 21.3 %collective-permute-start.5 = (bf16[576,512]{1,0:T(8,128)(2,1)}, bf16[576,512]{1,0:T(8,128)(2,1)S(1)}, u32[]{:S(2)}, u32[]{:S(2)}) collective-permute-start(bf16[576,512]{1,0:T(8,128)(2,1)} %get-tuple-element.38), channel_id=1, source_target_pairs={{0,3},{1,0},{2,1},{3,2},{4,7},{5,4},{6,5},{7,6},{8,11},{9,8},{10,9... | collective-permute-start | bytes 1769480 | tf_op jit(solution)/shard_map/ppermute | solution.py:22
  9.5 21.2 %collective-permute-start.4 = (bf16[576,512]{1,0:T(8,128)(2,1)}, bf16[576,512]{1,0:T(8,128)(2,1)S(1)}, u32[]{:S(2)}, u32[]{:S(2)}) collective-permute-start(bf16[576,512]{1,0:T(8,128)(2,1)} %get-tuple-element.38), channel_id=1, source_target_pairs={{0,1},{1,2},{2,3},{3,0},{4,5},{5,6},{6,7},{7,4},{8,9},{9,10},{10,1... | collective-permute-start | bytes 1769480 | tf_op jit(solution)/shard_map/ppermute | solution.py:22
  9.5 21.4 %collective-permute-start.1 = (bf16[272,1024]{1,0:T(8,128)(2,1)}, bf16[272,1024]{1,0:T(8,128)(2,1)S(1)}, u32[]{:S(2)}, u32[]{:S(2)}) collective-permute-start(bf16[272,1024]{1,0:T(8,128)(2,1)} %get-tuple-element.37.refs_1_), channel_id=1, source_target_pairs={{0,12},{4,0},{8,4},{12,8},{1,13},{5,1},{9,5},{13,9},{2,14},{6,2},{... | collective-permute-start | bytes 1671176 | tf_op jit(solution)/shard_map/ppermute | solution.py:22
  12.2 15.3 %collective-permute-start = (bf16[272,1024]{1,0:T(8,128)(2,1)}, bf16[272,1024]{1,0:T(8,128)(2,1)S(1)}, u32[]{:S(2)}, u32[]{:S(2)}) collective-permute-start(bf16[272,1024]{1,0:T(8,128)(2,1)} %get-tuple-element.37.refs_1_), channel_id=1, source_target_pairs={{0,4},{4,8},{8,12},{12,0},{1,5},{5,9},{9,13},{13,1},{2,6},{6,10},{... | collective-permute-start | bytes 1671176 | tf_op jit(solution)/shard_map/ppermute | solution.py:22
  15.0 24.1 %all-to-all-start = ((s32[16,1,128]{2,1,0:T(1,128)}), s32[16,1,128]{2,1,0:T(1,128)S(1)}, u32[]{:S(2)}, u32[]{:S(2)}) async-start(s32[16,1,128]{2,1,0:T(1,128)} %copy.28), calls=%async_computation | async-start | bytes 16384 | tf_op jit(solution)/shard_map/all_to_all | solution.py:572
  27.5 14.7 %copy-start.15 = (bf16[272,1024]{1,0:T(8,128)(2,1)}, bf16[272,1024]{1,0:T(8,128)(2,1)S(1)}, u32[]{:S(2)}) copy-start(bf16[272,1024]{1,0:T(8,128)(2,1)S(1)} %collective-permute-done.refs_2_) | copy-start | bytes 1671172
  27.5 7.8 %collective-permute-start.2 = (bf16[128,1024]{1,0:T(8,128)(2,1)S(1)}, bf16[128,1024]{1,0:T(8,128)(2,1)S(1)}, u32[]{:S(2)}, u32[]{:S(2)}) collective-permute-start(bf16[128,1024]{1,0:T(8,128)(2,1)S(1)} %slice.80), channel_id=1, source_target_pairs={{0,4},{4,8},{8,12},{12,0},{1,5},{5,9},{9,13},{13,1},{2,6},{6,10},{... | collective-permute-start | bytes 786440 | tf_op jit(solution)/shard_map/ppermute | solution.py:22
  27.6 14.6 %copy-start.6 = (bf16[576,512]{1,0:T(8,128)(2,1)}, bf16[576,512]{1,0:T(8,128)(2,1)S(1)}, u32[]{:S(2)}) copy-start(bf16[576,512]{1,0:T(8,128)(2,1)S(1)} %collective-permute-done.5.refs_10_) | copy-start | bytes 1769476
  27.7 10.8 %collective-permute-start.7 = (bf16[320,512]{1,0:T(8,128)(2,1)S(1)}, bf16[320,512]{1,0:T(8,128)(2,1)}, u32[]{:S(2)}, u32[]{:S(2)}) collective-permute-start(bf16[320,512]{1,0:T(8,128)(2,1)S(1)} %slice.83), channel_id=1, source_target_pairs={{0,3},{1,0},{2,1},{3,2},{4,7},{5,4},{6,5},{7,6},{8,11},{9,8},{10,9... | collective-permute-start | bytes 983048 | tf_op jit(solution)/shard_map/ppermute | solution.py:22
  30.7 11.5 %copy-start.16 = (bf16[576,512]{1,0:T(8,128)(2,1)}, bf16[576,512]{1,0:T(8,128)(2,1)S(1)}, u32[]{:S(2)}) copy-start(bf16[576,512]{1,0:T(8,128)(2,1)S(1)} %collective-permute-done.4.refs_9_) | copy-start | bytes 1769476
  30.7 7.8 %collective-permute-start.6 = (bf16[256,512]{1,0:T(8,128)(2,1)S(1)}, bf16[256,512]{1,0:T(8,128)(2,1)}, u32[]{:S(2)}, u32[]{:S(2)}) collective-permute-start(bf16[256,512]{1,0:T(8,128)(2,1)S(1)} %slice.82), channel_id=1, source_target_pairs={{0,1},{1,2},{2,3},{3,0},{4,5},{5,6},{6,7},{7,4},{8,9},{9,10},{10,1... | collective-permute-start | bytes 786440 | tf_op jit(solution)/shard_map/ppermute | solution.py:22
  30.8 11.4 %collective-permute-start.8 = (bf16[576,512]{1,0:T(8,128)(2,1)S(1)}, bf16[576,512]{1,0:T(8,128)(2,1)S(1)}, u32[]{:S(2)}, u32[]{:S(2)}) collective-permute-start(bf16[576,512]{1,0:T(8,128)(2,1)S(1)} %collective-permute-done.4.refs_9_), channel_id=1, source_target_pairs={{0,16},{16,0},{1,17},{17,1},{2,18},{18,2},{3,19},{19,3},{4,20},{20... | collective-permute-start | bytes 1769480 | tf_op jit(solution)/shard_map/ppermute | solution.py:22
  30.9 11.3 %copy-start.14 = (bf16[272,1024]{1,0:T(8,128)(2,1)}, bf16[272,1024]{1,0:T(8,128)(2,1)S(1)}, u32[]{:S(2)}) copy-start(bf16[272,1024]{1,0:T(8,128)(2,1)S(1)} %collective-permute-done.1.refs_3_) | copy-start | bytes 1671172
  30.9 11.3 %collective-permute-start.9 = (bf16[576,512]{1,0:T(8,128)(2,1)S(1)}, bf16[576,512]{1,0:T(8,128)(2,1)}, u32[]{:S(2)}, u32[]{:S(2)}) collective-permute-start(bf16[576,512]{1,0:T(8,128)(2,1)S(1)} %collective-permute-done.5.refs_10_), channel_id=1, source_target_pairs={{0,16},{16,0},{1,17},{17,1},{2,18},{18,2},{3,19},{19,3},{4,20},{20... | collective-permute-start | bytes 1769480 | tf_op jit(solution)/shard_map/ppermute | solution.py:22
  35.3 3.7 %copy-start.22 = (bf16[128,1024]{1,0:T(8,128)(2,1)}, bf16[128,1024]{1,0:T(8,128)(2,1)S(1)}, u32[]{:S(2)}) copy-start(bf16[128,1024]{1,0:T(8,128)(2,1)S(1)} %collective-permute-done.2.refs_4_) | copy-start | bytes 786436
  35.3 6.8 %collective-permute-start.3 = (bf16[144,1024]{1,0:T(8,128)(2,1)S(1)}, bf16[144,1024]{1,0:T(8,128)(2,1)}, u32[]{:S(2)}, u32[]{:S(2)}) collective-permute-start(bf16[144,1024]{1,0:T(8,128)(2,1)S(1)} %slice.81), channel_id=1, source_target_pairs={{0,12},{4,0},{8,4},{12,8},{1,13},{5,1},{9,5},{13,9},{2,14},{6,2},{... | collective-permute-start | bytes 884744 | tf_op jit(solution)/shard_map/ppermute | solution.py:22
  38.5 3.7 %collective-permute-start.10 = (bf16[256,512]{1,0:T(8,128)(2,1)}, bf16[256,512]{1,0:T(8,128)(2,1)}, u32[]{:S(2)}, u32[]{:S(2)}) collective-permute-start(bf16[256,512]{1,0:T(8,128)(2,1)} %collective-permute-done.6.refs_11_), channel_id=1, source_target_pairs={{0,16},{16,0},{1,17},{17,1},{2,18},{18,2},{3,19},{19,3},{4,20},{20... | collective-permute-start | bytes 786440 | tf_op jit(solution)/shard_map/ppermute | solution.py:22
  38.5 3.7 %collective-permute-start.11 = (bf16[320,512]{1,0:T(8,128)(2,1)}, bf16[320,512]{1,0:T(8,128)(2,1)}, u32[]{:S(2)}, u32[]{:S(2)}) collective-permute-start(bf16[320,512]{1,0:T(8,128)(2,1)} %collective-permute-done.7.refs_12_), channel_id=1, source_target_pairs={{0,16},{16,0},{1,17},{17,1},{2,18},{18,2},{3,19},{19,3},{4,20},{20... | collective-permute-start | bytes 983048 | tf_op jit(solution)/shard_map/ppermute | solution.py:22
  39.1 3.2 %copy-start.19 = (s32[16,1,128]{2,1,0:T(1,128)}, s32[16,1,128]{2,1,0:T(1,128)S(1)}, u32[]{:S(2)}) copy-start(s32[16,1,128]{2,1,0:T(1,128)S(1)} %all-to-all-done) | copy-start | bytes 24580
  42.2 0.9 copy-start.21
  54.8 14.3 %copy-start.1 = (bf16[1024,1024]{1,0:T(8,128)(2,1)S(1)}, bf16[1024,1024]{1,0:T(8,128)(2,1)}, u32[]{:S(2)}) copy-start(bf16[1024,1024]{1,0:T(8,128)(2,1)} %get-tuple-element.42) | copy-start | bytes 6291460
  54.8 19.0 %all-to-all-start.1 = ((bf16[16,16,1024]{2,1,0:T(8,128)(2,1)}), bf16[16,16,1024]{2,1,0:T(8,128)(2,1)S(1)}, u32[]{:S(2)}, u32[]{:S(2)}) async-start(bf16[16,16,1024]{2,1,0:T(8,128)(2,1)} %bitcast.35), calls=%async_computation.1 | async-start | bytes 1048576 | tf_op jit(solution)/shard_map/all_to_all | solution.py:636
  63.2 12.8 %collective-permute-start.12 = (bf16[80,1024]{1,0:T(8,128)(2,1)S(1)}, bf16[80,1024]{1,0:T(8,128)(2,1)S(1)}, u32[]{:S(2)}, u32[]{:S(2)}) collective-permute-start(bf16[80,1024]{1,0:T(8,128)(2,1)S(1)} %get-tuple-element.44), channel_id=1, source_target_pairs={{0,1},{1,2},{2,3},{3,4},{4,5},{5,6},{6,7},{7,8},{8,9},{9,10},{10,1... | collective-permute-start | bytes 491528 | tf_op jit(solution)/shard_map/ppermute | solution.py:22
  65.1 10.8 %collective-permute-start.13 = (bf16[80,1024]{1,0:T(8,128)(2,1)S(1)}, bf16[80,1024]{1,0:T(8,128)(2,1)S(1)}, u32[]{:S(2)}, u32[]{:S(2)}) collective-permute-start(bf16[80,1024]{1,0:T(8,128)(2,1)S(1)} %get-tuple-element.45), channel_id=1, source_target_pairs={{0,15},{1,0},{2,1},{3,2},{4,3},{5,4},{6,5},{7,6},{8,7},{9,8},{10,9... | collective-permute-start | bytes 491528 | tf_op jit(solution)/shard_map/ppermute | solution.py:22
  73.9 2.1 copy-start.3
  75.9 0.7 copy-start.23
  76.6 0.7 copy-start.24
  98.0 14.2 %all-to-all-start.2 = ((bf16[16,16,1024]{2,1,0:T(8,128)(2,1)}), bf16[16,16,1024]{2,1,0:T(8,128)(2,1)S(1)}, u32[]{:S(2)}, u32[]{:S(2)}) async-start(bf16[16,16,1024]{2,1,0:T(8,128)(2,1)} %bitcast.38), calls=%async_computation.2 | async-start | bytes 1048576 | tf_op jit(solution)/shard_map/all_to_all | solution.py:673
  112.3 0.8 copy-start.4
  113.1 21.4 %copy-start = (bf16[64,16,1024]{2,1,0:T(8,128)(2,1)S(1)}, bf16[64,16,1024]{2,1,0:T(8,128)(2,1)}, u32[]{:S(2)}) copy-start(bf16[64,16,1024]{2,1,0:T(8,128)(2,1)} %get-tuple-element.66) | copy-start | bytes 6291460
  126.3 18.5 %collective-permute-start.14 = (bf16[4,4,80,1024]{3,2,1,0:T(8,128)(2,1)}, bf16[4,4,80,1024]{3,2,1,0:T(8,128)(2,1)}, u32[]{:S(2)}, u32[]{:S(2)}) collective-permute-start(bf16[4,4,80,1024]{3,2,1,0:T(8,128)(2,1)} %get-tuple-element.62), channel_id=1, source_target_pairs={{0,16},{16,0},{1,17},{17,1},{2,18},{18,2},{3,19},{19,3},{4,20},{20... | collective-permute-start | bytes 7864328 | tf_op jit(solution)/shard_map/ppermute | solution.py:22
  126.4 8.1 %collective-permute-start.28 = (bf16[64,16,1024]{2,1,0:T(8,128)(2,1)}, bf16[64,16,1024]{2,1,0:T(8,128)(2,1)S(1)}, u32[]{:S(2)}, u32[]{:S(2)}) collective-permute-start(bf16[64,16,1024]{2,1,0:T(8,128)(2,1)} %get-tuple-element.67), channel_id=1, source_target_pairs={{0,16},{16,0},{1,17},{17,1},{2,18},{18,2},{3,19},{19,3},{4,20},{20... | collective-permute-start | bytes 6291464 | tf_op jit(solution)/shard_map/ppermute | solution.py:22
  136.9 90.8 %all-to-all-start.3 = ((bf16[64,16,1024]{2,1,0:T(8,128)(2,1)}), bf16[64,16,1024]{2,1,0:T(8,128)(2,1)S(1)}, u32[]{:S(2)}, u32[]{:S(2)}) async-start(bf16[64,16,1024]{2,1,0:T(8,128)(2,1)} %add_convert_fusion.1), calls=%async_computation.3 | async-start | bytes 4194304 | tf_op jit(solution)/shard_map/all_to_all | solution.py:682
  148.9 35.6 %collective-permute-start.15 = (bf16[320,1024]{1,0:T(8,128)(2,1)S(1)}, bf16[320,1024]{1,0:T(8,128)(2,1)S(1)}, u32[]{:S(2)}, u32[]{:S(2)}) collective-permute-start(bf16[320,1024]{1,0:T(8,128)(2,1)S(1)} %bitcast.33), channel_id=1, source_target_pairs={{0,3},{1,0},{2,1},{3,2},{4,7},{5,4},{6,5},{7,6},{8,11},{9,8},{10,9... | collective-permute-start | bytes 1966088 | tf_op jit(solution)/shard_map/ppermute | solution.py:22
  151.7 33.4 %collective-permute-start.16 = (bf16[320,1024]{1,0:T(8,128)(2,1)S(1)}, bf16[320,1024]{1,0:T(8,128)(2,1)S(1)}, u32[]{:S(2)}, u32[]{:S(2)}) collective-permute-start(bf16[320,1024]{1,0:T(8,128)(2,1)S(1)} %bitcast.32), channel_id=1, source_target_pairs={{0,1},{1,2},{2,3},{3,0},{4,5},{5,6},{6,7},{7,4},{8,9},{9,10},{10,1... | collective-permute-start | bytes 1966088 | tf_op jit(solution)/shard_map/ppermute | solution.py:22
  151.7 46.9 %collective-permute-start.17 = (bf16[320,1024]{1,0:T(8,128)(2,1)S(1)}, bf16[320,1024]{1,0:T(8,128)(2,1)S(1)}, u32[]{:S(2)}, u32[]{:S(2)}) collective-permute-start(bf16[320,1024]{1,0:T(8,128)(2,1)S(1)} %bitcast.31), channel_id=1, source_target_pairs={{0,2},{1,3},{2,0},{3,1},{4,6},{5,7},{6,4},{7,5},{8,10},{9,11},{10,... | collective-permute-start | bytes 1966088 | tf_op jit(solution)/shard_map/ppermute | solution.py:22
  199.1 7.6 %collective-permute-start.18 = (bf16[80,1024]{1,0:T(8,128)(2,1)S(1)}, bf16[80,1024]{1,0:T(8,128)(2,1)S(1)}, u32[]{:S(2)}, u32[]{:S(2)}) collective-permute-start(bf16[80,1024]{1,0:T(8,128)(2,1)S(1)} %get-tuple-element.72), channel_id=1, source_target_pairs={{0,96},{32,0},{64,32},{96,64},{1,97},{33,1},{65,33},{97,65},{2,98}... | collective-permute-start | bytes 491528 | tf_op jit(solution)/shard_map/ppermute | solution.py:22
  202.1 9.5 %collective-permute-start.19 = (bf16[80,1024]{1,0:T(8,128)(2,1)S(1)}, bf16[80,1024]{1,0:T(8,128)(2,1)S(1)}, u32[]{:S(2)}, u32[]{:S(2)}) collective-permute-start(bf16[80,1024]{1,0:T(8,128)(2,1)S(1)} %get-tuple-element.74), channel_id=1, source_target_pairs={{0,32},{32,64},{64,96},{96,0},{1,33},{33,65},{65,97},{97,1},{2,34}... | collective-permute-start | bytes 491528 | tf_op jit(solution)/shard_map/ppermute | solution.py:22
  202.1 9.5 %collective-permute-start.20 = (bf16[80,1024]{1,0:T(8,128)(2,1)S(1)}, bf16[80,1024]{1,0:T(8,128)(2,1)S(1)}, u32[]{:S(2)}, u32[]{:S(2)}) collective-permute-start(bf16[80,1024]{1,0:T(8,128)(2,1)S(1)} %get-tuple-element.73), channel_id=1, source_target_pairs={{0,64},{32,96},{64,0},{96,32},{1,65},{33,97},{65,1},{97,33},{2,66}... | collective-permute-start | bytes 491528 | tf_op jit(solution)/shard_map/ppermute | solution.py:22
  211.7 11.5 %copy-start.2 = (bf16[80,1024]{1,0:T(8,128)(2,1)}, bf16[80,1024]{1,0:T(8,128)(2,1)S(1)}, u32[]{:S(2)}) copy-start(bf16[80,1024]{1,0:T(8,128)(2,1)S(1)} %add_convert_fusion.2.refs_1_) | copy-start | bytes 491524
  211.7 7.9 %collective-permute-start.21 = (bf16[80,1024]{1,0:T(8,128)(2,1)S(1)}, bf16[80,1024]{1,0:T(8,128)(2,1)S(1)}, u32[]{:S(2)}, u32[]{:S(2)}) collective-permute-start(bf16[80,1024]{1,0:T(8,128)(2,1)S(1)} %add_convert_fusion.2.refs_1_), channel_id=1, source_target_pairs={{0,32},{32,64},{64,96},{96,0},{1,33},{33,65},{65,97},{97,1},{2,34}... | collective-permute-start | bytes 491528 | tf_op jit(solution)/shard_map/ppermute | solution.py:22
  211.8 7.8 %collective-permute-start.22 = (bf16[80,1024]{1,0:T(8,128)(2,1)S(1)}, bf16[80,1024]{1,0:T(8,128)(2,1)S(1)}, u32[]{:S(2)}, u32[]{:S(2)}) collective-permute-start(bf16[80,1024]{1,0:T(8,128)(2,1)S(1)} %add_convert_fusion.2.refs_1_), channel_id=1, source_target_pairs={{0,96},{32,0},{64,32},{96,64},{1,97},{33,1},{65,33},{97,65},{2,98}... | collective-permute-start | bytes 491528 | tf_op jit(solution)/shard_map/ppermute | solution.py:22
  215.0 6.8 %collective-permute-start.23 = (bf16[80,1024]{1,0:T(8,128)(2,1)S(1)}, bf16[80,1024]{1,0:T(8,128)(2,1)S(1)}, u32[]{:S(2)}, u32[]{:S(2)}) collective-permute-start(bf16[80,1024]{1,0:T(8,128)(2,1)S(1)} %add_convert_fusion.2.refs_1_), channel_id=1, source_target_pairs={{0,64},{32,96},{64,0},{96,32},{1,65},{33,97},{65,1},{97,33},{2,66}... | collective-permute-start | bytes 491528 | tf_op jit(solution)/shard_map/ppermute | solution.py:22
  215.0 6.8 %collective-permute-start.24 = (bf16[80,1024]{1,0:T(8,128)(2,1)S(1)}, bf16[80,1024]{1,0:T(8,128)(2,1)S(1)}, u32[]{:S(2)}, u32[]{:S(2)}) collective-permute-start(bf16[80,1024]{1,0:T(8,128)(2,1)S(1)} %add_convert_fusion.2.refs_1_), channel_id=1, source_target_pairs={{0,16},{16,0},{1,17},{17,1},{2,18},{18,2},{3,19},{19,3},{4,20},{20... | collective-permute-start | bytes 491528 | tf_op jit(solution)/shard_map/ppermute | solution.py:22
  219.6 3.6 %copy-start.7 = (bf16[80,1024]{1,0:T(8,128)(2,1)}, bf16[80,1024]{1,0:T(8,128)(2,1)S(1)}, u32[]{:S(2)}) copy-start(bf16[80,1024]{1,0:T(8,128)(2,1)S(1)} %collective-permute-done.21.refs_2_) | copy-start | bytes 491524
  219.6 2.3 collective-permute-start.25
  219.6 3.6 %copy-start.8 = (bf16[80,1024]{1,0:T(8,128)(2,1)}, bf16[80,1024]{1,0:T(8,128)(2,1)S(1)}, u32[]{:S(2)}) copy-start(bf16[80,1024]{1,0:T(8,128)(2,1)S(1)} %collective-permute-done.22.refs_3_) | copy-start | bytes 491524
  219.6 2.3 collective-permute-start.26
  221.9 1.4 copy-start.9
  221.9 1.4 collective-permute-start.27
  221.9 1.4 copy-start.10
  221.9 1.4 copy-start.11
  221.9 1.4 copy-start.12
  223.3 0.7 copy-start.13

commit v7 on v6

--- a/solution.py
+++ b/solution.py
@@ -440,7 +440,7 @@
                 for y in range(4):
                     at = (x * 4 + y) * 8
                     both = jnp.concatenate([msg[at : at + 8], own[at : at + 8]], axis=0)
-                    chunk_ref[z * 16 + x * 4 + y] = both.astype(BF)
+                    chunk_ref[x, z * 4 + y] = both.astype(BF)
 
         sent_out.append(copies.start(chunk_ref, chunk_hbm))
     wait_all(sent_out)
@@ -458,9 +458,9 @@
     copies,
     where_ref,
     returned_hbm, route_hbm, length_hbm, rel_hot_hbm, pooled_hbm, all_out_hbm, slope_hbm, normed_t_hbm,
-    given_hbm, kept_hbm,
+    in_given_hbm, out_given_hbm, in_kept_hbm, out_kept_hbm,
     returned_ref, route_ref, length_ref, rel_hot_ref, pooled_ref, all_out_ref, slope_ref, normed_t_ref,
-    given_ref, kept_ref,
+    in_given_ref, out_given_ref, in_kept_ref, out_kept_ref,
     scaled_ref, grad_ref,
 ):
     my_z, core, my_y = where_ref[0], where_ref[1], where_ref[3]
@@ -495,7 +495,10 @@
 
     wait_all(third)
     sent_out = []
-    for half, chunk_ref, chunk_hbm in ((1 - core, given_ref, given_hbm), (core, kept_ref, kept_hbm)):
+    for half, in_ref, in_hbm, out_ref, out_hbm in (
+        (1 - core, in_given_ref, in_given_hbm, out_given_ref, out_given_hbm),
+        (core, in_kept_ref, in_kept_hbm, out_kept_ref, out_kept_hbm),
+    ):
 
         @pl.loop(0, 4)
         def _(t):
@@ -508,13 +511,14 @@
             rel = dot(rel_hot_ref[rel_rows, :], returned_ref[...]).astype(BF)
             inner = dot(normed_t_ref[pl.ds(pl.multiple_of(half * 512, 512), 512), :], grad_ref[:, cols]).astype(BF)
             for z in range(4):
-                chunk_ref[t, places[z], 32:64, :] = out[z * 32 : (z + 1) * 32]
-                chunk_ref[t, places[z], 64:80, :] = rel[z * 16 : (z + 1) * 16]
+                out_ref[t, places[z], 0:32, :] = out[z * 32 : (z + 1) * 32]
+                out_ref[t, places[z], 32:48, :] = rel[z * 16 : (z + 1) * 16]
                 for i in range(4):
                     piece = inner[z * 128 + i * 32 : z * 128 + (i + 1) * 32]
-                    chunk_ref[t, places[z], 0:32, i * 256 : (i + 1) * 256] = piece
-
-        sent_out.append(copies.start(chunk_ref, chunk_hbm))
+                    in_ref[places[z], t, :, i * 256 : (i + 1) * 256] = piece
+
+        sent_out.append(copies.start(in_ref, in_hbm))
+        sent_out.append(copies.start(out_ref, out_hbm))
     wait_all(sent_out)
 
 
@@ -672,32 +676,37 @@
 
     returned = lax.all_to_all(grad_table.reshape(16, 16, width), GROUP, 0, 0, tiled=True).reshape(256, width)
 
-    outs = [((64, 16, width), BF)] * 2
+    outs = [((4, 16, 16, width), BF)] * 2
     operands = [aggregate, nodes, grad_pre]
     graph_kept, graph_given = local_call(
         weight_kernel, outs, [where, *operands], like(operands) + filled(outs), flops=10**9
     )
     returned, graph_kept, graph_given = lax.optimization_barrier((returned, graph_kept, graph_given))
     chip = (graph_kept.astype(F32) + shift_by(graph_given, "core", 1).astype(F32)).astype(BF)
-    plane = lax.all_to_all(chip, ("z", "x", "y"), 0, 0, tiled=True)
+    line = lax.all_to_all(chip, "x", 0, 0, tiled=True)
+    plane = lax.all_to_all(jnp.sum(line.astype(F32), axis=0).astype(BF), ("z", "y"), 0, 0, tiled=True)
     weight_rows = jnp.sum(plane.astype(F32), axis=0)
     grad_msg, grad_self = weight_rows[:8], weight_rows[8:]
 
-    outs = [((4, 4, 80, width), BF)] * 2
+    outs = [((4, 4, 32, width), BF), ((4, 4, 48, width), BF)] * 2
     operands = [returned, route, inverse, rel_hot, pooled, all_out, slope, normed_t]
-    given, kept = local_call(
+    in_given, out_given, in_kept, out_kept = local_call(
         back_kernel,
         outs,
         [where, *operands],
         like(operands)
         + filled(outs)
         + [pltpu.VMEM((4 * entities, width), BF), pltpu.VMEM((4 * tokens, 4 * units), BF)],
-        copies=12,
+        copies=14,
         flops=2 * 4 * tokens * width * 4 * units,
     )
-    mixed = (kept.astype(F32) + shift_by(given, "core", 1).astype(F32)).astype(BF)
-    part = reduce_ring([mixed[i].reshape(320, width) for i in range(4)], "y").reshape(4, 80, width)
-    part = reduce_ring([part[i] for i in range(4)], "z")
+    in_chip = (in_kept.astype(F32) + shift_by(in_given, "core", 1).astype(F32)).astype(BF)
+    out_chip = (out_kept.astype(F32) + shift_by(out_given, "core", 1).astype(F32)).astype(BF)
+    out_part = reduce_ring([out_chip[i].reshape(192, width) for i in range(4)], "y").reshape(4, 48, width)
+    in_part = reduce_ring([in_chip[i].reshape(128, width) for i in range(4)], "z").reshape(4, 32, width)
+    out_part = reduce_ring([out_part[i] for i in range(4)], "z")
+    in_part = reduce_ring([in_part[i] for i in range(4)], "y")
+    part = jnp.concatenate([in_part, out_part], axis=0)
     parts = [part] + [shift_by(part, "z", s) for s in SHIFTS]
     others = [shift_by(piece, "core", 1) for piece in parts]
     outs = [((width, units), F32), ((units, width), F32), ((shard_rows, width), F32)]

time: 230 us -> 200 us (0.87)
  waiting for transfers between devices: 88 us -> 41.1 us
  starting transfers between devices: 56.1 us -> 70.9 us
    ppermute x29 -> x36, waiting for transfers between devices: 81.4 us -> 34.6 us  [shift_by(): lax.ppermute(value, axis, [(i, (i + shift) % count) for i in range(count)])]
    ppermute x29 -> x36, starting transfers between devices: 30.3 us -> 44.1 us  [shift_by(): lax.ppermute(value, axis, [(i, (i + shift) % count) for i in range(count)])]
    all_to_all x1 -> x2, starting transfers between devices: 7.83 us -> 8.86 us  [the longest x1 5.25 us: shards(): lax.all_to_all(jnp.sum(line.astype(F32), axis=0).astype(BF), ('z', 'y'),...]
  transfers between devices with their start and end apart: 33 -> 41, of which waited for: 16 -> 14; matrix products, arithmetic and copies ran while one was open for 8% -> 10% of each run, Pallas kernels for 4% -> 12%
where the time goes in v7:
time: 200 us; the launch traced here: 198 us
  starting transfers between devices  70.9 us (35%)
  Pallas kernels  58.7 us (29%)
  waiting for transfers between devices  41.1 us (21%)
  other arithmetic  15.3 us (8%)
  local copies, waits for them, and re-layouts  10.5 us (5%)
    pallas_call x6, Pallas kernels, local_call(): pl.pallas_call(kernel, out_shape=[jax.ShapeDtypeStruct(shape, kind) for s...  58.7 us
    ppermute x36, starting transfers between devices, shift_by(): lax.ppermute(value, axis, [(i, (i + shift) % count) for i in range(count)])  44.1 us
    ppermute x36, waiting for transfers between devices, shift_by(): lax.ppermute(value, axis, [(i, (i + shift) % count) for i in range(count)])  34.6 us
    all_to_all x1, starting transfers between devices, shards(): lax.all_to_all(jnp.pad(numbers, ((0, 0), (0, 124))), GROUP, 0, 0, tiled=T...  7.28 us
    all_to_all x1, starting transfers between devices, shards(): lax.all_to_all(outgoing.reshape(16, 16, width), GROUP, 0, 0, tiled=True)  7.12 us
    all_to_all x1, starting transfers between devices, shards(): lax.all_to_all(jnp.sum(line.astype(F32), axis=0).astype(BF), ('z', 'y'),...  5.25 us
    all_to_all x1, waiting for transfers between devices, shards(): lax.all_to_all(grad_table.reshape(16, 16, width), GROUP, 0, 0, tiled=True)  4.32 us
  transfers between devices with their start and end apart: 41, of which 14 were waited for; matrix products, arithmetic and copies ran while one was open for 10% of the time, Pallas kernels for 12%

profile of v7, /device:TPU:0, one launch (start us, length us, event | category | flops | bytes accessed | tf_op | source)
XLA Modules:
  0.0 198.1 jit_solution(6138686495222620207)
XLA Ops:
  0.7 1.6 pad.27.refs_6_.refs_8_
  2.3 0.7 pad_add_fusion.refs_0_
  3.0 3.3 %shard_map.190 = (bf16[272,1024]{1,0:T(8,128)(2,1)}, f32[16,1024]{1,0:T(8,128)}, bf16[576,512]{1,0:T(8,128)(2,1)}) custom-call(s32[4]{0:T(128)} %pad_add_fusion.refs_0_, bf16[256,1024]{1,0:T(8,128)(2,1)} %bitcast.37, s32[1,16]{1,0:T(1,128)} %bitcast.50, s32[1,16]{1,0:T(1,128)} %refs_3_.1, bf16[1024,256]{1,0:T(8,128)(2,1)} %refs_6_.2, ...), custom_call_target="tpu_custom_call" | custom-call | bytes 1048576 | tf_op jit(solution)/shard_map/pallas_call | solution.py:88
  6.3 3.2 %collective-permute-start.5 = (bf16[576,512]{1,0:T(8,128)(2,1)}, bf16[576,512]{1,0:T(8,128)(2,1)S(1)}, u32[]{:S(2)}, u32[]{:S(2)}) collective-permute-start(bf16[576,512]{1,0:T(8,128)(2,1)} %get-tuple-element.40), channel_id=1, source_target_pairs={{0,3},{1,0},{2,1},{3,2},{4,7},{5,4},{6,5},{7,6},{8,11},{9,8},{10,9... | collective-permute-start | bytes 1769480 | tf_op jit(solution)/shard_map/ppermute | solution.py:22
  9.5 2.8 %collective-permute-start.1 = (bf16[272,1024]{1,0:T(8,128)(2,1)}, bf16[272,1024]{1,0:T(8,128)(2,1)S(1)}, u32[]{:S(2)}, u32[]{:S(2)}) collective-permute-start(bf16[272,1024]{1,0:T(8,128)(2,1)} %get-tuple-element.39.refs_1_), channel_id=1, source_target_pairs={{0,12},{4,0},{8,4},{12,8},{1,13},{5,1},{9,5},{13,9},{2,14},{6,2},{... | collective-permute-start | bytes 1671176 | tf_op jit(solution)/shard_map/ppermute | solution.py:22
  12.2 0.5 broadcast.63
  12.8 1.3 reduce.4
  14.4 0.7 copy.28
  15.0 7.3 %all-to-all-start = ((s32[16,1,128]{2,1,0:T(1,128)}), s32[16,1,128]{2,1,0:T(1,128)S(1)}, u32[]{:S(2)}, u32[]{:S(2)}) async-start(s32[16,1,128]{2,1,0:T(1,128)} %copy.28), calls=%async_computation | async-start | bytes 16384 | tf_op jit(solution)/shard_map/all_to_all | solution.py:576
  22.4 1.3 fusion.1.refs_4_
  24.0 1.5 fusion.refs_3_
  25.5 2.0 %collective-permute-done.refs_2_ = bf16[272,1024]{1,0:T(8,128)(2,1)S(1)} collective-permute-done((bf16[272,1024]{1,0:T(8,128)(2,1)}, bf16[272,1024]{1,0:T(8,128)(2,1)S(1)}, u32[]{:S(2)}, u32[]{:S(2)}) %collective-permute-start) | collective-permute-done | bytes 557088 | tf_op jit(solution)/shard_map/ppermute | solution.py:22
  27.7 3.0 %collective-permute-start.7 = (bf16[320,512]{1,0:T(8,128)(2,1)S(1)}, bf16[320,512]{1,0:T(8,128)(2,1)S(1)}, u32[]{:S(2)}, u32[]{:S(2)}) collective-permute-start(bf16[320,512]{1,0:T(8,128)(2,1)S(1)} %slice.119), channel_id=1, source_target_pairs={{0,3},{1,0},{2,1},{3,2},{4,7},{5,4},{6,5},{7,6},{8,11},{9,8},{10,9... | collective-permute-start | bytes 983048 | tf_op jit(solution)/shard_map/ppermute | solution.py:22
  31.6 3.8 %collective-permute-done.2.refs_4_ = bf16[128,1024]{1,0:T(8,128)(2,1)S(1)} collective-permute-done((bf16[128,1024]{1,0:T(8,128)(2,1)S(1)}, bf16[128,1024]{1,0:T(8,128)(2,1)S(1)}, u32[]{:S(2)}, u32[]{:S(2)}) %collective-permute-start.2) | collective-permute-done | bytes 262176 | tf_op jit(solution)/shard_map/ppermute | solution.py:22
  35.4 3.1 %collective-permute-done.6.refs_11_ = bf16[256,512]{1,0:T(8,128)(2,1)} collective-permute-done((bf16[256,512]{1,0:T(8,128)(2,1)S(1)}, bf16[256,512]{1,0:T(8,128)(2,1)}, u32[]{:S(2)}, u32[]{:S(2)}) %collective-permute-start.6) | collective-permute-done | bytes 262176 | tf_op jit(solution)/shard_map/ppermute | solution.py:22
  39.1 3.1 %collective-permute-done.3.refs_5_ = bf16[144,1024]{1,0:T(8,128)(2,1)} collective-permute-done((bf16[144,1024]{1,0:T(8,128)(2,1)S(1)}, bf16[144,1024]{1,0:T(8,128)(2,1)}, u32[]{:S(2)}, u32[]{:S(2)}) %collective-permute-start.3) | collective-permute-done | bytes 294944 | tf_op jit(solution)/shard_map/ppermute | solution.py:22
  42.3 11.8 %shard_map.191 = (bf16[256,1024]{1,0:T(8,128)(2,1)}, bf16[1024,1024]{1,0:T(8,128)(2,1)}, bf16[1024,1024]{1,0:T(8,128)(2,1)}, bf16[64,1024]{1,0:T(8,128)(2,1)}, b...) custom-call(s32[4]{0:T(128)} %pad_add_fusion.refs_0_, ...), custom_call_target="tpu_custom_call" | custom-call | flops 2147483648 | bytes 1048576 | tf_op jit(solution)/shard_map/pallas_call | solution.py:88
  54.1 7.1 %all-to-all-start.1 = ((bf16[16,16,1024]{2,1,0:T(8,128)(2,1)}), bf16[16,16,1024]{2,1,0:T(8,128)(2,1)S(1)}, u32[]{:S(2)}, u32[]{:S(2)}) async-start(bf16[16,16,1024]{2,1,0:T(8,128)(2,1)} %bitcast.38), calls=%async_computation.1 | async-start | bytes 1048576 | tf_op jit(solution)/shard_map/all_to_all | solution.py:640
  61.2 1.2 fusion.2.refs_5_
  62.4 1.9 collective-permute-start.12
  64.3 3.4 %collective-permute-start.13 = (bf16[80,1024]{1,0:T(8,128)(2,1)S(1)}, bf16[80,1024]{1,0:T(8,128)(2,1)S(1)}, u32[]{:S(2)}, u32[]{:S(2)}) collective-permute-start(bf16[80,1024]{1,0:T(8,128)(2,1)S(1)} %get-tuple-element.47), channel_id=1, source_target_pairs={{0,15},{1,0},{2,1},{3,2},{4,3},{5,4},{6,5},{7,6},{8,7},{9,8},{10,9... | collective-permute-start | bytes 491528 | tf_op jit(solution)/shard_map/ppermute | solution.py:22
  67.7 0.6 fusion.14.refs_2_
  68.3 2.6 %copy.29 = bf16[1024,1024]{0,1:T(8,128)(2,1)} copy(bf16[1024,1024]{1,0:T(8,128)(2,1)S(1)} %copy-done.1) | data formatting | bytes 4194304 | tf_op jit(solution)/shard_map/pallas_call | solution.py:88
  70.9 2.1 %all-to-all-done.1 = bf16[16,16,1024]{2,1,0:T(8,128)(2,1)S(1)} async-done(((bf16[16,16,1024]{2,1,0:T(8,128)(2,1)}), bf16[16,16,1024]{2,1,0:T(8,128)(2,1)S(1)}, u32[]{:S(2)}, u32[]{:S(2)}) %all-to-all-start.1) | async-done | bytes 524320 | tf_op jit(solution)/shard_map/all_to_all | solution.py:640
  73.1 2.1 %collective-permute-done.12.refs_10_ = bf16[80,1024]{1,0:T(8,128)(2,1)S(1)} collective-permute-done((bf16[80,1024]{1,0:T(8,128)(2,1)S(1)}, bf16[80,1024]{1,0:T(8,128)(2,1)S(1)}, u32[]{:S(2)}, u32[]{:S(2)}) %collective-permute-start.12) | collective-permute-done | bytes 163872 | tf_op jit(solution)/shard_map/ppermute | solution.py:22
  75.1 0.7 copy-done.23
  75.8 0.7 copy-done.24
  76.5 20.6 %shard_map.192 = (bf16[256,1024]{1,0:T(8,128)(2,1)}, bf16[256,1024]{1,0:T(8,128)(2,1)}, bf16[256,1024]{1,0:T(8,128)(2,1)}, bf16[256,1024]{1,0:T(8,128)(2,1)}, bf16[256,1024]{1,0:T(8,128)(2,1)}) custom-call(s32[4]{0:T(128)} %pad_add_fusion.refs_0_, bf16[256,1024]{1,0:T(8,128)(2,1)} %bitcast.39, bf16[64,256]{1,0:T(8,128)(2,1)} %fusion.14.refs_2_, ...), custom_call_target="tpu_custom_call" | custom-call | flops 6000000000 | bytes 1048576 | tf_op jit(solution)/shard_map/pallas_call | solution.py:88
  97.0 3.6 %all-to-all-start.2 = ((bf16[16,16,1024]{2,1,0:T(8,128)(2,1)}), bf16[16,16,1024]{2,1,0:T(8,128)(2,1)S(1)}, u32[]{:S(2)}, u32[]{:S(2)}) async-start(bf16[16,16,1024]{2,1,0:T(8,128)(2,1)} %bitcast.41), calls=%async_computation.2 | async-start | bytes 1048576 | tf_op jit(solution)/shard_map/all_to_all | solution.py:677
  100.6 6.3 %shard_map.193 = (bf16[4,16,16,1024]{3,2,1,0:T(8,128)(2,1)}, bf16[4,16,16,1024]{3,2,1,0:T(8,128)(2,1)}) custom-call(s32[4]{0:T(128)} %pad_add_fusion.refs_0_, bf16[256,1024]{1,0:T(8,128)(2,1)} %get-tuple-element.50.refs_1_, bf16[256,1024]{1,0:T(8,128)(2,1)} %get-tuple-element.51.refs_2_, bf16[256,1024]{1,0:T(8,128)(2,1)} %get-tuple-element.52.refs_3_), custom_call_target="tpu_custom_call" | custom-call | flops 1000000000 | bytes 1048576 | tf_op jit(solution)/shard_map/pallas_call | solution.py:88
  106.9 4.3 %all-to-all-done.2 = bf16[16,16,1024]{2,1,0:T(8,128)(2,1)S(1)} async-done(((bf16[16,16,1024]{2,1,0:T(8,128)(2,1)}), bf16[16,16,1024]{2,1,0:T(8,128)(2,1)S(1)}, u32[]{:S(2)}, u32[]{:S(2)}) %all-to-all-start.2) | async-done | bytes 524320 | tf_op jit(solution)/shard_map/all_to_all | solution.py:677
  111.2 0.8 copy-done.4
  112.0 13.1 %shard_map.194 = (bf16[4,4,32,1024]{3,2,1,0:T(8,128)(2,1)}, bf16[4,4,48,1024]{3,2,1,0:T(8,128)(2,1)}, bf16[4,4,32,1024]{3,2,1,0:T(8,128)(2,1)}, bf16[4,4,48,1024]{3,2,1,0:T(8,128)(2,1)}) custom-call(s32[4]{0:T(128)} %pad_add_fusion.refs_0_, bf16[256,1024]{1,0:T(8,128)(2,1)} %bitcast.40, bf16[64,256]{1,0:T(8,128)(2,1)} %get-tuple-element.56.refs_2_, ...), custom_call_target="tpu_custom_call" | custom-call | flops 2147483648 | bytes 1048576 | tf_op jit(solution)/shard_map/pallas_call | solution.py:88
  125.8 2.9 %collective-permute-done.14 = bf16[4,4,32,1024]{3,2,1,0:T(8,128)(2,1)S(1)} collective-permute-done((bf16[4,4,32,1024]{3,2,1,0:T(8,128)(2,1)}, bf16[4,4,32,1024]{3,2,1,0:T(8,128)(2,1)S(1)}, u32[]{:S(2)}, u32[]{:S(2)}) %collective-permute-start.14) | collective-permute-done | bytes 1048608 | tf_op jit(solution)/shard_map/ppermute | solution.py:22
  128.7 1.8 add_convert_fusion.2
  130.5 0.9 fusion.20
  131.4 4.0 %collective-permute-start.15 = (bf16[128,1024]{1,0:T(8,128)(2,1)}, bf16[128,1024]{1,0:T(8,128)(2,1)S(1)}, u32[]{:S(2)}, u32[]{:S(2)}) collective-permute-start(bf16[128,1024]{1,0:T(8,128)(2,1)} %bitcast.18), channel_id=1, source_target_pairs={{0,96},{32,0},{64,32},{96,64},{1,97},{33,1},{65,33},{97,65},{2,98}... | collective-permute-start | bytes 786440 | tf_op jit(solution)/shard_map/ppermute | solution.py:22
  135.4 1.9 collective-permute-start.17
  137.3 2.3 %add_convert_fusion = bf16[4,16,16,1024]{3,2,1,0:T(8,128)(2,1)} fusion(bf16[4,16,16,1024]{3,2,1,0:T(8,128)(2,1)S(1)} %collective-permute-done.35, bf16[4,16,16,1024]{3,2,1,0:T(8,128)(2,1)S(1)} %copy-done), kind=kLoop, calls=%fused_computation | loop fusion | flops 4194304 | bytes 6291456 | tf_op jit(solution)/shard_map/convert_element_type | solution.py:685
  139.5 3.6 %all-to-all-start.3 = ((bf16[4,16,16,1024]{3,2,1,0:T(8,128)(2,1)}), bf16[4,16,16,1024]{3,2,1,0:T(8,128)(2,1)S(1)}, u32[]{:S(2)}, u32[]{:S(2)}) async-start(bf16[4,16,16,1024]{3,2,1,0:T(8,128)(2,1)} %add_convert_fusion), calls=%async_computation.3 | async-start | bytes 4194304 | tf_op jit(solution)/shard_map/all_to_all | solution.py:686
  143.2 2.6 %add_convert_fusion.1 = bf16[4,4,48,1024]{3,2,1,0:T(8,128)(2,1)S(1)} fusion(bf16[4,4,48,1024]{3,2,1,0:T(8,128)(2,1)} %collective-permute-done.21, bf16[4,4,48,1024]{3,2,1,0:T(8,128)(2,1)} %get-tuple-element.65), kind=kLoop, calls=%fused_computation.1 | loop fusion | flops 3145728 | bytes 4718592 | tf_op jit(solution)/shard_map/convert_element_type | solution.py:704
  145.9 0.6 collective-permute-start.22
  146.5 1.5 collective-permute-start.23
  148.0 1.1 collective-permute-start.24
  149.1 1.4 collective-permute-done.16
  150.7 0.8 collective-permute-start.18
  151.5 1.3 collective-permute-start.19
  152.8 5.2 %collective-permute-done.22 = bf16[192,1024]{1,0:T(8,128)(2,1)S(1)} collective-permute-done((bf16[192,1024]{1,0:T(8,128)(2,1)S(1)}, bf16[192,1024]{1,0:T(8,128)(2,1)S(1)}, u32[]{:S(2)}, u32[]{:S(2)}) %collective-permute-start.22) | collective-permute-done | bytes 393248 | tf_op jit(solution)/shard_map/ppermute | solution.py:22
  158.0 6.4 %collective-permute-start.20 = (bf16[32,1024]{1,0:T(8,128)(2,1)S(1)}, bf16[32,1024]{1,0:T(8,128)(2,1)S(1)}, u32[]{:S(2)}, u32[]{:S(2)}) collective-permute-start(bf16[32,1024]{1,0:T(8,128)(2,1)S(1)} %get-tuple-element.84), channel_id=1, source_target_pairs={{0,2},{1,3},{2,0},{3,1},{4,6},{5,7},{6,4},{7,5},{8,10},{9,11},{10,... | collective-permute-start | bytes 196616 | tf_op jit(solution)/shard_map/ppermute | solution.py:22
  164.4 3.2 %collective-permute-done.23 = bf16[192,1024]{1,0:T(8,128)(2,1)S(1)} collective-permute-done((bf16[192,1024]{1,0:T(8,128)(2,1)S(1)}, bf16[192,1024]{1,0:T(8,128)(2,1)S(1)}, u32[]{:S(2)}, u32[]{:S(2)}) %collective-permute-start.23) | collective-permute-done | bytes 393248 | tf_op jit(solution)/shard_map/ppermute | solution.py:22
  167.9 1.7 collective-permute-start.25
  169.7 0.7 collective-permute-start.26
  170.3 2.0 %collective-permute-start.27 = (bf16[48,1024]{1,0:T(8,128)(2,1)S(1)}, bf16[48,1024]{1,0:T(8,128)(2,1)S(1)}, u32[]{:S(2)}, u32[]{:S(2)}) collective-permute-start(bf16[48,1024]{1,0:T(8,128)(2,1)S(1)} %get-tuple-element.81), channel_id=1, source_target_pairs={{0,64},{32,96},{64,0},{96,32},{1,65},{33,97},{65,1},{97,33},{2,66}... | collective-permute-start | bytes 294920 | tf_op jit(solution)/shard_map/ppermute | solution.py:22
  172.4 1.3 reduce_sum.31
  173.7 5.2 %all-to-all-start.4 = ((bf16[16,16,1024]{2,1,0:T(8,128)(2,1)}), bf16[16,16,1024]{2,1,0:T(8,128)(2,1)S(1)}, u32[]{:S(2)}, u32[]{:S(2)}) async-start(bf16[16,16,1024]{2,1,0:T(8,128)(2,1)} %reduce_sum.31), calls=%async_computation.4 | async-start | bytes 1048576 | tf_op jit(solution)/shard_map/all_to_all | solution.py:687
  179.1 2.0 %collective-permute-start.28 = (bf16[80,1024]{1,0:T(8,128)(2,1)S(1)}, bf16[80,1024]{1,0:T(8,128)(2,1)S(1)}, u32[]{:S(2)}, u32[]{:S(2)}) collective-permute-start(bf16[80,1024]{1,0:T(8,128)(2,1)S(1)} %pad_maximum_fusion.refs_1_), channel_id=1, source_target_pairs={{0,32},{32,64},{64,96},{96,0},{1,33},{33,65},{65,97},{97,1},{2,34}... | collective-permute-start | bytes 491528 | tf_op jit(solution)/shard_map/ppermute | solution.py:22
  181.1 1.3 collective-permute-start.29
  182.4 2.2 %collective-permute-start.30 = (bf16[80,1024]{1,0:T(8,128)(2,1)S(1)}, bf16[80,1024]{1,0:T(8,128)(2,1)S(1)}, u32[]{:S(2)}, u32[]{:S(2)}) collective-permute-start(bf16[80,1024]{1,0:T(8,128)(2,1)S(1)} %pad_maximum_fusion.refs_1_), channel_id=1, source_target_pairs={{0,64},{32,96},{64,0},{96,32},{1,65},{33,97},{65,1},{97,33},{2,66}... | collective-permute-start | bytes 491528 | tf_op jit(solution)/shard_map/ppermute | solution.py:22
  184.6 5.2 %collective-permute-done.28.refs_2_ = bf16[80,1024]{1,0:T(8,128)(2,1)S(1)} collective-permute-done((bf16[80,1024]{1,0:T(8,128)(2,1)S(1)}, bf16[80,1024]{1,0:T(8,128)(2,1)S(1)}, u32[]{:S(2)}, u32[]{:S(2)}) %collective-permute-start.28) | collective-permute-done | bytes 163872 | tf_op jit(solution)/shard_map/ppermute | solution.py:22
  190.3 1.2 collective-permute-done.30.refs_4_
  191.6 1.3 collective-permute-done.34.refs_8_
  193.0 0.7 copy-done.13
  193.7 3.7 %shard_map.195 = (f32[1024,256]{1,0:T(8,128)}, f32[256,1024]{1,0:T(8,128)}, f32[52,1024]{1,0:T(8,128)}) custom-call(s32[4]{0:T(128)} %pad_add_fusion.refs_0_, bf16[80,1024]{1,0:T(8,128)(2,1)} %copy-done.2, bf16[80,1024]{1,0:T(8,128)(2,1)} %copy-done.7, bf16[80,1024]{1,0:T(8,128)(2,1)} %copy-done.8, bf16[80,1024]{1,0:T(8,128)(2,1)} %copy-done.9, ...), custom_call_target="tpu_custom_call" | custom-call | bytes 1048576 | tf_op jit(solution)/shard_map/pallas_call | solution.py:88
  197.5 0.6 fusion.24
  (122 shorter events, 4.2 us)
Async XLA Ops:
  0.6 21.7 %copy-start.20 = (s32[1,128]{1,0:T(1,128)S(1)}, s32[1,128]{1,0:T(1,128)}, u32[]{:S(2)}) copy-start(s32[1,128]{1,0:T(1,128)} %param.22) | copy-start | bytes 1540
  0.6 21.7 %copy-start.25 = (s32[1,16]{1,0:T(1,128)S(1)}, s32[1,16]{1,0:T(1,128)}, u32[]{:S(2)}) copy-start(s32[1,16]{1,0:T(1,128)} %param.20) | copy-start | bytes 196
  0.7 21.8 %copy-start.17 = (s32[1,2048]{1,0:T(1,128)S(1)}, s32[1,2048]{1,0:T(1,128)}, u32[]{:S(2)}) copy-start(s32[1,2048]{1,0:T(1,128)} %param.24) | copy-start | bytes 24580
  0.7 23.1 %copy-start.5 = (bf16[240,1024]{1,0:T(8,128)(2,1)S(1)}, bf16[240,1024]{1,0:T(8,128)(2,1)}, u32[]{:S(2)}) copy-start(bf16[240,1024]{1,0:T(8,128)(2,1)} %refs_9_.1) | copy-start | bytes 1474564
  0.7 23.4 %copy-start.18 = (s32[1,2048]{1,0:T(1,128)S(1)}, s32[1,2048]{1,0:T(1,128)}, u32[]{:S(2)}) copy-start(s32[1,2048]{1,0:T(1,128)} %param.23) | copy-start | bytes 24580
  6.3 21.3 %collective-permute-start.5 = (bf16[576,512]{1,0:T(8,128)(2,1)}, bf16[576,512]{1,0:T(8,128)(2,1)S(1)}, u32[]{:S(2)}, u32[]{:S(2)}) collective-permute-start(bf16[576,512]{1,0:T(8,128)(2,1)} %get-tuple-element.40), channel_id=1, source_target_pairs={{0,3},{1,0},{2,1},{3,2},{4,7},{5,4},{6,5},{7,6},{8,11},{9,8},{10,9... | collective-permute-start | bytes 1769480 | tf_op jit(solution)/shard_map/ppermute | solution.py:22
  9.5 21.2 %collective-permute-start.4 = (bf16[576,512]{1,0:T(8,128)(2,1)}, bf16[576,512]{1,0:T(8,128)(2,1)S(1)}, u32[]{:S(2)}, u32[]{:S(2)}) collective-permute-start(bf16[576,512]{1,0:T(8,128)(2,1)} %get-tuple-element.40), channel_id=1, source_target_pairs={{0,1},{1,2},{2,3},{3,0},{4,5},{5,6},{6,7},{7,4},{8,9},{9,10},{10,1... | collective-permute-start | bytes 1769480 | tf_op jit(solution)/shard_map/ppermute | solution.py:22
  9.5 21.4 %collective-permute-start.1 = (bf16[272,1024]{1,0:T(8,128)(2,1)}, bf16[272,1024]{1,0:T(8,128)(2,1)S(1)}, u32[]{:S(2)}, u32[]{:S(2)}) collective-permute-start(bf16[272,1024]{1,0:T(8,128)(2,1)} %get-tuple-element.39.refs_1_), channel_id=1, source_target_pairs={{0,12},{4,0},{8,4},{12,8},{1,13},{5,1},{9,5},{13,9},{2,14},{6,2},{... | collective-permute-start | bytes 1671176 | tf_op jit(solution)/shard_map/ppermute | solution.py:22
  12.2 15.3 %collective-permute-start = (bf16[272,1024]{1,0:T(8,128)(2,1)}, bf16[272,1024]{1,0:T(8,128)(2,1)S(1)}, u32[]{:S(2)}, u32[]{:S(2)}) collective-permute-start(bf16[272,1024]{1,0:T(8,128)(2,1)} %get-tuple-element.39.refs_1_), channel_id=1, source_target_pairs={{0,4},{4,8},{8,12},{12,0},{1,5},{5,9},{9,13},{13,1},{2,6},{6,10},{... | collective-permute-start | bytes 1671176 | tf_op jit(solution)/shard_map/ppermute | solution.py:22
  15.0 24.1 %all-to-all-start = ((s32[16,1,128]{2,1,0:T(1,128)}), s32[16,1,128]{2,1,0:T(1,128)S(1)}, u32[]{:S(2)}, u32[]{:S(2)}) async-start(s32[16,1,128]{2,1,0:T(1,128)} %copy.28), calls=%async_computation | async-start | bytes 16384 | tf_op jit(solution)/shard_map/all_to_all | solution.py:576
  27.5 14.7 %copy-start.15 = (bf16[272,1024]{1,0:T(8,128)(2,1)}, bf16[272,1024]{1,0:T(8,128)(2,1)S(1)}, u32[]{:S(2)}) copy-start(bf16[272,1024]{1,0:T(8,128)(2,1)S(1)} %collective-permute-done.refs_2_) | copy-start | bytes 1671172
  27.5 7.8 %collective-permute-start.2 = (bf16[128,1024]{1,0:T(8,128)(2,1)S(1)}, bf16[128,1024]{1,0:T(8,128)(2,1)S(1)}, u32[]{:S(2)}, u32[]{:S(2)}) collective-permute-start(bf16[128,1024]{1,0:T(8,128)(2,1)S(1)} %slice.116), channel_id=1, source_target_pairs={{0,4},{4,8},{8,12},{12,0},{1,5},{5,9},{9,13},{13,1},{2,6},{6,10},{... | collective-permute-start | bytes 786440 | tf_op jit(solution)/shard_map/ppermute | solution.py:22
  27.6 14.6 %copy-start.6 = (bf16[576,512]{1,0:T(8,128)(2,1)}, bf16[576,512]{1,0:T(8,128)(2,1)S(1)}, u32[]{:S(2)}) copy-start(bf16[576,512]{1,0:T(8,128)(2,1)S(1)} %collective-permute-done.5.refs_10_) | copy-start | bytes 1769476
  27.7 10.8 %collective-permute-start.7 = (bf16[320,512]{1,0:T(8,128)(2,1)S(1)}, bf16[320,512]{1,0:T(8,128)(2,1)S(1)}, u32[]{:S(2)}, u32[]{:S(2)}) collective-permute-start(bf16[320,512]{1,0:T(8,128)(2,1)S(1)} %slice.119), channel_id=1, source_target_pairs={{0,3},{1,0},{2,1},{3,2},{4,7},{5,4},{6,5},{7,6},{8,11},{9,8},{10,9... | collective-permute-start | bytes 983048 | tf_op jit(solution)/shard_map/ppermute | solution.py:22
  30.7 11.5 %copy-start.16 = (bf16[576,512]{1,0:T(8,128)(2,1)}, bf16[576,512]{1,0:T(8,128)(2,1)S(1)}, u32[]{:S(2)}) copy-start(bf16[576,512]{1,0:T(8,128)(2,1)S(1)} %collective-permute-done.4.refs_9_) | copy-start | bytes 1769476
  30.7 7.8 %collective-permute-start.6 = (bf16[256,512]{1,0:T(8,128)(2,1)S(1)}, bf16[256,512]{1,0:T(8,128)(2,1)}, u32[]{:S(2)}, u32[]{:S(2)}) collective-permute-start(bf16[256,512]{1,0:T(8,128)(2,1)S(1)} %slice.118), channel_id=1, source_target_pairs={{0,1},{1,2},{2,3},{3,0},{4,5},{5,6},{6,7},{7,4},{8,9},{9,10},{10,1... | collective-permute-start | bytes 786440 | tf_op jit(solution)/shard_map/ppermute | solution.py:22
  30.8 11.4 %collective-permute-start.8 = (bf16[576,512]{1,0:T(8,128)(2,1)S(1)}, bf16[576,512]{1,0:T(8,128)(2,1)}, u32[]{:S(2)}, u32[]{:S(2)}) collective-permute-start(bf16[576,512]{1,0:T(8,128)(2,1)S(1)} %collective-permute-done.4.refs_9_), channel_id=1, source_target_pairs={{0,16},{16,0},{1,17},{17,1},{2,18},{18,2},{3,19},{19,3},{4,20},{20... | collective-permute-start | bytes 1769480 | tf_op jit(solution)/shard_map/ppermute | solution.py:22
  30.9 11.3 %copy-start.14 = (bf16[272,1024]{1,0:T(8,128)(2,1)}, bf16[272,1024]{1,0:T(8,128)(2,1)S(1)}, u32[]{:S(2)}) copy-start(bf16[272,1024]{1,0:T(8,128)(2,1)S(1)} %collective-permute-done.1.refs_3_) | copy-start | bytes 1671172
  30.9 11.3 %collective-permute-start.9 = (bf16[576,512]{1,0:T(8,128)(2,1)S(1)}, bf16[576,512]{1,0:T(8,128)(2,1)}, u32[]{:S(2)}, u32[]{:S(2)}) collective-permute-start(bf16[576,512]{1,0:T(8,128)(2,1)S(1)} %collective-permute-done.5.refs_10_), channel_id=1, source_target_pairs={{0,16},{16,0},{1,17},{17,1},{2,18},{18,2},{3,19},{19,3},{4,20},{20... | collective-permute-start | bytes 1769480 | tf_op jit(solution)/shard_map/ppermute | solution.py:22
  35.4 3.7 %copy-start.22 = (bf16[128,1024]{1,0:T(8,128)(2,1)}, bf16[128,1024]{1,0:T(8,128)(2,1)S(1)}, u32[]{:S(2)}) copy-start(bf16[128,1024]{1,0:T(8,128)(2,1)S(1)} %collective-permute-done.2.refs_4_) | copy-start | bytes 786436
  35.4 6.8 %collective-permute-start.3 = (bf16[144,1024]{1,0:T(8,128)(2,1)S(1)}, bf16[144,1024]{1,0:T(8,128)(2,1)}, u32[]{:S(2)}, u32[]{:S(2)}) collective-permute-start(bf16[144,1024]{1,0:T(8,128)(2,1)S(1)} %slice.117), channel_id=1, source_target_pairs={{0,12},{4,0},{8,4},{12,8},{1,13},{5,1},{9,5},{13,9},{2,14},{6,2},{... | collective-permute-start | bytes 884744 | tf_op jit(solution)/shard_map/ppermute | solution.py:22
  38.5 3.7 %collective-permute-start.10 = (bf16[256,512]{1,0:T(8,128)(2,1)}, bf16[256,512]{1,0:T(8,128)(2,1)}, u32[]{:S(2)}, u32[]{:S(2)}) collective-permute-start(bf16[256,512]{1,0:T(8,128)(2,1)} %collective-permute-done.6.refs_11_), channel_id=1, source_target_pairs={{0,16},{16,0},{1,17},{17,1},{2,18},{18,2},{3,19},{19,3},{4,20},{20... | collective-permute-start | bytes 786440 | tf_op jit(solution)/shard_map/ppermute | solution.py:22
  38.5 3.7 %copy-start.21 = (bf16[320,512]{1,0:T(8,128)(2,1)}, bf16[320,512]{1,0:T(8,128)(2,1)S(1)}, u32[]{:S(2)}) copy-start(bf16[320,512]{1,0:T(8,128)(2,1)S(1)} %collective-permute-done.7.refs_12_) | copy-start | bytes 983044
  38.5 3.7 %collective-permute-start.11 = (bf16[320,512]{1,0:T(8,128)(2,1)S(1)}, bf16[320,512]{1,0:T(8,128)(2,1)}, u32[]{:S(2)}, u32[]{:S(2)}) collective-permute-start(bf16[320,512]{1,0:T(8,128)(2,1)S(1)} %collective-permute-done.7.refs_12_), channel_id=1, source_target_pairs={{0,16},{16,0},{1,17},{17,1},{2,18},{18,2},{3,19},{19,3},{4,20},{20... | collective-permute-start | bytes 983048 | tf_op jit(solution)/shard_map/ppermute | solution.py:22
  39.1 3.2 %copy-start.19 = (s32[16,1,128]{2,1,0:T(1,128)}, s32[16,1,128]{2,1,0:T(1,128)S(1)}, u32[]{:S(2)}) copy-start(s32[16,1,128]{2,1,0:T(1,128)S(1)} %all-to-all-done) | copy-start | bytes 24580
  54.0 14.3 %copy-start.1 = (bf16[1024,1024]{1,0:T(8,128)(2,1)S(1)}, bf16[1024,1024]{1,0:T(8,128)(2,1)}, u32[]{:S(2)}) copy-start(bf16[1024,1024]{1,0:T(8,128)(2,1)} %get-tuple-element.44) | copy-start | bytes 6291460
  54.1 19.0 %all-to-all-start.1 = ((bf16[16,16,1024]{2,1,0:T(8,128)(2,1)}), bf16[16,16,1024]{2,1,0:T(8,128)(2,1)S(1)}, u32[]{:S(2)}, u32[]{:S(2)}) async-start(bf16[16,16,1024]{2,1,0:T(8,128)(2,1)} %bitcast.38), calls=%async_computation.1 | async-start | bytes 1048576 | tf_op jit(solution)/shard_map/all_to_all | solution.py:640
  62.4 12.8 %collective-permute-start.12 = (bf16[80,1024]{1,0:T(8,128)(2,1)S(1)}, bf16[80,1024]{1,0:T(8,128)(2,1)S(1)}, u32[]{:S(2)}, u32[]{:S(2)}) collective-permute-start(bf16[80,1024]{1,0:T(8,128)(2,1)S(1)} %get-tuple-element.46), channel_id=1, source_target_pairs={{0,1},{1,2},{2,3},{3,4},{4,5},{5,6},{6,7},{7,8},{8,9},{9,10},{10,1... | collective-permute-start | bytes 491528 | tf_op jit(solution)/shard_map/ppermute | solution.py:22
  64.3 10.8 %collective-permute-start.13 = (bf16[80,1024]{1,0:T(8,128)(2,1)S(1)}, bf16[80,1024]{1,0:T(8,128)(2,1)S(1)}, u32[]{:S(2)}, u32[]{:S(2)}) collective-permute-start(bf16[80,1024]{1,0:T(8,128)(2,1)S(1)} %get-tuple-element.47), channel_id=1, source_target_pairs={{0,15},{1,0},{2,1},{3,2},{4,3},{5,4},{6,5},{7,6},{8,7},{9,8},{10,9... | collective-permute-start | bytes 491528 | tf_op jit(solution)/shard_map/ppermute | solution.py:22
  73.0 2.1 %copy-start.3 = (bf16[16,16,1024]{2,1,0:T(8,128)(2,1)}, bf16[16,16,1024]{2,1,0:T(8,128)(2,1)S(1)}, u32[]{:S(2)}) copy-start(bf16[16,16,1024]{2,1,0:T(8,128)(2,1)S(1)} %all-to-all-done.1) | copy-start | bytes 1572868
  97.0 14.2 %all-to-all-start.2 = ((bf16[16,16,1024]{2,1,0:T(8,128)(2,1)}), bf16[16,16,1024]{2,1,0:T(8,128)(2,1)S(1)}, u32[]{:S(2)}, u32[]{:S(2)}) async-start(bf16[16,16,1024]{2,1,0:T(8,128)(2,1)} %bitcast.41), calls=%async_computation.2 | async-start | bytes 1048576 | tf_op jit(solution)/shard_map/all_to_all | solution.py:677
  111.2 0.8 copy-start.4
  111.2 26.0 %collective-permute-start.35 = (bf16[4,16,16,1024]{3,2,1,0:T(8,128)(2,1)}, bf16[4,16,16,1024]{3,2,1,0:T(8,128)(2,1)S(1)}, u32[]{:S(2)}, u32[]{:S(2)}) collective-permute-start(bf16[4,16,16,1024]{3,2,1,0:T(8,128)(2,1)} %get-tuple-element.71), channel_id=1, source_target_pairs={{0,16},{16,0},{1,17},{17,1},{2,18},{18,2},{3,19},{19,3},{4,20},{20... | collective-permute-start | bytes 6291464 | tf_op jit(solution)/shard_map/ppermute | solution.py:22
  125.2 3.5 %collective-permute-start.14 = (bf16[4,4,32,1024]{3,2,1,0:T(8,128)(2,1)}, bf16[4,4,32,1024]{3,2,1,0:T(8,128)(2,1)S(1)}, u32[]{:S(2)}, u32[]{:S(2)}) collective-permute-start(bf16[4,4,32,1024]{3,2,1,0:T(8,128)(2,1)} %get-tuple-element.64), channel_id=1, source_target_pairs={{0,16},{16,0},{1,17},{17,1},{2,18},{18,2},{3,19},{19,3},{4,20},{20... | collective-permute-start | bytes 3145736 | tf_op jit(solution)/shard_map/ppermute | solution.py:22
  125.3 17.9 %collective-permute-start.21 = (bf16[4,4,48,1024]{3,2,1,0:T(8,128)(2,1)}, bf16[4,4,48,1024]{3,2,1,0:T(8,128)(2,1)}, u32[]{:S(2)}, u32[]{:S(2)}) collective-permute-start(bf16[4,4,48,1024]{3,2,1,0:T(8,128)(2,1)} %get-tuple-element.66), channel_id=1, source_target_pairs={{0,16},{16,0},{1,17},{17,1},{2,18},{18,2},{3,19},{19,3},{4,20},{20... | collective-permute-start | bytes 4718600 | tf_op jit(solution)/shard_map/ppermute | solution.py:22
  128.7 8.6 %copy-start = (bf16[4,16,16,1024]{3,2,1,0:T(8,128)(2,1)S(1)}, bf16[4,16,16,1024]{3,2,1,0:T(8,128)(2,1)}, u32[]{:S(2)}) copy-start(bf16[4,16,16,1024]{3,2,1,0:T(8,128)(2,1)} %get-tuple-element.70) | copy-start | bytes 6291460
  131.4 16.6 %collective-permute-start.15 = (bf16[128,1024]{1,0:T(8,128)(2,1)}, bf16[128,1024]{1,0:T(8,128)(2,1)S(1)}, u32[]{:S(2)}, u32[]{:S(2)}) collective-permute-start(bf16[128,1024]{1,0:T(8,128)(2,1)} %bitcast.18), channel_id=1, source_target_pairs={{0,96},{32,0},{64,32},{96,64},{1,97},{33,1},{65,33},{97,65},{2,98}... | collective-permute-start | bytes 786440 | tf_op jit(solution)/shard_map/ppermute | solution.py:22
  135.4 15.1 %collective-permute-start.16 = (bf16[128,1024]{1,0:T(8,128)(2,1)}, bf16[128,1024]{1,0:T(8,128)(2,1)S(1)}, u32[]{:S(2)}, u32[]{:S(2)}) collective-permute-start(bf16[128,1024]{1,0:T(8,128)(2,1)} %bitcast.19), channel_id=1, source_target_pairs={{0,32},{32,64},{64,96},{96,0},{1,33},{33,65},{65,97},{97,1},{2,34}... | collective-permute-start | bytes 786440 | tf_op jit(solution)/shard_map/ppermute | solution.py:22
  135.4 15.1 %collective-permute-start.17 = (bf16[128,1024]{1,0:T(8,128)(2,1)S(1)}, bf16[128,1024]{1,0:T(8,128)(2,1)S(1)}, u32[]{:S(2)}, u32[]{:S(2)}) collective-permute-start(bf16[128,1024]{1,0:T(8,128)(2,1)S(1)} %bitcast.45), channel_id=1, source_target_pairs={{0,64},{32,96},{64,0},{96,32},{1,65},{33,97},{65,1},{97,33},{2,66}... | collective-permute-start | bytes 786440 | tf_op jit(solution)/shard_map/ppermute | solution.py:22
  139.5 32.8 %all-to-all-start.3 = ((bf16[4,16,16,1024]{3,2,1,0:T(8,128)(2,1)}), bf16[4,16,16,1024]{3,2,1,0:T(8,128)(2,1)S(1)}, u32[]{:S(2)}, u32[]{:S(2)}) async-start(bf16[4,16,16,1024]{3,2,1,0:T(8,128)(2,1)} %add_convert_fusion), calls=%async_computation.3 | async-start | bytes 4194304 | tf_op jit(solution)/shard_map/all_to_all | solution.py:686
  145.9 12.1 %collective-permute-start.22 = (bf16[192,1024]{1,0:T(8,128)(2,1)S(1)}, bf16[192,1024]{1,0:T(8,128)(2,1)S(1)}, u32[]{:S(2)}, u32[]{:S(2)}) collective-permute-start(bf16[192,1024]{1,0:T(8,128)(2,1)S(1)} %bitcast.44), channel_id=1, source_target_pairs={{0,3},{1,0},{2,1},{3,2},{4,7},{5,4},{6,5},{7,6},{8,11},{9,8},{10,9... | collective-permute-start | bytes 1179656 | tf_op jit(solution)/shard_map/ppermute | solution.py:22
  146.5 21.1 %collective-permute-start.23 = (bf16[192,1024]{1,0:T(8,128)(2,1)S(1)}, bf16[192,1024]{1,0:T(8,128)(2,1)S(1)}, u32[]{:S(2)}, u32[]{:S(2)}) collective-permute-start(bf16[192,1024]{1,0:T(8,128)(2,1)S(1)} %bitcast.43), channel_id=1, source_target_pairs={{0,1},{1,2},{2,3},{3,0},{4,5},{5,6},{6,7},{7,4},{8,9},{9,10},{10,1... | collective-permute-start | bytes 1179656 | tf_op jit(solution)/shard_map/ppermute | solution.py:22
  148.0 19.6 %collective-permute-start.24 = (bf16[192,1024]{1,0:T(8,128)(2,1)S(1)}, bf16[192,1024]{1,0:T(8,128)(2,1)S(1)}, u32[]{:S(2)}, u32[]{:S(2)}) collective-permute-start(bf16[192,1024]{1,0:T(8,128)(2,1)S(1)} %bitcast.42), channel_id=1, source_target_pairs={{0,2},{1,3},{2,0},{3,1},{4,6},{5,7},{6,4},{7,5},{8,10},{9,11},{10,... | collective-permute-start | bytes 1179656 | tf_op jit(solution)/shard_map/ppermute | solution.py:22
  150.7 19.6 %collective-permute-start.18 = (bf16[32,1024]{1,0:T(8,128)(2,1)S(1)}, bf16[32,1024]{1,0:T(8,128)(2,1)S(1)}, u32[]{:S(2)}, u32[]{:S(2)}) collective-permute-start(bf16[32,1024]{1,0:T(8,128)(2,1)S(1)} %get-tuple-element.83), channel_id=1, source_target_pairs={{0,3},{1,0},{2,1},{3,2},{4,7},{5,4},{6,5},{7,6},{8,11},{9,8},{10,9... | collective-permute-start | bytes 196616 | tf_op jit(solution)/shard_map/ppermute | solution.py:22
  151.5 20.8 %collective-permute-start.19 = (bf16[32,1024]{1,0:T(8,128)(2,1)S(1)}, bf16[32,1024]{1,0:T(8,128)(2,1)S(1)}, u32[]{:S(2)}, u32[]{:S(2)}) collective-permute-start(bf16[32,1024]{1,0:T(8,128)(2,1)S(1)} %get-tuple-element.85), channel_id=1, source_target_pairs={{0,1},{1,2},{2,3},{3,0},{4,5},{5,6},{6,7},{7,4},{8,9},{9,10},{10,1... | collective-permute-start | bytes 196616 | tf_op jit(solution)/shard_map/ppermute | solution.py:22
  158.0 14.3 %collective-permute-start.20 = (bf16[32,1024]{1,0:T(8,128)(2,1)S(1)}, bf16[32,1024]{1,0:T(8,128)(2,1)S(1)}, u32[]{:S(2)}, u32[]{:S(2)}) collective-permute-start(bf16[32,1024]{1,0:T(8,128)(2,1)S(1)} %get-tuple-element.84), channel_id=1, source_target_pairs={{0,2},{1,3},{2,0},{3,1},{4,6},{5,7},{6,4},{7,5},{8,10},{9,11},{10,... | collective-permute-start | bytes 196616 | tf_op jit(solution)/shard_map/ppermute | solution.py:22
  167.9 11.0 %collective-permute-start.25 = (bf16[48,1024]{1,0:T(8,128)(2,1)S(1)}, bf16[48,1024]{1,0:T(8,128)(2,1)S(1)}, u32[]{:S(2)}, u32[]{:S(2)}) collective-permute-start(bf16[48,1024]{1,0:T(8,128)(2,1)S(1)} %get-tuple-element.80), channel_id=1, source_target_pairs={{0,96},{32,0},{64,32},{96,64},{1,97},{33,1},{65,33},{97,65},{2,98}... | collective-permute-start | bytes 294920 | tf_op jit(solution)/shard_map/ppermute | solution.py:22
  169.7 9.3 %collective-permute-start.26 = (bf16[48,1024]{1,0:T(8,128)(2,1)S(1)}, bf16[48,1024]{1,0:T(8,128)(2,1)S(1)}, u32[]{:S(2)}, u32[]{:S(2)}) collective-permute-start(bf16[48,1024]{1,0:T(8,128)(2,1)S(1)} %get-tuple-element.82), channel_id=1, source_target_pairs={{0,32},{32,64},{64,96},{96,0},{1,33},{33,65},{65,97},{97,1},{2,34}... | collective-permute-start | bytes 294920 | tf_op jit(solution)/shard_map/ppermute | solution.py:22
  170.3 8.7 %collective-permute-start.27 = (bf16[48,1024]{1,0:T(8,128)(2,1)S(1)}, bf16[48,1024]{1,0:T(8,128)(2,1)S(1)}, u32[]{:S(2)}, u32[]{:S(2)}) collective-permute-start(bf16[48,1024]{1,0:T(8,128)(2,1)S(1)} %get-tuple-element.81), channel_id=1, source_target_pairs={{0,64},{32,96},{64,0},{96,32},{1,65},{33,97},{65,1},{97,33},{2,66}... | collective-permute-start | bytes 294920 | tf_op jit(solution)/shard_map/ppermute | solution.py:22
  173.7 23.7 %all-to-all-start.4 = ((bf16[16,16,1024]{2,1,0:T(8,128)(2,1)}), bf16[16,16,1024]{2,1,0:T(8,128)(2,1)S(1)}, u32[]{:S(2)}, u32[]{:S(2)}) async-start(bf16[16,16,1024]{2,1,0:T(8,128)(2,1)} %reduce_sum.31), calls=%async_computation.4 | async-start | bytes 1048576 | tf_op jit(solution)/shard_map/all_to_all | solution.py:687
  179.1 13.9 %copy-start.2 = (bf16[80,1024]{1,0:T(8,128)(2,1)}, bf16[80,1024]{1,0:T(8,128)(2,1)S(1)}, u32[]{:S(2)}) copy-start(bf16[80,1024]{1,0:T(8,128)(2,1)S(1)} %pad_maximum_fusion.refs_1_) | copy-start | bytes 491524
  179.1 10.7 %collective-permute-start.28 = (bf16[80,1024]{1,0:T(8,128)(2,1)S(1)}, bf16[80,1024]{1,0:T(8,128)(2,1)S(1)}, u32[]{:S(2)}, u32[]{:S(2)}) collective-permute-start(bf16[80,1024]{1,0:T(8,128)(2,1)S(1)} %pad_maximum_fusion.refs_1_), channel_id=1, source_target_pairs={{0,32},{32,64},{64,96},{96,0},{1,33},{33,65},{65,97},{97,1},{2,34}... | collective-permute-start | bytes 491528 | tf_op jit(solution)/shard_map/ppermute | solution.py:22
  181.1 8.7 %collective-permute-start.29 = (bf16[80,1024]{1,0:T(8,128)(2,1)S(1)}, bf16[80,1024]{1,0:T(8,128)(2,1)S(1)}, u32[]{:S(2)}, u32[]{:S(2)}) collective-permute-start(bf16[80,1024]{1,0:T(8,128)(2,1)S(1)} %pad_maximum_fusion.refs_1_), channel_id=1, source_target_pairs={{0,96},{32,0},{64,32},{96,64},{1,97},{33,1},{65,33},{97,65},{2,98}... | collective-permute-start | bytes 491528 | tf_op jit(solution)/shard_map/ppermute | solution.py:22
  182.4 9.2 %collective-permute-start.30 = (bf16[80,1024]{1,0:T(8,128)(2,1)S(1)}, bf16[80,1024]{1,0:T(8,128)(2,1)S(1)}, u32[]{:S(2)}, u32[]{:S(2)}) collective-permute-start(bf16[80,1024]{1,0:T(8,128)(2,1)S(1)} %pad_maximum_fusion.refs_1_), channel_id=1, source_target_pairs={{0,64},{32,96},{64,0},{96,32},{1,65},{33,97},{65,1},{97,33},{2,66}... | collective-permute-start | bytes 491528 | tf_op jit(solution)/shard_map/ppermute | solution.py:22
  184.6 6.9 %collective-permute-start.31 = (bf16[80,1024]{1,0:T(8,128)(2,1)S(1)}, bf16[80,1024]{1,0:T(8,128)(2,1)S(1)}, u32[]{:S(2)}, u32[]{:S(2)}) collective-permute-start(bf16[80,1024]{1,0:T(8,128)(2,1)S(1)} %pad_maximum_fusion.refs_1_), channel_id=1, source_target_pairs={{0,16},{16,0},{1,17},{17,1},{2,18},{18,2},{3,19},{19,3},{4,20},{20... | collective-permute-start | bytes 491528 | tf_op jit(solution)/shard_map/ppermute | solution.py:22
  189.8 3.2 %copy-start.7 = (bf16[80,1024]{1,0:T(8,128)(2,1)}, bf16[80,1024]{1,0:T(8,128)(2,1)S(1)}, u32[]{:S(2)}) copy-start(bf16[80,1024]{1,0:T(8,128)(2,1)S(1)} %collective-permute-done.28.refs_2_) | copy-start | bytes 491524
  189.8 1.8 collective-permute-start.32
  189.8 3.1 %copy-start.8 = (bf16[80,1024]{1,0:T(8,128)(2,1)}, bf16[80,1024]{1,0:T(8,128)(2,1)S(1)}, u32[]{:S(2)}) copy-start(bf16[80,1024]{1,0:T(8,128)(2,1)S(1)} %collective-permute-done.29.refs_3_) | copy-start | bytes 491524
  189.8 1.8 collective-permute-start.33
  191.6 1.4 copy-start.9
  191.6 1.4 collective-permute-start.34
  191.6 1.4 copy-start.10
  191.6 1.4 copy-start.11
  191.6 1.4 copy-start.12
  (3 other events, 2.0 us)

commit v8 on v7

--- a/solution.py
+++ b/solution.py
@@ -125,12 +125,13 @@
 def norm_kernel(
     copies,
     where_ref,
-    hidden_hbm, lens_hbm, order_hbm, in_hbm, out_hbm, table_hbm,
-    block_hbm, sum_hbm, weights_hbm,
-    hidden_ref, lens_ref, order_ref,
-    block_ref, sum_ref, weights_ref,
+    hidden_hbm, lens_hbm, order_hbm, table_hbm, in_hbm, out_hbm,
+    block_hbm, sum_hbm, weights_hbm, padded_hbm,
+    hidden_ref, lens_ref, order_ref, table_ref,
+    block_ref, sum_ref, weights_ref, padded_ref,
 ):
     core = where_ref[1]
+    table = copies.start(table_hbm, table_ref)
     packed = []
     for i in range(2):
         cols, wide = pl.ds(i * 256, 256), pl.ds(i * 512, 512)
@@ -138,15 +139,19 @@
         packed.append(copies.start(source, weights_ref.at[pl.ds(0, 256), cols]))
         source = out_hbm.at[pl.ds(pl.multiple_of(core * 128, 128), 128), wide]
         packed.append(copies.start(source, weights_ref.at[pl.ds(256 + i * 128, 128), :]))
-        source = table_hbm.at[pl.ds(pl.multiple_of(core * 32, 32), 32), wide]
-        packed.append(copies.start(source, weights_ref.at[pl.ds(512 + i * 32, 32), :]))
     first = [
         copies.start(hidden_hbm, hidden_ref),
         copies.start(lens_hbm, lens_ref),
         copies.start(order_hbm, order_ref),
     ]
+    table.wait()
+    spread = (lanes((64, 52)) == sublanes((64, 52))).astype(F32).astype(BF)
+    padded_ref[...] = dot(spread, table_ref[...]).astype(BF)
+    own = padded_ref[pl.ds(pl.multiple_of(core * 32, 32), 32), :]
+    weights_ref[512:544, :] = own[:, 0:512]
+    weights_ref[544:576, :] = own[:, 512:1024]
     wait_all(packed)
-    later = [copies.start(weights_ref, weights_hbm)]
+    later = [copies.start(weights_ref, weights_hbm), copies.start(padded_ref, padded_hbm)]
     wait_all(first)
     meta = jnp.zeros((16, 128), F32)
     for i, row in enumerate((lens_ref[...], order_ref[...])):
@@ -511,11 +516,11 @@
             rel = dot(rel_hot_ref[rel_rows, :], returned_ref[...]).astype(BF)
             inner = dot(normed_t_ref[pl.ds(pl.multiple_of(half * 512, 512), 512), :], grad_ref[:, cols]).astype(BF)
             for z in range(4):
-                out_ref[t, places[z], 0:32, :] = out[z * 32 : (z + 1) * 32]
-                out_ref[t, places[z], 32:48, :] = rel[z * 16 : (z + 1) * 16]
+                out_ref[t, places[z], :, :] = out[z * 32 : (z + 1) * 32]
+                in_ref[places[z], t, 32:48, :] = rel[z * 16 : (z + 1) * 16]
                 for i in range(4):
                     piece = inner[z * 128 + i * 32 : z * 128 + (i + 1) * 32]
-                    in_ref[places[z], t, :, i * 256 : (i + 1) * 256] = piece
+                    in_ref[places[z], t, 0:32, i * 256 : (i + 1) * 256] = piece
 
         sent_out.append(copies.start(in_ref, in_hbm))
         sent_out.append(copies.start(out_ref, out_hbm))
@@ -541,8 +546,8 @@
             for i in range(4):
                 rows = pl.ds(pl.multiple_of(half * 512 + z * 128 + i * 32, 32), 32)
                 in_ref[rows, :] = values[0:32, i * 256 : (i + 1) * 256]
-            out_ref[pl.ds(pl.multiple_of(half * 128 + z * 32, 32), 32), :] = values[32:64]
-            rel_ref[pl.ds(pl.multiple_of(half * 32 + z * 8, 8), 8), :] = values[64:72]
+            out_ref[pl.ds(pl.multiple_of(half * 128 + z * 32, 32), 32), :] = values[48:80]
+            rel_ref[pl.ds(pl.multiple_of(half * 32 + z * 8, 8), 8), :] = values[32:40]
     owned_ref[...] = rel_ref[0:52, :]
     wait_all([copies.start(in_ref, in_hbm), copies.start(out_ref, out_hbm), copies.start(owned_ref, rel_hbm)])
 
@@ -575,13 +580,12 @@
     numbers = jnp.broadcast_to(rel.reshape(1, 4, 4), (4, 4, 4)).reshape(16, 4)
     numbers = lax.all_to_all(jnp.pad(numbers, ((0, 0), (0, 124))), GROUP, 0, 0, tiled=True)
 
-    rel_pad = jnp.pad(rel_table, ((0, 64 - shard_rows), (0, 0)))
-    operands = [hidden.reshape(tokens, width), desc_len[None, :], send_order]
-    outs = [((tokens + 16, width), BF), ((entities, width), F32), ((576, 512), BF)]
-    block, hidden_sum, weights = local_call(
+    operands = [hidden.reshape(tokens, width), desc_len[None, :], send_order, rel_table]
+    outs = [((tokens + 16, width), BF), ((entities, width), F32), ((576, 512), BF), ((64, width), BF)]
+    block, hidden_sum, weights, rel_pad = local_call(
         norm_kernel,
         outs,
-        [where, *operands, w_in, w_out, rel_pad],
+        [where, *operands, w_in, w_out],
         like(operands) + filled(outs),
         copies=14,
     )
@@ -683,12 +687,8 @@
     )
     returned, graph_kept, graph_given = lax.optimization_barrier((returned, graph_kept, graph_given))
     chip = (graph_kept.astype(F32) + shift_by(graph_given, "core", 1).astype(F32)).astype(BF)
-    line = lax.all_to_all(chip, "x", 0, 0, tiled=True)
-    plane = lax.all_to_all(jnp.sum(line.astype(F32), axis=0).astype(BF), ("z", "y"), 0, 0, tiled=True)
-    weight_rows = jnp.sum(plane.astype(F32), axis=0)
-    grad_msg, grad_self = weight_rows[:8], weight_rows[8:]
-
-    outs = [((4, 4, 32, width), BF), ((4, 4, 48, width), BF)] * 2
+
+    outs = [((4, 4, 48, width), BF), ((4, 4, 32, width), BF)] * 2
     operands = [returned, route, inverse, rel_hot, pooled, all_out, slope, normed_t]
     in_given, out_given, in_kept, out_kept = local_call(
         back_kernel,
@@ -700,10 +700,16 @@
         copies=14,
         flops=2 * 4 * tokens * width * 4 * units,
     )
-    in_chip = (in_kept.astype(F32) + shift_by(in_given, "core", 1).astype(F32)).astype(BF)
+    in_other, chip = lax.optimization_barrier((shift_by(in_given, "core", 1), chip))
+    line = lax.all_to_all(chip, "x", 0, 0, tiled=True)
+    plane = lax.all_to_all(jnp.sum(line.astype(F32), axis=0).astype(BF), ("z", "y"), 0, 0, tiled=True)
+    weight_rows = jnp.sum(plane.astype(F32), axis=0)
+    grad_msg, grad_self = weight_rows[:8], weight_rows[8:]
+    in_chip = (in_kept.astype(F32) + in_other.astype(F32)).astype(BF)
+    in_chip, out_given = lax.optimization_barrier((in_chip, out_given))
     out_chip = (out_kept.astype(F32) + shift_by(out_given, "core", 1).astype(F32)).astype(BF)
-    out_part = reduce_ring([out_chip[i].reshape(192, width) for i in range(4)], "y").reshape(4, 48, width)
-    in_part = reduce_ring([in_chip[i].reshape(128, width) for i in range(4)], "z").reshape(4, 32, width)
+    out_part = reduce_ring([out_chip[i].reshape(128, width) for i in range(4)], "y").reshape(4, 32, width)
+    in_part = reduce_ring([in_chip[i].reshape(192, width) for i in range(4)], "z").reshape(4, 48, width)
     out_part = reduce_ring([out_part[i] for i in range(4)], "z")
     in_part = reduce_ring([in_part[i] for i in range(4)], "y")
     part = jnp.concatenate([in_part, out_part], axis=0)

time: 200 us -> 195 us (0.975)
  waiting for transfers between devices: 41.1 us -> 35.6 us
  other arithmetic: 15.3 us -> 18.1 us
    ppermute x36, waiting for transfers between devices: 34.6 us -> 30.5 us  [shift_by(): lax.ppermute(value, axis, [(i, (i + shift) % count) for i in range(count)])]
    unnamed x53 -> x55, local copies, waits for them, and re-layouts: 3.37 us -> 4.18 us
  transfers between devices with their start and end apart: 41 -> 41, of which waited for: 14 -> 12; matrix products, arithmetic and copies ran while one was open for 10% -> 12% of each run, Pallas kernels for 12% -> 12%
where the time goes in v8:
time: 195 us; the launch traced here: 193 us
  starting transfers between devices  69.2 us (35%)
  Pallas kernels  58.9 us (30%)
  waiting for transfers between devices  35.6 us (18%)
  other arithmetic  18.1 us (9%)
  local copies, waits for them, and re-layouts  9.71 us (5%)
    pallas_call x6, Pallas kernels, local_call(): pl.pallas_call(kernel, out_shape=[jax.ShapeDtypeStruct(shape, kind) for s...  58.9 us
    ppermute x36, starting transfers between devices, shift_by(): lax.ppermute(value, axis, [(i, (i + shift) % count) for i in range(count)])  43.2 us
    ppermute x36, waiting for transfers between devices, shift_by(): lax.ppermute(value, axis, [(i, (i + shift) % count) for i in range(count)])  30.5 us
    all_to_all x1, starting transfers between devices, shards(): lax.all_to_all(jnp.pad(numbers, ((0, 0), (0, 124))), GROUP, 0, 0, tiled=T...  7.28 us
    all_to_all x1, starting transfers between devices, shards(): lax.all_to_all(outgoing.reshape(16, 16, width), GROUP, 0, 0, tiled=True)  7.06 us
    all_to_all x1, starting transfers between devices, shards(): lax.all_to_all(jnp.sum(line.astype(F32), axis=0).astype(BF), ('z', 'y'),...  4.44 us
    unnamed x55, local copies, waits for them, and re-layouts  4.18 us
    convert_element_type x1, other arithmetic, shards(): (graph_kept.astype(F32) + shift_by(graph_given, 'core', 1).astype(F32)).a...  3.96 us
  transfers between devices with their start and end apart: 41, of which 12 were waited for; matrix products, arithmetic and copies ran while one was open for 12% of the time, Pallas kernels for 12%

profile of v8, /device:TPU:0, one launch (start us, length us, event | category | flops | bytes accessed | tf_op | source)
XLA Modules:
  0.0 193.0 jit_solution(18242938568815859149)
XLA Ops:
  1.2 3.4 %shard_map.190 = (bf16[272,1024]{1,0:T(8,128)(2,1)}, f32[16,1024]{1,0:T(8,128)}, bf16[576,512]{1,0:T(8,128)(2,1)}, bf16[64,1024]{1,0:T(8,128)(2,1)}) custom-call(s32[4]{0:T(128)} %pad_add_fusion.refs_0_, bf16[256,1024]{1,0:T(8,128)(2,1)} %bitcast.37, s32[1,16]{1,0:T(1,128)} %bitcast.49, s32[1,16]{1,0:T(1,128)} %refs_3_.1, bf16[52,1024]{1,0:T(8,128)(2,1)} %refs_4_.1, ...), custom_call_target="tpu_custom_call" | custom-call | bytes 1048576 | tf_op jit(solution)/shard_map/pallas_call | solution.py:88
  4.6 3.2 %collective-permute-start.5 = (bf16[576,512]{1,0:T(8,128)(2,1)}, bf16[576,512]{1,0:T(8,128)(2,1)S(1)}, u32[]{:S(2)}, u32[]{:S(2)}) collective-permute-start(bf16[576,512]{1,0:T(8,128)(2,1)} %get-tuple-element.46), channel_id=1, source_target_pairs={{0,3},{1,0},{2,1},{3,2},{4,7},{5,4},{6,5},{7,6},{8,11},{9,8},{10,9... | collective-permute-start | bytes 1769480 | tf_op jit(solution)/shard_map/ppermute | solution.py:22
  7.8 2.8 %collective-permute-start.1 = (bf16[272,1024]{1,0:T(8,128)(2,1)}, bf16[272,1024]{1,0:T(8,128)(2,1)S(1)}, u32[]{:S(2)}, u32[]{:S(2)}) collective-permute-start(bf16[272,1024]{1,0:T(8,128)(2,1)} %get-tuple-element.44.refs_1_), channel_id=1, source_target_pairs={{0,12},{4,0},{8,4},{12,8},{1,13},{5,1},{9,5},{13,9},{2,14},{6,2},{... | collective-permute-start | bytes 1671176 | tf_op jit(solution)/shard_map/ppermute | solution.py:22
  11.1 1.3 reduce.4
  12.7 0.7 copy.28
  13.3 7.3 %all-to-all-start = ((s32[16,1,128]{2,1,0:T(1,128)}), s32[16,1,128]{2,1,0:T(1,128)S(1)}, u32[]{:S(2)}, u32[]{:S(2)}) async-start(s32[16,1,128]{2,1,0:T(1,128)} %copy.28), calls=%async_computation | async-start | bytes 16384 | tf_op jit(solution)/shard_map/all_to_all | solution.py:581
  20.6 0.8 select_reduce_fusion
  21.4 0.7 broadcast_add_fusion
  22.0 2.0 %fusion.1.refs_4_ = bf16[2048,256]{1,0:T(8,128)(2,1)} fusion(s32[2048]{0:T(1024)} %bitcast.45), kind=kLoop, calls=%fused_computation.7 | loop fusion | flops 1048576 | bytes 1056768 | tf_op jit(solution)/shard_map/convert_element_type | solution.py:38
  24.3 1.5 fusion.refs_3_
  25.8 2.0 %collective-permute-start.2 = (bf16[128,1024]{1,0:T(8,128)(2,1)S(1)}, bf16[128,1024]{1,0:T(8,128)(2,1)S(1)}, u32[]{:S(2)}, u32[]{:S(2)}) collective-permute-start(bf16[128,1024]{1,0:T(8,128)(2,1)S(1)} %slice.116), channel_id=1, source_target_pairs={{0,4},{4,8},{8,12},{12,0},{1,5},{5,9},{9,13},{13,1},{2,6},{6,10},{... | collective-permute-start | bytes 786440 | tf_op jit(solution)/shard_map/ppermute | solution.py:22
  27.9 2.7 %collective-permute-start.7 = (bf16[320,512]{1,0:T(8,128)(2,1)S(1)}, bf16[320,512]{1,0:T(8,128)(2,1)}, u32[]{:S(2)}, u32[]{:S(2)}) collective-permute-start(bf16[320,512]{1,0:T(8,128)(2,1)S(1)} %slice.119), channel_id=1, source_target_pairs={{0,3},{1,0},{2,1},{3,2},{4,7},{5,4},{6,5},{7,6},{8,11},{9,8},{10,9... | collective-permute-start | bytes 983048 | tf_op jit(solution)/shard_map/ppermute | solution.py:22
  31.5 2.3 %collective-permute-done.2.refs_4_ = bf16[128,1024]{1,0:T(8,128)(2,1)S(1)} collective-permute-done((bf16[128,1024]{1,0:T(8,128)(2,1)S(1)}, bf16[128,1024]{1,0:T(8,128)(2,1)S(1)}, u32[]{:S(2)}, u32[]{:S(2)}) %collective-permute-start.2) | collective-permute-done | bytes 262176 | tf_op jit(solution)/shard_map/ppermute | solution.py:22
  33.8 1.7 collective-permute-start.3
  35.4 3.0 %collective-permute-done.6.refs_11_ = bf16[256,512]{1,0:T(8,128)(2,1)} collective-permute-done((bf16[256,512]{1,0:T(8,128)(2,1)S(1)}, bf16[256,512]{1,0:T(8,128)(2,1)}, u32[]{:S(2)}, u32[]{:S(2)}) %collective-permute-start.6) | collective-permute-done | bytes 262176 | tf_op jit(solution)/shard_map/ppermute | solution.py:22
  39.0 1.7 collective-permute-done.3.refs_5_
  40.7 0.8 copy-done.22
  41.6 11.8 %shard_map.191 = (bf16[256,1024]{1,0:T(8,128)(2,1)}, bf16[1024,1024]{1,0:T(8,128)(2,1)}, bf16[1024,1024]{1,0:T(8,128)(2,1)}, bf16[64,1024]{1,0:T(8,128)(2,1)}, b...) custom-call(s32[4]{0:T(128)} %pad_add_fusion.refs_0_, ...), custom_call_target="tpu_custom_call" | custom-call | flops 2147483648 | bytes 1048576 | tf_op jit(solution)/shard_map/pallas_call | solution.py:88
  53.3 7.1 %all-to-all-start.1 = ((bf16[16,16,1024]{2,1,0:T(8,128)(2,1)}), bf16[16,16,1024]{2,1,0:T(8,128)(2,1)S(1)}, u32[]{:S(2)}, u32[]{:S(2)}) async-start(bf16[16,16,1024]{2,1,0:T(8,128)(2,1)} %bitcast.38), calls=%async_computation.1 | async-start | bytes 1048576 | tf_op jit(solution)/shard_map/all_to_all | solution.py:644
  60.4 1.2 fusion.2.refs_5_
  61.6 1.9 collective-permute-start.12
  63.5 3.4 %collective-permute-start.13 = (bf16[80,1024]{1,0:T(8,128)(2,1)S(1)}, bf16[80,1024]{1,0:T(8,128)(2,1)S(1)}, u32[]{:S(2)}, u32[]{:S(2)}) collective-permute-start(bf16[80,1024]{1,0:T(8,128)(2,1)S(1)} %get-tuple-element.53), channel_id=1, source_target_pairs={{0,15},{1,0},{2,1},{3,2},{4,3},{5,4},{6,5},{7,6},{8,7},{9,8},{10,9... | collective-permute-start | bytes 491528 | tf_op jit(solution)/shard_map/ppermute | solution.py:22
  67.0 0.6 fusion.14.refs_2_
  67.6 2.6 %copy.29 = bf16[1024,1024]{0,1:T(8,128)(2,1)} copy(bf16[1024,1024]{1,0:T(8,128)(2,1)S(1)} %copy-done.1) | data formatting | bytes 4194304 | tf_op jit(solution)/shard_map/pallas_call | solution.py:88
  70.2 1.3 all-to-all-done.1
  71.5 1.7 collective-permute-done.12.refs_10_
  73.2 0.7 copy-done.24
  73.8 0.7 copy-done.25
  74.5 20.5 %shard_map.192 = (bf16[256,1024]{1,0:T(8,128)(2,1)}, bf16[256,1024]{1,0:T(8,128)(2,1)}, bf16[256,1024]{1,0:T(8,128)(2,1)}, bf16[256,1024]{1,0:T(8,128)(2,1)}, bf16[256,1024]{1,0:T(8,128)(2,1)}) custom-call(s32[4]{0:T(128)} %pad_add_fusion.refs_0_, bf16[256,1024]{1,0:T(8,128)(2,1)} %bitcast.39, bf16[64,256]{1,0:T(8,128)(2,1)} %fusion.14.refs_2_, ...), custom_call_target="tpu_custom_call" | custom-call | flops 6000000000 | bytes 1048576 | tf_op jit(solution)/shard_map/pallas_call | solution.py:88
  95.0 3.6 %all-to-all-start.2 = ((bf16[16,16,1024]{2,1,0:T(8,128)(2,1)}), bf16[16,16,1024]{2,1,0:T(8,128)(2,1)S(1)}, u32[]{:S(2)}, u32[]{:S(2)}) async-start(bf16[16,16,1024]{2,1,0:T(8,128)(2,1)} %bitcast.41), calls=%async_computation.2 | async-start | bytes 1048576 | tf_op jit(solution)/shard_map/all_to_all | solution.py:681
  98.6 6.3 %shard_map.193 = (bf16[4,16,16,1024]{3,2,1,0:T(8,128)(2,1)}, bf16[4,16,16,1024]{3,2,1,0:T(8,128)(2,1)}) custom-call(s32[4]{0:T(128)} %pad_add_fusion.refs_0_, bf16[256,1024]{1,0:T(8,128)(2,1)} %get-tuple-element.56.refs_1_, bf16[256,1024]{1,0:T(8,128)(2,1)} %get-tuple-element.57.refs_2_, bf16[256,1024]{1,0:T(8,128)(2,1)} %get-tuple-element.58.refs_3_), custom_call_target="tpu_custom_call" | custom-call | flops 1000000000 | bytes 1048576 | tf_op jit(solution)/shard_map/pallas_call | solution.py:88
  104.9 3.8 %all-to-all-done.2 = bf16[16,16,1024]{2,1,0:T(8,128)(2,1)S(1)} async-done(((bf16[16,16,1024]{2,1,0:T(8,128)(2,1)}), bf16[16,16,1024]{2,1,0:T(8,128)(2,1)S(1)}, u32[]{:S(2)}, u32[]{:S(2)}) %all-to-all-start.2) | async-done | bytes 524320 | tf_op jit(solution)/shard_map/all_to_all | solution.py:681
  108.7 0.8 copy-done.6
  109.6 13.3 %shard_map.194 = (bf16[4,4,48,1024]{3,2,1,0:T(8,128)(2,1)}, bf16[4,4,32,1024]{3,2,1,0:T(8,128)(2,1)}, bf16[4,4,48,1024]{3,2,1,0:T(8,128)(2,1)}, bf16[4,4,32,1024]{3,2,1,0:T(8,128)(2,1)}) custom-call(s32[4]{0:T(128)} %pad_add_fusion.refs_0_, bf16[256,1024]{1,0:T(8,128)(2,1)} %bitcast.40, bf16[64,256]{1,0:T(8,128)(2,1)} %get-tuple-element.62.refs_2_, ...), custom_call_target="tpu_custom_call" | custom-call | flops 2147483648 | bytes 1048576 | tf_op jit(solution)/shard_map/pallas_call | solution.py:88
  122.9 4.0 %add_convert_fusion = bf16[4,16,16,1024]{3,2,1,0:T(8,128)(2,1)} fusion(bf16[4,16,16,1024]{3,2,1,0:T(8,128)(2,1)} %collective-permute-done.15, bf16[4,16,16,1024]{3,2,1,0:T(8,128)(2,1)S(1)} %copy-done), kind=kLoop, calls=%fused_computation | loop fusion | flops 4194304 | bytes 6291456 | tf_op jit(solution)/shard_map/convert_element_type | solution.py:689
  126.9 0.7 add_convert_fusion.1
  128.1 1.0 fusion.19
  129.1 4.0 %collective-permute-start.16 = (bf16[192,1024]{1,0:T(8,128)(2,1)}, bf16[192,1024]{1,0:T(8,128)(2,1)}, u32[]{:S(2)}, u32[]{:S(2)}) collective-permute-start(bf16[192,1024]{1,0:T(8,128)(2,1)} %bitcast.18), channel_id=1, source_target_pairs={{0,96},{32,0},{64,32},{96,64},{1,97},{33,1},{65,33},{97,65},{2,98}... | collective-permute-start | bytes 1179656 | tf_op jit(solution)/shard_map/ppermute | solution.py:22
  133.1 1.9 collective-permute-start.18
  135.0 3.6 %all-to-all-start.3 = ((bf16[4,16,16,1024]{3,2,1,0:T(8,128)(2,1)}), bf16[4,16,16,1024]{3,2,1,0:T(8,128)(2,1)S(1)}, u32[]{:S(2)}, u32[]{:S(2)}) async-start(bf16[4,16,16,1024]{3,2,1,0:T(8,128)(2,1)} %add_convert_fusion), calls=%async_computation.3 | async-start | bytes 4194304 | tf_op jit(solution)/shard_map/all_to_all | solution.py:704
  138.6 1.6 add_convert_fusion.2
  140.4 0.6 collective-permute-start.23
  141.0 1.5 collective-permute-start.24
  142.5 8.1 %collective-permute-done.16 = bf16[192,1024]{1,0:T(8,128)(2,1)} collective-permute-done((bf16[192,1024]{1,0:T(8,128)(2,1)}, bf16[192,1024]{1,0:T(8,128)(2,1)}, u32[]{:S(2)}, u32[]{:S(2)}) %collective-permute-start.16) | collective-permute-done | bytes 393248 | tf_op jit(solution)/shard_map/ppermute | solution.py:22
  150.5 1.1 collective-permute-start.25
  151.7 2.3 %collective-permute-done.17 = bf16[192,1024]{1,0:T(8,128)(2,1)} collective-permute-done((bf16[192,1024]{1,0:T(8,128)(2,1)}, bf16[192,1024]{1,0:T(8,128)(2,1)}, u32[]{:S(2)}, u32[]{:S(2)}) %collective-permute-start.17) | collective-permute-done | bytes 393248 | tf_op jit(solution)/shard_map/ppermute | solution.py:22
  154.0 1.5 fusion.5
  155.5 0.6 collective-permute-start.19
  156.1 1.5 collective-permute-start.20
  157.6 1.1 collective-permute-start.21
  158.7 2.5 %collective-permute-done.25 = bf16[128,1024]{1,0:T(8,128)(2,1)S(1)} collective-permute-done((bf16[128,1024]{1,0:T(8,128)(2,1)S(1)}, bf16[128,1024]{1,0:T(8,128)(2,1)S(1)}, u32[]{:S(2)}, u32[]{:S(2)}) %collective-permute-start.25) | collective-permute-done | bytes 262176 | tf_op jit(solution)/shard_map/ppermute | solution.py:22
  161.4 4.0 %collective-permute-start.26 = (bf16[32,1024]{1,0:T(8,128)(2,1)S(1)}, bf16[32,1024]{1,0:T(8,128)(2,1)S(1)}, u32[]{:S(2)}, u32[]{:S(2)}) collective-permute-start(bf16[32,1024]{1,0:T(8,128)(2,1)S(1)} %get-tuple-element.93), channel_id=1, source_target_pairs={{0,96},{32,0},{64,32},{96,64},{1,97},{33,1},{65,33},{97,65},{2,98}... | collective-permute-start | bytes 196616 | tf_op jit(solution)/shard_map/ppermute | solution.py:22
  165.4 1.5 collective-permute-start.28
  167.0 1.3 reduce_sum.31
  168.3 4.4 %all-to-all-start.4 = ((bf16[16,16,1024]{2,1,0:T(8,128)(2,1)}), bf16[16,16,1024]{2,1,0:T(8,128)(2,1)S(1)}, u32[]{:S(2)}, u32[]{:S(2)}) async-start(bf16[16,16,1024]{2,1,0:T(8,128)(2,1)} %reduce_sum.31), calls=%async_computation.4 | async-start | bytes 1048576 | tf_op jit(solution)/shard_map/all_to_all | solution.py:705
  172.9 2.0 %collective-permute-start.29 = (bf16[80,1024]{1,0:T(8,128)(2,1)S(1)}, bf16[80,1024]{1,0:T(8,128)(2,1)S(1)}, u32[]{:S(2)}, u32[]{:S(2)}) collective-permute-start(bf16[80,1024]{1,0:T(8,128)(2,1)S(1)} %pad_maximum_fusion.refs_1_), channel_id=1, source_target_pairs={{0,32},{32,64},{64,96},{96,0},{1,33},{33,65},{65,97},{97,1},{2,34}... | collective-permute-start | bytes 491528 | tf_op jit(solution)/shard_map/ppermute | solution.py:22
  174.9 1.3 collective-permute-start.30
  176.2 2.2 %collective-permute-start.31 = (bf16[80,1024]{1,0:T(8,128)(2,1)S(1)}, bf16[80,1024]{1,0:T(8,128)(2,1)S(1)}, u32[]{:S(2)}, u32[]{:S(2)}) collective-permute-start(bf16[80,1024]{1,0:T(8,128)(2,1)S(1)} %pad_maximum_fusion.refs_1_), channel_id=1, source_target_pairs={{0,64},{32,96},{64,0},{96,32},{1,65},{33,97},{65,1},{97,33},{2,66}... | collective-permute-start | bytes 491528 | tf_op jit(solution)/shard_map/ppermute | solution.py:22
  178.4 5.9 %collective-permute-done.29.refs_2_ = bf16[80,1024]{1,0:T(8,128)(2,1)S(1)} collective-permute-done((bf16[80,1024]{1,0:T(8,128)(2,1)S(1)}, bf16[80,1024]{1,0:T(8,128)(2,1)S(1)}, u32[]{:S(2)}, u32[]{:S(2)}) %collective-permute-start.29) | collective-permute-done | bytes 163872 | tf_op jit(solution)/shard_map/ppermute | solution.py:22
  184.8 1.7 collective-permute-done.31.refs_4_
  186.6 1.3 collective-permute-done.35.refs_8_
  188.0 0.7 copy-done.15
  188.6 3.7 %shard_map.195 = (f32[1024,256]{1,0:T(8,128)}, f32[256,1024]{1,0:T(8,128)}, f32[52,1024]{1,0:T(8,128)}) custom-call(s32[4]{0:T(128)} %pad_add_fusion.refs_0_, bf16[80,1024]{1,0:T(8,128)(2,1)} %copy-done.4, bf16[80,1024]{1,0:T(8,128)(2,1)} %copy-done.9, bf16[80,1024]{1,0:T(8,128)(2,1)} %copy-done.10, bf16[80,1024]{1,0:T(8,128)(2,1)} %copy-done.11, ...), custom_call_target="tpu_custom_call" | custom-call | bytes 1048576 | tf_op jit(solution)/shard_map/pallas_call | solution.py:88
  192.4 0.6 fusion.24
  (123 shorter events, 4.8 us)
Async XLA Ops:
  0.6 23.4 %copy-start.7 = (bf16[240,1024]{1,0:T(8,128)(2,1)S(1)}, bf16[240,1024]{1,0:T(8,128)(2,1)}, u32[]{:S(2)}) copy-start(bf16[240,1024]{1,0:T(8,128)(2,1)} %refs_9_.1) | copy-start | bytes 1474564
  0.6 23.7 %copy-start.20 = (s32[1,2048]{1,0:T(1,128)S(1)}, s32[1,2048]{1,0:T(1,128)}, u32[]{:S(2)}) copy-start(s32[1,2048]{1,0:T(1,128)} %param.23) | copy-start | bytes 24580
  4.6 23.2 %collective-permute-start.5 = (bf16[576,512]{1,0:T(8,128)(2,1)}, bf16[576,512]{1,0:T(8,128)(2,1)S(1)}, u32[]{:S(2)}, u32[]{:S(2)}) collective-permute-start(bf16[576,512]{1,0:T(8,128)(2,1)} %get-tuple-element.46), channel_id=1, source_target_pairs={{0,3},{1,0},{2,1},{3,2},{4,7},{5,4},{6,5},{7,6},{8,11},{9,8},{10,9... | collective-permute-start | bytes 1769480 | tf_op jit(solution)/shard_map/ppermute | solution.py:22
  7.8 22.8 %collective-permute-start.4 = (bf16[576,512]{1,0:T(8,128)(2,1)}, bf16[576,512]{1,0:T(8,128)(2,1)S(1)}, u32[]{:S(2)}, u32[]{:S(2)}) collective-permute-start(bf16[576,512]{1,0:T(8,128)(2,1)} %get-tuple-element.46), channel_id=1, source_target_pairs={{0,1},{1,2},{2,3},{3,0},{4,5},{5,6},{6,7},{7,4},{8,9},{9,10},{10,1... | collective-permute-start | bytes 1769480 | tf_op jit(solution)/shard_map/ppermute | solution.py:22
  7.8 23.0 %collective-permute-start.1 = (bf16[272,1024]{1,0:T(8,128)(2,1)}, bf16[272,1024]{1,0:T(8,128)(2,1)S(1)}, u32[]{:S(2)}, u32[]{:S(2)}) collective-permute-start(bf16[272,1024]{1,0:T(8,128)(2,1)} %get-tuple-element.44.refs_1_), channel_id=1, source_target_pairs={{0,12},{4,0},{8,4},{12,8},{1,13},{5,1},{9,5},{13,9},{2,14},{6,2},{... | collective-permute-start | bytes 1671176 | tf_op jit(solution)/shard_map/ppermute | solution.py:22
  10.5 15.3 %collective-permute-start = (bf16[272,1024]{1,0:T(8,128)(2,1)}, bf16[272,1024]{1,0:T(8,128)(2,1)S(1)}, u32[]{:S(2)}, u32[]{:S(2)}) collective-permute-start(bf16[272,1024]{1,0:T(8,128)(2,1)} %get-tuple-element.44.refs_1_), channel_id=1, source_target_pairs={{0,4},{4,8},{8,12},{12,0},{1,5},{5,9},{9,13},{13,1},{2,6},{6,10},{... | collective-permute-start | bytes 1671176 | tf_op jit(solution)/shard_map/ppermute | solution.py:22
  13.3 25.7 %all-to-all-start = ((s32[16,1,128]{2,1,0:T(1,128)}), s32[16,1,128]{2,1,0:T(1,128)S(1)}, u32[]{:S(2)}, u32[]{:S(2)}) async-start(s32[16,1,128]{2,1,0:T(1,128)} %copy.28), calls=%async_computation | async-start | bytes 16384 | tf_op jit(solution)/shard_map/all_to_all | solution.py:581
  24.3 14.6 %copy-start.26 = (s32[1,16]{1,0:T(1,128)S(1)}, s32[1,16]{1,0:T(1,128)}, u32[]{:S(2)}) copy-start(s32[1,16]{1,0:T(1,128)} %param.20) | copy-start | bytes 196
  25.8 15.7 %copy-start.17 = (bf16[272,1024]{1,0:T(8,128)(2,1)}, bf16[272,1024]{1,0:T(8,128)(2,1)S(1)}, u32[]{:S(2)}) copy-start(bf16[272,1024]{1,0:T(8,128)(2,1)S(1)} %collective-permute-done.refs_2_) | copy-start | bytes 1671172
  25.8 7.9 %collective-permute-start.2 = (bf16[128,1024]{1,0:T(8,128)(2,1)S(1)}, bf16[128,1024]{1,0:T(8,128)(2,1)S(1)}, u32[]{:S(2)}, u32[]{:S(2)}) collective-permute-start(bf16[128,1024]{1,0:T(8,128)(2,1)S(1)} %slice.116), channel_id=1, source_target_pairs={{0,4},{4,8},{8,12},{12,0},{1,5},{5,9},{9,13},{13,1},{2,6},{6,10},{... | collective-permute-start | bytes 786440 | tf_op jit(solution)/shard_map/ppermute | solution.py:22
  27.8 13.7 %copy-start.8 = (bf16[576,512]{1,0:T(8,128)(2,1)}, bf16[576,512]{1,0:T(8,128)(2,1)S(1)}, u32[]{:S(2)}) copy-start(bf16[576,512]{1,0:T(8,128)(2,1)S(1)} %collective-permute-done.5.refs_10_) | copy-start | bytes 1769476
  27.9 10.5 %collective-permute-start.7 = (bf16[320,512]{1,0:T(8,128)(2,1)S(1)}, bf16[320,512]{1,0:T(8,128)(2,1)}, u32[]{:S(2)}, u32[]{:S(2)}) collective-permute-start(bf16[320,512]{1,0:T(8,128)(2,1)S(1)} %slice.119), channel_id=1, source_target_pairs={{0,3},{1,0},{2,1},{3,2},{4,7},{5,4},{6,5},{7,6},{8,11},{9,8},{10,9... | collective-permute-start | bytes 983048 | tf_op jit(solution)/shard_map/ppermute | solution.py:22
  30.6 10.9 %copy-start.18 = (bf16[576,512]{1,0:T(8,128)(2,1)}, bf16[576,512]{1,0:T(8,128)(2,1)S(1)}, u32[]{:S(2)}) copy-start(bf16[576,512]{1,0:T(8,128)(2,1)S(1)} %collective-permute-done.4.refs_9_) | copy-start | bytes 1769476
  30.6 7.8 %collective-permute-start.6 = (bf16[256,512]{1,0:T(8,128)(2,1)S(1)}, bf16[256,512]{1,0:T(8,128)(2,1)}, u32[]{:S(2)}, u32[]{:S(2)}) collective-permute-start(bf16[256,512]{1,0:T(8,128)(2,1)S(1)} %slice.118), channel_id=1, source_target_pairs={{0,1},{1,2},{2,3},{3,0},{4,5},{5,6},{6,7},{7,4},{8,9},{9,10},{10,1... | collective-permute-start | bytes 786440 | tf_op jit(solution)/shard_map/ppermute | solution.py:22
  30.7 10.0 %collective-permute-start.8 = (bf16[576,512]{1,0:T(8,128)(2,1)S(1)}, bf16[576,512]{1,0:T(8,128)(2,1)S(1)}, u32[]{:S(2)}, u32[]{:S(2)}) collective-permute-start(bf16[576,512]{1,0:T(8,128)(2,1)S(1)} %collective-permute-done.4.refs_9_), channel_id=1, source_target_pairs={{0,16},{16,0},{1,17},{17,1},{2,18},{18,2},{3,19},{19,3},{4,20},{20... | collective-permute-start | bytes 1769480 | tf_op jit(solution)/shard_map/ppermute | solution.py:22
  30.8 10.7 %copy-start.16 = (bf16[272,1024]{1,0:T(8,128)(2,1)}, bf16[272,1024]{1,0:T(8,128)(2,1)S(1)}, u32[]{:S(2)}) copy-start(bf16[272,1024]{1,0:T(8,128)(2,1)S(1)} %collective-permute-done.1.refs_3_) | copy-start | bytes 1671172
  30.8 9.9 %collective-permute-start.9 = (bf16[576,512]{1,0:T(8,128)(2,1)S(1)}, bf16[576,512]{1,0:T(8,128)(2,1)}, u32[]{:S(2)}, u32[]{:S(2)}) collective-permute-start(bf16[576,512]{1,0:T(8,128)(2,1)S(1)} %collective-permute-done.5.refs_10_), channel_id=1, source_target_pairs={{0,16},{16,0},{1,17},{17,1},{2,18},{18,2},{3,19},{19,3},{4,20},{20... | collective-permute-start | bytes 1769480 | tf_op jit(solution)/shard_map/ppermute | solution.py:22
  33.8 5.2 %copy-start.23 = (bf16[128,1024]{1,0:T(8,128)(2,1)}, bf16[128,1024]{1,0:T(8,128)(2,1)S(1)}, u32[]{:S(2)}) copy-start(bf16[128,1024]{1,0:T(8,128)(2,1)S(1)} %collective-permute-done.2.refs_4_) | copy-start | bytes 786436
  33.8 6.9 %collective-permute-start.3 = (bf16[144,1024]{1,0:T(8,128)(2,1)S(1)}, bf16[144,1024]{1,0:T(8,128)(2,1)}, u32[]{:S(2)}, u32[]{:S(2)}) collective-permute-start(bf16[144,1024]{1,0:T(8,128)(2,1)S(1)} %slice.117), channel_id=1, source_target_pairs={{0,12},{4,0},{8,4},{12,8},{1,13},{5,1},{9,5},{13,9},{2,14},{6,2},{... | collective-permute-start | bytes 884744 | tf_op jit(solution)/shard_map/ppermute | solution.py:22
  38.4 2.3 %collective-permute-start.10 = (bf16[256,512]{1,0:T(8,128)(2,1)}, bf16[256,512]{1,0:T(8,128)(2,1)}, u32[]{:S(2)}, u32[]{:S(2)}) collective-permute-start(bf16[256,512]{1,0:T(8,128)(2,1)} %collective-permute-done.6.refs_11_), channel_id=1, source_target_pairs={{0,16},{16,0},{1,17},{17,1},{2,18},{18,2},{3,19},{19,3},{4,20},{20... | collective-permute-start | bytes 786440 | tf_op jit(solution)/shard_map/ppermute | solution.py:22
  38.4 2.3 %collective-permute-start.11 = (bf16[320,512]{1,0:T(8,128)(2,1)}, bf16[320,512]{1,0:T(8,128)(2,1)}, u32[]{:S(2)}, u32[]{:S(2)}) collective-permute-start(bf16[320,512]{1,0:T(8,128)(2,1)} %collective-permute-done.7.refs_12_), channel_id=1, source_target_pairs={{0,16},{16,0},{1,17},{17,1},{2,18},{18,2},{3,19},{19,3},{4,20},{20... | collective-permute-start | bytes 983048 | tf_op jit(solution)/shard_map/ppermute | solution.py:22
  39.0 2.5 %copy-start.21 = (s32[16,1,128]{2,1,0:T(1,128)}, s32[16,1,128]{2,1,0:T(1,128)S(1)}, u32[]{:S(2)}) copy-start(s32[16,1,128]{2,1,0:T(1,128)S(1)} %all-to-all-done) | copy-start | bytes 24580
  40.7 0.8 copy-start.22
  41.5 18.9 %copy-start.19 = (s32[1,2048]{1,0:T(1,128)S(1)}, s32[1,2048]{1,0:T(1,128)}, u32[]{:S(2)}) copy-start(s32[1,2048]{1,0:T(1,128)} %param.24) | copy-start | bytes 24580
  53.3 14.3 %copy-start.1 = (bf16[1024,1024]{1,0:T(8,128)(2,1)S(1)}, bf16[1024,1024]{1,0:T(8,128)(2,1)}, u32[]{:S(2)}) copy-start(bf16[1024,1024]{1,0:T(8,128)(2,1)} %get-tuple-element.50) | copy-start | bytes 6291460
  53.3 18.1 %all-to-all-start.1 = ((bf16[16,16,1024]{2,1,0:T(8,128)(2,1)}), bf16[16,16,1024]{2,1,0:T(8,128)(2,1)S(1)}, u32[]{:S(2)}, u32[]{:S(2)}) async-start(bf16[16,16,1024]{2,1,0:T(8,128)(2,1)} %bitcast.38), calls=%async_computation.1 | async-start | bytes 1048576 | tf_op jit(solution)/shard_map/all_to_all | solution.py:644
  61.6 11.5 %collective-permute-start.12 = (bf16[80,1024]{1,0:T(8,128)(2,1)S(1)}, bf16[80,1024]{1,0:T(8,128)(2,1)S(1)}, u32[]{:S(2)}, u32[]{:S(2)}) collective-permute-start(bf16[80,1024]{1,0:T(8,128)(2,1)S(1)} %get-tuple-element.52), channel_id=1, source_target_pairs={{0,1},{1,2},{2,3},{3,4},{4,5},{5,6},{6,7},{7,8},{8,9},{9,10},{10,1... | collective-permute-start | bytes 491528 | tf_op jit(solution)/shard_map/ppermute | solution.py:22
  63.5 9.6 %collective-permute-start.13 = (bf16[80,1024]{1,0:T(8,128)(2,1)S(1)}, bf16[80,1024]{1,0:T(8,128)(2,1)S(1)}, u32[]{:S(2)}, u32[]{:S(2)}) collective-permute-start(bf16[80,1024]{1,0:T(8,128)(2,1)S(1)} %get-tuple-element.53), channel_id=1, source_target_pairs={{0,15},{1,0},{2,1},{3,2},{4,3},{5,4},{6,5},{7,6},{8,7},{9,8},{10,9... | collective-permute-start | bytes 491528 | tf_op jit(solution)/shard_map/ppermute | solution.py:22
  71.5 1.7 copy-start.5
  95.0 13.7 %all-to-all-start.2 = ((bf16[16,16,1024]{2,1,0:T(8,128)(2,1)}), bf16[16,16,1024]{2,1,0:T(8,128)(2,1)S(1)}, u32[]{:S(2)}, u32[]{:S(2)}) async-start(bf16[16,16,1024]{2,1,0:T(8,128)(2,1)} %bitcast.41), calls=%async_computation.2 | async-start | bytes 1048576 | tf_op jit(solution)/shard_map/all_to_all | solution.py:681
  108.7 14.2 %collective-permute-start.15 = (bf16[4,16,16,1024]{3,2,1,0:T(8,128)(2,1)}, bf16[4,16,16,1024]{3,2,1,0:T(8,128)(2,1)}, u32[]{:S(2)}, u32[]{:S(2)}) collective-permute-start(bf16[4,16,16,1024]{3,2,1,0:T(8,128)(2,1)} %get-tuple-element.72), channel_id=1, source_target_pairs={{0,16},{16,0},{1,17},{17,1},{2,18},{18,2},{3,19},{19,3},{4,20},{20... | collective-permute-start | bytes 6291464 | tf_op jit(solution)/shard_map/ppermute | solution.py:22
  109.6 13.4 %copy-start = (bf16[4,16,16,1024]{3,2,1,0:T(8,128)(2,1)S(1)}, bf16[4,16,16,1024]{3,2,1,0:T(8,128)(2,1)}, u32[]{:S(2)}) copy-start(bf16[4,16,16,1024]{3,2,1,0:T(8,128)(2,1)} %get-tuple-element.71) | copy-start | bytes 6291460
  122.8 4.1 %copy-start.2 = (bf16[4,4,48,1024]{3,2,1,0:T(8,128)(2,1)S(1)}, bf16[4,4,48,1024]{3,2,1,0:T(8,128)(2,1)}, u32[]{:S(2)}) copy-start(bf16[4,4,48,1024]{3,2,1,0:T(8,128)(2,1)} %get-tuple-element.69) | copy-start | bytes 4718596
  122.8 4.1 %collective-permute-start.14 = (bf16[4,4,48,1024]{3,2,1,0:T(8,128)(2,1)}, bf16[4,4,48,1024]{3,2,1,0:T(8,128)(2,1)S(1)}, u32[]{:S(2)}, u32[]{:S(2)}) collective-permute-start(bf16[4,4,48,1024]{3,2,1,0:T(8,128)(2,1)} %get-tuple-element.70), channel_id=1, source_target_pairs={{0,16},{16,0},{1,17},{17,1},{2,18},{18,2},{3,19},{19,3},{4,20},{20... | collective-permute-start | bytes 4718600 | tf_op jit(solution)/shard_map/ppermute | solution.py:22
  127.6 11.0 %collective-permute-start.22 = (bf16[4,4,32,1024]{3,2,1,0:T(8,128)(2,1)}, bf16[4,4,32,1024]{3,2,1,0:T(8,128)(2,1)}, u32[]{:S(2)}, u32[]{:S(2)}) collective-permute-start(bf16[4,4,32,1024]{3,2,1,0:T(8,128)(2,1)} %get-tuple-element.77), channel_id=1, source_target_pairs={{0,16},{16,0},{1,17},{17,1},{2,18},{18,2},{3,19},{19,3},{4,20},{20... | collective-permute-start | bytes 3145736 | tf_op jit(solution)/shard_map/ppermute | solution.py:22
  129.1 21.4 %collective-permute-start.16 = (bf16[192,1024]{1,0:T(8,128)(2,1)}, bf16[192,1024]{1,0:T(8,128)(2,1)}, u32[]{:S(2)}, u32[]{:S(2)}) collective-permute-start(bf16[192,1024]{1,0:T(8,128)(2,1)} %bitcast.18), channel_id=1, source_target_pairs={{0,96},{32,0},{64,32},{96,64},{1,97},{33,1},{65,33},{97,65},{2,98}... | collective-permute-start | bytes 1179656 | tf_op jit(solution)/shard_map/ppermute | solution.py:22
  133.1 20.8 %collective-permute-start.17 = (bf16[192,1024]{1,0:T(8,128)(2,1)}, bf16[192,1024]{1,0:T(8,128)(2,1)}, u32[]{:S(2)}, u32[]{:S(2)}) collective-permute-start(bf16[192,1024]{1,0:T(8,128)(2,1)} %bitcast.19), channel_id=1, source_target_pairs={{0,32},{32,64},{64,96},{96,0},{1,33},{33,65},{65,97},{97,1},{2,34}... | collective-permute-start | bytes 1179656 | tf_op jit(solution)/shard_map/ppermute | solution.py:22
  133.1 5.5 %copy-start.3 = (bf16[4,4,32,1024]{3,2,1,0:T(8,128)(2,1)S(1)}, bf16[4,4,32,1024]{3,2,1,0:T(8,128)(2,1)}, u32[]{:S(2)}) copy-start(bf16[4,4,32,1024]{3,2,1,0:T(8,128)(2,1)} %get-tuple-element.76) | copy-start | bytes 3145732
  133.1 20.8 %collective-permute-start.18 = (bf16[192,1024]{1,0:T(8,128)(2,1)}, bf16[192,1024]{1,0:T(8,128)(2,1)}, u32[]{:S(2)}, u32[]{:S(2)}) collective-permute-start(bf16[192,1024]{1,0:T(8,128)(2,1)} %bitcast.20), channel_id=1, source_target_pairs={{0,64},{32,96},{64,0},{96,32},{1,65},{33,97},{65,1},{97,33},{2,66}... | collective-permute-start | bytes 1179656 | tf_op jit(solution)/shard_map/ppermute | solution.py:22
  135.0 32.0 %all-to-all-start.3 = ((bf16[4,16,16,1024]{3,2,1,0:T(8,128)(2,1)}), bf16[4,16,16,1024]{3,2,1,0:T(8,128)(2,1)S(1)}, u32[]{:S(2)}, u32[]{:S(2)}) async-start(bf16[4,16,16,1024]{3,2,1,0:T(8,128)(2,1)} %add_convert_fusion), calls=%async_computation.3 | async-start | bytes 4194304 | tf_op jit(solution)/shard_map/all_to_all | solution.py:704
  140.4 17.2 %collective-permute-start.23 = (bf16[128,1024]{1,0:T(8,128)(2,1)S(1)}, bf16[128,1024]{1,0:T(8,128)(2,1)S(1)}, u32[]{:S(2)}, u32[]{:S(2)}) collective-permute-start(bf16[128,1024]{1,0:T(8,128)(2,1)S(1)} %bitcast.44), channel_id=1, source_target_pairs={{0,3},{1,0},{2,1},{3,2},{4,7},{5,4},{6,5},{7,6},{8,11},{9,8},{10,9... | collective-permute-start | bytes 786440 | tf_op jit(solution)/shard_map/ppermute | solution.py:22
  141.0 17.7 %collective-permute-start.24 = (bf16[128,1024]{1,0:T(8,128)(2,1)S(1)}, bf16[128,1024]{1,0:T(8,128)(2,1)S(1)}, u32[]{:S(2)}, u32[]{:S(2)}) collective-permute-start(bf16[128,1024]{1,0:T(8,128)(2,1)S(1)} %bitcast.43), channel_id=1, source_target_pairs={{0,1},{1,2},{2,3},{3,0},{4,5},{5,6},{6,7},{7,4},{8,9},{9,10},{10,1... | collective-permute-start | bytes 786440 | tf_op jit(solution)/shard_map/ppermute | solution.py:22
  150.5 10.6 %collective-permute-start.25 = (bf16[128,1024]{1,0:T(8,128)(2,1)S(1)}, bf16[128,1024]{1,0:T(8,128)(2,1)S(1)}, u32[]{:S(2)}, u32[]{:S(2)}) collective-permute-start(bf16[128,1024]{1,0:T(8,128)(2,1)S(1)} %bitcast.42), channel_id=1, source_target_pairs={{0,2},{1,3},{2,0},{3,1},{4,6},{5,7},{6,4},{7,5},{8,10},{9,11},{10,... | collective-permute-start | bytes 786440 | tf_op jit(solution)/shard_map/ppermute | solution.py:22
  155.5 9.9 %collective-permute-start.19 = (bf16[48,1024]{1,0:T(8,128)(2,1)S(1)}, bf16[48,1024]{1,0:T(8,128)(2,1)S(1)}, u32[]{:S(2)}, u32[]{:S(2)}) collective-permute-start(bf16[48,1024]{1,0:T(8,128)(2,1)S(1)} %get-tuple-element.90), channel_id=1, source_target_pairs={{0,3},{1,0},{2,1},{3,2},{4,7},{5,4},{6,5},{7,6},{8,11},{9,8},{10,9... | collective-permute-start | bytes 294920 | tf_op jit(solution)/shard_map/ppermute | solution.py:22
  156.1 10.8 %collective-permute-start.20 = (bf16[48,1024]{1,0:T(8,128)(2,1)S(1)}, bf16[48,1024]{1,0:T(8,128)(2,1)S(1)}, u32[]{:S(2)}, u32[]{:S(2)}) collective-permute-start(bf16[48,1024]{1,0:T(8,128)(2,1)S(1)} %get-tuple-element.92), channel_id=1, source_target_pairs={{0,1},{1,2},{2,3},{3,0},{4,5},{5,6},{6,7},{7,4},{8,9},{9,10},{10,1... | collective-permute-start | bytes 294920 | tf_op jit(solution)/shard_map/ppermute | solution.py:22
  157.6 9.3 %collective-permute-start.21 = (bf16[48,1024]{1,0:T(8,128)(2,1)S(1)}, bf16[48,1024]{1,0:T(8,128)(2,1)S(1)}, u32[]{:S(2)}, u32[]{:S(2)}) collective-permute-start(bf16[48,1024]{1,0:T(8,128)(2,1)S(1)} %get-tuple-element.91), channel_id=1, source_target_pairs={{0,2},{1,3},{2,0},{3,1},{4,6},{5,7},{6,4},{7,5},{8,10},{9,11},{10,... | collective-permute-start | bytes 294920 | tf_op jit(solution)/shard_map/ppermute | solution.py:22
  161.4 11.4 %collective-permute-start.26 = (bf16[32,1024]{1,0:T(8,128)(2,1)S(1)}, bf16[32,1024]{1,0:T(8,128)(2,1)S(1)}, u32[]{:S(2)}, u32[]{:S(2)}) collective-permute-start(bf16[32,1024]{1,0:T(8,128)(2,1)S(1)} %get-tuple-element.93), channel_id=1, source_target_pairs={{0,96},{32,0},{64,32},{96,64},{1,97},{33,1},{65,33},{97,65},{2,98}... | collective-permute-start | bytes 196616 | tf_op jit(solution)/shard_map/ppermute | solution.py:22
  165.4 7.4 %collective-permute-start.27 = (bf16[32,1024]{1,0:T(8,128)(2,1)S(1)}, bf16[32,1024]{1,0:T(8,128)(2,1)S(1)}, u32[]{:S(2)}, u32[]{:S(2)}) collective-permute-start(bf16[32,1024]{1,0:T(8,128)(2,1)S(1)} %get-tuple-element.95), channel_id=1, source_target_pairs={{0,32},{32,64},{64,96},{96,0},{1,33},{33,65},{65,97},{97,1},{2,34}... | collective-permute-start | bytes 196616 | tf_op jit(solution)/shard_map/ppermute | solution.py:22
  165.4 7.4 %collective-permute-start.28 = (bf16[32,1024]{1,0:T(8,128)(2,1)S(1)}, bf16[32,1024]{1,0:T(8,128)(2,1)S(1)}, u32[]{:S(2)}, u32[]{:S(2)}) collective-permute-start(bf16[32,1024]{1,0:T(8,128)(2,1)S(1)} %get-tuple-element.94), channel_id=1, source_target_pairs={{0,64},{32,96},{64,0},{96,32},{1,65},{33,97},{65,1},{97,33},{2,66}... | collective-permute-start | bytes 196616 | tf_op jit(solution)/shard_map/ppermute | solution.py:22
  168.3 24.0 %all-to-all-start.4 = ((bf16[16,16,1024]{2,1,0:T(8,128)(2,1)}), bf16[16,16,1024]{2,1,0:T(8,128)(2,1)S(1)}, u32[]{:S(2)}, u32[]{:S(2)}) async-start(bf16[16,16,1024]{2,1,0:T(8,128)(2,1)} %reduce_sum.31), calls=%async_computation.4 | async-start | bytes 1048576 | tf_op jit(solution)/shard_map/all_to_all | solution.py:705
  172.9 15.0 %copy-start.4 = (bf16[80,1024]{1,0:T(8,128)(2,1)}, bf16[80,1024]{1,0:T(8,128)(2,1)S(1)}, u32[]{:S(2)}) copy-start(bf16[80,1024]{1,0:T(8,128)(2,1)S(1)} %pad_maximum_fusion.refs_1_) | copy-start | bytes 491524
  172.9 11.4 %collective-permute-start.29 = (bf16[80,1024]{1,0:T(8,128)(2,1)S(1)}, bf16[80,1024]{1,0:T(8,128)(2,1)S(1)}, u32[]{:S(2)}, u32[]{:S(2)}) collective-permute-start(bf16[80,1024]{1,0:T(8,128)(2,1)S(1)} %pad_maximum_fusion.refs_1_), channel_id=1, source_target_pairs={{0,32},{32,64},{64,96},{96,0},{1,33},{33,65},{65,97},{97,1},{2,34}... | collective-permute-start | bytes 491528 | tf_op jit(solution)/shard_map/ppermute | solution.py:22
  174.9 9.5 %collective-permute-start.30 = (bf16[80,1024]{1,0:T(8,128)(2,1)S(1)}, bf16[80,1024]{1,0:T(8,128)(2,1)S(1)}, u32[]{:S(2)}, u32[]{:S(2)}) collective-permute-start(bf16[80,1024]{1,0:T(8,128)(2,1)S(1)} %pad_maximum_fusion.refs_1_), channel_id=1, source_target_pairs={{0,96},{32,0},{64,32},{96,64},{1,97},{33,1},{65,33},{97,65},{2,98}... | collective-permute-start | bytes 491528 | tf_op jit(solution)/shard_map/ppermute | solution.py:22
  176.2 10.3 %collective-permute-start.31 = (bf16[80,1024]{1,0:T(8,128)(2,1)S(1)}, bf16[80,1024]{1,0:T(8,128)(2,1)S(1)}, u32[]{:S(2)}, u32[]{:S(2)}) collective-permute-start(bf16[80,1024]{1,0:T(8,128)(2,1)S(1)} %pad_maximum_fusion.refs_1_), channel_id=1, source_target_pairs={{0,64},{32,96},{64,0},{96,32},{1,65},{33,97},{65,1},{97,33},{2,66}... | collective-permute-start | bytes 491528 | tf_op jit(solution)/shard_map/ppermute | solution.py:22
  178.4 8.1 %collective-permute-start.32 = (bf16[80,1024]{1,0:T(8,128)(2,1)S(1)}, bf16[80,1024]{1,0:T(8,128)(2,1)S(1)}, u32[]{:S(2)}, u32[]{:S(2)}) collective-permute-start(bf16[80,1024]{1,0:T(8,128)(2,1)S(1)} %pad_maximum_fusion.refs_1_), channel_id=1, source_target_pairs={{0,16},{16,0},{1,17},{17,1},{2,18},{18,2},{3,19},{19,3},{4,20},{20... | collective-permute-start | bytes 491528 | tf_op jit(solution)/shard_map/ppermute | solution.py:22
  184.3 3.6 %copy-start.9 = (bf16[80,1024]{1,0:T(8,128)(2,1)}, bf16[80,1024]{1,0:T(8,128)(2,1)S(1)}, u32[]{:S(2)}) copy-start(bf16[80,1024]{1,0:T(8,128)(2,1)S(1)} %collective-permute-done.29.refs_2_) | copy-start | bytes 491524
  184.3 2.2 %collective-permute-start.33 = (bf16[80,1024]{1,0:T(8,128)(2,1)S(1)}, bf16[80,1024]{1,0:T(8,128)(2,1)S(1)}, u32[]{:S(2)}, u32[]{:S(2)}) collective-permute-start(bf16[80,1024]{1,0:T(8,128)(2,1)S(1)} %collective-permute-done.29.refs_2_), channel_id=1, source_target_pairs={{0,16},{16,0},{1,17},{17,1},{2,18},{18,2},{3,19},{19,3},{4,20},{20... | collective-permute-start | bytes 491528 | tf_op jit(solution)/shard_map/ppermute | solution.py:22
  184.3 3.6 %copy-start.10 = (bf16[80,1024]{1,0:T(8,128)(2,1)}, bf16[80,1024]{1,0:T(8,128)(2,1)S(1)}, u32[]{:S(2)}) copy-start(bf16[80,1024]{1,0:T(8,128)(2,1)S(1)} %collective-permute-done.30.refs_3_) | copy-start | bytes 491524
  184.4 2.2 %collective-permute-start.34 = (bf16[80,1024]{1,0:T(8,128)(2,1)S(1)}, bf16[80,1024]{1,0:T(8,128)(2,1)S(1)}, u32[]{:S(2)}, u32[]{:S(2)}) collective-permute-start(bf16[80,1024]{1,0:T(8,128)(2,1)S(1)} %collective-permute-done.30.refs_3_), channel_id=1, source_target_pairs={{0,16},{16,0},{1,17},{17,1},{2,18},{18,2},{3,19},{19,3},{4,20},{20... | collective-permute-start | bytes 491528 | tf_op jit(solution)/shard_map/ppermute | solution.py:22
  186.5 1.4 copy-start.11
  186.5 1.4 collective-permute-start.35
  186.5 1.4 copy-start.12
  186.6 1.4 copy-start.13
  186.6 1.4 copy-start.14
  (4 other events, 2.8 us)

commit v9 on v8

--- a/solution.py
+++ b/solution.py
@@ -593,6 +593,22 @@
     mine = gather_ring(weights, "y", 256)
     other = [shift_by(part, "core", 1) for part in mine]
 
+    halo = halo_rows[0]
+    place = place_order[0]
+    side = halo.shape[0] // 2
+    cache_count = cache.shape[0]
+    boundary = dot(one_hot(halo - entities, cache_count), cache).astype(BF)
+    halo_hot = halo[:, None] == jnp.arange(entities, dtype=I32)[None, :]
+    halo_place = jnp.where(halo < entities, jnp.sum(jnp.where(halo_hot, place[None, :], 0), axis=1), 16)
+
+    def edge_of(rows, places):
+        return jnp.concatenate([rows, jnp.pad(row_of(places, width), ((0, 15), (0, 0)))], axis=0)
+
+    to_high, to_low = edge_of(boundary[side:], halo_place[side:]), edge_of(boundary[:side], halo_place[:side])
+    from_low = shift_by(to_high, GROUP, 1)
+    from_high = shift_by(to_low, GROUP, 15)
+    mine[2], from_low, from_high = lax.optimization_barrier((mine[2], from_low, from_high))
+
     outs = [
         ((256, width), BF),
         ((4 * tokens, width), BF),
@@ -620,21 +636,6 @@
         flops=2 * 4 * tokens * width * 4 * units,
     )
 
-    halo = halo_rows[0]
-    place = place_order[0]
-    side = halo.shape[0] // 2
-    cache_count = cache.shape[0]
-    boundary = dot(one_hot(halo - entities, cache_count), cache).astype(BF)
-    halo_hot = halo[:, None] == jnp.arange(entities, dtype=I32)[None, :]
-    halo_place = jnp.where(halo < entities, jnp.sum(jnp.where(halo_hot, place[None, :], 0), axis=1), 16)
-
-    def edge_of(rows, places):
-        return jnp.concatenate([rows, jnp.pad(row_of(places, width), ((0, 15), (0, 0)))], axis=0)
-
-    to_high, to_low = edge_of(boundary[side:], halo_place[side:]), edge_of(boundary[:side], halo_place[:side])
-    to_high, to_low, outgoing = lax.optimization_barrier((to_high, to_low, outgoing))
-    from_low = shift_by(to_high, GROUP, 1)
-    from_high = shift_by(to_low, GROUP, 15)
     own_row = jnp.concatenate([fresh_row(0, place), jnp.full((cache_count,), -1, I32)])
     node_count = entities + cache_count
     extended_count = node_count + 2 * side

time: 195 us -> 195 us (level)
  waiting for transfers between devices: 35.6 us -> 38.9 us
  starting transfers between devices: 69.2 us -> 66.7 us
    all_to_all x1, waiting for transfers between devices: 1.29 us -> 7.48 us  [shards(): lax.all_to_all(outgoing.reshape(16, 16, width), GROUP, 0, 0, tiled=True)]
    ppermute x36, waiting for transfers between devices: 30.5 us -> 26.8 us  [shift_by(): lax.ppermute(value, axis, [(i, (i + shift) % count) for i in range(count)])]
    unnamed x55 -> x53, local copies, waits for them, and re-layouts: 4.18 us -> 3.74 us
  transfers between devices with their start and end apart: 41 -> 41, of which waited for: 12 -> 12; matrix products, arithmetic and copies ran while one was open for 12% -> 11% of each run, Pallas kernels for 12% -> 12%
where the time goes in v9:
time: 195 us; the launch traced here: 193 us
  starting transfers between devices  66.7 us (34%)
  Pallas kernels  59 us (30%)
  waiting for transfers between devices  38.9 us (20%)
  other arithmetic  16.8 us (9%)
  local copies, waits for them, and re-layouts  9.27 us (5%)
    pallas_call x6, Pallas kernels, local_call(): pl.pallas_call(kernel, out_shape=[jax.ShapeDtypeStruct(shape, kind) for s...  59 us
    ppermute x36, starting transfers between devices, shift_by(): lax.ppermute(value, axis, [(i, (i + shift) % count) for i in range(count)])  41.9 us
    ppermute x36, waiting for transfers between devices, shift_by(): lax.ppermute(value, axis, [(i, (i + shift) % count) for i in range(count)])  26.8 us
    all_to_all x1, starting transfers between devices, shards(): lax.all_to_all(jnp.pad(numbers, ((0, 0), (0, 124))), GROUP, 0, 0, tiled=T...  7.82 us
    all_to_all x1, waiting for transfers between devices, shards(): lax.all_to_all(outgoing.reshape(16, 16, width), GROUP, 0, 0, tiled=True)  7.48 us
    all_to_all x1, starting transfers between devices, shards(): lax.all_to_all(outgoing.reshape(16, 16, width), GROUP, 0, 0, tiled=True)  5.4 us
    all_to_all x1, waiting for transfers between devices, shards(): lax.all_to_all(grad_table.reshape(16, 16, width), GROUP, 0, 0, tiled=True)  4.64 us
    all_to_all x1, starting transfers between devices, shards(): lax.all_to_all(jnp.sum(line.astype(F32), axis=0).astype(BF), ('z', 'y'),...  4.44 us
  transfers between devices with their start and end apart: 41, of which 12 were waited for; matrix products, arithmetic and copies ran while one was open for 11% of the time, Pallas kernels for 12%

profile of v9, /device:TPU:0, one launch (start us, length us, event | category | flops | bytes accessed | tf_op | source)
XLA Modules:
  0.0 193.3 jit_solution(3571010603461020517)
XLA Ops:
  0.6 0.6 pad_add_fusion.refs_0_
  1.3 3.3 %shard_map.190 = (bf16[272,1024]{1,0:T(8,128)(2,1)}, f32[16,1024]{1,0:T(8,128)}, bf16[576,512]{1,0:T(8,128)(2,1)}, bf16[64,1024]{1,0:T(8,128)(2,1)}) custom-call(s32[4]{0:T(128)} %pad_add_fusion.refs_0_, bf16[256,1024]{1,0:T(8,128)(2,1)} %bitcast.37, s32[1,16]{1,0:T(1,128)} %bitcast.49, s32[1,16]{1,0:T(1,128)} %refs_3_.1, bf16[52,1024]{1,0:T(8,128)(2,1)} %refs_4_.1, ...), custom_call_target="tpu_custom_call" | custom-call | bytes 1048576 | tf_op jit(solution)/shard_map/pallas_call | solution.py:88
  4.6 1.7 collective-permute-start.4
  6.4 1.6 collective-permute-start.5
  7.9 2.8 %collective-permute-start.1 = (bf16[272,1024]{1,0:T(8,128)(2,1)}, bf16[272,1024]{1,0:T(8,128)(2,1)S(1)}, u32[]{:S(2)}, u32[]{:S(2)}) collective-permute-start(bf16[272,1024]{1,0:T(8,128)(2,1)} %get-tuple-element.44.refs_1_), channel_id=1, source_target_pairs={{0,12},{4,0},{8,4},{12,8},{1,13},{5,1},{9,5},{13,9},{2,14},{6,2},{... | collective-permute-start | bytes 1671176 | tf_op jit(solution)/shard_map/ppermute | solution.py:22
  10.8 0.8 select_reduce_fusion
  11.5 0.7 broadcast_add_fusion
  12.2 1.3 convolution_convert_fusion
  14.6 0.7 reduce.4
  15.5 0.7 copy.28
  16.2 7.8 %all-to-all-start = ((s32[16,1,128]{2,1,0:T(1,128)}), s32[16,1,128]{2,1,0:T(1,128)S(1)}, u32[]{:S(2)}, u32[]{:S(2)}) async-start(s32[16,1,128]{2,1,0:T(1,128)} %copy.28), calls=%async_computation | async-start | bytes 16384 | tf_op jit(solution)/shard_map/all_to_all | solution.py:581
  24.1 1.8 collective-permute-done.refs_2_
  25.9 3.6 %collective-permute-start.8 = (bf16[80,1024]{1,0:T(8,128)(2,1)S(1)}, bf16[80,1024]{1,0:T(8,128)(2,1)}, u32[]{:S(2)}, u32[]{:S(2)}) collective-permute-start(bf16[80,1024]{1,0:T(8,128)(2,1)S(1)} %fusion.12), channel_id=1, source_target_pairs={{0,15},{1,0},{2,1},{3,2},{4,3},{5,4},{6,5},{7,6},{8,7},{9,8},{10,9... | collective-permute-start | bytes 491528 | tf_op jit(solution)/shard_map/ppermute | solution.py:22
  29.5 1.4 collective-permute-start.2
  31.1 3.3 %collective-permute-start.9 = (bf16[320,512]{1,0:T(8,128)(2,1)S(1)}, bf16[320,512]{1,0:T(8,128)(2,1)}, u32[]{:S(2)}, u32[]{:S(2)}) collective-permute-start(bf16[320,512]{1,0:T(8,128)(2,1)S(1)} %slice.119), channel_id=1, source_target_pairs={{0,3},{1,0},{2,1},{3,2},{4,7},{5,4},{6,5},{7,6},{8,11},{9,8},{10,9... | collective-permute-start | bytes 983048 | tf_op jit(solution)/shard_map/ppermute | solution.py:22
  34.4 1.3 fusion.1.refs_4_
  35.7 1.9 %collective-permute-start.3 = (bf16[144,1024]{1,0:T(8,128)(2,1)S(1)}, bf16[144,1024]{1,0:T(8,128)(2,1)}, u32[]{:S(2)}, u32[]{:S(2)}) collective-permute-start(bf16[144,1024]{1,0:T(8,128)(2,1)S(1)} %slice.115), channel_id=1, source_target_pairs={{0,12},{4,0},{8,4},{12,8},{1,13},{5,1},{9,5},{13,9},{2,14},{6,2},{... | collective-permute-start | bytes 884744 | tf_op jit(solution)/shard_map/ppermute | solution.py:22
  38.7 0.7 collective-permute-done.9.refs_12_
  39.4 1.2 fusion.2.refs_5_
  40.6 2.0 %collective-permute-done.3.refs_5_ = bf16[144,1024]{1,0:T(8,128)(2,1)} collective-permute-done((bf16[144,1024]{1,0:T(8,128)(2,1)S(1)}, bf16[144,1024]{1,0:T(8,128)(2,1)}, u32[]{:S(2)}, u32[]{:S(2)}) %collective-permute-start.3) | collective-permute-done | bytes 294944 | tf_op jit(solution)/shard_map/ppermute | solution.py:22
  42.7 0.8 copy-done.21
  43.5 11.9 %shard_map.191 = (bf16[256,1024]{1,0:T(8,128)(2,1)}, bf16[1024,1024]{1,0:T(8,128)(2,1)}, bf16[1024,1024]{1,0:T(8,128)(2,1)}, bf16[64,1024]{1,0:T(8,128)(2,1)}, b...) custom-call(s32[4]{0:T(128)} %pad_add_fusion.refs_0_, ...), custom_call_target="tpu_custom_call" | custom-call | flops 2147483648 | bytes 1048576 | tf_op jit(solution)/shard_map/pallas_call | solution.py:88
  55.4 5.4 %all-to-all-start.1 = ((bf16[16,16,1024]{2,1,0:T(8,128)(2,1)}), bf16[16,16,1024]{2,1,0:T(8,128)(2,1)S(1)}, u32[]{:S(2)}, u32[]{:S(2)}) async-start(bf16[16,16,1024]{2,1,0:T(8,128)(2,1)} %bitcast.38), calls=%async_computation.1 | async-start | bytes 1048576 | tf_op jit(solution)/shard_map/all_to_all | solution.py:645
  60.8 0.6 fusion.14.refs_2_
  61.4 1.5 fusion.refs_3_
  62.9 2.6 %copy.29 = bf16[1024,1024]{0,1:T(8,128)(2,1)} copy(bf16[1024,1024]{1,0:T(8,128)(2,1)S(1)} %copy-done.1) | data formatting | bytes 4194304 | tf_op jit(solution)/shard_map/pallas_call | solution.py:88
  65.5 7.5 %all-to-all-done.1 = bf16[16,16,1024]{2,1,0:T(8,128)(2,1)S(1)} async-done(((bf16[16,16,1024]{2,1,0:T(8,128)(2,1)}), bf16[16,16,1024]{2,1,0:T(8,128)(2,1)S(1)}, u32[]{:S(2)}, u32[]{:S(2)}) %all-to-all-start.1) | async-done | bytes 524320 | tf_op jit(solution)/shard_map/all_to_all | solution.py:645
  73.0 0.8 copy-done.6
  73.8 20.5 %shard_map.192 = (bf16[256,1024]{1,0:T(8,128)(2,1)}, bf16[256,1024]{1,0:T(8,128)(2,1)}, bf16[256,1024]{1,0:T(8,128)(2,1)}, bf16[256,1024]{1,0:T(8,128)(2,1)}, bf16[256,1024]{1,0:T(8,128)(2,1)}) custom-call(s32[4]{0:T(128)} %pad_add_fusion.refs_0_, bf16[256,1024]{1,0:T(8,128)(2,1)} %bitcast.40, bf16[64,256]{1,0:T(8,128)(2,1)} %fusion.14.refs_2_, ...), custom_call_target="tpu_custom_call" | custom-call | flops 6000000000 | bytes 1048576 | tf_op jit(solution)/shard_map/pallas_call | solution.py:88
  94.4 3.6 %all-to-all-start.2 = ((bf16[16,16,1024]{2,1,0:T(8,128)(2,1)}), bf16[16,16,1024]{2,1,0:T(8,128)(2,1)S(1)}, u32[]{:S(2)}, u32[]{:S(2)}) async-start(bf16[16,16,1024]{2,1,0:T(8,128)(2,1)} %bitcast.41), calls=%async_computation.2 | async-start | bytes 1048576 | tf_op jit(solution)/shard_map/all_to_all | solution.py:682
  98.0 6.3 %shard_map.193 = (bf16[4,16,16,1024]{3,2,1,0:T(8,128)(2,1)}, bf16[4,16,16,1024]{3,2,1,0:T(8,128)(2,1)}) custom-call(s32[4]{0:T(128)} %pad_add_fusion.refs_0_, bf16[256,1024]{1,0:T(8,128)(2,1)} %get-tuple-element.56.refs_1_, bf16[256,1024]{1,0:T(8,128)(2,1)} %get-tuple-element.57.refs_2_, bf16[256,1024]{1,0:T(8,128)(2,1)} %get-tuple-element.58.refs_3_), custom_call_target="tpu_custom_call" | custom-call | flops 1000000000 | bytes 1048576 | tf_op jit(solution)/shard_map/pallas_call | solution.py:88
  104.3 4.6 %all-to-all-done.2 = bf16[16,16,1024]{2,1,0:T(8,128)(2,1)S(1)} async-done(((bf16[16,16,1024]{2,1,0:T(8,128)(2,1)}), bf16[16,16,1024]{2,1,0:T(8,128)(2,1)S(1)}, u32[]{:S(2)}, u32[]{:S(2)}) %all-to-all-start.2) | async-done | bytes 524320 | tf_op jit(solution)/shard_map/all_to_all | solution.py:682
  108.9 0.8 copy-done.5
  109.7 13.3 %shard_map.194 = (bf16[4,4,48,1024]{3,2,1,0:T(8,128)(2,1)}, bf16[4,4,32,1024]{3,2,1,0:T(8,128)(2,1)}, bf16[4,4,48,1024]{3,2,1,0:T(8,128)(2,1)}, bf16[4,4,32,1024]{3,2,1,0:T(8,128)(2,1)}) custom-call(s32[4]{0:T(128)} %pad_add_fusion.refs_0_, bf16[256,1024]{1,0:T(8,128)(2,1)} %bitcast.39, bf16[64,256]{1,0:T(8,128)(2,1)} %get-tuple-element.62.refs_2_, ...), custom_call_target="tpu_custom_call" | custom-call | flops 2147483648 | bytes 1048576 | tf_op jit(solution)/shard_map/pallas_call | solution.py:88
  123.1 4.0 %add_convert_fusion = bf16[4,16,16,1024]{3,2,1,0:T(8,128)(2,1)} fusion(bf16[4,16,16,1024]{3,2,1,0:T(8,128)(2,1)} %collective-permute-done.15, bf16[4,16,16,1024]{3,2,1,0:T(8,128)(2,1)S(1)} %copy-done), kind=kLoop, calls=%fused_computation | loop fusion | flops 4194304 | bytes 6291456 | tf_op jit(solution)/shard_map/convert_element_type | solution.py:690
  127.1 0.7 add_convert_fusion.1
  128.3 1.0 fusion.19
  129.3 4.1 %collective-permute-start.16 = (bf16[192,1024]{1,0:T(8,128)(2,1)}, bf16[192,1024]{1,0:T(8,128)(2,1)}, u32[]{:S(2)}, u32[]{:S(2)}) collective-permute-start(bf16[192,1024]{1,0:T(8,128)(2,1)} %bitcast.18), channel_id=1, source_target_pairs={{0,96},{32,0},{64,32},{96,64},{1,97},{33,1},{65,33},{97,65},{2,98}... | collective-permute-start | bytes 1179656 | tf_op jit(solution)/shard_map/ppermute | solution.py:22
  133.4 1.9 collective-permute-start.18
  135.2 3.6 %all-to-all-start.3 = ((bf16[4,16,16,1024]{3,2,1,0:T(8,128)(2,1)}), bf16[4,16,16,1024]{3,2,1,0:T(8,128)(2,1)S(1)}, u32[]{:S(2)}, u32[]{:S(2)}) async-start(bf16[4,16,16,1024]{3,2,1,0:T(8,128)(2,1)} %add_convert_fusion), calls=%async_computation.3 | async-start | bytes 4194304 | tf_op jit(solution)/shard_map/all_to_all | solution.py:705
  138.9 1.6 add_convert_fusion.2
  140.6 0.6 collective-permute-start.23
  141.2 1.5 collective-permute-start.24
  142.7 8.1 %collective-permute-done.16 = bf16[192,1024]{1,0:T(8,128)(2,1)} collective-permute-done((bf16[192,1024]{1,0:T(8,128)(2,1)}, bf16[192,1024]{1,0:T(8,128)(2,1)}, u32[]{:S(2)}, u32[]{:S(2)}) %collective-permute-start.16) | collective-permute-done | bytes 393248 | tf_op jit(solution)/shard_map/ppermute | solution.py:22
  150.8 1.1 collective-permute-start.25
  151.9 2.3 %collective-permute-done.17 = bf16[192,1024]{1,0:T(8,128)(2,1)} collective-permute-done((bf16[192,1024]{1,0:T(8,128)(2,1)}, bf16[192,1024]{1,0:T(8,128)(2,1)}, u32[]{:S(2)}, u32[]{:S(2)}) %collective-permute-start.17) | collective-permute-done | bytes 393248 | tf_op jit(solution)/shard_map/ppermute | solution.py:22
  154.2 1.5 fusion.5
  155.7 0.6 collective-permute-start.19
  156.3 1.5 collective-permute-start.20
  157.8 1.1 collective-permute-start.21
  158.9 2.5 %collective-permute-done.25 = bf16[128,1024]{1,0:T(8,128)(2,1)S(1)} collective-permute-done((bf16[128,1024]{1,0:T(8,128)(2,1)S(1)}, bf16[128,1024]{1,0:T(8,128)(2,1)S(1)}, u32[]{:S(2)}, u32[]{:S(2)}) %collective-permute-start.25) | collective-permute-done | bytes 262176 | tf_op jit(solution)/shard_map/ppermute | solution.py:22
  161.6 4.0 %collective-permute-start.26 = (bf16[32,1024]{1,0:T(8,128)(2,1)S(1)}, bf16[32,1024]{1,0:T(8,128)(2,1)S(1)}, u32[]{:S(2)}, u32[]{:S(2)}) collective-permute-start(bf16[32,1024]{1,0:T(8,128)(2,1)S(1)} %get-tuple-element.93), channel_id=1, source_target_pairs={{0,96},{32,0},{64,32},{96,64},{1,97},{33,1},{65,33},{97,65},{2,98}... | collective-permute-start | bytes 196616 | tf_op jit(solution)/shard_map/ppermute | solution.py:22
  165.6 1.5 collective-permute-start.28
  167.2 1.4 reduce_sum.31
  168.6 4.4 %all-to-all-start.4 = ((bf16[16,16,1024]{2,1,0:T(8,128)(2,1)}), bf16[16,16,1024]{2,1,0:T(8,128)(2,1)S(1)}, u32[]{:S(2)}, u32[]{:S(2)}) async-start(bf16[16,16,1024]{2,1,0:T(8,128)(2,1)} %reduce_sum.31), calls=%async_computation.4 | async-start | bytes 1048576 | tf_op jit(solution)/shard_map/all_to_all | solution.py:706
  173.1 2.0 %collective-permute-start.29 = (bf16[80,1024]{1,0:T(8,128)(2,1)S(1)}, bf16[80,1024]{1,0:T(8,128)(2,1)S(1)}, u32[]{:S(2)}, u32[]{:S(2)}) collective-permute-start(bf16[80,1024]{1,0:T(8,128)(2,1)S(1)} %pad_maximum_fusion.refs_1_), channel_id=1, source_target_pairs={{0,32},{32,64},{64,96},{96,0},{1,33},{33,65},{65,97},{97,1},{2,34}... | collective-permute-start | bytes 491528 | tf_op jit(solution)/shard_map/ppermute | solution.py:22
  175.1 1.3 collective-permute-start.30
  176.4 2.2 %collective-permute-start.31 = (bf16[80,1024]{1,0:T(8,128)(2,1)S(1)}, bf16[80,1024]{1,0:T(8,128)(2,1)S(1)}, u32[]{:S(2)}, u32[]{:S(2)}) collective-permute-start(bf16[80,1024]{1,0:T(8,128)(2,1)S(1)} %pad_maximum_fusion.refs_1_), channel_id=1, source_target_pairs={{0,64},{32,96},{64,0},{96,32},{1,65},{33,97},{65,1},{97,33},{2,66}... | collective-permute-start | bytes 491528 | tf_op jit(solution)/shard_map/ppermute | solution.py:22
  178.7 5.9 %collective-permute-done.29.refs_2_ = bf16[80,1024]{1,0:T(8,128)(2,1)S(1)} collective-permute-done((bf16[80,1024]{1,0:T(8,128)(2,1)S(1)}, bf16[80,1024]{1,0:T(8,128)(2,1)S(1)}, u32[]{:S(2)}, u32[]{:S(2)}) %collective-permute-start.29) | collective-permute-done | bytes 163872 | tf_op jit(solution)/shard_map/ppermute | solution.py:22
  185.1 1.7 collective-permute-done.31.refs_4_
  186.8 1.3 collective-permute-done.35.refs_8_
  188.2 0.7 copy-done.14
  188.9 3.7 %shard_map.195 = (f32[1024,256]{1,0:T(8,128)}, f32[256,1024]{1,0:T(8,128)}, f32[52,1024]{1,0:T(8,128)}) custom-call(s32[4]{0:T(128)} %pad_add_fusion.refs_0_, bf16[80,1024]{1,0:T(8,128)(2,1)} %copy-done.4, bf16[80,1024]{1,0:T(8,128)(2,1)} %copy-done.8, bf16[80,1024]{1,0:T(8,128)(2,1)} %copy-done.9, bf16[80,1024]{1,0:T(8,128)(2,1)} %copy-done.10, ...), custom_call_target="tpu_custom_call" | custom-call | bytes 1048576 | tf_op jit(solution)/shard_map/pallas_call | solution.py:88
  192.7 0.6 fusion.24
  (122 shorter events, 4.3 us)
Async XLA Ops:
  0.6 14.0 %copy-start.24 = (s32[1,16]{1,0:T(1,128)S(1)}, s32[1,16]{1,0:T(1,128)}, u32[]{:S(2)}) copy-start(s32[1,16]{1,0:T(1,128)} %param.25) | copy-start | bytes 196
  4.6 29.8 %copy-start.18 = (s32[1,2048]{1,0:T(1,128)S(1)}, s32[1,2048]{1,0:T(1,128)}, u32[]{:S(2)}) copy-start(s32[1,2048]{1,0:T(1,128)} %param.24) | copy-start | bytes 24580
  4.6 24.8 %collective-permute-start.4 = (bf16[576,512]{1,0:T(8,128)(2,1)}, bf16[576,512]{1,0:T(8,128)(2,1)S(1)}, u32[]{:S(2)}, u32[]{:S(2)}) collective-permute-start(bf16[576,512]{1,0:T(8,128)(2,1)} %get-tuple-element.46), channel_id=1, source_target_pairs={{0,1},{1,2},{2,3},{3,0},{4,5},{5,6},{6,7},{7,4},{8,9},{9,10},{10,1... | collective-permute-start | bytes 1769480 | tf_op jit(solution)/shard_map/ppermute | solution.py:22
  6.4 24.6 %collective-permute-start.5 = (bf16[576,512]{1,0:T(8,128)(2,1)}, bf16[576,512]{1,0:T(8,128)(2,1)S(1)}, u32[]{:S(2)}, u32[]{:S(2)}) collective-permute-start(bf16[576,512]{1,0:T(8,128)(2,1)} %get-tuple-element.46), channel_id=1, source_target_pairs={{0,3},{1,0},{2,1},{3,2},{4,7},{5,4},{6,5},{7,6},{8,11},{9,8},{10,9... | collective-permute-start | bytes 1769480 | tf_op jit(solution)/shard_map/ppermute | solution.py:22
  7.9 23.1 %collective-permute-start.1 = (bf16[272,1024]{1,0:T(8,128)(2,1)}, bf16[272,1024]{1,0:T(8,128)(2,1)S(1)}, u32[]{:S(2)}, u32[]{:S(2)}) collective-permute-start(bf16[272,1024]{1,0:T(8,128)(2,1)} %get-tuple-element.44.refs_1_), channel_id=1, source_target_pairs={{0,12},{4,0},{8,4},{12,8},{1,13},{5,1},{9,5},{13,9},{2,14},{6,2},{... | collective-permute-start | bytes 1671176 | tf_op jit(solution)/shard_map/ppermute | solution.py:22
  10.8 15.1 %collective-permute-start = (bf16[272,1024]{1,0:T(8,128)(2,1)}, bf16[272,1024]{1,0:T(8,128)(2,1)S(1)}, u32[]{:S(2)}, u32[]{:S(2)}) collective-permute-start(bf16[272,1024]{1,0:T(8,128)(2,1)} %get-tuple-element.44.refs_1_), channel_id=1, source_target_pairs={{0,4},{4,8},{8,12},{12,0},{1,5},{5,9},{9,13},{13,1},{2,6},{6,10},{... | collective-permute-start | bytes 1671176 | tf_op jit(solution)/shard_map/ppermute | solution.py:22
  13.6 22.1 %collective-permute-start.7 = (bf16[80,1024]{1,0:T(8,128)(2,1)S(1)}, bf16[80,1024]{1,0:T(8,128)(2,1)S(1)}, u32[]{:S(2)}, u32[]{:S(2)}) collective-permute-start(bf16[80,1024]{1,0:T(8,128)(2,1)S(1)} %fusion.11), channel_id=1, source_target_pairs={{0,1},{1,2},{2,3},{3,4},{4,5},{5,6},{6,7},{7,8},{8,9},{9,10},{10,1... | collective-permute-start | bytes 491528 | tf_op jit(solution)/shard_map/ppermute | solution.py:22
  16.2 24.4 %all-to-all-start = ((s32[16,1,128]{2,1,0:T(1,128)}), s32[16,1,128]{2,1,0:T(1,128)S(1)}, u32[]{:S(2)}, u32[]{:S(2)}) async-start(s32[16,1,128]{2,1,0:T(1,128)} %copy.28), calls=%async_computation | async-start | bytes 16384 | tf_op jit(solution)/shard_map/all_to_all | solution.py:581
  24.1 16.5 %copy-start.25 = (s32[1,16]{1,0:T(1,128)S(1)}, s32[1,16]{1,0:T(1,128)}, u32[]{:S(2)}) copy-start(s32[1,16]{1,0:T(1,128)} %param.20) | copy-start | bytes 196
  25.9 14.7 %copy-start.16 = (bf16[272,1024]{1,0:T(8,128)(2,1)}, bf16[272,1024]{1,0:T(8,128)(2,1)S(1)}, u32[]{:S(2)}) copy-start(bf16[272,1024]{1,0:T(8,128)(2,1)S(1)} %collective-permute-done.refs_2_) | copy-start | bytes 1671172
  25.9 11.8 %collective-permute-start.8 = (bf16[80,1024]{1,0:T(8,128)(2,1)S(1)}, bf16[80,1024]{1,0:T(8,128)(2,1)}, u32[]{:S(2)}, u32[]{:S(2)}) collective-permute-start(bf16[80,1024]{1,0:T(8,128)(2,1)S(1)} %fusion.12), channel_id=1, source_target_pairs={{0,15},{1,0},{2,1},{3,2},{4,3},{5,4},{6,5},{7,6},{8,7},{9,8},{10,9... | collective-permute-start | bytes 491528 | tf_op jit(solution)/shard_map/ppermute | solution.py:22
  29.5 13.2 %copy-start.17 = (bf16[576,512]{1,0:T(8,128)(2,1)}, bf16[576,512]{1,0:T(8,128)(2,1)S(1)}, u32[]{:S(2)}) copy-start(bf16[576,512]{1,0:T(8,128)(2,1)S(1)} %collective-permute-done.4.refs_9_) | copy-start | bytes 1769476
  29.5 8.2 %collective-permute-start.2 = (bf16[128,1024]{1,0:T(8,128)(2,1)S(1)}, bf16[128,1024]{1,0:T(8,128)(2,1)S(1)}, u32[]{:S(2)}, u32[]{:S(2)}) collective-permute-start(bf16[128,1024]{1,0:T(8,128)(2,1)S(1)} %slice.114), channel_id=1, source_target_pairs={{0,4},{4,8},{8,12},{12,0},{1,5},{5,9},{9,13},{13,1},{2,6},{6,10},{... | collective-permute-start | bytes 786440 | tf_op jit(solution)/shard_map/ppermute | solution.py:22
  30.9 11.7 %copy-start.7 = (bf16[576,512]{1,0:T(8,128)(2,1)}, bf16[576,512]{1,0:T(8,128)(2,1)S(1)}, u32[]{:S(2)}) copy-start(bf16[576,512]{1,0:T(8,128)(2,1)S(1)} %collective-permute-done.5.refs_10_) | copy-start | bytes 1769476
  30.9 7.8 %collective-permute-start.6 = (bf16[256,512]{1,0:T(8,128)(2,1)S(1)}, bf16[256,512]{1,0:T(8,128)(2,1)}, u32[]{:S(2)}, u32[]{:S(2)}) collective-permute-start(bf16[256,512]{1,0:T(8,128)(2,1)S(1)} %slice.116), channel_id=1, source_target_pairs={{0,1},{1,2},{2,3},{3,0},{4,5},{5,6},{6,7},{7,4},{8,9},{9,10},{10,1... | collective-permute-start | bytes 786440 | tf_op jit(solution)/shard_map/ppermute | solution.py:22
  31.1 11.6 %copy-start.15 = (bf16[272,1024]{1,0:T(8,128)(2,1)}, bf16[272,1024]{1,0:T(8,128)(2,1)S(1)}, u32[]{:S(2)}) copy-start(bf16[272,1024]{1,0:T(8,128)(2,1)S(1)} %collective-permute-done.1.refs_3_) | copy-start | bytes 1671172
  31.1 8.3 %collective-permute-start.9 = (bf16[320,512]{1,0:T(8,128)(2,1)S(1)}, bf16[320,512]{1,0:T(8,128)(2,1)}, u32[]{:S(2)}, u32[]{:S(2)}) collective-permute-start(bf16[320,512]{1,0:T(8,128)(2,1)S(1)} %slice.119), channel_id=1, source_target_pairs={{0,3},{1,0},{2,1},{3,2},{4,7},{5,4},{6,5},{7,6},{8,11},{9,8},{10,9... | collective-permute-start | bytes 983048 | tf_op jit(solution)/shard_map/ppermute | solution.py:22
  35.7 19.7 %copy-start.23 = (bf16[80,1024]{1,0:T(8,128)(2,1)}, bf16[80,1024]{1,0:T(8,128)(2,1)S(1)}, u32[]{:S(2)}) copy-start(bf16[80,1024]{1,0:T(8,128)(2,1)S(1)} %collective-permute-done.7.refs_10_) | copy-start | bytes 491524
  35.7 6.9 %collective-permute-start.3 = (bf16[144,1024]{1,0:T(8,128)(2,1)S(1)}, bf16[144,1024]{1,0:T(8,128)(2,1)}, u32[]{:S(2)}, u32[]{:S(2)}) collective-permute-start(bf16[144,1024]{1,0:T(8,128)(2,1)S(1)} %slice.115), channel_id=1, source_target_pairs={{0,12},{4,0},{8,4},{12,8},{1,13},{5,1},{9,5},{13,9},{2,14},{6,2},{... | collective-permute-start | bytes 884744 | tf_op jit(solution)/shard_map/ppermute | solution.py:22
  37.7 5.0 %collective-permute-start.10 = (bf16[576,512]{1,0:T(8,128)(2,1)S(1)}, bf16[576,512]{1,0:T(8,128)(2,1)S(1)}, u32[]{:S(2)}, u32[]{:S(2)}) collective-permute-start(bf16[576,512]{1,0:T(8,128)(2,1)S(1)} %collective-permute-done.4.refs_9_), channel_id=1, source_target_pairs={{0,16},{16,0},{1,17},{17,1},{2,18},{18,2},{3,19},{19,3},{4,20},{20... | collective-permute-start | bytes 1769480 | tf_op jit(solution)/shard_map/ppermute | solution.py:22
  37.7 2.9 %copy-start.22 = (bf16[128,1024]{1,0:T(8,128)(2,1)}, bf16[128,1024]{1,0:T(8,128)(2,1)S(1)}, u32[]{:S(2)}) copy-start(bf16[128,1024]{1,0:T(8,128)(2,1)S(1)} %collective-permute-done.2.refs_4_) | copy-start | bytes 786436
  37.7 4.9 %collective-permute-start.11 = (bf16[576,512]{1,0:T(8,128)(2,1)S(1)}, bf16[576,512]{1,0:T(8,128)(2,1)}, u32[]{:S(2)}, u32[]{:S(2)}) collective-permute-start(bf16[576,512]{1,0:T(8,128)(2,1)S(1)} %collective-permute-done.5.refs_10_), channel_id=1, source_target_pairs={{0,16},{16,0},{1,17},{17,1},{2,18},{18,2},{3,19},{19,3},{4,20},{20... | collective-permute-start | bytes 1769480 | tf_op jit(solution)/shard_map/ppermute | solution.py:22
  38.7 3.9 %collective-permute-start.12 = (bf16[256,512]{1,0:T(8,128)(2,1)}, bf16[256,512]{1,0:T(8,128)(2,1)}, u32[]{:S(2)}, u32[]{:S(2)}) collective-permute-start(bf16[256,512]{1,0:T(8,128)(2,1)} %collective-permute-done.6.refs_11_), channel_id=1, source_target_pairs={{0,16},{16,0},{1,17},{17,1},{2,18},{18,2},{3,19},{19,3},{4,20},{20... | collective-permute-start | bytes 786440 | tf_op jit(solution)/shard_map/ppermute | solution.py:22
  39.4 3.3 %collective-permute-start.13 = (bf16[320,512]{1,0:T(8,128)(2,1)}, bf16[320,512]{1,0:T(8,128)(2,1)}, u32[]{:S(2)}, u32[]{:S(2)}) collective-permute-start(bf16[320,512]{1,0:T(8,128)(2,1)} %collective-permute-done.9.refs_12_), channel_id=1, source_target_pairs={{0,16},{16,0},{1,17},{17,1},{2,18},{18,2},{3,19},{19,3},{4,20},{20... | collective-permute-start | bytes 983048 | tf_op jit(solution)/shard_map/ppermute | solution.py:22
  40.6 2.1 %copy-start.20 = (s32[16,1,128]{2,1,0:T(1,128)}, s32[16,1,128]{2,1,0:T(1,128)S(1)}, u32[]{:S(2)}) copy-start(s32[16,1,128]{2,1,0:T(1,128)S(1)} %all-to-all-done) | copy-start | bytes 24580
  42.6 0.9 copy-start.21
  43.5 17.9 %copy-start.19 = (s32[1,2048]{1,0:T(1,128)S(1)}, s32[1,2048]{1,0:T(1,128)}, u32[]{:S(2)}) copy-start(s32[1,2048]{1,0:T(1,128)} %param.23) | copy-start | bytes 24580
  55.4 7.5 %copy-start.1 = (bf16[1024,1024]{1,0:T(8,128)(2,1)S(1)}, bf16[1024,1024]{1,0:T(8,128)(2,1)}, u32[]{:S(2)}) copy-start(bf16[1024,1024]{1,0:T(8,128)(2,1)} %get-tuple-element.50) | copy-start | bytes 6291460
  55.4 17.6 %all-to-all-start.1 = ((bf16[16,16,1024]{2,1,0:T(8,128)(2,1)}), bf16[16,16,1024]{2,1,0:T(8,128)(2,1)S(1)}, u32[]{:S(2)}, u32[]{:S(2)}) async-start(bf16[16,16,1024]{2,1,0:T(8,128)(2,1)} %bitcast.38), calls=%async_computation.1 | async-start | bytes 1048576 | tf_op jit(solution)/shard_map/all_to_all | solution.py:645
  94.4 14.5 %all-to-all-start.2 = ((bf16[16,16,1024]{2,1,0:T(8,128)(2,1)}), bf16[16,16,1024]{2,1,0:T(8,128)(2,1)S(1)}, u32[]{:S(2)}, u32[]{:S(2)}) async-start(bf16[16,16,1024]{2,1,0:T(8,128)(2,1)} %bitcast.41), calls=%async_computation.2 | async-start | bytes 1048576 | tf_op jit(solution)/shard_map/all_to_all | solution.py:682
  108.9 14.2 %collective-permute-start.15 = (bf16[4,16,16,1024]{3,2,1,0:T(8,128)(2,1)}, bf16[4,16,16,1024]{3,2,1,0:T(8,128)(2,1)}, u32[]{:S(2)}, u32[]{:S(2)}) collective-permute-start(bf16[4,16,16,1024]{3,2,1,0:T(8,128)(2,1)} %get-tuple-element.72), channel_id=1, source_target_pairs={{0,16},{16,0},{1,17},{17,1},{2,18},{18,2},{3,19},{19,3},{4,20},{20... | collective-permute-start | bytes 6291464 | tf_op jit(solution)/shard_map/ppermute | solution.py:22
  109.7 13.4 %copy-start = (bf16[4,16,16,1024]{3,2,1,0:T(8,128)(2,1)S(1)}, bf16[4,16,16,1024]{3,2,1,0:T(8,128)(2,1)}, u32[]{:S(2)}) copy-start(bf16[4,16,16,1024]{3,2,1,0:T(8,128)(2,1)} %get-tuple-element.71) | copy-start | bytes 6291460
  123.0 4.1 %copy-start.2 = (bf16[4,4,48,1024]{3,2,1,0:T(8,128)(2,1)S(1)}, bf16[4,4,48,1024]{3,2,1,0:T(8,128)(2,1)}, u32[]{:S(2)}) copy-start(bf16[4,4,48,1024]{3,2,1,0:T(8,128)(2,1)} %get-tuple-element.69) | copy-start | bytes 4718596
  123.0 4.1 %collective-permute-start.14 = (bf16[4,4,48,1024]{3,2,1,0:T(8,128)(2,1)}, bf16[4,4,48,1024]{3,2,1,0:T(8,128)(2,1)S(1)}, u32[]{:S(2)}, u32[]{:S(2)}) collective-permute-start(bf16[4,4,48,1024]{3,2,1,0:T(8,128)(2,1)} %get-tuple-element.70), channel_id=1, source_target_pairs={{0,16},{16,0},{1,17},{17,1},{2,18},{18,2},{3,19},{19,3},{4,20},{20... | collective-permute-start | bytes 4718600 | tf_op jit(solution)/shard_map/ppermute | solution.py:22
  127.8 11.1 %collective-permute-start.22 = (bf16[4,4,32,1024]{3,2,1,0:T(8,128)(2,1)}, bf16[4,4,32,1024]{3,2,1,0:T(8,128)(2,1)}, u32[]{:S(2)}, u32[]{:S(2)}) collective-permute-start(bf16[4,4,32,1024]{3,2,1,0:T(8,128)(2,1)} %get-tuple-element.77), channel_id=1, source_target_pairs={{0,16},{16,0},{1,17},{17,1},{2,18},{18,2},{3,19},{19,3},{4,20},{20... | collective-permute-start | bytes 3145736 | tf_op jit(solution)/shard_map/ppermute | solution.py:22
  129.3 21.5 %collective-permute-start.16 = (bf16[192,1024]{1,0:T(8,128)(2,1)}, bf16[192,1024]{1,0:T(8,128)(2,1)}, u32[]{:S(2)}, u32[]{:S(2)}) collective-permute-start(bf16[192,1024]{1,0:T(8,128)(2,1)} %bitcast.18), channel_id=1, source_target_pairs={{0,96},{32,0},{64,32},{96,64},{1,97},{33,1},{65,33},{97,65},{2,98}... | collective-permute-start | bytes 1179656 | tf_op jit(solution)/shard_map/ppermute | solution.py:22
  133.4 20.8 %collective-permute-start.17 = (bf16[192,1024]{1,0:T(8,128)(2,1)}, bf16[192,1024]{1,0:T(8,128)(2,1)}, u32[]{:S(2)}, u32[]{:S(2)}) collective-permute-start(bf16[192,1024]{1,0:T(8,128)(2,1)} %bitcast.19), channel_id=1, source_target_pairs={{0,32},{32,64},{64,96},{96,0},{1,33},{33,65},{65,97},{97,1},{2,34}... | collective-permute-start | bytes 1179656 | tf_op jit(solution)/shard_map/ppermute | solution.py:22
  133.4 5.5 %copy-start.3 = (bf16[4,4,32,1024]{3,2,1,0:T(8,128)(2,1)S(1)}, bf16[4,4,32,1024]{3,2,1,0:T(8,128)(2,1)}, u32[]{:S(2)}) copy-start(bf16[4,4,32,1024]{3,2,1,0:T(8,128)(2,1)} %get-tuple-element.76) | copy-start | bytes 3145732
  133.4 20.8 %collective-permute-start.18 = (bf16[192,1024]{1,0:T(8,128)(2,1)}, bf16[192,1024]{1,0:T(8,128)(2,1)}, u32[]{:S(2)}, u32[]{:S(2)}) collective-permute-start(bf16[192,1024]{1,0:T(8,128)(2,1)} %bitcast.20), channel_id=1, source_target_pairs={{0,64},{32,96},{64,0},{96,32},{1,65},{33,97},{65,1},{97,33},{2,66}... | collective-permute-start | bytes 1179656 | tf_op jit(solution)/shard_map/ppermute | solution.py:22
  135.2 32.0 %all-to-all-start.3 = ((bf16[4,16,16,1024]{3,2,1,0:T(8,128)(2,1)}), bf16[4,16,16,1024]{3,2,1,0:T(8,128)(2,1)S(1)}, u32[]{:S(2)}, u32[]{:S(2)}) async-start(bf16[4,16,16,1024]{3,2,1,0:T(8,128)(2,1)} %add_convert_fusion), calls=%async_computation.3 | async-start | bytes 4194304 | tf_op jit(solution)/shard_map/all_to_all | solution.py:705
  140.6 17.2 %collective-permute-start.23 = (bf16[128,1024]{1,0:T(8,128)(2,1)S(1)}, bf16[128,1024]{1,0:T(8,128)(2,1)S(1)}, u32[]{:S(2)}, u32[]{:S(2)}) collective-permute-start(bf16[128,1024]{1,0:T(8,128)(2,1)S(1)} %bitcast.44), channel_id=1, source_target_pairs={{0,3},{1,0},{2,1},{3,2},{4,7},{5,4},{6,5},{7,6},{8,11},{9,8},{10,9... | collective-permute-start | bytes 786440 | tf_op jit(solution)/shard_map/ppermute | solution.py:22
  141.2 17.7 %collective-permute-start.24 = (bf16[128,1024]{1,0:T(8,128)(2,1)S(1)}, bf16[128,1024]{1,0:T(8,128)(2,1)S(1)}, u32[]{:S(2)}, u32[]{:S(2)}) collective-permute-start(bf16[128,1024]{1,0:T(8,128)(2,1)S(1)} %bitcast.43), channel_id=1, source_target_pairs={{0,1},{1,2},{2,3},{3,0},{4,5},{5,6},{6,7},{7,4},{8,9},{9,10},{10,1... | collective-permute-start | bytes 786440 | tf_op jit(solution)/shard_map/ppermute | solution.py:22
  150.8 10.6 %collective-permute-start.25 = (bf16[128,1024]{1,0:T(8,128)(2,1)S(1)}, bf16[128,1024]{1,0:T(8,128)(2,1)S(1)}, u32[]{:S(2)}, u32[]{:S(2)}) collective-permute-start(bf16[128,1024]{1,0:T(8,128)(2,1)S(1)} %bitcast.42), channel_id=1, source_target_pairs={{0,2},{1,3},{2,0},{3,1},{4,6},{5,7},{6,4},{7,5},{8,10},{9,11},{10,... | collective-permute-start | bytes 786440 | tf_op jit(solution)/shard_map/ppermute | solution.py:22
  155.7 9.9 %collective-permute-start.19 = (bf16[48,1024]{1,0:T(8,128)(2,1)S(1)}, bf16[48,1024]{1,0:T(8,128)(2,1)S(1)}, u32[]{:S(2)}, u32[]{:S(2)}) collective-permute-start(bf16[48,1024]{1,0:T(8,128)(2,1)S(1)} %get-tuple-element.90), channel_id=1, source_target_pairs={{0,3},{1,0},{2,1},{3,2},{4,7},{5,4},{6,5},{7,6},{8,11},{9,8},{10,9... | collective-permute-start | bytes 294920 | tf_op jit(solution)/shard_map/ppermute | solution.py:22
  156.3 10.8 %collective-permute-start.20 = (bf16[48,1024]{1,0:T(8,128)(2,1)S(1)}, bf16[48,1024]{1,0:T(8,128)(2,1)S(1)}, u32[]{:S(2)}, u32[]{:S(2)}) collective-permute-start(bf16[48,1024]{1,0:T(8,128)(2,1)S(1)} %get-tuple-element.92), channel_id=1, source_target_pairs={{0,1},{1,2},{2,3},{3,0},{4,5},{5,6},{6,7},{7,4},{8,9},{9,10},{10,1... | collective-permute-start | bytes 294920 | tf_op jit(solution)/shard_map/ppermute | solution.py:22
  157.8 9.3 %collective-permute-start.21 = (bf16[48,1024]{1,0:T(8,128)(2,1)S(1)}, bf16[48,1024]{1,0:T(8,128)(2,1)S(1)}, u32[]{:S(2)}, u32[]{:S(2)}) collective-permute-start(bf16[48,1024]{1,0:T(8,128)(2,1)S(1)} %get-tuple-element.91), channel_id=1, source_target_pairs={{0,2},{1,3},{2,0},{3,1},{4,6},{5,7},{6,4},{7,5},{8,10},{9,11},{10,... | collective-permute-start | bytes 294920 | tf_op jit(solution)/shard_map/ppermute | solution.py:22
  161.6 11.4 %collective-permute-start.26 = (bf16[32,1024]{1,0:T(8,128)(2,1)S(1)}, bf16[32,1024]{1,0:T(8,128)(2,1)S(1)}, u32[]{:S(2)}, u32[]{:S(2)}) collective-permute-start(bf16[32,1024]{1,0:T(8,128)(2,1)S(1)} %get-tuple-element.93), channel_id=1, source_target_pairs={{0,96},{32,0},{64,32},{96,64},{1,97},{33,1},{65,33},{97,65},{2,98}... | collective-permute-start | bytes 196616 | tf_op jit(solution)/shard_map/ppermute | solution.py:22
  165.6 7.5 %collective-permute-start.27 = (bf16[32,1024]{1,0:T(8,128)(2,1)S(1)}, bf16[32,1024]{1,0:T(8,128)(2,1)S(1)}, u32[]{:S(2)}, u32[]{:S(2)}) collective-permute-start(bf16[32,1024]{1,0:T(8,128)(2,1)S(1)} %get-tuple-element.95), channel_id=1, source_target_pairs={{0,32},{32,64},{64,96},{96,0},{1,33},{33,65},{65,97},{97,1},{2,34}... | collective-permute-start | bytes 196616 | tf_op jit(solution)/shard_map/ppermute | solution.py:22
  165.6 7.5 %collective-permute-start.28 = (bf16[32,1024]{1,0:T(8,128)(2,1)S(1)}, bf16[32,1024]{1,0:T(8,128)(2,1)S(1)}, u32[]{:S(2)}, u32[]{:S(2)}) collective-permute-start(bf16[32,1024]{1,0:T(8,128)(2,1)S(1)} %get-tuple-element.94), channel_id=1, source_target_pairs={{0,64},{32,96},{64,0},{96,32},{1,65},{33,97},{65,1},{97,33},{2,66}... | collective-permute-start | bytes 196616 | tf_op jit(solution)/shard_map/ppermute | solution.py:22
  168.6 24.0 %all-to-all-start.4 = ((bf16[16,16,1024]{2,1,0:T(8,128)(2,1)}), bf16[16,16,1024]{2,1,0:T(8,128)(2,1)S(1)}, u32[]{:S(2)}, u32[]{:S(2)}) async-start(bf16[16,16,1024]{2,1,0:T(8,128)(2,1)} %reduce_sum.31), calls=%async_computation.4 | async-start | bytes 1048576 | tf_op jit(solution)/shard_map/all_to_all | solution.py:706
  173.1 15.0 %copy-start.4 = (bf16[80,1024]{1,0:T(8,128)(2,1)}, bf16[80,1024]{1,0:T(8,128)(2,1)S(1)}, u32[]{:S(2)}) copy-start(bf16[80,1024]{1,0:T(8,128)(2,1)S(1)} %pad_maximum_fusion.refs_1_) | copy-start | bytes 491524
  173.1 11.4 %collective-permute-start.29 = (bf16[80,1024]{1,0:T(8,128)(2,1)S(1)}, bf16[80,1024]{1,0:T(8,128)(2,1)S(1)}, u32[]{:S(2)}, u32[]{:S(2)}) collective-permute-start(bf16[80,1024]{1,0:T(8,128)(2,1)S(1)} %pad_maximum_fusion.refs_1_), channel_id=1, source_target_pairs={{0,32},{32,64},{64,96},{96,0},{1,33},{33,65},{65,97},{97,1},{2,34}... | collective-permute-start | bytes 491528 | tf_op jit(solution)/shard_map/ppermute | solution.py:22
  175.1 9.5 %collective-permute-start.30 = (bf16[80,1024]{1,0:T(8,128)(2,1)S(1)}, bf16[80,1024]{1,0:T(8,128)(2,1)S(1)}, u32[]{:S(2)}, u32[]{:S(2)}) collective-permute-start(bf16[80,1024]{1,0:T(8,128)(2,1)S(1)} %pad_maximum_fusion.refs_1_), channel_id=1, source_target_pairs={{0,96},{32,0},{64,32},{96,64},{1,97},{33,1},{65,33},{97,65},{2,98}... | collective-permute-start | bytes 491528 | tf_op jit(solution)/shard_map/ppermute | solution.py:22
  176.4 10.3 %collective-permute-start.31 = (bf16[80,1024]{1,0:T(8,128)(2,1)S(1)}, bf16[80,1024]{1,0:T(8,128)(2,1)S(1)}, u32[]{:S(2)}, u32[]{:S(2)}) collective-permute-start(bf16[80,1024]{1,0:T(8,128)(2,1)S(1)} %pad_maximum_fusion.refs_1_), channel_id=1, source_target_pairs={{0,64},{32,96},{64,0},{96,32},{1,65},{33,97},{65,1},{97,33},{2,66}... | collective-permute-start | bytes 491528 | tf_op jit(solution)/shard_map/ppermute | solution.py:22
  178.7 8.1 %collective-permute-start.32 = (bf16[80,1024]{1,0:T(8,128)(2,1)S(1)}, bf16[80,1024]{1,0:T(8,128)(2,1)S(1)}, u32[]{:S(2)}, u32[]{:S(2)}) collective-permute-start(bf16[80,1024]{1,0:T(8,128)(2,1)S(1)} %pad_maximum_fusion.refs_1_), channel_id=1, source_target_pairs={{0,16},{16,0},{1,17},{17,1},{2,18},{18,2},{3,19},{19,3},{4,20},{20... | collective-permute-start | bytes 491528 | tf_op jit(solution)/shard_map/ppermute | solution.py:22
  184.6 3.6 %copy-start.8 = (bf16[80,1024]{1,0:T(8,128)(2,1)}, bf16[80,1024]{1,0:T(8,128)(2,1)S(1)}, u32[]{:S(2)}) copy-start(bf16[80,1024]{1,0:T(8,128)(2,1)S(1)} %collective-permute-done.29.refs_2_) | copy-start | bytes 491524
  184.6 2.2 %collective-permute-start.33 = (bf16[80,1024]{1,0:T(8,128)(2,1)S(1)}, bf16[80,1024]{1,0:T(8,128)(2,1)S(1)}, u32[]{:S(2)}, u32[]{:S(2)}) collective-permute-start(bf16[80,1024]{1,0:T(8,128)(2,1)S(1)} %collective-permute-done.29.refs_2_), channel_id=1, source_target_pairs={{0,16},{16,0},{1,17},{17,1},{2,18},{18,2},{3,19},{19,3},{4,20},{20... | collective-permute-start | bytes 491528 | tf_op jit(solution)/shard_map/ppermute | solution.py:22
  184.6 3.6 %copy-start.9 = (bf16[80,1024]{1,0:T(8,128)(2,1)}, bf16[80,1024]{1,0:T(8,128)(2,1)S(1)}, u32[]{:S(2)}) copy-start(bf16[80,1024]{1,0:T(8,128)(2,1)S(1)} %collective-permute-done.30.refs_3_) | copy-start | bytes 491524
  184.6 2.2 %collective-permute-start.34 = (bf16[80,1024]{1,0:T(8,128)(2,1)S(1)}, bf16[80,1024]{1,0:T(8,128)(2,1)S(1)}, u32[]{:S(2)}, u32[]{:S(2)}) collective-permute-start(bf16[80,1024]{1,0:T(8,128)(2,1)S(1)} %collective-permute-done.30.refs_3_), channel_id=1, source_target_pairs={{0,16},{16,0},{1,17},{17,1},{2,18},{18,2},{3,19},{19,3},{4,20},{20... | collective-permute-start | bytes 491528 | tf_op jit(solution)/shard_map/ppermute | solution.py:22
  186.8 1.4 copy-start.10
  186.8 1.4 collective-permute-start.35
  186.8 1.4 copy-start.11
  186.8 1.4 copy-start.12
  186.8 1.4 copy-start.13
  (3 other events, 2.3 us)

commit v10 on v9

--- a/solution.py
+++ b/solution.py
@@ -606,8 +606,7 @@
 
     to_high, to_low = edge_of(boundary[side:], halo_place[side:]), edge_of(boundary[:side], halo_place[:side])
     from_low = shift_by(to_high, GROUP, 1)
-    from_high = shift_by(to_low, GROUP, 15)
-    mine[2], from_low, from_high = lax.optimization_barrier((mine[2], from_low, from_high))
+    mine[2], from_low = lax.optimization_barrier((mine[2], from_low))
 
     outs = [
         ((256, width), BF),
@@ -636,6 +635,8 @@
         flops=2 * 4 * tokens * width * 4 * units,
     )
 
+    to_low, outgoing = lax.optimization_barrier((to_low, outgoing))
+    from_high = shift_by(to_low, GROUP, 15)
     own_row = jnp.concatenate([fresh_row(0, place), jnp.full((cache_count,), -1, I32)])
     node_count = entities + cache_count
     extended_count = node_count + 2 * side

time: 195 us -> 195 us (level)
  waiting for transfers between devices: 38.9 us -> 34 us
  starting transfers between devices: 66.7 us -> 71.3 us
    all_to_all x1, waiting for transfers between devices: 7.48 us -> 0.45 us  [shards(): lax.all_to_all(outgoing.reshape(16, 16, width), GROUP, 0, 0, tiled=True)]
    ppermute x36, waiting for transfers between devices: 26.8 us -> 29.3 us  [shift_by(): lax.ppermute(value, axis, [(i, (i + shift) % count) for i in range(count)])]
    ppermute x36, starting transfers between devices: 41.9 us -> 43.9 us  [shift_by(): lax.ppermute(value, axis, [(i, (i + shift) % count) for i in range(count)])]
    all_to_all x1, starting transfers between devices: 3.58 us -> 5.55 us  [shards(): lax.all_to_all(grad_table.reshape(16, 16, width), GROUP, 0, 0, tiled=True)]
  transfers between devices with their start and end apart: 41 -> 41, of which waited for: 12 -> 13; matrix products, arithmetic and copies ran while one was open for 11% -> 11% of each run, Pallas kernels for 12% -> 12%
where the time goes in v10:
time: 195 us; the launch traced here: 193 us
  starting transfers between devices  71.3 us (37%)
  Pallas kernels  58.9 us (30%)
  waiting for transfers between devices  34 us (17%)
  other arithmetic  16.8 us (9%)
  local copies, waits for them, and re-layouts  9.09 us (5%)
    pallas_call x6, Pallas kernels, local_call(): pl.pallas_call(kernel, out_shape=[jax.ShapeDtypeStruct(shape, kind) for s...  58.9 us
    ppermute x36, starting transfers between devices, shift_by(): lax.ppermute(value, axis, [(i, (i + shift) % count) for i in range(count)])  43.9 us
    ppermute x36, waiting for transfers between devices, shift_by(): lax.ppermute(value, axis, [(i, (i + shift) % count) for i in range(count)])  29.3 us
    all_to_all x1, starting transfers between devices, shards(): lax.all_to_all(jnp.pad(numbers, ((0, 0), (0, 124))), GROUP, 0, 0, tiled=T...  7.82 us
    all_to_all x1, starting transfers between devices, shards(): lax.all_to_all(outgoing.reshape(16, 16, width), GROUP, 0, 0, tiled=True)  6.02 us
    all_to_all x1, starting transfers between devices, shards(): lax.all_to_all(grad_table.reshape(16, 16, width), GROUP, 0, 0, tiled=True)  5.55 us
    all_to_all x1, starting transfers between devices, shards(): lax.all_to_all(jnp.sum(line.astype(F32), axis=0).astype(BF), ('z', 'y'),...  4.44 us
    all_to_all x1, waiting for transfers between devices, shards(): lax.all_to_all(grad_table.reshape(16, 16, width), GROUP, 0, 0, tiled=True)  4.31 us
  transfers between devices with their start and end apart: 41, of which 13 were waited for; matrix products, arithmetic and copies ran while one was open for 11% of the time, Pallas kernels for 12%

profile of v10, /device:TPU:0, one launch (start us, length us, event | category | flops | bytes accessed | tf_op | source)
XLA Modules:
  0.0 192.6 jit_solution(1501393769205178218)
XLA Ops:
  0.7 0.7 pad_add_fusion.refs_0_
  1.3 3.3 %shard_map.190 = (bf16[272,1024]{1,0:T(8,128)(2,1)}, f32[16,1024]{1,0:T(8,128)}, bf16[576,512]{1,0:T(8,128)(2,1)}, bf16[64,1024]{1,0:T(8,128)(2,1)}) custom-call(s32[4]{0:T(128)} %pad_add_fusion.refs_0_, bf16[256,1024]{1,0:T(8,128)(2,1)} %bitcast.37, s32[1,16]{1,0:T(1,128)} %bitcast.49, s32[1,16]{1,0:T(1,128)} %refs_3_.1, bf16[52,1024]{1,0:T(8,128)(2,1)} %refs_4_.1, ...), custom_call_target="tpu_custom_call" | custom-call | bytes 1048576 | tf_op jit(solution)/shard_map/pallas_call | solution.py:88
  4.7 1.7 collective-permute-start.4
  6.4 1.6 collective-permute-start.5
  8.0 2.8 %collective-permute-start.1 = (bf16[272,1024]{1,0:T(8,128)(2,1)}, bf16[272,1024]{1,0:T(8,128)(2,1)S(1)}, u32[]{:S(2)}, u32[]{:S(2)}) collective-permute-start(bf16[272,1024]{1,0:T(8,128)(2,1)} %get-tuple-element.45.refs_1_), channel_id=1, source_target_pairs={{0,12},{4,0},{8,4},{12,8},{1,13},{5,1},{9,5},{13,9},{2,14},{6,2},{... | collective-permute-start | bytes 1671176 | tf_op jit(solution)/shard_map/ppermute | solution.py:22
  10.8 0.8 select_reduce_fusion
  11.6 0.7 broadcast_add_fusion
  12.2 1.3 convolution_convert_fusion
  14.6 0.7 reduce.4
  15.6 0.7 copy.28
  16.3 7.8 %all-to-all-start = ((s32[16,1,128]{2,1,0:T(1,128)}), s32[16,1,128]{2,1,0:T(1,128)S(1)}, u32[]{:S(2)}, u32[]{:S(2)}) async-start(s32[16,1,128]{2,1,0:T(1,128)} %copy.28), calls=%async_computation | async-start | bytes 16384 | tf_op jit(solution)/shard_map/all_to_all | solution.py:581
  24.1 1.5 fusion.refs_3_
  25.9 1.7 collective-permute-start.2
  27.7 1.5 collective-permute-start.6
  29.2 1.8 collective-permute-start.8
  31.6 1.3 fusion.1.refs_4_
  32.9 0.7 collective-permute-done.2.refs_4_
  33.7 1.6 collective-permute-start.3
  35.2 1.1 collective-permute-done.6.refs_11_
  36.9 5.2 %collective-permute-done.3.refs_5_ = bf16[144,1024]{1,0:T(8,128)(2,1)} collective-permute-done((bf16[144,1024]{1,0:T(8,128)(2,1)S(1)}, bf16[144,1024]{1,0:T(8,128)(2,1)}, u32[]{:S(2)}, u32[]{:S(2)}) %collective-permute-start.3) | collective-permute-done | bytes 294944 | tf_op jit(solution)/shard_map/ppermute | solution.py:22
  42.2 11.8 %shard_map.191 = (bf16[256,1024]{1,0:T(8,128)(2,1)}, bf16[1024,1024]{1,0:T(8,128)(2,1)}, bf16[1024,1024]{1,0:T(8,128)(2,1)}, bf16[64,1024]{1,0:T(8,128)(2,1)}, b...) custom-call(s32[4]{0:T(128)} %pad_add_fusion.refs_0_, ...), custom_call_target="tpu_custom_call" | custom-call | flops 2147483648 | bytes 1048576 | tf_op jit(solution)/shard_map/pallas_call | solution.py:88
  54.0 6.0 %all-to-all-start.1 = ((bf16[16,16,1024]{2,1,0:T(8,128)(2,1)}), bf16[16,16,1024]{2,1,0:T(8,128)(2,1)S(1)}, u32[]{:S(2)}, u32[]{:S(2)}) async-start(bf16[16,16,1024]{2,1,0:T(8,128)(2,1)} %bitcast.38), calls=%async_computation.1 | async-start | bytes 1048576 | tf_op jit(solution)/shard_map/all_to_all | solution.py:646
  60.0 1.2 fusion.2.refs_5_
  61.2 5.3 %collective-permute-start.13 = (bf16[80,1024]{1,0:T(8,128)(2,1)S(1)}, bf16[80,1024]{1,0:T(8,128)(2,1)S(1)}, u32[]{:S(2)}, u32[]{:S(2)}) collective-permute-start(bf16[80,1024]{1,0:T(8,128)(2,1)S(1)} %fusion.11), channel_id=1, source_target_pairs={{0,15},{1,0},{2,1},{3,2},{4,3},{5,4},{6,5},{7,6},{8,7},{9,8},{10,9... | collective-permute-start | bytes 491528 | tf_op jit(solution)/shard_map/ppermute | solution.py:22
  66.5 0.6 fusion.14.refs_2_
  67.1 2.6 %copy.29 = bf16[1024,1024]{0,1:T(8,128)(2,1)} copy(bf16[1024,1024]{1,0:T(8,128)(2,1)S(1)} %copy-done.1) | data formatting | bytes 4194304 | tf_op jit(solution)/shard_map/pallas_call | solution.py:88
  70.1 0.8 copy-done.6
  71.0 0.7 copy-done.24
  71.6 20.5 %shard_map.192 = (bf16[256,1024]{1,0:T(8,128)(2,1)}, bf16[256,1024]{1,0:T(8,128)(2,1)}, bf16[256,1024]{1,0:T(8,128)(2,1)}, bf16[256,1024]{1,0:T(8,128)(2,1)}, bf16[256,1024]{1,0:T(8,128)(2,1)}) custom-call(s32[4]{0:T(128)} %pad_add_fusion.refs_0_, bf16[256,1024]{1,0:T(8,128)(2,1)} %bitcast.40, bf16[64,256]{1,0:T(8,128)(2,1)} %fusion.14.refs_2_, ...), custom_call_target="tpu_custom_call" | custom-call | flops 6000000000 | bytes 1048576 | tf_op jit(solution)/shard_map/pallas_call | solution.py:88
  92.2 5.6 %all-to-all-start.2 = ((bf16[16,16,1024]{2,1,0:T(8,128)(2,1)}), bf16[16,16,1024]{2,1,0:T(8,128)(2,1)S(1)}, u32[]{:S(2)}, u32[]{:S(2)}) async-start(bf16[16,16,1024]{2,1,0:T(8,128)(2,1)} %bitcast.41), calls=%async_computation.2 | async-start | bytes 1048576 | tf_op jit(solution)/shard_map/all_to_all | solution.py:683
  97.7 6.3 %shard_map.193 = (bf16[4,16,16,1024]{3,2,1,0:T(8,128)(2,1)}, bf16[4,16,16,1024]{3,2,1,0:T(8,128)(2,1)}) custom-call(s32[4]{0:T(128)} %pad_add_fusion.refs_0_, bf16[256,1024]{1,0:T(8,128)(2,1)} %get-tuple-element.58.refs_1_, bf16[256,1024]{1,0:T(8,128)(2,1)} %get-tuple-element.59.refs_2_, bf16[256,1024]{1,0:T(8,128)(2,1)} %get-tuple-element.60.refs_3_), custom_call_target="tpu_custom_call" | custom-call | flops 1000000000 | bytes 1048576 | tf_op jit(solution)/shard_map/pallas_call | solution.py:88
  104.0 4.3 %all-to-all-done.2 = bf16[16,16,1024]{2,1,0:T(8,128)(2,1)S(1)} async-done(((bf16[16,16,1024]{2,1,0:T(8,128)(2,1)}), bf16[16,16,1024]{2,1,0:T(8,128)(2,1)S(1)}, u32[]{:S(2)}, u32[]{:S(2)}) %all-to-all-start.2) | async-done | bytes 524320 | tf_op jit(solution)/shard_map/all_to_all | solution.py:683
  108.3 0.8 copy-done.5
  109.1 13.3 %shard_map.194 = (bf16[4,4,48,1024]{3,2,1,0:T(8,128)(2,1)}, bf16[4,4,32,1024]{3,2,1,0:T(8,128)(2,1)}, bf16[4,4,48,1024]{3,2,1,0:T(8,128)(2,1)}, bf16[4,4,32,1024]{3,2,1,0:T(8,128)(2,1)}) custom-call(s32[4]{0:T(128)} %pad_add_fusion.refs_0_, bf16[256,1024]{1,0:T(8,128)(2,1)} %bitcast.39, bf16[64,256]{1,0:T(8,128)(2,1)} %get-tuple-element.64.refs_2_, ...), custom_call_target="tpu_custom_call" | custom-call | flops 2147483648 | bytes 1048576 | tf_op jit(solution)/shard_map/pallas_call | solution.py:88
  122.5 4.0 %add_convert_fusion = bf16[4,16,16,1024]{3,2,1,0:T(8,128)(2,1)} fusion(bf16[4,16,16,1024]{3,2,1,0:T(8,128)(2,1)} %collective-permute-done.15, bf16[4,16,16,1024]{3,2,1,0:T(8,128)(2,1)S(1)} %copy-done), kind=kLoop, calls=%fused_computation | loop fusion | flops 4194304 | bytes 6291456 | tf_op jit(solution)/shard_map/convert_element_type | solution.py:691
  126.5 0.7 add_convert_fusion.1
  127.6 1.0 fusion.19
  128.7 4.1 %collective-permute-start.16 = (bf16[192,1024]{1,0:T(8,128)(2,1)}, bf16[192,1024]{1,0:T(8,128)(2,1)}, u32[]{:S(2)}, u32[]{:S(2)}) collective-permute-start(bf16[192,1024]{1,0:T(8,128)(2,1)} %bitcast.18), channel_id=1, source_target_pairs={{0,96},{32,0},{64,32},{96,64},{1,97},{33,1},{65,33},{97,65},{2,98}... | collective-permute-start | bytes 1179656 | tf_op jit(solution)/shard_map/ppermute | solution.py:22
  132.7 1.9 collective-permute-start.18
  134.6 3.6 %all-to-all-start.3 = ((bf16[4,16,16,1024]{3,2,1,0:T(8,128)(2,1)}), bf16[4,16,16,1024]{3,2,1,0:T(8,128)(2,1)S(1)}, u32[]{:S(2)}, u32[]{:S(2)}) async-start(bf16[4,16,16,1024]{3,2,1,0:T(8,128)(2,1)} %add_convert_fusion), calls=%async_computation.3 | async-start | bytes 4194304 | tf_op jit(solution)/shard_map/all_to_all | solution.py:706
  138.2 1.6 add_convert_fusion.2
  139.9 0.6 collective-permute-start.23
  140.6 1.5 collective-permute-start.24
  142.0 8.1 %collective-permute-done.16 = bf16[192,1024]{1,0:T(8,128)(2,1)} collective-permute-done((bf16[192,1024]{1,0:T(8,128)(2,1)}, bf16[192,1024]{1,0:T(8,128)(2,1)}, u32[]{:S(2)}, u32[]{:S(2)}) %collective-permute-start.16) | collective-permute-done | bytes 393248 | tf_op jit(solution)/shard_map/ppermute | solution.py:22
  150.1 1.1 collective-permute-start.25
  151.2 2.3 %collective-permute-done.17 = bf16[192,1024]{1,0:T(8,128)(2,1)} collective-permute-done((bf16[192,1024]{1,0:T(8,128)(2,1)}, bf16[192,1024]{1,0:T(8,128)(2,1)}, u32[]{:S(2)}, u32[]{:S(2)}) %collective-permute-start.17) | collective-permute-done | bytes 393248 | tf_op jit(solution)/shard_map/ppermute | solution.py:22
  153.5 1.5 fusion.5
  155.1 0.6 collective-permute-start.19
  155.7 1.5 collective-permute-start.20
  157.2 1.1 collective-permute-start.21
  158.3 2.5 %collective-permute-done.25 = bf16[128,1024]{1,0:T(8,128)(2,1)S(1)} collective-permute-done((bf16[128,1024]{1,0:T(8,128)(2,1)S(1)}, bf16[128,1024]{1,0:T(8,128)(2,1)S(1)}, u32[]{:S(2)}, u32[]{:S(2)}) %collective-permute-start.25) | collective-permute-done | bytes 262176 | tf_op jit(solution)/shard_map/ppermute | solution.py:22
  161.0 4.0 %collective-permute-start.26 = (bf16[32,1024]{1,0:T(8,128)(2,1)S(1)}, bf16[32,1024]{1,0:T(8,128)(2,1)S(1)}, u32[]{:S(2)}, u32[]{:S(2)}) collective-permute-start(bf16[32,1024]{1,0:T(8,128)(2,1)S(1)} %get-tuple-element.95), channel_id=1, source_target_pairs={{0,96},{32,0},{64,32},{96,64},{1,97},{33,1},{65,33},{97,65},{2,98}... | collective-permute-start | bytes 196616 | tf_op jit(solution)/shard_map/ppermute | solution.py:22
  165.0 1.5 collective-permute-start.28
  166.6 1.3 reduce_sum.31
  167.9 4.4 %all-to-all-start.4 = ((bf16[16,16,1024]{2,1,0:T(8,128)(2,1)}), bf16[16,16,1024]{2,1,0:T(8,128)(2,1)S(1)}, u32[]{:S(2)}, u32[]{:S(2)}) async-start(bf16[16,16,1024]{2,1,0:T(8,128)(2,1)} %reduce_sum.31), calls=%async_computation.4 | async-start | bytes 1048576 | tf_op jit(solution)/shard_map/all_to_all | solution.py:707
  172.5 2.0 %collective-permute-start.29 = (bf16[80,1024]{1,0:T(8,128)(2,1)S(1)}, bf16[80,1024]{1,0:T(8,128)(2,1)S(1)}, u32[]{:S(2)}, u32[]{:S(2)}) collective-permute-start(bf16[80,1024]{1,0:T(8,128)(2,1)S(1)} %pad_maximum_fusion.refs_1_), channel_id=1, source_target_pairs={{0,32},{32,64},{64,96},{96,0},{1,33},{33,65},{65,97},{97,1},{2,34}... | collective-permute-start | bytes 491528 | tf_op jit(solution)/shard_map/ppermute | solution.py:22
  174.5 1.3 collective-permute-start.30
  175.8 2.2 %collective-permute-start.31 = (bf16[80,1024]{1,0:T(8,128)(2,1)S(1)}, bf16[80,1024]{1,0:T(8,128)(2,1)S(1)}, u32[]{:S(2)}, u32[]{:S(2)}) collective-permute-start(bf16[80,1024]{1,0:T(8,128)(2,1)S(1)} %pad_maximum_fusion.refs_1_), channel_id=1, source_target_pairs={{0,64},{32,96},{64,0},{96,32},{1,65},{33,97},{65,1},{97,33},{2,66}... | collective-permute-start | bytes 491528 | tf_op jit(solution)/shard_map/ppermute | solution.py:22
  178.0 5.9 %collective-permute-done.29.refs_2_ = bf16[80,1024]{1,0:T(8,128)(2,1)S(1)} collective-permute-done((bf16[80,1024]{1,0:T(8,128)(2,1)S(1)}, bf16[80,1024]{1,0:T(8,128)(2,1)S(1)}, u32[]{:S(2)}, u32[]{:S(2)}) %collective-permute-start.29) | collective-permute-done | bytes 163872 | tf_op jit(solution)/shard_map/ppermute | solution.py:22
  184.4 1.7 collective-permute-done.31.refs_4_
  186.2 1.3 collective-permute-done.35.refs_8_
  187.6 0.7 copy-done.14
  188.2 3.7 %shard_map.195 = (f32[1024,256]{1,0:T(8,128)}, f32[256,1024]{1,0:T(8,128)}, f32[52,1024]{1,0:T(8,128)}) custom-call(s32[4]{0:T(128)} %pad_add_fusion.refs_0_, bf16[80,1024]{1,0:T(8,128)(2,1)} %copy-done.4, bf16[80,1024]{1,0:T(8,128)(2,1)} %copy-done.8, bf16[80,1024]{1,0:T(8,128)(2,1)} %copy-done.9, bf16[80,1024]{1,0:T(8,128)(2,1)} %copy-done.10, ...), custom_call_target="tpu_custom_call" | custom-call | bytes 1048576 | tf_op jit(solution)/shard_map/pallas_call | solution.py:88
  192.0 0.6 fusion.24
  (124 shorter events, 5.0 us)
Async XLA Ops:
  0.6 14.0 %copy-start.25 = (s32[1,16]{1,0:T(1,128)S(1)}, s32[1,16]{1,0:T(1,128)}, u32[]{:S(2)}) copy-start(s32[1,16]{1,0:T(1,128)} %param.25) | copy-start | bytes 196
  0.6 23.4 %copy-start.19 = (s32[1,2048]{1,0:T(1,128)S(1)}, s32[1,2048]{1,0:T(1,128)}, u32[]{:S(2)}) copy-start(s32[1,2048]{1,0:T(1,128)} %param.23) | copy-start | bytes 24580
  4.7 23.0 %collective-permute-start.4 = (bf16[576,512]{1,0:T(8,128)(2,1)}, bf16[576,512]{1,0:T(8,128)(2,1)S(1)}, u32[]{:S(2)}, u32[]{:S(2)}) collective-permute-start(bf16[576,512]{1,0:T(8,128)(2,1)} %get-tuple-element.47), channel_id=1, source_target_pairs={{0,1},{1,2},{2,3},{3,0},{4,5},{5,6},{6,7},{7,4},{8,9},{9,10},{10,1... | collective-permute-start | bytes 1769480 | tf_op jit(solution)/shard_map/ppermute | solution.py:22
  6.4 22.8 %collective-permute-start.5 = (bf16[576,512]{1,0:T(8,128)(2,1)}, bf16[576,512]{1,0:T(8,128)(2,1)S(1)}, u32[]{:S(2)}, u32[]{:S(2)}) collective-permute-start(bf16[576,512]{1,0:T(8,128)(2,1)} %get-tuple-element.47), channel_id=1, source_target_pairs={{0,3},{1,0},{2,1},{3,2},{4,7},{5,4},{6,5},{7,6},{8,11},{9,8},{10,9... | collective-permute-start | bytes 1769480 | tf_op jit(solution)/shard_map/ppermute | solution.py:22
  8.0 23.1 %collective-permute-start.1 = (bf16[272,1024]{1,0:T(8,128)(2,1)}, bf16[272,1024]{1,0:T(8,128)(2,1)S(1)}, u32[]{:S(2)}, u32[]{:S(2)}) collective-permute-start(bf16[272,1024]{1,0:T(8,128)(2,1)} %get-tuple-element.45.refs_1_), channel_id=1, source_target_pairs={{0,12},{4,0},{8,4},{12,8},{1,13},{5,1},{9,5},{13,9},{2,14},{6,2},{... | collective-permute-start | bytes 1671176 | tf_op jit(solution)/shard_map/ppermute | solution.py:22
  10.8 15.1 %collective-permute-start = (bf16[272,1024]{1,0:T(8,128)(2,1)}, bf16[272,1024]{1,0:T(8,128)(2,1)S(1)}, u32[]{:S(2)}, u32[]{:S(2)}) collective-permute-start(bf16[272,1024]{1,0:T(8,128)(2,1)} %get-tuple-element.45.refs_1_), channel_id=1, source_target_pairs={{0,4},{4,8},{8,12},{12,0},{1,5},{5,9},{9,13},{13,1},{2,6},{6,10},{... | collective-permute-start | bytes 1671176 | tf_op jit(solution)/shard_map/ppermute | solution.py:22
  13.5 18.1 %copy-start.18 = (s32[1,2048]{1,0:T(1,128)S(1)}, s32[1,2048]{1,0:T(1,128)}, u32[]{:S(2)}) copy-start(s32[1,2048]{1,0:T(1,128)} %param.24) | copy-start | bytes 24580
  13.7 17.4 %collective-permute-start.7 = (bf16[80,1024]{1,0:T(8,128)(2,1)S(1)}, bf16[80,1024]{1,0:T(8,128)(2,1)S(1)}, u32[]{:S(2)}, u32[]{:S(2)}) collective-permute-start(bf16[80,1024]{1,0:T(8,128)(2,1)S(1)} %fusion.12), channel_id=1, source_target_pairs={{0,1},{1,2},{2,3},{3,4},{4,5},{5,6},{6,7},{7,8},{8,9},{9,10},{10,1... | collective-permute-start | bytes 491528 | tf_op jit(solution)/shard_map/ppermute | solution.py:22
  16.3 20.7 %all-to-all-start = ((s32[16,1,128]{2,1,0:T(1,128)}), s32[16,1,128]{2,1,0:T(1,128)S(1)}, u32[]{:S(2)}, u32[]{:S(2)}) async-start(s32[16,1,128]{2,1,0:T(1,128)} %copy.28), calls=%async_computation | async-start | bytes 16384 | tf_op jit(solution)/shard_map/all_to_all | solution.py:581
  24.1 12.8 %copy-start.26 = (s32[1,16]{1,0:T(1,128)S(1)}, s32[1,16]{1,0:T(1,128)}, u32[]{:S(2)}) copy-start(s32[1,16]{1,0:T(1,128)} %param.20) | copy-start | bytes 196
  25.9 16.3 %copy-start.16 = (bf16[272,1024]{1,0:T(8,128)(2,1)}, bf16[272,1024]{1,0:T(8,128)(2,1)S(1)}, u32[]{:S(2)}) copy-start(bf16[272,1024]{1,0:T(8,128)(2,1)S(1)} %collective-permute-done.refs_2_) | copy-start | bytes 1671172
  25.9 7.7 %collective-permute-start.2 = (bf16[128,1024]{1,0:T(8,128)(2,1)S(1)}, bf16[128,1024]{1,0:T(8,128)(2,1)S(1)}, u32[]{:S(2)}, u32[]{:S(2)}) collective-permute-start(bf16[128,1024]{1,0:T(8,128)(2,1)S(1)} %slice.115), channel_id=1, source_target_pairs={{0,4},{4,8},{8,12},{12,0},{1,5},{5,9},{9,13},{13,1},{2,6},{6,10},{... | collective-permute-start | bytes 786440 | tf_op jit(solution)/shard_map/ppermute | solution.py:22
  27.6 14.5 %copy-start.17 = (bf16[576,512]{1,0:T(8,128)(2,1)}, bf16[576,512]{1,0:T(8,128)(2,1)S(1)}, u32[]{:S(2)}) copy-start(bf16[576,512]{1,0:T(8,128)(2,1)S(1)} %collective-permute-done.4.refs_9_) | copy-start | bytes 1769476
  27.7 8.7 %collective-permute-start.6 = (bf16[256,512]{1,0:T(8,128)(2,1)S(1)}, bf16[256,512]{1,0:T(8,128)(2,1)}, u32[]{:S(2)}, u32[]{:S(2)}) collective-permute-start(bf16[256,512]{1,0:T(8,128)(2,1)S(1)} %slice.117), channel_id=1, source_target_pairs={{0,1},{1,2},{2,3},{3,0},{4,5},{5,6},{6,7},{7,4},{8,9},{9,10},{10,1... | collective-permute-start | bytes 786440 | tf_op jit(solution)/shard_map/ppermute | solution.py:22
  29.2 13.0 %copy-start.7 = (bf16[576,512]{1,0:T(8,128)(2,1)}, bf16[576,512]{1,0:T(8,128)(2,1)S(1)}, u32[]{:S(2)}) copy-start(bf16[576,512]{1,0:T(8,128)(2,1)S(1)} %collective-permute-done.5.refs_10_) | copy-start | bytes 1769476
  29.2 7.2 %collective-permute-start.8 = (bf16[320,512]{1,0:T(8,128)(2,1)S(1)}, bf16[320,512]{1,0:T(8,128)(2,1)S(1)}, u32[]{:S(2)}, u32[]{:S(2)}) collective-permute-start(bf16[320,512]{1,0:T(8,128)(2,1)S(1)} %slice.119), channel_id=1, source_target_pairs={{0,3},{1,0},{2,1},{3,2},{4,7},{5,4},{6,5},{7,6},{8,11},{9,8},{10,9... | collective-permute-start | bytes 983048 | tf_op jit(solution)/shard_map/ppermute | solution.py:22
  31.1 22.9 %copy-start.23 = (bf16[80,1024]{1,0:T(8,128)(2,1)}, bf16[80,1024]{1,0:T(8,128)(2,1)S(1)}, u32[]{:S(2)}) copy-start(bf16[80,1024]{1,0:T(8,128)(2,1)S(1)} %collective-permute-done.7.refs_10_) | copy-start | bytes 491524
  31.1 11.1 %collective-permute-start.10 = (bf16[576,512]{1,0:T(8,128)(2,1)S(1)}, bf16[576,512]{1,0:T(8,128)(2,1)}, u32[]{:S(2)}, u32[]{:S(2)}) collective-permute-start(bf16[576,512]{1,0:T(8,128)(2,1)S(1)} %collective-permute-done.5.refs_10_), channel_id=1, source_target_pairs={{0,16},{16,0},{1,17},{17,1},{2,18},{18,2},{3,19},{19,3},{4,20},{20... | collective-permute-start | bytes 1769480 | tf_op jit(solution)/shard_map/ppermute | solution.py:22
  31.1 11.1 %copy-start.15 = (bf16[272,1024]{1,0:T(8,128)(2,1)}, bf16[272,1024]{1,0:T(8,128)(2,1)S(1)}, u32[]{:S(2)}) copy-start(bf16[272,1024]{1,0:T(8,128)(2,1)S(1)} %collective-permute-done.1.refs_3_) | copy-start | bytes 1671172
  31.1 11.0 %collective-permute-start.9 = (bf16[576,512]{1,0:T(8,128)(2,1)S(1)}, bf16[576,512]{1,0:T(8,128)(2,1)}, u32[]{:S(2)}, u32[]{:S(2)}) collective-permute-start(bf16[576,512]{1,0:T(8,128)(2,1)S(1)} %collective-permute-done.4.refs_9_), channel_id=1, source_target_pairs={{0,16},{16,0},{1,17},{17,1},{2,18},{18,2},{3,19},{19,3},{4,20},{20... | collective-permute-start | bytes 1769480 | tf_op jit(solution)/shard_map/ppermute | solution.py:22
  33.7 3.2 %copy-start.22 = (bf16[128,1024]{1,0:T(8,128)(2,1)}, bf16[128,1024]{1,0:T(8,128)(2,1)S(1)}, u32[]{:S(2)}) copy-start(bf16[128,1024]{1,0:T(8,128)(2,1)S(1)} %collective-permute-done.2.refs_4_) | copy-start | bytes 786436
  33.7 8.5 %collective-permute-start.3 = (bf16[144,1024]{1,0:T(8,128)(2,1)S(1)}, bf16[144,1024]{1,0:T(8,128)(2,1)}, u32[]{:S(2)}, u32[]{:S(2)}) collective-permute-start(bf16[144,1024]{1,0:T(8,128)(2,1)S(1)} %slice.116), channel_id=1, source_target_pairs={{0,12},{4,0},{8,4},{12,8},{1,13},{5,1},{9,5},{13,9},{2,14},{6,2},{... | collective-permute-start | bytes 884744 | tf_op jit(solution)/shard_map/ppermute | solution.py:22
  36.3 5.8 %collective-permute-start.11 = (bf16[256,512]{1,0:T(8,128)(2,1)}, bf16[256,512]{1,0:T(8,128)(2,1)}, u32[]{:S(2)}, u32[]{:S(2)}) collective-permute-start(bf16[256,512]{1,0:T(8,128)(2,1)} %collective-permute-done.6.refs_11_), channel_id=1, source_target_pairs={{0,16},{16,0},{1,17},{17,1},{2,18},{18,2},{3,19},{19,3},{4,20},{20... | collective-permute-start | bytes 786440 | tf_op jit(solution)/shard_map/ppermute | solution.py:22
  36.4 5.8 %copy-start.21 = (bf16[320,512]{1,0:T(8,128)(2,1)}, bf16[320,512]{1,0:T(8,128)(2,1)S(1)}, u32[]{:S(2)}) copy-start(bf16[320,512]{1,0:T(8,128)(2,1)S(1)} %collective-permute-done.8.refs_12_) | copy-start | bytes 983044
  36.4 5.8 %collective-permute-start.12 = (bf16[320,512]{1,0:T(8,128)(2,1)S(1)}, bf16[320,512]{1,0:T(8,128)(2,1)}, u32[]{:S(2)}, u32[]{:S(2)}) collective-permute-start(bf16[320,512]{1,0:T(8,128)(2,1)S(1)} %collective-permute-done.8.refs_12_), channel_id=1, source_target_pairs={{0,16},{16,0},{1,17},{17,1},{2,18},{18,2},{3,19},{19,3},{4,20},{20... | collective-permute-start | bytes 983048 | tf_op jit(solution)/shard_map/ppermute | solution.py:22
  36.9 5.3 %copy-start.20 = (s32[16,1,128]{2,1,0:T(1,128)}, s32[16,1,128]{2,1,0:T(1,128)S(1)}, u32[]{:S(2)}) copy-start(s32[16,1,128]{2,1,0:T(1,128)S(1)} %all-to-all-done) | copy-start | bytes 24580
  54.0 13.1 %copy-start.1 = (bf16[1024,1024]{1,0:T(8,128)(2,1)S(1)}, bf16[1024,1024]{1,0:T(8,128)(2,1)}, u32[]{:S(2)}) copy-start(bf16[1024,1024]{1,0:T(8,128)(2,1)} %get-tuple-element.52) | copy-start | bytes 6291460
  54.0 16.1 %all-to-all-start.1 = ((bf16[16,16,1024]{2,1,0:T(8,128)(2,1)}), bf16[16,16,1024]{2,1,0:T(8,128)(2,1)S(1)}, u32[]{:S(2)}, u32[]{:S(2)}) async-start(bf16[16,16,1024]{2,1,0:T(8,128)(2,1)} %bitcast.38), calls=%async_computation.1 | async-start | bytes 1048576 | tf_op jit(solution)/shard_map/all_to_all | solution.py:646
  61.2 8.9 %collective-permute-start.13 = (bf16[80,1024]{1,0:T(8,128)(2,1)S(1)}, bf16[80,1024]{1,0:T(8,128)(2,1)S(1)}, u32[]{:S(2)}, u32[]{:S(2)}) collective-permute-start(bf16[80,1024]{1,0:T(8,128)(2,1)S(1)} %fusion.11), channel_id=1, source_target_pairs={{0,15},{1,0},{2,1},{3,2},{4,3},{5,4},{6,5},{7,6},{8,7},{9,8},{10,9... | collective-permute-start | bytes 491528 | tf_op jit(solution)/shard_map/ppermute | solution.py:22
  92.2 16.1 %all-to-all-start.2 = ((bf16[16,16,1024]{2,1,0:T(8,128)(2,1)}), bf16[16,16,1024]{2,1,0:T(8,128)(2,1)S(1)}, u32[]{:S(2)}, u32[]{:S(2)}) async-start(bf16[16,16,1024]{2,1,0:T(8,128)(2,1)} %bitcast.41), calls=%async_computation.2 | async-start | bytes 1048576 | tf_op jit(solution)/shard_map/all_to_all | solution.py:683
  108.3 14.2 %collective-permute-start.15 = (bf16[4,16,16,1024]{3,2,1,0:T(8,128)(2,1)}, bf16[4,16,16,1024]{3,2,1,0:T(8,128)(2,1)}, u32[]{:S(2)}, u32[]{:S(2)}) collective-permute-start(bf16[4,16,16,1024]{3,2,1,0:T(8,128)(2,1)} %get-tuple-element.74), channel_id=1, source_target_pairs={{0,16},{16,0},{1,17},{17,1},{2,18},{18,2},{3,19},{19,3},{4,20},{20... | collective-permute-start | bytes 6291464 | tf_op jit(solution)/shard_map/ppermute | solution.py:22
  109.1 13.4 %copy-start = (bf16[4,16,16,1024]{3,2,1,0:T(8,128)(2,1)S(1)}, bf16[4,16,16,1024]{3,2,1,0:T(8,128)(2,1)}, u32[]{:S(2)}) copy-start(bf16[4,16,16,1024]{3,2,1,0:T(8,128)(2,1)} %get-tuple-element.73) | copy-start | bytes 6291460
  122.4 4.1 %copy-start.2 = (bf16[4,4,48,1024]{3,2,1,0:T(8,128)(2,1)S(1)}, bf16[4,4,48,1024]{3,2,1,0:T(8,128)(2,1)}, u32[]{:S(2)}) copy-start(bf16[4,4,48,1024]{3,2,1,0:T(8,128)(2,1)} %get-tuple-element.71) | copy-start | bytes 4718596
  122.4 4.1 %collective-permute-start.14 = (bf16[4,4,48,1024]{3,2,1,0:T(8,128)(2,1)}, bf16[4,4,48,1024]{3,2,1,0:T(8,128)(2,1)S(1)}, u32[]{:S(2)}, u32[]{:S(2)}) collective-permute-start(bf16[4,4,48,1024]{3,2,1,0:T(8,128)(2,1)} %get-tuple-element.72), channel_id=1, source_target_pairs={{0,16},{16,0},{1,17},{17,1},{2,18},{18,2},{3,19},{19,3},{4,20},{20... | collective-permute-start | bytes 4718600 | tf_op jit(solution)/shard_map/ppermute | solution.py:22
  127.2 11.0 %collective-permute-start.22 = (bf16[4,4,32,1024]{3,2,1,0:T(8,128)(2,1)}, bf16[4,4,32,1024]{3,2,1,0:T(8,128)(2,1)}, u32[]{:S(2)}, u32[]{:S(2)}) collective-permute-start(bf16[4,4,32,1024]{3,2,1,0:T(8,128)(2,1)} %get-tuple-element.79), channel_id=1, source_target_pairs={{0,16},{16,0},{1,17},{17,1},{2,18},{18,2},{3,19},{19,3},{4,20},{20... | collective-permute-start | bytes 3145736 | tf_op jit(solution)/shard_map/ppermute | solution.py:22
  128.7 21.5 %collective-permute-start.16 = (bf16[192,1024]{1,0:T(8,128)(2,1)}, bf16[192,1024]{1,0:T(8,128)(2,1)}, u32[]{:S(2)}, u32[]{:S(2)}) collective-permute-start(bf16[192,1024]{1,0:T(8,128)(2,1)} %bitcast.18), channel_id=1, source_target_pairs={{0,96},{32,0},{64,32},{96,64},{1,97},{33,1},{65,33},{97,65},{2,98}... | collective-permute-start | bytes 1179656 | tf_op jit(solution)/shard_map/ppermute | solution.py:22
  132.7 20.8 %collective-permute-start.17 = (bf16[192,1024]{1,0:T(8,128)(2,1)}, bf16[192,1024]{1,0:T(8,128)(2,1)}, u32[]{:S(2)}, u32[]{:S(2)}) collective-permute-start(bf16[192,1024]{1,0:T(8,128)(2,1)} %bitcast.19), channel_id=1, source_target_pairs={{0,32},{32,64},{64,96},{96,0},{1,33},{33,65},{65,97},{97,1},{2,34}... | collective-permute-start | bytes 1179656 | tf_op jit(solution)/shard_map/ppermute | solution.py:22
  132.7 5.5 %copy-start.3 = (bf16[4,4,32,1024]{3,2,1,0:T(8,128)(2,1)S(1)}, bf16[4,4,32,1024]{3,2,1,0:T(8,128)(2,1)}, u32[]{:S(2)}) copy-start(bf16[4,4,32,1024]{3,2,1,0:T(8,128)(2,1)} %get-tuple-element.78) | copy-start | bytes 3145732
  132.7 20.8 %collective-permute-start.18 = (bf16[192,1024]{1,0:T(8,128)(2,1)}, bf16[192,1024]{1,0:T(8,128)(2,1)}, u32[]{:S(2)}, u32[]{:S(2)}) collective-permute-start(bf16[192,1024]{1,0:T(8,128)(2,1)} %bitcast.20), channel_id=1, source_target_pairs={{0,64},{32,96},{64,0},{96,32},{1,65},{33,97},{65,1},{97,33},{2,66}... | collective-permute-start | bytes 1179656 | tf_op jit(solution)/shard_map/ppermute | solution.py:22
  134.6 32.0 %all-to-all-start.3 = ((bf16[4,16,16,1024]{3,2,1,0:T(8,128)(2,1)}), bf16[4,16,16,1024]{3,2,1,0:T(8,128)(2,1)S(1)}, u32[]{:S(2)}, u32[]{:S(2)}) async-start(bf16[4,16,16,1024]{3,2,1,0:T(8,128)(2,1)} %add_convert_fusion), calls=%async_computation.3 | async-start | bytes 4194304 | tf_op jit(solution)/shard_map/all_to_all | solution.py:706
  139.9 17.2 %collective-permute-start.23 = (bf16[128,1024]{1,0:T(8,128)(2,1)S(1)}, bf16[128,1024]{1,0:T(8,128)(2,1)S(1)}, u32[]{:S(2)}, u32[]{:S(2)}) collective-permute-start(bf16[128,1024]{1,0:T(8,128)(2,1)S(1)} %bitcast.44), channel_id=1, source_target_pairs={{0,3},{1,0},{2,1},{3,2},{4,7},{5,4},{6,5},{7,6},{8,11},{9,8},{10,9... | collective-permute-start | bytes 786440 | tf_op jit(solution)/shard_map/ppermute | solution.py:22
  140.6 17.7 %collective-permute-start.24 = (bf16[128,1024]{1,0:T(8,128)(2,1)S(1)}, bf16[128,1024]{1,0:T(8,128)(2,1)S(1)}, u32[]{:S(2)}, u32[]{:S(2)}) collective-permute-start(bf16[128,1024]{1,0:T(8,128)(2,1)S(1)} %bitcast.43), channel_id=1, source_target_pairs={{0,1},{1,2},{2,3},{3,0},{4,5},{5,6},{6,7},{7,4},{8,9},{9,10},{10,1... | collective-permute-start | bytes 786440 | tf_op jit(solution)/shard_map/ppermute | solution.py:22
  150.1 10.6 %collective-permute-start.25 = (bf16[128,1024]{1,0:T(8,128)(2,1)S(1)}, bf16[128,1024]{1,0:T(8,128)(2,1)S(1)}, u32[]{:S(2)}, u32[]{:S(2)}) collective-permute-start(bf16[128,1024]{1,0:T(8,128)(2,1)S(1)} %bitcast.42), channel_id=1, source_target_pairs={{0,2},{1,3},{2,0},{3,1},{4,6},{5,7},{6,4},{7,5},{8,10},{9,11},{10,... | collective-permute-start | bytes 786440 | tf_op jit(solution)/shard_map/ppermute | solution.py:22
  155.1 9.9 %collective-permute-start.19 = (bf16[48,1024]{1,0:T(8,128)(2,1)S(1)}, bf16[48,1024]{1,0:T(8,128)(2,1)S(1)}, u32[]{:S(2)}, u32[]{:S(2)}) collective-permute-start(bf16[48,1024]{1,0:T(8,128)(2,1)S(1)} %get-tuple-element.92), channel_id=1, source_target_pairs={{0,3},{1,0},{2,1},{3,2},{4,7},{5,4},{6,5},{7,6},{8,11},{9,8},{10,9... | collective-permute-start | bytes 294920 | tf_op jit(solution)/shard_map/ppermute | solution.py:22
  155.7 10.8 %collective-permute-start.20 = (bf16[48,1024]{1,0:T(8,128)(2,1)S(1)}, bf16[48,1024]{1,0:T(8,128)(2,1)S(1)}, u32[]{:S(2)}, u32[]{:S(2)}) collective-permute-start(bf16[48,1024]{1,0:T(8,128)(2,1)S(1)} %get-tuple-element.94), channel_id=1, source_target_pairs={{0,1},{1,2},{2,3},{3,0},{4,5},{5,6},{6,7},{7,4},{8,9},{9,10},{10,1... | collective-permute-start | bytes 294920 | tf_op jit(solution)/shard_map/ppermute | solution.py:22
  157.2 9.3 %collective-permute-start.21 = (bf16[48,1024]{1,0:T(8,128)(2,1)S(1)}, bf16[48,1024]{1,0:T(8,128)(2,1)S(1)}, u32[]{:S(2)}, u32[]{:S(2)}) collective-permute-start(bf16[48,1024]{1,0:T(8,128)(2,1)S(1)} %get-tuple-element.93), channel_id=1, source_target_pairs={{0,2},{1,3},{2,0},{3,1},{4,6},{5,7},{6,4},{7,5},{8,10},{9,11},{10,... | collective-permute-start | bytes 294920 | tf_op jit(solution)/shard_map/ppermute | solution.py:22
  161.0 11.4 %collective-permute-start.26 = (bf16[32,1024]{1,0:T(8,128)(2,1)S(1)}, bf16[32,1024]{1,0:T(8,128)(2,1)S(1)}, u32[]{:S(2)}, u32[]{:S(2)}) collective-permute-start(bf16[32,1024]{1,0:T(8,128)(2,1)S(1)} %get-tuple-element.95), channel_id=1, source_target_pairs={{0,96},{32,0},{64,32},{96,64},{1,97},{33,1},{65,33},{97,65},{2,98}... | collective-permute-start | bytes 196616 | tf_op jit(solution)/shard_map/ppermute | solution.py:22
  165.0 7.4 %collective-permute-start.27 = (bf16[32,1024]{1,0:T(8,128)(2,1)S(1)}, bf16[32,1024]{1,0:T(8,128)(2,1)S(1)}, u32[]{:S(2)}, u32[]{:S(2)}) collective-permute-start(bf16[32,1024]{1,0:T(8,128)(2,1)S(1)} %get-tuple-element.97), channel_id=1, source_target_pairs={{0,32},{32,64},{64,96},{96,0},{1,33},{33,65},{65,97},{97,1},{2,34}... | collective-permute-start | bytes 196616 | tf_op jit(solution)/shard_map/ppermute | solution.py:22
  165.0 7.4 %collective-permute-start.28 = (bf16[32,1024]{1,0:T(8,128)(2,1)S(1)}, bf16[32,1024]{1,0:T(8,128)(2,1)S(1)}, u32[]{:S(2)}, u32[]{:S(2)}) collective-permute-start(bf16[32,1024]{1,0:T(8,128)(2,1)S(1)} %get-tuple-element.96), channel_id=1, source_target_pairs={{0,64},{32,96},{64,0},{96,32},{1,65},{33,97},{65,1},{97,33},{2,66}... | collective-permute-start | bytes 196616 | tf_op jit(solution)/shard_map/ppermute | solution.py:22
  167.9 24.0 %all-to-all-start.4 = ((bf16[16,16,1024]{2,1,0:T(8,128)(2,1)}), bf16[16,16,1024]{2,1,0:T(8,128)(2,1)S(1)}, u32[]{:S(2)}, u32[]{:S(2)}) async-start(bf16[16,16,1024]{2,1,0:T(8,128)(2,1)} %reduce_sum.31), calls=%async_computation.4 | async-start | bytes 1048576 | tf_op jit(solution)/shard_map/all_to_all | solution.py:707
  172.5 15.0 %copy-start.4 = (bf16[80,1024]{1,0:T(8,128)(2,1)}, bf16[80,1024]{1,0:T(8,128)(2,1)S(1)}, u32[]{:S(2)}) copy-start(bf16[80,1024]{1,0:T(8,128)(2,1)S(1)} %pad_maximum_fusion.refs_1_) | copy-start | bytes 491524
  172.5 11.4 %collective-permute-start.29 = (bf16[80,1024]{1,0:T(8,128)(2,1)S(1)}, bf16[80,1024]{1,0:T(8,128)(2,1)S(1)}, u32[]{:S(2)}, u32[]{:S(2)}) collective-permute-start(bf16[80,1024]{1,0:T(8,128)(2,1)S(1)} %pad_maximum_fusion.refs_1_), channel_id=1, source_target_pairs={{0,32},{32,64},{64,96},{96,0},{1,33},{33,65},{65,97},{97,1},{2,34}... | collective-permute-start | bytes 491528 | tf_op jit(solution)/shard_map/ppermute | solution.py:22
  174.5 9.5 %collective-permute-start.30 = (bf16[80,1024]{1,0:T(8,128)(2,1)S(1)}, bf16[80,1024]{1,0:T(8,128)(2,1)S(1)}, u32[]{:S(2)}, u32[]{:S(2)}) collective-permute-start(bf16[80,1024]{1,0:T(8,128)(2,1)S(1)} %pad_maximum_fusion.refs_1_), channel_id=1, source_target_pairs={{0,96},{32,0},{64,32},{96,64},{1,97},{33,1},{65,33},{97,65},{2,98}... | collective-permute-start | bytes 491528 | tf_op jit(solution)/shard_map/ppermute | solution.py:22
  175.8 10.3 %collective-permute-start.31 = (bf16[80,1024]{1,0:T(8,128)(2,1)S(1)}, bf16[80,1024]{1,0:T(8,128)(2,1)S(1)}, u32[]{:S(2)}, u32[]{:S(2)}) collective-permute-start(bf16[80,1024]{1,0:T(8,128)(2,1)S(1)} %pad_maximum_fusion.refs_1_), channel_id=1, source_target_pairs={{0,64},{32,96},{64,0},{96,32},{1,65},{33,97},{65,1},{97,33},{2,66}... | collective-permute-start | bytes 491528 | tf_op jit(solution)/shard_map/ppermute | solution.py:22
  178.0 8.1 %collective-permute-start.32 = (bf16[80,1024]{1,0:T(8,128)(2,1)S(1)}, bf16[80,1024]{1,0:T(8,128)(2,1)S(1)}, u32[]{:S(2)}, u32[]{:S(2)}) collective-permute-start(bf16[80,1024]{1,0:T(8,128)(2,1)S(1)} %pad_maximum_fusion.refs_1_), channel_id=1, source_target_pairs={{0,16},{16,0},{1,17},{17,1},{2,18},{18,2},{3,19},{19,3},{4,20},{20... | collective-permute-start | bytes 491528 | tf_op jit(solution)/shard_map/ppermute | solution.py:22
  183.9 3.6 %copy-start.8 = (bf16[80,1024]{1,0:T(8,128)(2,1)}, bf16[80,1024]{1,0:T(8,128)(2,1)S(1)}, u32[]{:S(2)}) copy-start(bf16[80,1024]{1,0:T(8,128)(2,1)S(1)} %collective-permute-done.29.refs_2_) | copy-start | bytes 491524
  183.9 2.2 %collective-permute-start.33 = (bf16[80,1024]{1,0:T(8,128)(2,1)S(1)}, bf16[80,1024]{1,0:T(8,128)(2,1)S(1)}, u32[]{:S(2)}, u32[]{:S(2)}) collective-permute-start(bf16[80,1024]{1,0:T(8,128)(2,1)S(1)} %collective-permute-done.29.refs_2_), channel_id=1, source_target_pairs={{0,16},{16,0},{1,17},{17,1},{2,18},{18,2},{3,19},{19,3},{4,20},{20... | collective-permute-start | bytes 491528 | tf_op jit(solution)/shard_map/ppermute | solution.py:22
  183.9 3.6 %copy-start.9 = (bf16[80,1024]{1,0:T(8,128)(2,1)}, bf16[80,1024]{1,0:T(8,128)(2,1)S(1)}, u32[]{:S(2)}) copy-start(bf16[80,1024]{1,0:T(8,128)(2,1)S(1)} %collective-permute-done.30.refs_3_) | copy-start | bytes 491524
  183.9 2.2 %collective-permute-start.34 = (bf16[80,1024]{1,0:T(8,128)(2,1)S(1)}, bf16[80,1024]{1,0:T(8,128)(2,1)S(1)}, u32[]{:S(2)}, u32[]{:S(2)}) collective-permute-start(bf16[80,1024]{1,0:T(8,128)(2,1)S(1)} %collective-permute-done.30.refs_3_), channel_id=1, source_target_pairs={{0,16},{16,0},{1,17},{17,1},{2,18},{18,2},{3,19},{19,3},{4,20},{20... | collective-permute-start | bytes 491528 | tf_op jit(solution)/shard_map/ppermute | solution.py:22
  186.1 1.4 copy-start.10
  186.1 1.4 collective-permute-start.35
  186.1 1.4 copy-start.11
  186.1 1.4 copy-start.12
  186.2 1.4 copy-start.13
  (4 other events, 3.0 us)
